TPU v7x, 32 devices: a whole 2x2x4 slice. The times are simulated.
32 devices in a mesh: groups: 2 (over y), dp: 4 (over z), tensor: 4 (over x, core).
Axes of the slice: x: 2, y: 2, z: 4, core: 2. Of those that a mesh axis runs over, the one named last changes fastest.
Arguments:
- inputs: bfloat16 [2048, 11008], P(('groups', 'dp'), 'tensor'), parts along dimension 0, may hold values from -6 to 6
- out_grads: bfloat16 [2048, 4096], P(('groups', 'dp'), 'tensor'), parts along dimension 0
- in_proj: bfloat16 [11008, 64], P('tensor'), may hold values from -0.0546875 to 0.0546875
- out_proj: bfloat16 [4096, 64], P('tensor'), may hold values from -0.09375 to 0.09375
- seq_ids: int32 [2048], P(('groups', 'dp')), parts along dimension 0, may hold values from 0 to 63, as said below
- counts: int32 [128], P(('groups', 'dp')), parts along dimension 0, may hold values from 1 to 241, as said below
- queries: float32 [32, 4096], P(('groups', 'dp')), parts along dimension 0, may hold values from -128 to 128
Outputs:
- scores: float32 [32, 64], P('groups', 'dp'), parts along dimension 0
There are 2 independent parts, one for each index of `groups`. A program takes and returns all parts, laid end to end along the dimension named above; an argument that names none is the same for every part. Nothing has to cross between parts.
Inputs may be any that keep to these rules, and one draw needn't show every extreme that they name: `seq_ids`: never falls along the tokens; tokens 256 * b to 256 * (b + 1) - 1 belong to sequences 16 * b to 16 * (b + 1) - 1, each of which has one token or more. counts[s] is at most the number of tokens of sequence s; some sequence's count equals its number of tokens.
All inputs are finite; a program needn't handle non-finite values.
Results may differ from a plain program's by a relative error of at most 0.0003.
Values sent between devices are 32-bit elements; how exact they have to be, the bound alone decides.
No kernel may reach another device: no remote copies, remote signals or barrier semaphores. Data moves between devices by JAX's collectives and lax.ppermute only.
A program may use at most 128 MiB of HBM per device.

v0:
```python
import jax
import jax.numpy as jnp
from jax import lax
from jax.sharding import PartitionSpec as P

damping = 0.5


def token_weights(seq_ids, counts, first):
    seq_dev = counts.shape[0]
    local_ids = seq_ids - first
    slots = jnp.arange(seq_dev, dtype=jnp.int32)
    member = local_ids[:, None] == slots[None, :]
    starts = jnp.sum((local_ids[:, None] < slots[None, :]).astype(jnp.int32), axis=0)
    tok_start = jnp.sum(jnp.where(member, starts[None, :], 0), axis=1)
    tok_count = jnp.sum(jnp.where(member, counts[None, :], 0), axis=1)
    offset = jnp.arange(seq_ids.shape[0], dtype=jnp.int32) - tok_start
    scale = jnp.where(offset < tok_count, 1.0 / tok_count.astype(jnp.float32), 0.0)
    return member.astype(jnp.float32) * scale[:, None]


def per_example(projected, weights, rank):
    grad_part = projected[:, :rank]
    input_part = projected[:, rank:]
    spread = (weights[:, :, None] * grad_part[:, None, :]).reshape(projected.shape[0], -1)
    stacked = jnp.einsum("tk,tb->kb", spread, input_part, precision=lax.Precision.HIGHEST)
    return stacked.reshape(weights.shape[1], rank * rank)


def inner_rows(left, right):
    return jnp.einsum("ik,jk->ij", left, right, precision=lax.Precision.HIGHEST)


def solve_own(kernel, total, first, seq_dev):
    count_all = kernel.shape[0]
    damp = damping * total / count_all
    system = kernel + damp * jnp.eye(count_all, dtype=jnp.float32)
    factor = jnp.linalg.cholesky(system)
    picks = lax.dynamic_slice_in_dim(jnp.eye(count_all, dtype=jnp.float32), first, seq_dev, 1)
    return jax.scipy.linalg.cho_solve((factor, True), picks)


def per_device(inputs, out_grads, in_proj, out_proj, seq_ids, counts, queries):
    rank = in_proj.shape[1]
    seq_dev = counts.shape[0]
    first = lax.axis_index("dp") * seq_dev
    weights = token_weights(seq_ids, counts, first)
    projected = jnp.concatenate(
        [
            jnp.dot(out_grads, out_proj, preferred_element_type=jnp.float32),
            jnp.dot(inputs, in_proj, preferred_element_type=jnp.float32),
        ],
        axis=1,
    )
    summed = lax.psum(projected, "tensor")
    grads = per_example(summed, weights, rank)
    total = lax.psum(jnp.sum(grads * grads), "dp")
    every = lax.all_gather(grads, "dp", axis=0, tiled=True)
    kernel = inner_rows(every, every)
    solved = solve_own(kernel, total, first, seq_dev)
    precond = jnp.einsum("sk,sc->kc", every, solved, precision=lax.Precision.HIGHEST)
    return jnp.dot(
        lax.all_gather(queries, "dp", axis=0, tiled=True),
        precond,
        precision=lax.Precision.HIGHEST,
        preferred_element_type=jnp.float32,
    )


def solution(mesh):
    in_specs = (
        P(("groups", "dp"), "tensor"),
        P(("groups", "dp"), "tensor"),
        P("tensor", None),
        P("tensor", None),
        P(("groups", "dp")),
        P(("groups", "dp")),
        P(("groups", "dp"), None),
    )
    out_specs = P("groups", "dp")
    return jax.shard_map(
        per_device, mesh=mesh, in_specs=in_specs, out_specs=out_specs, check_vma=False
    )
```

profile of v0, /device:TPU:0, one launch (start us, length us, event | category | flops | bytes accessed | tf_op | source)
XLA Modules:
  0.0 102.7 jit_solution(9940382212446416986)
XLA Ops:
  6.5 1.5 %fusion.12 = f32[256,64]{0,1:T(8,128)S(1)} fusion(bf16[256,1024]{1,0:T(8,128)(2,1)} %param.8, bf16[1024,64]{0,1:T(8,128)(2,1)} %param.10), kind=kOutput, calls=%fused_computation.30 | convolution fusion | flops 33554432 | bytes 720896 | tf_op jit(solution)/shard_map/dot_general | solution.py:50
  8.1 1.3 %fusion.15 = f32[256,64]{0,1:T(8,128)S(1)} fusion(bf16[2752,64]{0,1:T(8,128)(2,1)} %param.9, bf16[256,2752]{0,1:T(8,128)(2,1)S(1)} %copy-done), kind=kOutput, calls=%fused_computation.33 | convolution fusion | flops 90177536 | bytes 1826816 | tf_op jit(solution)/shard_map/dot_general | solution.py:51
  9.4 0.7 pad_maximum_fusion
  10.2 0.1 convert_reduce_fusion
  10.4 33.9 %all-reduce.2.cloned.1.call-done = f32[256,128]{0,1:T(8,128)} async-done(((f32[256,128]{0,1:T(8,128)}), f32[256,128]{0,1:T(8,128)}) %all-reduce.2.cloned.1.call-update) | async-done | bytes 131088 | tf_op jit(solution)/shard_map/psum | solution.py:55
  44.4 0.8 slice.26
  45.2 0.1 broadcast_multiply_fusion
  45.3 2.6 %multiply_reduce_fusion = (f32[]{:T(128)}, f32[1024,64]{0,1:T(8,128)S(1)}) fusion(f32[256,1024]{0,1:T(8,128)S(1)} %bitcast.29, f32[256,128]{0,1:T(8,128)} %all-reduce.2.cloned.1.call-done), kind=kOutput, calls=%fused_computation.2 | convolution fusion | flops 201457664 | bytes 1376260 | tf_op jit(solution)/shard_map/tk,tb->kb/dot_general | solution.py:26
  48.0 0.2 copy.14
  48.2 0.9 reshape.71
  49.1 14.8 %all-gather = f32[4,4,4096]{2,1,0:T(4,128)S(1)} all-gather(f32[1,4,4096]{2,1,0:T(4,128)S(1)} %bitcast.30), channel_id=1, replica_groups=mesh['groups'=2,'dp'=4,'tensor'=4] {'dp'}, dimensions={0}, use_global_device_ids=true | all-gather | bytes 327680 | tf_op jit(solution)/shard_map/all_gather | solution.py:63
  63.9 0.1 reshape.73
  64.0 13.2 %psum.15 = f32[]{:T(128)} all-reduce(f32[]{:T(128)} %get-tuple-element.7), channel_id=1, replica_groups=mesh['groups'=2,'dp'=4,'tensor'=4] {'dp'}, use_global_device_ids=true, to_apply=%region_5.6 | all-reduce | flops 1 | bytes 8 | tf_op jit(solution)/shard_map/psum | solution.py:57
  77.8 0.9 all-gather.3.cloned.1.call-done
  78.7 2.6 %fusion.13 = f32[64,64]{1,0:T(8,128)S(1)} fusion(f32[64,4096]{1,0:T(8,128)} %all-gather.3.cloned.1.call-done), kind=kOutput, calls=%fused_computation.31 | convolution fusion | flops 201326592 | bytes 1064960 | tf_op jit(solution)/shard_map/ik,jk->ij/dot_general | solution.py:31
  81.5 5.8 %cholesky.17 = f32[64,64]{1,0:T(8,128)S(1)} custom-call(f32[64,64]{1,0:T(8,128)S(1)} %fusion.8), custom_call_target="Cholesky" | custom-call | tf_op jit(solution)/shard_map/jit(cholesky)/cholesky | solution.py:38
  87.3 0.6 compare_reduce_fusion
  88.0 0.7 fusion.2
  88.6 4.9 %custom-call.10 = f32[1,64,64]{1,2,0:T(8,128)S(1)} custom-call(f32[1,64,64]{2,1,0:T(8,128)S(1)} %fusion.2), custom_call_target="InvertDiagBlocksLowerTriangular" | custom-call | tf_op jit(solution)/shard_map/jit(_cho_solve)/triangular_solve | solution.py:40
  93.5 0.3 fusion.5
  93.8 0.2 fusion.3
  94.0 0.7 fusion.14
  94.7 0.4 convolution_bitcast_fusion
  95.1 0.7 copy.16
  (22 shorter events, 0.4 us)
Async XLA Ops:
  6.5 1.5 %copy-start = (bf16[256,2752]{0,1:T(8,128)(2,1)S(1)}, bf16[256,2752]{0,1:T(8,128)(2,1)}, u32[]{:S(2)}) copy-start(bf16[256,2752]{0,1:T(8,128)(2,1)} %param.7) | copy-start | bytes 4227076
  6.5 3.6 %copy-start.3 = (s32[256]{0:T(256)S(1)}, s32[256]{0:T(256)}, u32[]{:S(2)}) copy-start(s32[256]{0:T(256)} %param.11) | copy-start | bytes 3076
  6.5 3.8 %copy-start.4 = (s32[16]{0:T(128)S(1)}, s32[16]{0:T(128)}, u32[]{:S(2)}) copy-start(s32[16]{0:T(128)} %param.12) | copy-start | bytes 196
  6.5 37.8 %all-reduce.2.cloned.1.call-start = ((), (), s32[]{:S(2)}) async-start(), calls=%async_computation | async-start | bytes 262144 | tf_op jit(solution)/shard_map/psum | solution.py:55
  10.1 68.6 %all-gather.3.cloned.1.call-start = ((), (), s32[]{:S(2)}) async-start(), calls=%async_computation.1 | async-start | bytes 1310720 | tf_op jit(solution)/shard_map/all_gather | solution.py:58
  45.3 3.8 %copy-start.2 = (f32[4,4096]{1,0:T(4,128)S(1)}, f32[4,4096]{1,0:T(4,128)}, u32[]{:S(2)}) copy-start(f32[4,4096]{1,0:T(4,128)} %param.13) | copy-start | bytes 196612
  78.7 15.2 %copy-start.1 = (f32[64,4096]{1,0:T(8,128)S(1)}, f32[64,4096]{1,0:T(8,128)}, u32[]{:S(2)}) copy-start(f32[64,4096]{1,0:T(8,128)} %all-gather.3.cloned.1.call-done) | copy-start | bytes 3145732
Sparse Core Ops, SparseCore 0:
  10.2 34.0 all-reduce.1
  49.2 29.4 all-gather.2
where the time goes:
time: 103 us
  waiting for transfers between devices  34.9 us (34%)
  blocking collectives  28 us (27%)
  between operations  14.2 us (14%)
  other arithmetic  13.1 us (13%)
  matrix products  9.59 us (9%)
  local copies, waits for them, and re-layouts  2.91 us (3%)
    psum x1, waiting for transfers between devices, per_device(): summed = lax.psum(projected, 'tensor')  33.9 us
    all_gather x1, blocking collectives, per_device(): lax.all_gather(queries, 'dp', axis=0, tiled=True)  14.8 us
    psum x1, blocking collectives, per_device(): total = lax.psum(jnp.sum(grads * grads), 'dp')  13.2 us
    another operation x4, other arithmetic, solve_own(): factor = jnp.linalg.cholesky(system)  6.53 us
    another operation x2, other arithmetic, solve_own(): return jax.scipy.linalg.cho_solve((factor, True), picks)  5.55 us
    dot_general x1, matrix products, per_example(): jnp.einsum('tk,tb->kb', spread, input_part, precision=lax.Precision.HIGHEST)  2.63 us
    dot_general x1, matrix products, inner_rows(): return jnp.einsum('ik,jk->ij', left, right, precision=lax.Precision.HIGHEST)  2.6 us
  transfers between devices with their start and end apart: 2, of which 2 were waited for; matrix products, arithmetic and copies ran while one was open for 0% of the time, Pallas kernels for 0%

commit v1 on v0

v1 whole, which is shorter than its diff:
```python
import functools

import jax
import jax.numpy as jnp
from jax import lax
from jax.experimental import pallas as pl
from jax.experimental.pallas import tpu as pltpu
from jax.sharding import PartitionSpec as P

damping = 0.5
VMEM_LIMIT = 32 * 1024 * 1024
SMALL = 4


def token_weights(seq_ids, counts, first):
    local_ids = seq_ids - first
    slots = jnp.arange(counts.shape[0], dtype=jnp.int32)
    member = local_ids[None, :] == slots[:, None]
    starts = jnp.sum((local_ids[None, :] < slots[:, None]).astype(jnp.int32), axis=1)
    offset = jnp.arange(seq_ids.shape[0], dtype=jnp.int32)[None, :] - starts[:, None]
    scale = 1.0 / counts.astype(jnp.float32)
    return jnp.where(member & (offset < counts[:, None]), scale[:, None], 0.0)


def cuts_of(extent, step):
    return [(at, min(step, extent - at)) for at in range(0, extent, step)]


def two_terms(value):
    high = value.astype(jnp.bfloat16)
    low = (value - high.astype(jnp.float32)).astype(jnp.bfloat16)
    return high, low


def dot_nt(left, right):
    dims = (((1,), (1,)), ((), ()))
    lh, ll = two_terms(left)
    rh, rl = two_terms(right)
    mul = functools.partial(
        lax.dot_general, dimension_numbers=dims, preferred_element_type=jnp.float32
    )
    return mul(lh, rh) + (mul(lh, rl) + mul(ll, rh))


def project_kernel(parts, own, rank_ref, x_hbm, g_hbm, wx_hbm, wg_hbm, *rest):
    outs = rest[:parts]
    x_ref, g_ref, wx_ref, wg_ref, grad_ref, sems = rest[parts:]
    copies = []

    def fetch(src, dst, index):
        copy = pltpu.make_async_copy(src, dst, sems.at[index])
        copy.start()
        return copy

    g_cuts = cuts_of(g_ref.shape[1], 512)
    x_cuts = cuts_of(x_ref.shape[0], 768)
    wg_copy = fetch(wg_hbm, wg_ref, 0)
    index = 2
    g_copies = []
    for at, size in g_cuts:
        columns = pl.ds(at, size)
        g_copies.append(fetch(g_hbm.at[:, columns], g_ref.at[:, columns], index))
        index += 1
    wx_copy = fetch(wx_hbm, wx_ref, 1)
    x_copies = []
    for at, size in x_cuts:
        rows = pl.ds(at, size)
        x_copies.append(fetch(x_hbm.at[rows, :], x_ref.at[rows, :], index))
        index += 1

    def project(w_copy, w_ref, cuts, copies, ref, along):
        order = 1 if along == 0 else -1
        total = None
        w_copy.wait()
        for (at, size), copy in zip(cuts, copies):
            copy.wait()
            term = lax.dot_general(
                w_ref[:, at : at + size],
                ref[(slice(at, at + size), slice(None))[::order]],
                (((1,), (along,)), ((), ())),
                preferred_element_type=jnp.float32,
            )
            total = term if total is None else total + term
        return total

    grad_ref[...] = project(wg_copy, wg_ref, g_cuts, g_copies, g_ref, 1)
    inputs_t = project(wx_copy, wx_ref, x_cuts, x_copies, x_ref, 0)
    me = rank_ref[0]
    for m in range(parts):
        start = pl.multiple_of((me ^ m) * own, own)
        outs[m][:own, :] = grad_ref[pl.ds(start, own), :]
        outs[m][own:, :] = inputs_t


def project(inputs, out_grads, in_proj, out_proj, me, parts):
    rank = in_proj.shape[1]
    own = rank // parts
    tokens, hidden = inputs.shape
    width = out_grads.shape[1]
    copies = 2 + len(cuts_of(width, 512)) + len(cuts_of(hidden, 768))
    anywhere = pl.BlockSpec(memory_space=pltpu.HBM)
    return pl.pallas_call(
        functools.partial(project_kernel, parts, own),
        out_shape=[jax.ShapeDtypeStruct((own + rank, tokens), jnp.float32)] * parts,
        in_specs=[pl.BlockSpec(memory_space=pltpu.SMEM)] + [anywhere] * 4,
        out_specs=[pl.BlockSpec(memory_space=pltpu.VMEM)] * parts,
        scratch_shapes=[
            pltpu.VMEM((hidden, tokens), jnp.bfloat16),
            pltpu.VMEM((tokens, width), jnp.bfloat16),
            pltpu.VMEM((rank, hidden), jnp.bfloat16),
            pltpu.VMEM((rank, width), jnp.bfloat16),
            pltpu.VMEM((rank, tokens), jnp.float32),
            pltpu.SemaphoreType.DMA((copies,)),
        ],
        compiler_params=pltpu.CompilerParams(vmem_limit_bytes=VMEM_LIMIT),
        name="project",
    )(me, inputs.T, out_grads, in_proj.T, out_proj.T)


def grads_kernel(own, pair, weights_ref, *refs):
    parts, out_ref = refs[:-1], refs[-1]
    while len(parts) > 1:
        parts = [
            (a[...] + b[...]) if b is not None else a[...]
            for a, b in zip(parts[::2], list(parts[1::2]) + [None])
        ]
    summed = parts[0][...]
    weights = weights_ref[...]
    seqs = weights.shape[0]
    inputs_t = summed[own:, :]
    zero = jnp.zeros_like(inputs_t)
    right = jnp.concatenate(
        [
            jnp.concatenate([inputs_t if j == k else zero for k in range(pair)], axis=1)
            for j in range(pair)
        ],
        axis=0,
    )
    rows = []
    for i in range(own // pair):
        rows.append(
            jnp.concatenate(
                [weights * summed[pair * i + j : pair * i + j + 1, :] for j in range(pair)],
                axis=1,
            )
        )
    left = jnp.concatenate(rows, axis=0)
    out_ref[...] = dot_nt(left, right).reshape(own // pair, seqs, right.shape[0])


def gradients(weights, pieces, rank):
    own = pieces[0].shape[0] - rank
    pair = 128 // rank
    return pl.pallas_call(
        functools.partial(grads_kernel, own, pair),
        out_shape=jax.ShapeDtypeStruct(
            (own // pair, weights.shape[0], pair * rank), jnp.float32
        ),
        compiler_params=pltpu.CompilerParams(vmem_limit_bytes=VMEM_LIMIT),
        name="gradients",
    )(weights, *pieces)


def grams_kernel(count, me_ref, *refs):
    grads, queries, out_ref = refs[:count], refs[count:-1], refs[-1]
    me = me_ref[0]
    lanes = [
        jnp.concatenate([block[i] for block in grads], axis=0)
        for i in range(grads[0].shape[0])
    ]
    every = jnp.concatenate(lanes, axis=1)
    given = [block[...] for block in queries]
    ordered = []
    for place in range(count):
        chosen = given[0]
        for m in range(1, count):
            chosen = jnp.where((me ^ place) == m, given[m], chosen)
        ordered.append(chosen)
    both = jnp.concatenate([every] + ordered, axis=0)
    result = dot_nt(both, every)
    half = result.shape[0] // 2
    out_ref[...] = jnp.concatenate([result[:half, :], result[half:, :]], axis=1)


def grams(me, grads, queries):
    seqs = len(grads) * grads[0].shape[1]
    asked = len(queries) * queries[0].shape[0]
    whole = pl.BlockSpec(memory_space=pltpu.VMEM)
    return pl.pallas_call(
        functools.partial(grams_kernel, len(grads)),
        out_shape=jax.ShapeDtypeStruct(((seqs + asked) // 2, 2 * seqs), jnp.float32),
        in_specs=[pl.BlockSpec(memory_space=pltpu.SMEM)] + [whole] * (2 * len(grads)),
        out_specs=whole,
        compiler_params=pltpu.CompilerParams(vmem_limit_bytes=VMEM_LIMIT),
        name="grams",
    )(me, *grads, *queries)


def scales(count):
    first = 2.0 / (1.0 + 1.0 / count)
    off = count / (count + 1.0)
    steps = []
    while off > 1e-7:
        steps.append(2.0 / (2.0 - off * off))
        off = off * off / (2.0 - off * off)
    return first, steps


def solve_kernel(seqs, *refs):
    parts, out_ref = refs[:-1], refs[-1]
    packed = (parts[0][...] + parts[1][...]) + (parts[2][...] + parts[3][...])
    half = packed.shape[0]
    lane = lax.broadcasted_iota(jnp.int32, packed.shape, 1)
    turned = pltpu.roll(packed, seqs, 1)
    both = jnp.concatenate(
        [jnp.where(lane < seqs, packed, turned), jnp.where(lane < seqs, turned, packed)], axis=0
    )
    lane = lax.broadcasted_iota(jnp.int32, both.shape, 1)
    row = lax.broadcasted_iota(jnp.int32, both.shape, 0)
    unit = jnp.where((lane & (seqs - 1)) == row, 1.0, 0.0)
    total = jnp.sum(jnp.where(lane == row, both, 0.0)[:seqs], axis=(0, 1), keepdims=True)
    first, steps = scales(seqs)
    state = first * (both / total + unit * (damping / seqs))
    left_lanes = lane < seqs
    for at, step in enumerate(steps):
        high = state.astype(jnp.bfloat16).astype(jnp.float32)
        low = state - high
        left = jnp.where(left_lanes, high, low).astype(jnp.bfloat16)
        high = high[:seqs].astype(jnp.bfloat16)
        low = low[:seqs].astype(jnp.bfloat16)
        right = jnp.concatenate([high, high, low, low], axis=0)
        if at + 1 == len(steps):
            left, state = left[seqs:], state[seqs:]
        product = jnp.dot(
            jnp.concatenate([left, left], axis=1), right, preferred_element_type=jnp.float32
        )
        state = step * (2.0 * state - product)
    out_ref[...] = state[:, : out_ref.shape[1]]


def solve(parts, seqs, asked, seq_dev):
    return pl.pallas_call(
        functools.partial(solve_kernel, seqs),
        out_shape=jax.ShapeDtypeStruct((asked, seq_dev), jnp.float32),
        compiler_params=pltpu.CompilerParams(vmem_limit_bytes=VMEM_LIMIT),
        name="solve",
    )(*parts)


def from_partners(values, axis, size):
    taken = [values[0]]
    for m in range(1, size):
        taken.append(lax.ppermute(values[m], axis, [(i, i ^ m) for i in range(size)]))
    return taken


def finish_long(grads, queries, first, seq_dev):
    every = lax.all_gather(grads, "dp", axis=0)
    steps, seqs, lanes = grads.shape
    every = every.transpose(0, 2, 1, 3).reshape(-1, steps * lanes)
    asked = lax.all_gather(queries, "dp", axis=0, tiled=True)
    both = jnp.einsum(
        "ik,jk->ij", jnp.concatenate([every, asked], axis=0), every,
        precision=lax.Precision.HIGHEST,
    )
    both = lax.psum(both, "tensor")
    count = every.shape[0]
    kernel, products = both[:count], both[count:]
    damp = damping * jnp.trace(kernel) / count
    unit = jnp.eye(count, dtype=jnp.float32)
    factor = jnp.linalg.cholesky(kernel + damp * unit)
    picks = lax.dynamic_slice_in_dim(unit, first, seq_dev, 1)
    solved = jax.scipy.linalg.cho_solve((factor, True), picks)
    return jnp.dot(products, solved, precision=lax.Precision.HIGHEST)


def per_device(sizes, inputs, out_grads, in_proj, out_proj, seq_ids, counts, queries):
    parts, blocks = sizes
    rank = in_proj.shape[1]
    seq_dev = counts.shape[0]
    me = lax.axis_index("tensor")
    place = lax.axis_index("dp")
    first = place * seq_dev
    own = rank // parts
    pieces = project(inputs, out_grads, in_proj, out_proj, me.reshape(1), parts)
    asked = lax.dynamic_slice_in_dim(queries, me * (own * rank), own * rank, 1)
    weights = token_weights(seq_ids, counts, first)
    pieces = from_partners(pieces, "tensor", parts)
    grads = gradients(weights, pieces, rank)
    if blocks > SMALL:
        return finish_long(grads, asked, first, seq_dev)
    asked = from_partners([asked] * blocks, "dp", blocks)
    grads = from_partners([grads] * blocks, "dp", blocks)
    partial = grams(place.reshape(1), grads, asked)
    partial = from_partners([partial] * parts, "tensor", parts)
    return solve(partial, blocks * seq_dev, blocks * queries.shape[0], seq_dev)


def solution(mesh):
    in_specs = (
        P(("groups", "dp"), "tensor"),
        P(("groups", "dp"), "tensor"),
        P("tensor", None),
        P("tensor", None),
        P(("groups", "dp")),
        P(("groups", "dp")),
        P(("groups", "dp"), None),
    )
    sizes = (mesh.shape["tensor"], mesh.shape["dp"])
    return jax.shard_map(
        functools.partial(per_device, sizes),
        mesh=mesh,
        in_specs=in_specs,
        out_specs=P("groups", "dp"),
        check_vma=False,
    )
```

time: 103 us -> 35.8 us (0.35)
  blocking collectives: 28 us -> 0 us
  waiting for transfers between devices: 34.9 us -> 8.84 us
  starting transfers between devices: 0.04 us -> 17.5 us
  between operations: 14.2 us -> 0.05 us
  other arithmetic: 13.1 us -> 0.2 us
  matrix products: 9.59 us -> 0 us
  Pallas kernels: 0 us -> 4.64 us
  local copies, waits for them, and re-layouts: 2.91 us -> 4.32 us
    psum x1 -> x0, waiting for transfers between devices: 33.9 us -> none  [per_device(): summed = lax.psum(projected, 'tensor')]
    ppermute x0 -> x12, starting transfers between devices: none -> 17.5 us  [from_partners(): lax.ppermute(values[m], axis, [(i, i ^ m) for i in range(size)])]
    all_gather x1 -> x0, blocking collectives: 14.8 us -> none  [per_device(): lax.all_gather(queries, 'dp', axis=0, tiled=True)]
    psum x1 -> x0, blocking collectives: 13.2 us -> none  [per_device(): total = lax.psum(jnp.sum(grads * grads), 'dp')]
    another operation x6 -> x0, other arithmetic: 12.1 us -> none  [the longest x4 6.53 us: solve_own(): factor = jnp.linalg.cholesky(system)]
    dot_general x6 -> x0, matrix products: 9.15 us -> none  [the longest x1 2.63 us: per_example(): jnp.einsum('tk,tb->kb', spread, input_part, precision=lax.Precision.HIGHEST)]
    ppermute x0 -> x12, waiting for transfers between devices: none -> 8.84 us  [from_partners(): lax.ppermute(values[m], axis, [(i, i ^ m) for i in range(size)])]
    pallas_call x0 -> x4, Pallas kernels: none -> 4.64 us  [the longest x1 2.22 us: project(): pl.pallas_call(functools.partial(project_kernel, parts, own), out_shape=[...]
  transfers between devices with their start and end apart: 2 -> 12, of which waited for: 2 -> 5; matrix products, arithmetic and copies ran while one was open for 0% -> 1% of each run, Pallas kernels for 0% -> 0%
where the time goes in v1:
time: 35.8 us; the launch traced here: 35.6 us
  starting transfers between devices  17.5 us (49%)
  waiting for transfers between devices  8.84 us (25%)
  Pallas kernels  4.64 us (13%)
  local copies, waits for them, and re-layouts  4.32 us (12%)
    ppermute x12, starting transfers between devices, from_partners(): lax.ppermute(values[m], axis, [(i, i ^ m) for i in range(size)])  17.5 us
    ppermute x12, waiting for transfers between devices, from_partners(): lax.ppermute(values[m], axis, [(i, i ^ m) for i in range(size)])  8.84 us
    unnamed x14, local copies, waits for them, and re-layouts  4.32 us
    pallas_call x1, Pallas kernels, project(): pl.pallas_call(functools.partial(project_kernel, parts, own), out_shape=[...  2.22 us
    pallas_call x1, Pallas kernels, solve(): pl.pallas_call(functools.partial(solve_kernel, seqs), out_shape=jax.Shape...  1.82 us
  transfers between devices with their start and end apart: 12, of which 5 were waited for; matrix products, arithmetic and copies ran while one was open for 1% of the time, Pallas kernels for 0%

profile of v1, /device:TPU:0, one launch (start us, length us, event | category | flops | bytes accessed | tf_op | source)
XLA Modules:
  0.0 35.6 jit_solution(12354245037068974976)
XLA Ops:
  0.0 1.4 %copy-done.1 = bf16[256,2752]{0,1:T(8,128)(2,1)S(1)} copy-done((bf16[256,2752]{0,1:T(8,128)(2,1)S(1)}, bf16[256,2752]{0,1:T(8,128)(2,1)}, u32[]{:S(2)}) %copy-start.1) | copy-done | bytes 1409048
  1.4 1.0 %copy-done.2 = bf16[256,1024]{1,0:T(8,128)(2,1)S(1)} copy-done((bf16[256,1024]{1,0:T(8,128)(2,1)S(1)}, bf16[256,1024]{1,0:T(8,128)(2,1)}, u32[]{:S(2)}) %copy-start.2) | copy-done | bytes 524312
  2.4 1.0 %copy-done.3 = bf16[2752,64]{0,1:T(8,128)(2,1)S(1)} copy-done((bf16[2752,64]{0,1:T(8,128)(2,1)S(1)}, bf16[2752,64]{0,1:T(8,128)(2,1)}, u32[]{:S(2)}) %copy-start.3) | copy-done | bytes 352280
  3.4 0.9 %copy-done.4 = bf16[1024,64]{0,1:T(8,128)(2,1)S(1)} copy-done((bf16[1024,64]{0,1:T(8,128)(2,1)S(1)}, bf16[1024,64]{0,1:T(8,128)(2,1)}, u32[]{:S(2)}) %copy-start.4) | copy-done | bytes 131096
  4.3 2.2 %project.1 = (f32[80,256]{1,0:T(8,128)S(1)}, f32[80,256]{1,0:T(8,128)S(1)}, f32[80,256]{1,0:T(8,128)S(1)}, f32[80,256]{1,0:T(8,128)S(1)}) custom-call(s32[1]{0:T(128)} %bitcast.1.rank_ref, bf16[2752,256]{1,0:T(8,128)(2,1)S(1)} %bitcast.5, bf16[256,1024]{1,0:T(8,128)(2,1)S(1)} %copy-done.2, bf16[64,2752]{1,0:T(8,128)(2,1)S(1)} %bitcast.6, ...), custom_call_target="tpu_custom_call" | custom-call | tf_op jit(solution)/shard_map/project/pallas_call | solution.py:102
  6.5 0.5 %collective-permute-start = (f32[80,256]{1,0:T(8,128)S(1)}, f32[80,256]{1,0:T(8,128)S(1)}, u32[]{:S(2)}, u32[]{:S(2)}) collective-permute-start(f32[80,256]{1,0:T(8,128)S(1)} %get-tuple-element.10), channel_id=1, source_target_pairs={{0,1},{1,0},{2,3},{3,2},{4,5},{5,4},{6,7},{7,6},{8,9},{9,8},{10,11... | collective-permute-start | bytes 245768 | tf_op jit(solution)/shard_map/ppermute | solution.py:253
  7.1 2.6 %collective-permute-start.1 = (f32[80,256]{1,0:T(8,128)S(1)}, f32[80,256]{1,0:T(8,128)S(1)}, u32[]{:S(2)}, u32[]{:S(2)}) collective-permute-start(f32[80,256]{1,0:T(8,128)S(1)} %get-tuple-element.11), channel_id=1, source_target_pairs={{0,2},{1,3},{2,0},{3,1},{4,6},{5,7},{6,4},{7,5},{8,10},{9,11},{10,... | collective-permute-start | bytes 245768 | tf_op jit(solution)/shard_map/ppermute | solution.py:253
  9.7 0.1 convert_reduce_fusion
  9.8 0.1 fusion.1.weights_ref
  9.9 2.7 %collective-permute-done.1.refs_2_ = f32[80,256]{1,0:T(8,128)S(1)} collective-permute-done((f32[80,256]{1,0:T(8,128)S(1)}, f32[80,256]{1,0:T(8,128)S(1)}, u32[]{:S(2)}, u32[]{:S(2)}) %collective-permute-start.1) | collective-permute-done | bytes 81952 | tf_op jit(solution)/shard_map/ppermute | solution.py:253
  12.7 1.5 %collective-permute-done.2.refs_3_ = f32[80,256]{1,0:T(8,128)S(1)} collective-permute-done((f32[80,256]{1,0:T(8,128)S(1)}, f32[80,256]{1,0:T(8,128)S(1)}, u32[]{:S(2)}, u32[]{:S(2)}) %collective-permute-start.2) | collective-permute-done | bytes 81952 | tf_op jit(solution)/shard_map/ppermute | solution.py:253
  14.1 0.3 gradients.1.refs_0_
  14.4 1.9 %collective-permute-start.3 = (f32[8,16,128]{2,1,0:T(8,128)S(1)}, f32[8,16,128]{2,1,0:T(8,128)S(1)}, u32[]{:S(2)}, u32[]{:S(2)}) collective-permute-start(f32[8,16,128]{2,1,0:T(8,128)S(1)} %gradients.1.refs_0_), channel_id=1, source_target_pairs={{0,4},{4,0},{8,12},{12,8},{1,5},{5,1},{9,13},{13,9},{2,6},{6,2},{1... | collective-permute-start | bytes 196616 | tf_op jit(solution)/shard_map/ppermute | solution.py:253
  16.3 2.6 %collective-permute-start.4 = (f32[8,16,128]{2,1,0:T(8,128)S(1)}, f32[8,16,128]{2,1,0:T(8,128)S(1)}, u32[]{:S(2)}, u32[]{:S(2)}) collective-permute-start(f32[8,16,128]{2,1,0:T(8,128)S(1)} %gradients.1.refs_0_), channel_id=1, source_target_pairs={{0,8},{4,12},{8,0},{12,4},{1,9},{5,13},{9,1},{13,5},{2,10},{6,14},... | collective-permute-start | bytes 196616 | tf_op jit(solution)/shard_map/ppermute | solution.py:253
  18.9 0.9 %collective-permute-start.6 = (f32[4,1024]{1,0:T(4,128)S(1)}, f32[4,1024]{1,0:T(4,128)S(1)}, u32[]{:S(2)}, u32[]{:S(2)}) collective-permute-start(f32[4,1024]{1,0:T(4,128)S(1)} %constant_dynamic-slice_fusion.refs_4_), channel_id=1, source_target_pairs={{0,4},{4,0},{8,12},{12,8},{1,5},{5,1},{9,13},{13,9},{2,6},{6,2},{1... | collective-permute-start | bytes 49160 | tf_op jit(solution)/shard_map/ppermute | solution.py:253
  19.8 3.5 %collective-permute-start.7 = (f32[4,1024]{1,0:T(4,128)S(1)}, f32[4,1024]{1,0:T(4,128)S(1)}, u32[]{:S(2)}, u32[]{:S(2)}) collective-permute-start(f32[4,1024]{1,0:T(4,128)S(1)} %constant_dynamic-slice_fusion.refs_4_), channel_id=1, source_target_pairs={{0,8},{4,12},{8,0},{12,4},{1,9},{5,13},{9,1},{13,5},{2,10},{6,14},... | collective-permute-start | bytes 49160 | tf_op jit(solution)/shard_map/ppermute | solution.py:253
  23.3 3.3 %collective-permute-start.8 = (f32[4,1024]{1,0:T(4,128)S(1)}, f32[4,1024]{1,0:T(4,128)S(1)}, u32[]{:S(2)}, u32[]{:S(2)}) collective-permute-start(f32[4,1024]{1,0:T(4,128)S(1)} %constant_dynamic-slice_fusion.refs_4_), channel_id=1, source_target_pairs={{0,12},{4,8},{8,4},{12,0},{1,13},{5,9},{9,5},{13,1},{2,14},{6,10},... | collective-permute-start | bytes 49160 | tf_op jit(solution)/shard_map/ppermute | solution.py:253
  26.6 2.2 %collective-permute-done.8.refs_7_ = f32[4,1024]{1,0:T(4,128)S(1)} collective-permute-done((f32[4,1024]{1,0:T(4,128)S(1)}, f32[4,1024]{1,0:T(4,128)S(1)}, u32[]{:S(2)}, u32[]{:S(2)}) %collective-permute-start.8) | collective-permute-done | bytes 16416 | tf_op jit(solution)/shard_map/ppermute | solution.py:253
  28.8 0.3 grams.1.refs_0_
  29.2 1.4 %collective-permute-start.10 = (f32[40,128]{1,0:T(8,128)S(1)}, f32[40,128]{1,0:T(8,128)S(1)}, u32[]{:S(2)}, u32[]{:S(2)}) collective-permute-start(f32[40,128]{1,0:T(8,128)S(1)} %grams.1.refs_0_), channel_id=1, source_target_pairs={{0,2},{1,3},{2,0},{3,1},{4,6},{5,7},{6,4},{7,5},{8,10},{9,11},{10,... | collective-permute-start | bytes 61448 | tf_op jit(solution)/shard_map/ppermute | solution.py:253
  30.5 0.8 %collective-permute-start.9 = (f32[40,128]{1,0:T(8,128)S(1)}, f32[40,128]{1,0:T(8,128)S(1)}, u32[]{:S(2)}, u32[]{:S(2)}) collective-permute-start(f32[40,128]{1,0:T(8,128)S(1)} %grams.1.refs_0_), channel_id=1, source_target_pairs={{0,1},{1,0},{2,3},{3,2},{4,5},{5,4},{6,7},{7,6},{8,9},{9,8},{10,11... | collective-permute-start | bytes 61448 | tf_op jit(solution)/shard_map/ppermute | solution.py:253
  31.3 1.6 %collective-permute-done.10.refs_2_ = f32[40,128]{1,0:T(8,128)S(1)} collective-permute-done((f32[40,128]{1,0:T(8,128)S(1)}, f32[40,128]{1,0:T(8,128)S(1)}, u32[]{:S(2)}, u32[]{:S(2)}) %collective-permute-start.10) | collective-permute-done | bytes 20512 | tf_op jit(solution)/shard_map/ppermute | solution.py:253
  33.0 0.8 %collective-permute-done.11.refs_3_ = f32[40,128]{1,0:T(8,128)S(1)} collective-permute-done((f32[40,128]{1,0:T(8,128)S(1)}, f32[40,128]{1,0:T(8,128)S(1)}, u32[]{:S(2)}, u32[]{:S(2)}) %collective-permute-start.11) | collective-permute-done | bytes 20512 | tf_op jit(solution)/shard_map/ppermute | solution.py:253
  33.8 1.8 %solve.1 = f32[16,16]{1,0:T(8,128)} custom-call(f32[40,128]{1,0:T(8,128)S(1)} %grams.1.refs_0_, f32[40,128]{1,0:T(8,128)S(1)} %collective-permute-done.9.refs_1_, f32[40,128]{1,0:T(8,128)S(1)} %collective-permute-done.10.refs_2_, f32[40,128]{1,0:T(8,128)S(1)} %collective-permute-done.11.refs_3_), custom_call_target="tpu_custom_call" | custom-call | tf_op jit(solution)/shard_map/solve/pallas_call | solution.py:242
  (23 shorter events, 0.1 us)
Async XLA Ops:
  0.0 18.9 %copy-start = (f32[4,4096]{1,0:T(4,128)S(1)}, f32[4,4096]{1,0:T(4,128)}, u32[]{:S(2)}) copy-start(f32[4,4096]{1,0:T(4,128)} %param.13) | copy-start | bytes 196612
  0.0 9.7 %copy-start.5 = (s32[256]{0:T(256)S(1)}, s32[256]{0:T(256)}, u32[]{:S(2)}) copy-start(s32[256]{0:T(256)} %param.11) | copy-start | bytes 3076
  0.0 9.8 %copy-start.6 = (s32[16]{0:T(128)S(1)}, s32[16]{0:T(128)}, u32[]{:S(2)}) copy-start(s32[16]{0:T(128)} %param.12) | copy-start | bytes 196
  0.0 1.4 %copy-start.1 = (bf16[256,2752]{0,1:T(8,128)(2,1)S(1)}, bf16[256,2752]{0,1:T(8,128)(2,1)}, u32[]{:S(2)}) copy-start(bf16[256,2752]{0,1:T(8,128)(2,1)} %param.7) | copy-start | bytes 4227076
  1.4 1.0 %copy-start.2 = (bf16[256,1024]{1,0:T(8,128)(2,1)S(1)}, bf16[256,1024]{1,0:T(8,128)(2,1)}, u32[]{:S(2)}) copy-start(bf16[256,1024]{1,0:T(8,128)(2,1)} %g_hbm.1) | copy-start | bytes 1572868
  2.4 1.0 %copy-start.3 = (bf16[2752,64]{0,1:T(8,128)(2,1)S(1)}, bf16[2752,64]{0,1:T(8,128)(2,1)}, u32[]{:S(2)}) copy-start(bf16[2752,64]{0,1:T(8,128)(2,1)} %param.9) | copy-start | bytes 1056772
  3.4 0.9 %copy-start.4 = (bf16[1024,64]{0,1:T(8,128)(2,1)S(1)}, bf16[1024,64]{0,1:T(8,128)(2,1)}, u32[]{:S(2)}) copy-start(bf16[1024,64]{0,1:T(8,128)(2,1)} %param.10) | copy-start | bytes 393220
  6.5 3.4 %collective-permute-start = (f32[80,256]{1,0:T(8,128)S(1)}, f32[80,256]{1,0:T(8,128)S(1)}, u32[]{:S(2)}, u32[]{:S(2)}) collective-permute-start(f32[80,256]{1,0:T(8,128)S(1)} %get-tuple-element.10), channel_id=1, source_target_pairs={{0,1},{1,0},{2,3},{3,2},{4,5},{5,4},{6,7},{7,6},{8,9},{9,8},{10,11... | collective-permute-start | bytes 245768 | tf_op jit(solution)/shard_map/ppermute | solution.py:253
  7.1 5.6 %collective-permute-start.1 = (f32[80,256]{1,0:T(8,128)S(1)}, f32[80,256]{1,0:T(8,128)S(1)}, u32[]{:S(2)}, u32[]{:S(2)}) collective-permute-start(f32[80,256]{1,0:T(8,128)S(1)} %get-tuple-element.11), channel_id=1, source_target_pairs={{0,2},{1,3},{2,0},{3,1},{4,6},{5,7},{6,4},{7,5},{8,10},{9,11},{10,... | collective-permute-start | bytes 245768 | tf_op jit(solution)/shard_map/ppermute | solution.py:253
  9.6 4.5 %collective-permute-start.2 = (f32[80,256]{1,0:T(8,128)S(1)}, f32[80,256]{1,0:T(8,128)S(1)}, u32[]{:S(2)}, u32[]{:S(2)}) collective-permute-start(f32[80,256]{1,0:T(8,128)S(1)} %get-tuple-element.12), channel_id=1, source_target_pairs={{0,3},{1,2},{2,1},{3,0},{4,7},{5,6},{6,5},{7,4},{8,11},{9,10},{10,... | collective-permute-start | bytes 245768 | tf_op jit(solution)/shard_map/ppermute | solution.py:253
  14.4 14.4 %collective-permute-start.3 = (f32[8,16,128]{2,1,0:T(8,128)S(1)}, f32[8,16,128]{2,1,0:T(8,128)S(1)}, u32[]{:S(2)}, u32[]{:S(2)}) collective-permute-start(f32[8,16,128]{2,1,0:T(8,128)S(1)} %gradients.1.refs_0_), channel_id=1, source_target_pairs={{0,4},{4,0},{8,12},{12,8},{1,5},{5,1},{9,13},{13,9},{2,6},{6,2},{1... | collective-permute-start | bytes 196616 | tf_op jit(solution)/shard_map/ppermute | solution.py:253
  16.3 12.5 %collective-permute-start.4 = (f32[8,16,128]{2,1,0:T(8,128)S(1)}, f32[8,16,128]{2,1,0:T(8,128)S(1)}, u32[]{:S(2)}, u32[]{:S(2)}) collective-permute-start(f32[8,16,128]{2,1,0:T(8,128)S(1)} %gradients.1.refs_0_), channel_id=1, source_target_pairs={{0,8},{4,12},{8,0},{12,4},{1,9},{5,13},{9,1},{13,5},{2,10},{6,14},... | collective-permute-start | bytes 196616 | tf_op jit(solution)/shard_map/ppermute | solution.py:253
  18.9 9.9 %collective-permute-start.5 = (f32[8,16,128]{2,1,0:T(8,128)S(1)}, f32[8,16,128]{2,1,0:T(8,128)S(1)}, u32[]{:S(2)}, u32[]{:S(2)}) collective-permute-start(f32[8,16,128]{2,1,0:T(8,128)S(1)} %gradients.1.refs_0_), channel_id=1, source_target_pairs={{0,12},{4,8},{8,4},{12,0},{1,13},{5,9},{9,5},{13,1},{2,14},{6,10},... | collective-permute-start | bytes 196616 | tf_op jit(solution)/shard_map/ppermute | solution.py:253
  18.9 4.4 %collective-permute-start.6 = (f32[4,1024]{1,0:T(4,128)S(1)}, f32[4,1024]{1,0:T(4,128)S(1)}, u32[]{:S(2)}, u32[]{:S(2)}) collective-permute-start(f32[4,1024]{1,0:T(4,128)S(1)} %constant_dynamic-slice_fusion.refs_4_), channel_id=1, source_target_pairs={{0,4},{4,0},{8,12},{12,8},{1,5},{5,1},{9,13},{13,9},{2,6},{6,2},{1... | collective-permute-start | bytes 49160 | tf_op jit(solution)/shard_map/ppermute | solution.py:253
  19.8 6.8 %collective-permute-start.7 = (f32[4,1024]{1,0:T(4,128)S(1)}, f32[4,1024]{1,0:T(4,128)S(1)}, u32[]{:S(2)}, u32[]{:S(2)}) collective-permute-start(f32[4,1024]{1,0:T(4,128)S(1)} %constant_dynamic-slice_fusion.refs_4_), channel_id=1, source_target_pairs={{0,8},{4,12},{8,0},{12,4},{1,9},{5,13},{9,1},{13,5},{2,10},{6,14},... | collective-permute-start | bytes 49160 | tf_op jit(solution)/shard_map/ppermute | solution.py:253
  23.3 5.5 %collective-permute-start.8 = (f32[4,1024]{1,0:T(4,128)S(1)}, f32[4,1024]{1,0:T(4,128)S(1)}, u32[]{:S(2)}, u32[]{:S(2)}) collective-permute-start(f32[4,1024]{1,0:T(4,128)S(1)} %constant_dynamic-slice_fusion.refs_4_), channel_id=1, source_target_pairs={{0,12},{4,8},{8,4},{12,0},{1,13},{5,9},{9,5},{13,1},{2,14},{6,10},... | collective-permute-start | bytes 49160 | tf_op jit(solution)/shard_map/ppermute | solution.py:253
  29.2 3.8 %collective-permute-start.10 = (f32[40,128]{1,0:T(8,128)S(1)}, f32[40,128]{1,0:T(8,128)S(1)}, u32[]{:S(2)}, u32[]{:S(2)}) collective-permute-start(f32[40,128]{1,0:T(8,128)S(1)} %grams.1.refs_0_), channel_id=1, source_target_pairs={{0,2},{1,3},{2,0},{3,1},{4,6},{5,7},{6,4},{7,5},{8,10},{9,11},{10,... | collective-permute-start | bytes 61448 | tf_op jit(solution)/shard_map/ppermute | solution.py:253
  30.5 3.2 %collective-permute-start.11 = (f32[40,128]{1,0:T(8,128)S(1)}, f32[40,128]{1,0:T(8,128)S(1)}, u32[]{:S(2)}, u32[]{:S(2)}) collective-permute-start(f32[40,128]{1,0:T(8,128)S(1)} %grams.1.refs_0_), channel_id=1, source_target_pairs={{0,3},{1,2},{2,1},{3,0},{4,7},{5,6},{6,5},{7,4},{8,11},{9,10},{10,... | collective-permute-start | bytes 61448 | tf_op jit(solution)/shard_map/ppermute | solution.py:253
  30.5 3.2 %collective-permute-start.9 = (f32[40,128]{1,0:T(8,128)S(1)}, f32[40,128]{1,0:T(8,128)S(1)}, u32[]{:S(2)}, u32[]{:S(2)}) collective-permute-start(f32[40,128]{1,0:T(8,128)S(1)} %grams.1.refs_0_), channel_id=1, source_target_pairs={{0,1},{1,0},{2,3},{3,2},{4,5},{5,4},{6,7},{7,6},{8,9},{9,8},{10,11... | collective-permute-start | bytes 61448 | tf_op jit(solution)/shard_map/ppermute | solution.py:253

commit v2 on v1

--- a/solution.py
+++ b/solution.py
@@ -43,8 +43,8 @@
 
 
 def project_kernel(parts, own, rank_ref, x_hbm, g_hbm, wx_hbm, wg_hbm, *rest):
-    outs = rest[:parts]
-    x_ref, g_ref, wx_ref, wg_ref, grad_ref, sems = rest[parts:]
+    outs = rest[:2]
+    x_ref, g_ref, wx_ref, wg_ref, grad_ref, sems = rest[2:]
     copies = []
 
     def fetch(src, dst, index):
@@ -86,10 +86,11 @@
     grad_ref[...] = project(wg_copy, wg_ref, g_cuts, g_copies, g_ref, 1)
     inputs_t = project(wx_copy, wx_ref, x_cuts, x_copies, x_ref, 0)
     me = rank_ref[0]
-    for m in range(parts):
-        start = pl.multiple_of((me ^ m) * own, own)
-        outs[m][:own, :] = grad_ref[pl.ds(start, own), :]
-        outs[m][own:, :] = inputs_t
+    for out, side in zip(outs, (me & 1, (me & 1) ^ 1)):
+        for place in range(parts // 2):
+            start = pl.multiple_of((2 * place + side) * own, own)
+            out[place * own : (place + 1) * own, :] = grad_ref[pl.ds(start, own), :]
+        out[parts // 2 * own :, :] = inputs_t
 
 
 def project(inputs, out_grads, in_proj, out_proj, me, parts):
@@ -98,12 +99,13 @@
     tokens, hidden = inputs.shape
     width = out_grads.shape[1]
     copies = 2 + len(cuts_of(width, 512)) + len(cuts_of(hidden, 768))
-    anywhere = pl.BlockSpec(memory_space=pltpu.HBM)
+    arrays = (inputs.T, out_grads, in_proj.T, out_proj.T)
+    in_hbm = pl.BlockSpec(memory_space=pltpu.HBM)
     return pl.pallas_call(
         functools.partial(project_kernel, parts, own),
-        out_shape=[jax.ShapeDtypeStruct((own + rank, tokens), jnp.float32)] * parts,
-        in_specs=[pl.BlockSpec(memory_space=pltpu.SMEM)] + [anywhere] * 4,
-        out_specs=[pl.BlockSpec(memory_space=pltpu.VMEM)] * parts,
+        out_shape=[jax.ShapeDtypeStruct((parts // 2 * own + rank, tokens), jnp.float32)] * 2,
+        in_specs=[pl.BlockSpec(memory_space=pltpu.SMEM)] + [in_hbm] * len(arrays),
+        out_specs=[pl.BlockSpec(memory_space=pltpu.VMEM)] * 2,
         scratch_shapes=[
             pltpu.VMEM((hidden, tokens), jnp.bfloat16),
             pltpu.VMEM((tokens, width), jnp.bfloat16),
@@ -114,17 +116,36 @@
         ],
         compiler_params=pltpu.CompilerParams(vmem_limit_bytes=VMEM_LIMIT),
         name="project",
-    )(me, inputs.T, out_grads, in_proj.T, out_proj.T)
+    )(me, *(pltpu.with_memory_space_constraint(array, pltpu.HBM) for array in arrays))
+
+
+def halve_kernel(parts, own, rank_ref, kept_ref, came_ref, keep_ref, send_ref, sum_ref):
+    sum_ref[...] = kept_ref[...] + came_ref[...]
+    me = rank_ref[0]
+    for out, place in ((keep_ref, me // 2), (send_ref, me // 2 ^ 1)):
+        start = pl.multiple_of(place * own, own)
+        out[:own, :] = sum_ref[pl.ds(start, own), :]
+        out[own:, :] = sum_ref[parts // 2 * own :, :]
+
+
+def halve(kept, came, me, parts, own):
+    rows, tokens = kept.shape
+    left = rows - (parts // 2 - 1) * own
+    whole = pl.BlockSpec(memory_space=pltpu.VMEM)
+    return pl.pallas_call(
+        functools.partial(halve_kernel, parts, own),
+        out_shape=[jax.ShapeDtypeStruct((left, tokens), jnp.float32)] * 2,
+        in_specs=[pl.BlockSpec(memory_space=pltpu.SMEM), whole, whole],
+        out_specs=[whole] * 2,
+        scratch_shapes=[pltpu.VMEM((rows, tokens), jnp.float32)],
+        compiler_params=pltpu.CompilerParams(vmem_limit_bytes=VMEM_LIMIT),
+        name="halve",
+    )(me, kept, came)
 
 
 def grads_kernel(own, pair, weights_ref, *refs):
-    parts, out_ref = refs[:-1], refs[-1]
-    while len(parts) > 1:
-        parts = [
-            (a[...] + b[...]) if b is not None else a[...]
-            for a, b in zip(parts[::2], list(parts[1::2]) + [None])
-        ]
-    summed = parts[0][...]
+    kept_ref, came_ref, out_ref = refs
+    summed = kept_ref[...] + came_ref[...]
     weights = weights_ref[...]
     seqs = weights.shape[0]
     inputs_t = summed[own:, :]
@@ -247,10 +268,14 @@
     )(*parts)
 
 
+def from_partner(value, axis, size, m):
+    return lax.ppermute(value, axis, [(i, i ^ m) for i in range(size)])
+
+
 def from_partners(values, axis, size):
     taken = [values[0]]
     for m in range(1, size):
-        taken.append(lax.ppermute(values[m], axis, [(i, i ^ m) for i in range(size)]))
+        taken.append(from_partner(values[m], axis, size, m))
     return taken
 
 
@@ -282,14 +307,18 @@
     place = lax.axis_index("dp")
     first = place * seq_dev
     own = rank // parts
-    pieces = project(inputs, out_grads, in_proj, out_proj, me.reshape(1), parts)
+    rank_of = me.reshape(1)
+    kept, sent = project(inputs, out_grads, in_proj, out_proj, rank_of, parts)
     asked = lax.dynamic_slice_in_dim(queries, me * (own * rank), own * rank, 1)
     weights = token_weights(seq_ids, counts, first)
-    pieces = from_partners(pieces, "tensor", parts)
-    grads = gradients(weights, pieces, rank)
+    came = from_partner(sent, "tensor", parts, 1)
+    kept, sent = halve(kept, came, rank_of, parts, own)
+    came = from_partner(sent, "tensor", parts, 2)
+    grads = gradients(weights, [kept, came], rank)
     if blocks > SMALL:
         return finish_long(grads, asked, first, seq_dev)
     asked = from_partners([asked] * blocks, "dp", blocks)
+    grads, *asked = lax.optimization_barrier((grads, *asked))
     grads = from_partners([grads] * blocks, "dp", blocks)
     partial = grams(place.reshape(1), grads, asked)
     partial = from_partners([partial] * parts, "tensor", parts)

time: 35.8 us -> 33.1 us (0.925)
  waiting for transfers between devices: 8.84 us -> 13.1 us
  local copies, waits for them, and re-layouts: 4.32 us -> 0.84 us
  starting transfers between devices: 17.5 us -> 14.1 us
    ppermute x12 -> x11, waiting for transfers between devices: 8.84 us -> 13.1 us  [from_partner(): return lax.ppermute(value, axis, [(i, i ^ m) for i in range(size)])]
    unnamed x14 -> x6, local copies, waits for them, and re-layouts: 4.32 us -> 0.84 us
    ppermute x12 -> x11, starting transfers between devices: 17.5 us -> 14.1 us  [from_partner(): return lax.ppermute(value, axis, [(i, i ^ m) for i in range(size)])]
  transfers between devices with their start and end apart: 12 -> 11, of which waited for: 5 -> 6; matrix products, arithmetic and copies ran while one was open for 1% -> 1% of each run, Pallas kernels for 0% -> 7%
where the time goes in v2:
time: 33.1 us; the launch traced here: 32.9 us
  starting transfers between devices  14.1 us (43%)
  waiting for transfers between devices  13.1 us (40%)
  Pallas kernels  4.55 us (14%)
  local copies, waits for them, and re-layouts  0.84 us (3%)
    ppermute x11, starting transfers between devices, from_partner(): return lax.ppermute(value, axis, [(i, i ^ m) for i in range(size)])  14.1 us
    ppermute x11, waiting for transfers between devices, from_partner(): return lax.ppermute(value, axis, [(i, i ^ m) for i in range(size)])  13.1 us
    pallas_call x1, Pallas kernels, project(): pl.pallas_call(functools.partial(project_kernel, parts, own), out_shape=[...  2.12 us
    pallas_call x1, Pallas kernels, solve(): pl.pallas_call(functools.partial(solve_kernel, seqs), out_shape=jax.Shape...  1.81 us
    unnamed x6, local copies, waits for them, and re-layouts  0.84 us
  transfers between devices with their start and end apart: 11, of which 6 were waited for; matrix products, arithmetic and copies ran while one was open for 1% of the time, Pallas kernels for 7%

profile of v2, /device:TPU:0, one launch (start us, length us, event | category | flops | bytes accessed | tf_op | source)
XLA Modules:
  0.0 32.9 jit_solution(4814943620925973146)
XLA Ops:
  0.0 0.8 %copy-done = f32[4,4096]{1,0:T(4,128)S(1)} copy-done((f32[4,4096]{1,0:T(4,128)S(1)}, f32[4,4096]{1,0:T(4,128)}, u32[]{:S(2)}) %copy-start) | copy-done | bytes 65560
  0.8 3.0 %collective-permute-start.2 = (f32[4,1024]{1,0:T(4,128)S(1)}, f32[4,1024]{1,0:T(4,128)S(1)}, u32[]{:S(2)}, u32[]{:S(2)}) collective-permute-start(f32[4,1024]{1,0:T(4,128)S(1)} %constant_dynamic-slice_fusion.refs_4_), channel_id=1, source_target_pairs={{0,4},{4,0},{8,12},{12,8},{1,5},{5,1},{9,13},{13,9},{2,6},{6,2},{1... | collective-permute-start | bytes 49160 | tf_op jit(solution)/shard_map/ppermute | solution.py:272
  3.9 2.6 %collective-permute-start.3 = (f32[4,1024]{1,0:T(4,128)S(1)}, f32[4,1024]{1,0:T(4,128)S(1)}, u32[]{:S(2)}, u32[]{:S(2)}) collective-permute-start(f32[4,1024]{1,0:T(4,128)S(1)} %constant_dynamic-slice_fusion.refs_4_), channel_id=1, source_target_pairs={{0,8},{4,12},{8,0},{12,4},{1,9},{5,13},{9,1},{13,5},{2,10},{6,14},... | collective-permute-start | bytes 49160 | tf_op jit(solution)/shard_map/ppermute | solution.py:272
  6.5 2.1 %project.1 = (f32[96,256]{1,0:T(8,128)S(1)}, f32[96,256]{1,0:T(8,128)S(1)}) custom-call(s32[1]{0:T(128)} %bitcast.1.rank_ref, bf16[2752,256]{1,0:T(8,128)(2,1)} %bitcast.5, bf16[256,1024]{1,0:T(8,128)(2,1)} %g_hbm.1, bf16[64,2752]{1,0:T(8,128)(2,1)} %bitcast.6, bf16[64,1024]{1,0:T(8,128)(2,1)} %bitcast.7), custom_call_target="tpu_custom_call" | custom-call | tf_op jit(solution)/shard_map/project/pallas_call | solution.py:104
  8.6 0.1 collective-permute-start
  8.7 0.1 convert_reduce_fusion
  8.8 1.1 %collective-permute-done.came_ref = f32[96,256]{1,0:T(8,128)S(1)} collective-permute-done((f32[96,256]{1,0:T(8,128)S(1)}, f32[96,256]{1,0:T(8,128)S(1)}, u32[]{:S(2)}, u32[]{:S(2)}) %collective-permute-start) | collective-permute-done | bytes 98336 | tf_op jit(solution)/shard_map/ppermute | solution.py:272
  10.0 1.8 %collective-permute-start.1 = (f32[80,256]{1,0:T(8,128)S(1)}, f32[80,256]{1,0:T(8,128)S(1)}, u32[]{:S(2)}, u32[]{:S(2)}) collective-permute-start(f32[80,256]{1,0:T(8,128)S(1)} %get-tuple-element.17), channel_id=1, source_target_pairs={{0,2},{1,3},{2,0},{3,1},{4,6},{5,7},{6,4},{7,5},{8,10},{9,11},{10,... | collective-permute-start | bytes 245768 | tf_op jit(solution)/shard_map/ppermute | solution.py:272
  11.8 0.1 fusion.1.weights_ref
  11.8 2.7 %collective-permute-done.1.refs_1_ = f32[80,256]{1,0:T(8,128)S(1)} collective-permute-done((f32[80,256]{1,0:T(8,128)S(1)}, f32[80,256]{1,0:T(8,128)S(1)}, u32[]{:S(2)}, u32[]{:S(2)}) %collective-permute-start.1) | collective-permute-done | bytes 81952 | tf_op jit(solution)/shard_map/ppermute | solution.py:272
  14.5 0.3 gradients.1.refs_0_
  14.8 0.0 collective-permute-done.2.refs_5_
  14.8 0.0 collective-permute-done.4.refs_7_
  14.8 1.0 %collective-permute-start.5 = (f32[8,16,128]{2,1,0:T(8,128)S(1)}, f32[8,16,128]{2,1,0:T(8,128)S(1)}, u32[]{:S(2)}, u32[]{:S(2)}) collective-permute-start(f32[8,16,128]{2,1,0:T(8,128)S(1)} %gradients.1.refs_0_), channel_id=1, source_target_pairs={{0,4},{4,0},{8,12},{12,8},{1,5},{5,1},{9,13},{13,9},{2,6},{6,2},{1... | collective-permute-start | bytes 196616 | tf_op jit(solution)/shard_map/ppermute | solution.py:272
  15.8 3.5 %collective-permute-start.6 = (f32[8,16,128]{2,1,0:T(8,128)S(1)}, f32[8,16,128]{2,1,0:T(8,128)S(1)}, u32[]{:S(2)}, u32[]{:S(2)}) collective-permute-start(f32[8,16,128]{2,1,0:T(8,128)S(1)} %gradients.1.refs_0_), channel_id=1, source_target_pairs={{0,8},{4,12},{8,0},{12,4},{1,9},{5,13},{9,1},{13,5},{2,10},{6,14},... | collective-permute-start | bytes 196616 | tf_op jit(solution)/shard_map/ppermute | solution.py:272
  19.3 4.1 %collective-permute-done.6.refs_2_ = f32[8,16,128]{2,1,0:T(8,128)S(1)} collective-permute-done((f32[8,16,128]{2,1,0:T(8,128)S(1)}, f32[8,16,128]{2,1,0:T(8,128)S(1)}, u32[]{:S(2)}, u32[]{:S(2)}) %collective-permute-start.6) | collective-permute-done | bytes 65568 | tf_op jit(solution)/shard_map/ppermute | solution.py:272
  23.4 2.0 %collective-permute-done.7.refs_3_ = f32[8,16,128]{2,1,0:T(8,128)S(1)} collective-permute-done((f32[8,16,128]{2,1,0:T(8,128)S(1)}, f32[8,16,128]{2,1,0:T(8,128)S(1)}, u32[]{:S(2)}, u32[]{:S(2)}) %collective-permute-start.7) | collective-permute-done | bytes 65568 | tf_op jit(solution)/shard_map/ppermute | solution.py:272
  25.4 0.3 %grams.1.refs_0_ = f32[40,128]{1,0:T(8,128)S(1)} custom-call(s32[1]{0:T(128)} %bitcast.me_ref, f32[8,16,128]{2,1,0:T(8,128)S(1)} %gradients.1.refs_0_, f32[8,16,128]{2,1,0:T(8,128)S(1)} %collective-permute-done.5.refs_1_, f32[8,16,128]{2,1,0:T(8,128)S(1)} %collective-permute-done.6.refs_2_, f32[8,16,128]{2,1,0:T(8,128)S(1)} %collective-permute-done.7.refs_3_, ...), custom_call_target="tpu_custom_call" | custom-call | tf_op jit(solution)/shard_map/grams/pallas_call | solution.py:210
  25.7 0.0 collective-permute-start.10
  25.7 1.6 %collective-permute-start.8 = (f32[40,128]{1,0:T(8,128)S(1)}, f32[40,128]{1,0:T(8,128)S(1)}, u32[]{:S(2)}, u32[]{:S(2)}) collective-permute-start(f32[40,128]{1,0:T(8,128)S(1)} %grams.1.refs_0_), channel_id=1, source_target_pairs={{0,1},{1,0},{2,3},{3,2},{4,5},{5,4},{6,7},{7,6},{8,9},{9,8},{10,11... | collective-permute-start | bytes 61448 | tf_op jit(solution)/shard_map/ppermute | solution.py:272
  27.3 0.5 %collective-permute-start.9 = (f32[40,128]{1,0:T(8,128)S(1)}, f32[40,128]{1,0:T(8,128)S(1)}, u32[]{:S(2)}, u32[]{:S(2)}) collective-permute-start(f32[40,128]{1,0:T(8,128)S(1)} %grams.1.refs_0_), channel_id=1, source_target_pairs={{0,2},{1,3},{2,0},{3,1},{4,6},{5,7},{6,4},{7,5},{8,10},{9,11},{10,... | collective-permute-start | bytes 61448 | tf_op jit(solution)/shard_map/ppermute | solution.py:272
  27.9 1.2 %collective-permute-done.10.refs_3_ = f32[40,128]{1,0:T(8,128)S(1)} collective-permute-done((f32[40,128]{1,0:T(8,128)S(1)}, f32[40,128]{1,0:T(8,128)S(1)}, u32[]{:S(2)}, u32[]{:S(2)}) %collective-permute-start.10) | collective-permute-done | bytes 20512 | tf_op jit(solution)/shard_map/ppermute | solution.py:272
  29.1 2.0 %collective-permute-done.9.refs_2_ = f32[40,128]{1,0:T(8,128)S(1)} collective-permute-done((f32[40,128]{1,0:T(8,128)S(1)}, f32[40,128]{1,0:T(8,128)S(1)}, u32[]{:S(2)}, u32[]{:S(2)}) %collective-permute-start.9) | collective-permute-done | bytes 20512 | tf_op jit(solution)/shard_map/ppermute | solution.py:272
  31.1 1.8 %solve.1 = f32[16,16]{1,0:T(8,128)} custom-call(f32[40,128]{1,0:T(8,128)S(1)} %grams.1.refs_0_, f32[40,128]{1,0:T(8,128)S(1)} %collective-permute-done.8.refs_1_, f32[40,128]{1,0:T(8,128)S(1)} %collective-permute-done.9.refs_2_, f32[40,128]{1,0:T(8,128)S(1)} %collective-permute-done.10.refs_3_), custom_call_target="tpu_custom_call" | custom-call | tf_op jit(solution)/shard_map/solve/pallas_call | solution.py:263
  (14 shorter events, 0.1 us)
Async XLA Ops:
  0.0 0.8 %copy-start = (f32[4,4096]{1,0:T(4,128)S(1)}, f32[4,4096]{1,0:T(4,128)}, u32[]{:S(2)}) copy-start(f32[4,4096]{1,0:T(4,128)} %param.13) | copy-start | bytes 196612
  0.0 8.7 %copy-start.2 = (s32[16]{0:T(128)S(1)}, s32[16]{0:T(128)}, u32[]{:S(2)}) copy-start(s32[16]{0:T(128)} %param.12) | copy-start | bytes 196
  0.0 8.7 %copy-start.1 = (s32[256]{0:T(256)S(1)}, s32[256]{0:T(256)}, u32[]{:S(2)}) copy-start(s32[256]{0:T(256)} %param.11) | copy-start | bytes 3076
  0.8 14.0 %collective-permute-start.2 = (f32[4,1024]{1,0:T(4,128)S(1)}, f32[4,1024]{1,0:T(4,128)S(1)}, u32[]{:S(2)}, u32[]{:S(2)}) collective-permute-start(f32[4,1024]{1,0:T(4,128)S(1)} %constant_dynamic-slice_fusion.refs_4_), channel_id=1, source_target_pairs={{0,4},{4,0},{8,12},{12,8},{1,5},{5,1},{9,13},{13,9},{2,6},{6,2},{1... | collective-permute-start | bytes 49160 | tf_op jit(solution)/shard_map/ppermute | solution.py:272
  3.9 11.0 %collective-permute-start.3 = (f32[4,1024]{1,0:T(4,128)S(1)}, f32[4,1024]{1,0:T(4,128)S(1)}, u32[]{:S(2)}, u32[]{:S(2)}) collective-permute-start(f32[4,1024]{1,0:T(4,128)S(1)} %constant_dynamic-slice_fusion.refs_4_), channel_id=1, source_target_pairs={{0,8},{4,12},{8,0},{12,4},{1,9},{5,13},{9,1},{13,5},{2,10},{6,14},... | collective-permute-start | bytes 49160 | tf_op jit(solution)/shard_map/ppermute | solution.py:272
  6.5 8.4 %collective-permute-start.4 = (f32[4,1024]{1,0:T(4,128)S(1)}, f32[4,1024]{1,0:T(4,128)S(1)}, u32[]{:S(2)}, u32[]{:S(2)}) collective-permute-start(f32[4,1024]{1,0:T(4,128)S(1)} %constant_dynamic-slice_fusion.refs_4_), channel_id=1, source_target_pairs={{0,12},{4,8},{8,4},{12,0},{1,13},{5,9},{9,5},{13,1},{2,14},{6,10},... | collective-permute-start | bytes 49160 | tf_op jit(solution)/shard_map/ppermute | solution.py:272
  8.6 1.4 %collective-permute-start = (f32[96,256]{1,0:T(8,128)S(1)}, f32[96,256]{1,0:T(8,128)S(1)}, u32[]{:S(2)}, u32[]{:S(2)}) collective-permute-start(f32[96,256]{1,0:T(8,128)S(1)} %get-tuple-element.15), channel_id=1, source_target_pairs={{0,1},{1,0},{2,3},{3,2},{4,5},{5,4},{6,7},{7,6},{8,9},{9,8},{10,11... | collective-permute-start | bytes 294920 | tf_op jit(solution)/shard_map/ppermute | solution.py:272
  10.0 4.6 %collective-permute-start.1 = (f32[80,256]{1,0:T(8,128)S(1)}, f32[80,256]{1,0:T(8,128)S(1)}, u32[]{:S(2)}, u32[]{:S(2)}) collective-permute-start(f32[80,256]{1,0:T(8,128)S(1)} %get-tuple-element.17), channel_id=1, source_target_pairs={{0,2},{1,3},{2,0},{3,1},{4,6},{5,7},{6,4},{7,5},{8,10},{9,11},{10,... | collective-permute-start | bytes 245768 | tf_op jit(solution)/shard_map/ppermute | solution.py:272
  14.8 4.5 %collective-permute-start.5 = (f32[8,16,128]{2,1,0:T(8,128)S(1)}, f32[8,16,128]{2,1,0:T(8,128)S(1)}, u32[]{:S(2)}, u32[]{:S(2)}) collective-permute-start(f32[8,16,128]{2,1,0:T(8,128)S(1)} %gradients.1.refs_0_), channel_id=1, source_target_pairs={{0,4},{4,0},{8,12},{12,8},{1,5},{5,1},{9,13},{13,9},{2,6},{6,2},{1... | collective-permute-start | bytes 196616 | tf_op jit(solution)/shard_map/ppermute | solution.py:272
  15.8 7.6 %collective-permute-start.6 = (f32[8,16,128]{2,1,0:T(8,128)S(1)}, f32[8,16,128]{2,1,0:T(8,128)S(1)}, u32[]{:S(2)}, u32[]{:S(2)}) collective-permute-start(f32[8,16,128]{2,1,0:T(8,128)S(1)} %gradients.1.refs_0_), channel_id=1, source_target_pairs={{0,8},{4,12},{8,0},{12,4},{1,9},{5,13},{9,1},{13,5},{2,10},{6,14},... | collective-permute-start | bytes 196616 | tf_op jit(solution)/shard_map/ppermute | solution.py:272
  19.3 6.1 %collective-permute-start.7 = (f32[8,16,128]{2,1,0:T(8,128)S(1)}, f32[8,16,128]{2,1,0:T(8,128)S(1)}, u32[]{:S(2)}, u32[]{:S(2)}) collective-permute-start(f32[8,16,128]{2,1,0:T(8,128)S(1)} %gradients.1.refs_0_), channel_id=1, source_target_pairs={{0,12},{4,8},{8,4},{12,0},{1,13},{5,9},{9,5},{13,1},{2,14},{6,10},... | collective-permute-start | bytes 196616 | tf_op jit(solution)/shard_map/ppermute | solution.py:272
  25.7 3.4 %collective-permute-start.10 = (f32[40,128]{1,0:T(8,128)S(1)}, f32[40,128]{1,0:T(8,128)S(1)}, u32[]{:S(2)}, u32[]{:S(2)}) collective-permute-start(f32[40,128]{1,0:T(8,128)S(1)} %grams.1.refs_0_), channel_id=1, source_target_pairs={{0,3},{1,2},{2,1},{3,0},{4,7},{5,6},{6,5},{7,4},{8,11},{9,10},{10,... | collective-permute-start | bytes 61448 | tf_op jit(solution)/shard_map/ppermute | solution.py:272
  25.7 3.4 %collective-permute-start.8 = (f32[40,128]{1,0:T(8,128)S(1)}, f32[40,128]{1,0:T(8,128)S(1)}, u32[]{:S(2)}, u32[]{:S(2)}) collective-permute-start(f32[40,128]{1,0:T(8,128)S(1)} %grams.1.refs_0_), channel_id=1, source_target_pairs={{0,1},{1,0},{2,3},{3,2},{4,5},{5,4},{6,7},{7,6},{8,9},{9,8},{10,11... | collective-permute-start | bytes 61448 | tf_op jit(solution)/shard_map/ppermute | solution.py:272
  27.3 3.8 %collective-permute-start.9 = (f32[40,128]{1,0:T(8,128)S(1)}, f32[40,128]{1,0:T(8,128)S(1)}, u32[]{:S(2)}, u32[]{:S(2)}) collective-permute-start(f32[40,128]{1,0:T(8,128)S(1)} %grams.1.refs_0_), channel_id=1, source_target_pairs={{0,2},{1,3},{2,0},{3,1},{4,6},{5,7},{6,4},{7,5},{8,10},{9,11},{10,... | collective-permute-start | bytes 61448 | tf_op jit(solution)/shard_map/ppermute | solution.py:272

commit v3 on v2

--- a/solution.py
+++ b/solution.py
@@ -166,55 +166,48 @@
             )
         )
     left = jnp.concatenate(rows, axis=0)
-    out_ref[...] = dot_nt(left, right).reshape(own // pair, seqs, right.shape[0])
-
-
-def gradients(weights, pieces, rank):
+    made = dot_nt(left, right).reshape(out_ref.shape[1:])
+    for place in range(out_ref.shape[0]):
+        out_ref[place] = made
+
+
+def gradients(weights, pieces, rank, copies):
     own = pieces[0].shape[0] - rank
     pair = 128 // rank
     return pl.pallas_call(
         functools.partial(grads_kernel, own, pair),
         out_shape=jax.ShapeDtypeStruct(
-            (own // pair, weights.shape[0], pair * rank), jnp.float32
+            (copies, own // pair, weights.shape[0], pair * rank), jnp.float32
         ),
         compiler_params=pltpu.CompilerParams(vmem_limit_bytes=VMEM_LIMIT),
         name="gradients",
     )(weights, *pieces)
 
 
-def grams_kernel(count, me_ref, *refs):
-    grads, queries, out_ref = refs[:count], refs[count:-1], refs[-1]
-    me = me_ref[0]
+def grams_kernel(grads_ref, queries_ref, out_ref):
+    count, steps = grads_ref.shape[:2]
     lanes = [
-        jnp.concatenate([block[i] for block in grads], axis=0)
-        for i in range(grads[0].shape[0])
+        jnp.concatenate([grads_ref[place, i] for place in range(count)], axis=0)
+        for i in range(steps)
     ]
     every = jnp.concatenate(lanes, axis=1)
-    given = [block[...] for block in queries]
-    ordered = []
-    for place in range(count):
-        chosen = given[0]
-        for m in range(1, count):
-            chosen = jnp.where((me ^ place) == m, given[m], chosen)
-        ordered.append(chosen)
-    both = jnp.concatenate([every] + ordered, axis=0)
+    both = jnp.concatenate([every] + [queries_ref[place] for place in range(count)], axis=0)
     result = dot_nt(both, every)
     half = result.shape[0] // 2
-    out_ref[...] = jnp.concatenate([result[:half, :], result[half:, :]], axis=1)
-
-
-def grams(me, grads, queries):
-    seqs = len(grads) * grads[0].shape[1]
-    asked = len(queries) * queries[0].shape[0]
-    whole = pl.BlockSpec(memory_space=pltpu.VMEM)
-    return pl.pallas_call(
-        functools.partial(grams_kernel, len(grads)),
-        out_shape=jax.ShapeDtypeStruct(((seqs + asked) // 2, 2 * seqs), jnp.float32),
-        in_specs=[pl.BlockSpec(memory_space=pltpu.SMEM)] + [whole] * (2 * len(grads)),
-        out_specs=whole,
+    packed = jnp.concatenate([result[:half, :], result[half:, :]], axis=1)
+    for place in range(out_ref.shape[0]):
+        out_ref[place] = packed
+
+
+def grams(grads, queries, copies):
+    seqs = grads.shape[0] * grads.shape[2]
+    asked = queries.shape[0] * queries.shape[1]
+    return pl.pallas_call(
+        grams_kernel,
+        out_shape=jax.ShapeDtypeStruct((copies, (seqs + asked) // 2, 2 * seqs), jnp.float32),
         compiler_params=pltpu.CompilerParams(vmem_limit_bytes=VMEM_LIMIT),
         name="grams",
-    )(me, *grads, *queries)
+    )(grads, queries)
 
 
 def scales(count):
@@ -227,10 +220,10 @@
     return first, steps
 
 
-def solve_kernel(seqs, *refs):
-    parts, out_ref = refs[:-1], refs[-1]
-    packed = (parts[0][...] + parts[1][...]) + (parts[2][...] + parts[3][...])
-    half = packed.shape[0]
+def solve_kernel(seqs, place_ref, parts_ref, out_ref):
+    packed = parts_ref[0]
+    for part in range(1, parts_ref.shape[0]):
+        packed = packed + parts_ref[part]
     lane = lax.broadcasted_iota(jnp.int32, packed.shape, 1)
     turned = pltpu.roll(packed, seqs, 1)
     both = jnp.concatenate(
@@ -256,27 +249,29 @@
             jnp.concatenate([left, left], axis=1), right, preferred_element_type=jnp.float32
         )
         state = step * (2.0 * state - product)
-    out_ref[...] = state[:, : out_ref.shape[1]]
-
-
-def solve(parts, seqs, asked, seq_dev):
+    turn = 2 * seqs - place_ref[0] * out_ref.shape[1]
+    out_ref[...] = pltpu.roll(state, turn, 1)[:, : out_ref.shape[1]]
+
+
+def solve(place, parts, seqs, asked, seq_dev):
     return pl.pallas_call(
         functools.partial(solve_kernel, seqs),
         out_shape=jax.ShapeDtypeStruct((asked, seq_dev), jnp.float32),
+        in_specs=[
+            pl.BlockSpec(memory_space=pltpu.SMEM),
+            pl.BlockSpec(memory_space=pltpu.VMEM),
+        ],
         compiler_params=pltpu.CompilerParams(vmem_limit_bytes=VMEM_LIMIT),
         name="solve",
-    )(*parts)
+    )(place, parts)
 
 
 def from_partner(value, axis, size, m):
     return lax.ppermute(value, axis, [(i, i ^ m) for i in range(size)])
 
 
-def from_partners(values, axis, size):
-    taken = [values[0]]
-    for m in range(1, size):
-        taken.append(from_partner(values[m], axis, size, m))
-    return taken
+def swap(copies, axis):
+    return lax.all_to_all(copies, axis, 0, 0, tiled=True)
 
 
 def finish_long(grads, queries, first, seq_dev):
@@ -314,15 +309,14 @@
     came = from_partner(sent, "tensor", parts, 1)
     kept, sent = halve(kept, came, rank_of, parts, own)
     came = from_partner(sent, "tensor", parts, 2)
-    grads = gradients(weights, [kept, came], rank)
+    grads = gradients(weights, [kept, came], rank, blocks if blocks <= SMALL else 1)
     if blocks > SMALL:
-        return finish_long(grads, asked, first, seq_dev)
-    asked = from_partners([asked] * blocks, "dp", blocks)
-    grads, *asked = lax.optimization_barrier((grads, *asked))
-    grads = from_partners([grads] * blocks, "dp", blocks)
-    partial = grams(place.reshape(1), grads, asked)
-    partial = from_partners([partial] * parts, "tensor", parts)
-    return solve(partial, blocks * seq_dev, blocks * queries.shape[0], seq_dev)
+        return finish_long(grads[0], asked, first, seq_dev)
+    asked = swap(jnp.broadcast_to(asked, (blocks, *asked.shape)), "dp")
+    grads, asked = lax.optimization_barrier((grads, asked))
+    partial = grams(swap(grads, "dp"), asked, parts)
+    summed = swap(partial, "tensor")
+    return solve(place.reshape(1), summed, blocks * seq_dev, blocks * queries.shape[0], seq_dev)
 
 
 def solution(mesh):

time: 33.1 us -> 38.8 us (1.17)
  blocking collectives: 0 us -> 20 us
  waiting for transfers between devices: 13.1 us -> 4.06 us
  starting transfers between devices: 14.1 us -> 7.94 us
  local copies, waits for them, and re-layouts: 0.84 us -> 1.49 us
    all_to_all x0 -> x2, blocking collectives: none -> 20 us  [swap(): return lax.all_to_all(copies, axis, 0, 0, tiled=True)]
    ppermute x11 -> x2, starting transfers between devices: 14.1 us -> 1.63 us  [from_partner(): return lax.ppermute(value, axis, [(i, i ^ m) for i in range(size)])]
    ppermute x11 -> x2, waiting for transfers between devices: 13.1 us -> 4.06 us  [from_partner(): return lax.ppermute(value, axis, [(i, i ^ m) for i in range(size)])]
    all_to_all x0 -> x1, starting transfers between devices: none -> 6.32 us  [swap(): return lax.all_to_all(copies, axis, 0, 0, tiled=True)]
    broadcast_in_dim x0 -> x1, local copies, waits for them, and re-layouts: none -> 0.64 us  [per_device(): asked = swap(jnp.broadcast_to(asked, (blocks, *asked.shape)), 'dp')]
  transfers between devices with their start and end apart: 11 -> 3, of which waited for: 6 -> 2; matrix products, arithmetic and copies ran while one was open for 1% -> 1% of each run, Pallas kernels for 7% -> 6%
where the time goes in v3:
time: 38.8 us; the launch traced here: 38.4 us
  blocking collectives  20 us (52%)
  starting transfers between devices  7.94 us (20%)
  Pallas kernels  4.62 us (12%)
  waiting for transfers between devices  4.06 us (10%)
  local copies, waits for them, and re-layouts  1.49 us (4%)
    all_to_all x2, blocking collectives, swap(): return lax.all_to_all(copies, axis, 0, 0, tiled=True)  20 us
    all_to_all x1, starting transfers between devices, swap(): return lax.all_to_all(copies, axis, 0, 0, tiled=True)  6.32 us
    ppermute x2, waiting for transfers between devices, from_partner(): return lax.ppermute(value, axis, [(i, i ^ m) for i in range(size)])  4.06 us
    pallas_call x1, Pallas kernels, project(): pl.pallas_call(functools.partial(project_kernel, parts, own), out_shape=[...  2.12 us
    pallas_call x1, Pallas kernels, solve(): pl.pallas_call(functools.partial(solve_kernel, seqs), out_shape=jax.Shape...  1.88 us
    ppermute x2, starting transfers between devices, from_partner(): return lax.ppermute(value, axis, [(i, i ^ m) for i in range(size)])  1.63 us
    unnamed x6, local copies, waits for them, and re-layouts  0.84 us
  transfers between devices with their start and end apart: 3, of which 2 were waited for; matrix products, arithmetic and copies ran while one was open for 1% of the time, Pallas kernels for 6%

profile of v3, /device:TPU:0, one launch (start us, length us, event | category | flops | bytes accessed | tf_op | source)
XLA Modules:
  0.0 38.4 jit_solution(2690250898643353836)
XLA Ops:
  0.0 0.0 copy-start
  0.0 0.0 copy-start.2
  0.0 0.0 copy-start.1
  0.0 0.8 %copy-done = f32[4,4096]{1,0:T(4,128)S(1)} copy-done((f32[4,4096]{1,0:T(4,128)S(1)}, f32[4,4096]{1,0:T(4,128)}, u32[]{:S(2)}) %copy-start) | copy-done | bytes 65560
  0.8 0.6 %broadcast_in_dim.16 = f32[4,4,1024]{2,1,0:T(4,128)} broadcast(f32[4,1024]{1,0:T(4,128)S(1)} %constant_dynamic-slice_fusion), dimensions={1,2} | broadcast | bytes 81920 | tf_op jit(solution)/shard_map/broadcast_in_dim | solution.py:315
  1.5 6.3 %all-to-all-start = ((f32[4,4,1024]{2,1,0:T(4,128)}), f32[4,4,1024]{2,1,0:T(4,128)S(1)}, u32[]{:S(2)}, u32[]{:S(2)}) async-start(f32[4,4,1024]{2,1,0:T(4,128)} %broadcast_in_dim.16), calls=%async_computation | async-start | bytes 131072 | tf_op jit(solution)/shard_map/all_to_all | solution.py:274
  7.8 2.1 %project.1 = (f32[96,256]{1,0:T(8,128)S(1)}, f32[96,256]{1,0:T(8,128)S(1)}) custom-call(s32[1]{0:T(128)} %bitcast.1.rank_ref, bf16[2752,256]{1,0:T(8,128)(2,1)} %bitcast.5, bf16[256,1024]{1,0:T(8,128)(2,1)} %g_hbm.1, bf16[64,2752]{1,0:T(8,128)(2,1)} %bitcast.6, bf16[64,1024]{1,0:T(8,128)(2,1)} %bitcast.7), custom_call_target="tpu_custom_call" | custom-call | tf_op jit(solution)/shard_map/project/pallas_call | solution.py:104
  9.9 0.1 collective-permute-start
  10.0 0.0 copy-done.2
  10.0 0.0 copy-done.1
  10.1 0.1 convert_reduce_fusion
  10.2 1.1 %collective-permute-done.came_ref = f32[96,256]{1,0:T(8,128)S(1)} collective-permute-done((f32[96,256]{1,0:T(8,128)S(1)}, f32[96,256]{1,0:T(8,128)S(1)}, u32[]{:S(2)}, u32[]{:S(2)}) %collective-permute-start) | collective-permute-done | bytes 98336 | tf_op jit(solution)/shard_map/ppermute | solution.py:270
  11.3 1.6 %collective-permute-start.1 = (f32[80,256]{1,0:T(8,128)S(1)}, f32[80,256]{1,0:T(8,128)S(1)}, u32[]{:S(2)}, u32[]{:S(2)}) collective-permute-start(f32[80,256]{1,0:T(8,128)S(1)} %get-tuple-element.14), channel_id=1, source_target_pairs={{0,2},{1,3},{2,0},{3,1},{4,6},{5,7},{6,4},{7,5},{8,10},{9,11},{10,... | collective-permute-start | bytes 245768 | tf_op jit(solution)/shard_map/ppermute | solution.py:270
  12.9 0.1 fusion.1.weights_ref
  13.0 2.9 %collective-permute-done.1.refs_1_ = f32[80,256]{1,0:T(8,128)S(1)} collective-permute-done((f32[80,256]{1,0:T(8,128)S(1)}, f32[80,256]{1,0:T(8,128)S(1)}, u32[]{:S(2)}, u32[]{:S(2)}) %collective-permute-start.1) | collective-permute-done | bytes 81952 | tf_op jit(solution)/shard_map/ppermute | solution.py:270
  15.9 0.3 gradients.1
  16.2 0.0 all-to-all-done.queries_ref
  16.2 13.3 %all_to_all.15.grads_ref = f32[4,8,16,128]{3,2,1,0:T(8,128)S(1)} all-to-all(f32[4,8,16,128]{3,2,1,0:T(8,128)S(1)} %gradients.1), channel_id=1, replica_groups=mesh['groups'=2,'dp'=4,'tensor'=4] {'dp'}, dimensions={0} | all-to-all | bytes 524288 | tf_op jit(solution)/shard_map/all_to_all | solution.py:274
  29.4 0.3 grams.1
  29.8 6.8 %all_to_all.16.parts_ref = f32[4,40,128]{2,1,0:T(8,128)S(1)} all-to-all(f32[4,40,128]{2,1,0:T(8,128)S(1)} %grams.1), channel_id=1, replica_groups=mesh['groups'=2,'dp'=4,'tensor'=4] {'tensor'}, dimensions={0} | all-to-all | bytes 163840 | tf_op jit(solution)/shard_map/all_to_all | solution.py:274
  36.5 1.9 %solve.1 = f32[16,16]{1,0:T(8,128)} custom-call(s32[1]{0:T(128)} %bitcast.place_ref, f32[4,40,128]{2,1,0:T(8,128)S(1)} %all_to_all.16.parts_ref), custom_call_target="tpu_custom_call" | custom-call | tf_op jit(solution)/shard_map/solve/pallas_call | solution.py:257
  (4 shorter events, 0.0 us)
Async XLA Ops:
  0.0 0.8 %copy-start = (f32[4,4096]{1,0:T(4,128)S(1)}, f32[4,4096]{1,0:T(4,128)}, u32[]{:S(2)}) copy-start(f32[4,4096]{1,0:T(4,128)} %param.13) | copy-start | bytes 196612
  0.0 10.0 %copy-start.2 = (s32[16]{0:T(128)S(1)}, s32[16]{0:T(128)}, u32[]{:S(2)}) copy-start(s32[16]{0:T(128)} %param.12) | copy-start | bytes 196
  0.0 10.0 %copy-start.1 = (s32[256]{0:T(256)S(1)}, s32[256]{0:T(256)}, u32[]{:S(2)}) copy-start(s32[256]{0:T(256)} %param.11) | copy-start | bytes 3076
  1.5 14.7 %all-to-all-start = ((f32[4,4,1024]{2,1,0:T(4,128)}), f32[4,4,1024]{2,1,0:T(4,128)S(1)}, u32[]{:S(2)}, u32[]{:S(2)}) async-start(f32[4,4,1024]{2,1,0:T(4,128)} %broadcast_in_dim.16), calls=%async_computation | async-start | bytes 131072 | tf_op jit(solution)/shard_map/all_to_all | solution.py:274
  9.9 1.4 %collective-permute-start = (f32[96,256]{1,0:T(8,128)S(1)}, f32[96,256]{1,0:T(8,128)S(1)}, u32[]{:S(2)}, u32[]{:S(2)}) collective-permute-start(f32[96,256]{1,0:T(8,128)S(1)} %get-tuple-element.12), channel_id=1, source_target_pairs={{0,1},{1,0},{2,3},{3,2},{4,5},{5,4},{6,7},{7,6},{8,9},{9,8},{10,11... | collective-permute-start | bytes 294920 | tf_op jit(solution)/shard_map/ppermute | solution.py:270
  11.3 4.6 %collective-permute-start.1 = (f32[80,256]{1,0:T(8,128)S(1)}, f32[80,256]{1,0:T(8,128)S(1)}, u32[]{:S(2)}, u32[]{:S(2)}) collective-permute-start(f32[80,256]{1,0:T(8,128)S(1)} %get-tuple-element.14), channel_id=1, source_target_pairs={{0,2},{1,3},{2,0},{3,1},{4,6},{5,7},{6,4},{7,5},{8,10},{9,11},{10,... | collective-permute-start | bytes 245768 | tf_op jit(solution)/shard_map/ppermute | solution.py:270

commit v4 on v2

--- a/solution.py
+++ b/solution.py
@@ -185,6 +185,7 @@
 def grams_kernel(count, me_ref, *refs):
     grads, queries, out_ref = refs[:count], refs[count:-1], refs[-1]
     me = me_ref[0]
+    grads, queries = grads[::-1], queries[::-1]
     lanes = [
         jnp.concatenate([block[i] for block in grads], axis=0)
         for i in range(grads[0].shape[0])
@@ -229,8 +230,7 @@
 
 def solve_kernel(seqs, *refs):
     parts, out_ref = refs[:-1], refs[-1]
-    packed = (parts[0][...] + parts[1][...]) + (parts[2][...] + parts[3][...])
-    half = packed.shape[0]
+    packed = parts[0][...] + parts[1][...]
     lane = lax.broadcasted_iota(jnp.int32, packed.shape, 1)
     turned = pltpu.roll(packed, seqs, 1)
     both = jnp.concatenate(
@@ -268,15 +268,25 @@
     )(*parts)
 
 
+def add_kernel(left_ref, right_ref, out_ref):
+    out_ref[...] = left_ref[...] + right_ref[...]
+
+
+def add(left, right):
+    return pl.pallas_call(
+        add_kernel,
+        out_shape=jax.ShapeDtypeStruct(left.shape, left.dtype),
+        compiler_params=pltpu.CompilerParams(vmem_limit_bytes=VMEM_LIMIT),
+        name="add",
+    )(left, right)
+
+
 def from_partner(value, axis, size, m):
     return lax.ppermute(value, axis, [(i, i ^ m) for i in range(size)])
 
 
-def from_partners(values, axis, size):
-    taken = [values[0]]
-    for m in range(1, size):
-        taken.append(from_partner(values[m], axis, size, m))
-    return taken
+def from_partners(value, axis, size):
+    return [from_partner(value, axis, size, m) for m in reversed(range(1, size))] + [value]
 
 
 def finish_long(grads, queries, first, seq_dev):
@@ -310,18 +320,21 @@
     rank_of = me.reshape(1)
     kept, sent = project(inputs, out_grads, in_proj, out_proj, rank_of, parts)
     asked = lax.dynamic_slice_in_dim(queries, me * (own * rank), own * rank, 1)
-    weights = token_weights(seq_ids, counts, first)
     came = from_partner(sent, "tensor", parts, 1)
     kept, sent = halve(kept, came, rank_of, parts, own)
     came = from_partner(sent, "tensor", parts, 2)
+    kept, counts = lax.optimization_barrier((kept, counts))
+    weights = token_weights(seq_ids, counts, first)
+    if blocks <= SMALL:
+        weights, asked = lax.optimization_barrier((weights, asked))
+        asked = from_partners(asked, "dp", blocks)
     grads = gradients(weights, [kept, came], rank)
     if blocks > SMALL:
         return finish_long(grads, asked, first, seq_dev)
-    asked = from_partners([asked] * blocks, "dp", blocks)
     grads, *asked = lax.optimization_barrier((grads, *asked))
-    grads = from_partners([grads] * blocks, "dp", blocks)
-    partial = grams(place.reshape(1), grads, asked)
-    partial = from_partners([partial] * parts, "tensor", parts)
+    partial = grams(place.reshape(1), from_partners(grads, "dp", blocks), asked)
+    partial = add(partial, from_partner(partial, "tensor", parts, 1))
+    partial = [partial, from_partner(partial, "tensor", parts, 2)]
     return solve(partial, blocks * seq_dev, blocks * queries.shape[0], seq_dev)
 
 

time: 33.1 us -> 30 us (0.906)
  starting transfers between devices: 14.1 us -> 12.8 us
  waiting for transfers between devices: 13.1 us -> 12.2 us
  local copies, waits for them, and re-layouts: 0.84 us -> 0.02 us
    ppermute x11 -> x10, starting transfers between devices: 14.1 us -> 12.8 us  [from_partner(): return lax.ppermute(value, axis, [(i, i ^ m) for i in range(size)])]
    ppermute x11 -> x10, waiting for transfers between devices: 13.1 us -> 12.2 us  [from_partner(): return lax.ppermute(value, axis, [(i, i ^ m) for i in range(size)])]
    unnamed x6, local copies, waits for them, and re-layouts: 0.84 us -> 0.01 us
  transfers between devices with their start and end apart: 11 -> 10, of which waited for: 6 -> 7; matrix products, arithmetic and copies ran while one was open for 1% -> 1% of each run, Pallas kernels for 7% -> 1%
where the time goes in v4:
time: 30 us; the launch traced here: 29.8 us
  starting transfers between devices  12.8 us (43%)
  waiting for transfers between devices  12.2 us (41%)
  Pallas kernels  4.59 us (15%)
    ppermute x10, starting transfers between devices, from_partner(): return lax.ppermute(value, axis, [(i, i ^ m) for i in range(size)])  12.8 us
    ppermute x10, waiting for transfers between devices, from_partner(): return lax.ppermute(value, axis, [(i, i ^ m) for i in range(size)])  12.2 us
    pallas_call x1, Pallas kernels, project(): pl.pallas_call(functools.partial(project_kernel, parts, own), out_shape=[...  2.15 us
    pallas_call x1, Pallas kernels, solve(): pl.pallas_call(functools.partial(solve_kernel, seqs), out_shape=jax.Shape...  1.81 us
  transfers between devices with their start and end apart: 10, of which 7 were waited for; matrix products, arithmetic and copies ran while one was open for 1% of the time, Pallas kernels for 1%

profile of v4, /device:TPU:0, one launch (start us, length us, event | category | flops | bytes accessed | tf_op | source)
XLA Modules:
  0.0 29.8 jit_solution(9682127138071746680)
XLA Ops:
  0.0 2.2 %project.1 = (f32[96,256]{1,0:T(8,128)S(1)}, f32[96,256]{1,0:T(8,128)S(1)}) custom-call(s32[1]{0:T(128)} %bitcast.1.rank_ref, bf16[2752,256]{1,0:T(8,128)(2,1)} %bitcast.5, bf16[256,1024]{1,0:T(8,128)(2,1)} %g_hbm.1, bf16[64,2752]{1,0:T(8,128)(2,1)} %bitcast.6, bf16[64,1024]{1,0:T(8,128)(2,1)} %bitcast.7), custom_call_target="tpu_custom_call" | custom-call | tf_op jit(solution)/shard_map/project/pallas_call | solution.py:104
  2.2 0.5 %collective-permute-start = (f32[96,256]{1,0:T(8,128)S(1)}, f32[96,256]{1,0:T(8,128)S(1)}, u32[]{:S(2)}, u32[]{:S(2)}) collective-permute-start(f32[96,256]{1,0:T(8,128)S(1)} %get-tuple-element.19), channel_id=1, source_target_pairs={{0,1},{1,0},{2,3},{3,2},{4,5},{5,4},{6,7},{7,6},{8,9},{9,8},{10,11... | collective-permute-start | bytes 294920 | tf_op jit(solution)/shard_map/ppermute | solution.py:285
  2.7 0.1 convert_reduce_fusion
  2.8 0.8 %collective-permute-done.came_ref = f32[96,256]{1,0:T(8,128)S(1)} collective-permute-done((f32[96,256]{1,0:T(8,128)S(1)}, f32[96,256]{1,0:T(8,128)S(1)}, u32[]{:S(2)}, u32[]{:S(2)}) %collective-permute-start) | collective-permute-done | bytes 98336 | tf_op jit(solution)/shard_map/ppermute | solution.py:285
  3.7 2.9 %collective-permute-start.1 = (f32[80,256]{1,0:T(8,128)S(1)}, f32[80,256]{1,0:T(8,128)S(1)}, u32[]{:S(2)}, u32[]{:S(2)}) collective-permute-start(f32[80,256]{1,0:T(8,128)S(1)} %get-tuple-element.24), channel_id=1, source_target_pairs={{0,2},{1,3},{2,0},{3,1},{4,6},{5,7},{6,4},{7,5},{8,10},{9,11},{10,... | collective-permute-start | bytes 245768 | tf_op jit(solution)/shard_map/ppermute | solution.py:285
  6.6 0.1 fusion.1.weights_ref
  6.7 3.6 %collective-permute-start.2 = (f32[4,1024]{1,0:T(4,128)S(1)}, f32[4,1024]{1,0:T(4,128)S(1)}, u32[]{:S(2)}, u32[]{:S(2)}) collective-permute-start(f32[4,1024]{1,0:T(4,128)S(1)} %constant_dynamic-slice_fusion.refs_7_), channel_id=1, source_target_pairs={{0,12},{4,8},{8,4},{12,0},{1,13},{5,9},{9,5},{13,1},{2,14},{6,10},... | collective-permute-start | bytes 49160 | tf_op jit(solution)/shard_map/ppermute | solution.py:285
  10.3 0.0 collective-permute-start.3
  10.3 0.8 %collective-permute-start.4 = (f32[4,1024]{1,0:T(4,128)S(1)}, f32[4,1024]{1,0:T(4,128)S(1)}, u32[]{:S(2)}, u32[]{:S(2)}) collective-permute-start(f32[4,1024]{1,0:T(4,128)S(1)} %constant_dynamic-slice_fusion.refs_7_), channel_id=1, source_target_pairs={{0,4},{4,0},{8,12},{12,8},{1,5},{5,1},{9,13},{13,9},{2,6},{6,2},{1... | collective-permute-start | bytes 49160 | tf_op jit(solution)/shard_map/ppermute | solution.py:285
  11.1 0.0 collective-permute-done.1.refs_1_
  11.1 0.3 gradients.1.refs_3_
  11.3 0.9 %collective-permute-done.2.refs_4_ = f32[4,1024]{1,0:T(4,128)S(1)} collective-permute-done((f32[4,1024]{1,0:T(4,128)S(1)}, f32[4,1024]{1,0:T(4,128)S(1)}, u32[]{:S(2)}, u32[]{:S(2)}) %collective-permute-start.2) | collective-permute-done | bytes 16416 | tf_op jit(solution)/shard_map/ppermute | solution.py:285
  12.2 2.7 %collective-permute-done.3.refs_5_ = f32[4,1024]{1,0:T(4,128)S(1)} collective-permute-done((f32[4,1024]{1,0:T(4,128)S(1)}, f32[4,1024]{1,0:T(4,128)S(1)}, u32[]{:S(2)}, u32[]{:S(2)}) %collective-permute-start.3) | collective-permute-done | bytes 16416 | tf_op jit(solution)/shard_map/ppermute | solution.py:285
  14.9 1.5 %collective-permute-start.5 = (f32[8,16,128]{2,1,0:T(8,128)S(1)}, f32[8,16,128]{2,1,0:T(8,128)S(1)}, u32[]{:S(2)}, u32[]{:S(2)}) collective-permute-start(f32[8,16,128]{2,1,0:T(8,128)S(1)} %gradients.1.refs_3_), channel_id=1, source_target_pairs={{0,12},{4,8},{8,4},{12,0},{1,13},{5,9},{9,5},{13,1},{2,14},{6,10},... | collective-permute-start | bytes 196616 | tf_op jit(solution)/shard_map/ppermute | solution.py:285
  16.4 0.6 %collective-permute-start.6 = (f32[8,16,128]{2,1,0:T(8,128)S(1)}, f32[8,16,128]{2,1,0:T(8,128)S(1)}, u32[]{:S(2)}, u32[]{:S(2)}) collective-permute-start(f32[8,16,128]{2,1,0:T(8,128)S(1)} %gradients.1.refs_3_), channel_id=1, source_target_pairs={{0,8},{4,12},{8,0},{12,4},{1,9},{5,13},{9,1},{13,5},{2,10},{6,14},... | collective-permute-start | bytes 196616 | tf_op jit(solution)/shard_map/ppermute | solution.py:285
  16.9 2.4 %collective-permute-start.7 = (f32[8,16,128]{2,1,0:T(8,128)S(1)}, f32[8,16,128]{2,1,0:T(8,128)S(1)}, u32[]{:S(2)}, u32[]{:S(2)}) collective-permute-start(f32[8,16,128]{2,1,0:T(8,128)S(1)} %gradients.1.refs_3_), channel_id=1, source_target_pairs={{0,4},{4,0},{8,12},{12,8},{1,5},{5,1},{9,13},{13,9},{2,6},{6,2},{1... | collective-permute-start | bytes 196616 | tf_op jit(solution)/shard_map/ppermute | solution.py:285
  19.3 1.8 %collective-permute-done.5.refs_0_ = f32[8,16,128]{2,1,0:T(8,128)S(1)} collective-permute-done((f32[8,16,128]{2,1,0:T(8,128)S(1)}, f32[8,16,128]{2,1,0:T(8,128)S(1)}, u32[]{:S(2)}, u32[]{:S(2)}) %collective-permute-start.5) | collective-permute-done | bytes 65568 | tf_op jit(solution)/shard_map/ppermute | solution.py:285
  21.1 1.6 %collective-permute-done.6.refs_1_ = f32[8,16,128]{2,1,0:T(8,128)S(1)} collective-permute-done((f32[8,16,128]{2,1,0:T(8,128)S(1)}, f32[8,16,128]{2,1,0:T(8,128)S(1)}, u32[]{:S(2)}, u32[]{:S(2)}) %collective-permute-start.6) | collective-permute-done | bytes 65568 | tf_op jit(solution)/shard_map/ppermute | solution.py:285
  22.7 0.3 %grams.1.left_ref = f32[40,128]{1,0:T(8,128)S(1)} custom-call(s32[1]{0:T(128)} %bitcast.me_ref, f32[8,16,128]{2,1,0:T(8,128)S(1)} %collective-permute-done.5.refs_0_, f32[8,16,128]{2,1,0:T(8,128)S(1)} %collective-permute-done.6.refs_1_, f32[8,16,128]{2,1,0:T(8,128)S(1)} %collective-permute-done.7.refs_2_, f32[8,16,128]{2,1,0:T(8,128)S(1)} %gradients.1.refs_3_, ...), custom_call_target="tpu_custom_call" | custom-call | tf_op jit(solution)/shard_map/grams/pallas_call | solution.py:211
  23.0 0.0 collective-permute-start.8
  23.0 1.2 %collective-permute-done.8.right_ref = f32[40,128]{1,0:T(8,128)S(1)} collective-permute-done((f32[40,128]{1,0:T(8,128)S(1)}, f32[40,128]{1,0:T(8,128)S(1)}, u32[]{:S(2)}, u32[]{:S(2)}) %collective-permute-start.8) | collective-permute-done | bytes 20512 | tf_op jit(solution)/shard_map/ppermute | solution.py:285
  24.2 0.5 %collective-permute-start.9 = (f32[40,128]{1,0:T(8,128)S(1)}, f32[40,128]{1,0:T(8,128)S(1)}, u32[]{:S(2)}, u32[]{:S(2)}) collective-permute-start(f32[40,128]{1,0:T(8,128)S(1)} %add.5.refs_0_), channel_id=1, source_target_pairs={{0,2},{1,3},{2,0},{3,1},{4,6},{5,7},{6,4},{7,5},{8,10},{9,11},{10,... | collective-permute-start | bytes 61448 | tf_op jit(solution)/shard_map/ppermute | solution.py:285
  24.8 3.2 %collective-permute-done.9.refs_1_ = f32[40,128]{1,0:T(8,128)S(1)} collective-permute-done((f32[40,128]{1,0:T(8,128)S(1)}, f32[40,128]{1,0:T(8,128)S(1)}, u32[]{:S(2)}, u32[]{:S(2)}) %collective-permute-start.9) | collective-permute-done | bytes 20512 | tf_op jit(solution)/shard_map/ppermute | solution.py:285
  28.0 1.8 %solve.1 = f32[16,16]{1,0:T(8,128)} custom-call(f32[40,128]{1,0:T(8,128)S(1)} %add.5.refs_0_, f32[40,128]{1,0:T(8,128)S(1)} %collective-permute-done.9.refs_1_), custom_call_target="tpu_custom_call" | custom-call | tf_op jit(solution)/shard_map/solve/pallas_call | solution.py:263
  (13 shorter events, 0.1 us)
Async XLA Ops:
  0.0 2.7 %copy-start = (f32[4,4096]{1,0:T(4,128)S(1)}, f32[4,4096]{1,0:T(4,128)}, u32[]{:S(2)}) copy-start(f32[4,4096]{1,0:T(4,128)} %param.13) | copy-start | bytes 196612
  0.0 2.7 %copy-start.1 = (s32[256]{0:T(256)S(1)}, s32[256]{0:T(256)}, u32[]{:S(2)}) copy-start(s32[256]{0:T(256)} %param.11) | copy-start | bytes 3076
  0.0 3.7 %copy-start.2 = (s32[16]{0:T(128)S(1)}, s32[16]{0:T(128)}, u32[]{:S(2)}) copy-start(s32[16]{0:T(128)} %param.12) | copy-start | bytes 196
  2.2 1.5 %collective-permute-start = (f32[96,256]{1,0:T(8,128)S(1)}, f32[96,256]{1,0:T(8,128)S(1)}, u32[]{:S(2)}, u32[]{:S(2)}) collective-permute-start(f32[96,256]{1,0:T(8,128)S(1)} %get-tuple-element.19), channel_id=1, source_target_pairs={{0,1},{1,0},{2,3},{3,2},{4,5},{5,4},{6,7},{7,6},{8,9},{9,8},{10,11... | collective-permute-start | bytes 294920 | tf_op jit(solution)/shard_map/ppermute | solution.py:285
  3.7 7.4 %collective-permute-start.1 = (f32[80,256]{1,0:T(8,128)S(1)}, f32[80,256]{1,0:T(8,128)S(1)}, u32[]{:S(2)}, u32[]{:S(2)}) collective-permute-start(f32[80,256]{1,0:T(8,128)S(1)} %get-tuple-element.24), channel_id=1, source_target_pairs={{0,2},{1,3},{2,0},{3,1},{4,6},{5,7},{6,4},{7,5},{8,10},{9,11},{10,... | collective-permute-start | bytes 245768 | tf_op jit(solution)/shard_map/ppermute | solution.py:285
  6.7 5.5 %collective-permute-start.2 = (f32[4,1024]{1,0:T(4,128)S(1)}, f32[4,1024]{1,0:T(4,128)S(1)}, u32[]{:S(2)}, u32[]{:S(2)}) collective-permute-start(f32[4,1024]{1,0:T(4,128)S(1)} %constant_dynamic-slice_fusion.refs_7_), channel_id=1, source_target_pairs={{0,12},{4,8},{8,4},{12,0},{1,13},{5,9},{9,5},{13,1},{2,14},{6,10},... | collective-permute-start | bytes 49160 | tf_op jit(solution)/shard_map/ppermute | solution.py:285
  10.3 4.6 %collective-permute-start.3 = (f32[4,1024]{1,0:T(4,128)S(1)}, f32[4,1024]{1,0:T(4,128)S(1)}, u32[]{:S(2)}, u32[]{:S(2)}) collective-permute-start(f32[4,1024]{1,0:T(4,128)S(1)} %constant_dynamic-slice_fusion.refs_7_), channel_id=1, source_target_pairs={{0,8},{4,12},{8,0},{12,4},{1,9},{5,13},{9,1},{13,5},{2,10},{6,14},... | collective-permute-start | bytes 49160 | tf_op jit(solution)/shard_map/ppermute | solution.py:285
  10.3 4.6 %collective-permute-start.4 = (f32[4,1024]{1,0:T(4,128)S(1)}, f32[4,1024]{1,0:T(4,128)S(1)}, u32[]{:S(2)}, u32[]{:S(2)}) collective-permute-start(f32[4,1024]{1,0:T(4,128)S(1)} %constant_dynamic-slice_fusion.refs_7_), channel_id=1, source_target_pairs={{0,4},{4,0},{8,12},{12,8},{1,5},{5,1},{9,13},{13,9},{2,6},{6,2},{1... | collective-permute-start | bytes 49160 | tf_op jit(solution)/shard_map/ppermute | solution.py:285
  14.9 6.2 %collective-permute-start.5 = (f32[8,16,128]{2,1,0:T(8,128)S(1)}, f32[8,16,128]{2,1,0:T(8,128)S(1)}, u32[]{:S(2)}, u32[]{:S(2)}) collective-permute-start(f32[8,16,128]{2,1,0:T(8,128)S(1)} %gradients.1.refs_3_), channel_id=1, source_target_pairs={{0,12},{4,8},{8,4},{12,0},{1,13},{5,9},{9,5},{13,1},{2,14},{6,10},... | collective-permute-start | bytes 196616 | tf_op jit(solution)/shard_map/ppermute | solution.py:285
  16.4 6.3 %collective-permute-start.6 = (f32[8,16,128]{2,1,0:T(8,128)S(1)}, f32[8,16,128]{2,1,0:T(8,128)S(1)}, u32[]{:S(2)}, u32[]{:S(2)}) collective-permute-start(f32[8,16,128]{2,1,0:T(8,128)S(1)} %gradients.1.refs_3_), channel_id=1, source_target_pairs={{0,8},{4,12},{8,0},{12,4},{1,9},{5,13},{9,1},{13,5},{2,10},{6,14},... | collective-permute-start | bytes 196616 | tf_op jit(solution)/shard_map/ppermute | solution.py:285
  16.9 5.7 %collective-permute-start.7 = (f32[8,16,128]{2,1,0:T(8,128)S(1)}, f32[8,16,128]{2,1,0:T(8,128)S(1)}, u32[]{:S(2)}, u32[]{:S(2)}) collective-permute-start(f32[8,16,128]{2,1,0:T(8,128)S(1)} %gradients.1.refs_3_), channel_id=1, source_target_pairs={{0,4},{4,0},{8,12},{12,8},{1,5},{5,1},{9,13},{13,9},{2,6},{6,2},{1... | collective-permute-start | bytes 196616 | tf_op jit(solution)/shard_map/ppermute | solution.py:285
  23.0 1.2 %collective-permute-start.8 = (f32[40,128]{1,0:T(8,128)S(1)}, f32[40,128]{1,0:T(8,128)S(1)}, u32[]{:S(2)}, u32[]{:S(2)}) collective-permute-start(f32[40,128]{1,0:T(8,128)S(1)} %grams.1.left_ref), channel_id=1, source_target_pairs={{0,1},{1,0},{2,3},{3,2},{4,5},{5,4},{6,7},{7,6},{8,9},{9,8},{10,11... | collective-permute-start | bytes 61448 | tf_op jit(solution)/shard_map/ppermute | solution.py:285
  24.2 3.8 %collective-permute-start.9 = (f32[40,128]{1,0:T(8,128)S(1)}, f32[40,128]{1,0:T(8,128)S(1)}, u32[]{:S(2)}, u32[]{:S(2)}) collective-permute-start(f32[40,128]{1,0:T(8,128)S(1)} %add.5.refs_0_), channel_id=1, source_target_pairs={{0,2},{1,3},{2,0},{3,1},{4,6},{5,7},{6,4},{7,5},{8,10},{9,11},{10,... | collective-permute-start | bytes 61448 | tf_op jit(solution)/shard_map/ppermute | solution.py:285

commit v5 on v2

--- a/solution.py
+++ b/solution.py
@@ -12,13 +12,13 @@
 SMALL = 4
 
 
-def token_weights(seq_ids, counts, first):
+def token_weights(seq_ids, counts, first, works):
     local_ids = seq_ids - first
     slots = jnp.arange(counts.shape[0], dtype=jnp.int32)
     member = local_ids[None, :] == slots[:, None]
     starts = jnp.sum((local_ids[None, :] < slots[:, None]).astype(jnp.int32), axis=1)
     offset = jnp.arange(seq_ids.shape[0], dtype=jnp.int32)[None, :] - starts[:, None]
-    scale = 1.0 / counts.astype(jnp.float32)
+    scale = works.astype(jnp.float32) / counts.astype(jnp.float32)
     return jnp.where(member & (offset < counts[:, None]), scale[:, None], 0.0)
 
 
@@ -42,9 +42,7 @@
     return mul(lh, rh) + (mul(lh, rl) + mul(ll, rh))
 
 
-def project_kernel(parts, own, rank_ref, x_hbm, g_hbm, wx_hbm, wg_hbm, *rest):
-    outs = rest[:2]
-    x_ref, g_ref, wx_ref, wg_ref, grad_ref, sems = rest[2:]
+def project_kernel(x_hbm, g_hbm, wx_hbm, wg_hbm, out_ref, x_ref, g_ref, wx_ref, wg_ref, sems):
     copies = []
 
     def fetch(src, dst, index):
@@ -83,58 +81,49 @@
             total = term if total is None else total + term
         return total
 
-    grad_ref[...] = project(wg_copy, wg_ref, g_cuts, g_copies, g_ref, 1)
-    inputs_t = project(wx_copy, wx_ref, x_cuts, x_copies, x_ref, 0)
-    me = rank_ref[0]
-    for out, side in zip(outs, (me & 1, (me & 1) ^ 1)):
-        for place in range(parts // 2):
-            start = pl.multiple_of((2 * place + side) * own, own)
-            out[place * own : (place + 1) * own, :] = grad_ref[pl.ds(start, own), :]
-        out[parts // 2 * own :, :] = inputs_t
-
-
-def project(inputs, out_grads, in_proj, out_proj, me, parts):
+    rank = wg_ref.shape[0]
+    out_ref[:rank, :] = project(wg_copy, wg_ref, g_cuts, g_copies, g_ref, 1)
+    out_ref[rank:, :] = project(wx_copy, wx_ref, x_cuts, x_copies, x_ref, 0)
+
+
+def project(inputs, out_grads, in_proj, out_proj):
     rank = in_proj.shape[1]
-    own = rank // parts
     tokens, hidden = inputs.shape
     width = out_grads.shape[1]
     copies = 2 + len(cuts_of(width, 512)) + len(cuts_of(hidden, 768))
     arrays = (inputs.T, out_grads, in_proj.T, out_proj.T)
-    in_hbm = pl.BlockSpec(memory_space=pltpu.HBM)
-    return pl.pallas_call(
-        functools.partial(project_kernel, parts, own),
-        out_shape=[jax.ShapeDtypeStruct((parts // 2 * own + rank, tokens), jnp.float32)] * 2,
-        in_specs=[pl.BlockSpec(memory_space=pltpu.SMEM)] + [in_hbm] * len(arrays),
-        out_specs=[pl.BlockSpec(memory_space=pltpu.VMEM)] * 2,
+    return pl.pallas_call(
+        project_kernel,
+        out_shape=jax.ShapeDtypeStruct((2 * rank, tokens), jnp.float32),
+        in_specs=[pl.BlockSpec(memory_space=pltpu.HBM)] * len(arrays),
+        out_specs=pl.BlockSpec(memory_space=pltpu.VMEM),
         scratch_shapes=[
             pltpu.VMEM((hidden, tokens), jnp.bfloat16),
             pltpu.VMEM((tokens, width), jnp.bfloat16),
             pltpu.VMEM((rank, hidden), jnp.bfloat16),
             pltpu.VMEM((rank, width), jnp.bfloat16),
-            pltpu.VMEM((rank, tokens), jnp.float32),
             pltpu.SemaphoreType.DMA((copies,)),
         ],
         compiler_params=pltpu.CompilerParams(vmem_limit_bytes=VMEM_LIMIT),
         name="project",
-    )(me, *(pltpu.with_memory_space_constraint(array, pltpu.HBM) for array in arrays))
-
-
-def halve_kernel(parts, own, rank_ref, kept_ref, came_ref, keep_ref, send_ref, sum_ref):
+    )(*(pltpu.with_memory_space_constraint(array, pltpu.HBM) for array in arrays))
+
+
+def halve_kernel(own, rank_ref, kept_ref, came_ref, keep_ref, send_ref, sum_ref):
     sum_ref[...] = kept_ref[...] + came_ref[...]
-    me = rank_ref[0]
-    for out, place in ((keep_ref, me // 2), (send_ref, me // 2 ^ 1)):
-        start = pl.multiple_of(place * own, own)
-        out[:own, :] = sum_ref[pl.ds(start, own), :]
-        out[own:, :] = sum_ref[parts // 2 * own :, :]
-
-
-def halve(kept, came, me, parts, own):
+    rank = sum_ref.shape[0] // 2
+    place = rank_ref[0] // 2
+    for out, taken in ((keep_ref, place), (send_ref, place ^ 1)):
+        out[:own, :] = sum_ref[pl.ds(pl.multiple_of(taken * own, own), own), :]
+        out[own:, :] = sum_ref[rank:, :]
+
+
+def halve(kept, came, me, own):
     rows, tokens = kept.shape
-    left = rows - (parts // 2 - 1) * own
     whole = pl.BlockSpec(memory_space=pltpu.VMEM)
     return pl.pallas_call(
-        functools.partial(halve_kernel, parts, own),
-        out_shape=[jax.ShapeDtypeStruct((left, tokens), jnp.float32)] * 2,
+        functools.partial(halve_kernel, own),
+        out_shape=[jax.ShapeDtypeStruct((own + rows // 2, tokens), jnp.float32)] * 2,
         in_specs=[pl.BlockSpec(memory_space=pltpu.SMEM), whole, whole],
         out_specs=[whole] * 2,
         scratch_shapes=[pltpu.VMEM((rows, tokens), jnp.float32)],
@@ -182,39 +171,53 @@
     )(weights, *pieces)
 
 
-def grams_kernel(count, me_ref, *refs):
-    grads, queries, out_ref = refs[:count], refs[count:-1], refs[-1]
-    me = me_ref[0]
+def collect_kernel(place_ref, *refs):
+    given, out_ref = [ref[...] for ref in refs[:-1]], refs[-1]
+    count = len(given)
+    rows = given[0].shape[0]
+    ordered = []
+    for place in range(count):
+        chosen = given[0]
+        for m in range(1, count):
+            chosen = jnp.where((place_ref[0] ^ place) == m, given[m], chosen)
+        ordered.append(chosen)
+    out_ref[...] = jnp.concatenate(ordered, axis=0)
+
+
+def collect(place, blocks):
+    rows, columns = blocks[0].shape
+    whole = pl.BlockSpec(memory_space=pltpu.VMEM)
+    return pl.pallas_call(
+        collect_kernel,
+        out_shape=jax.ShapeDtypeStruct((len(blocks) * rows, columns), jnp.float32),
+        in_specs=[pl.BlockSpec(memory_space=pltpu.SMEM)] + [whole] * len(blocks),
+        out_specs=whole,
+        compiler_params=pltpu.CompilerParams(vmem_limit_bytes=VMEM_LIMIT),
+        name="collect",
+    )(place, *blocks)
+
+
+def grams_kernel(*refs):
+    grads, queries_ref, out_ref = refs[-3::-1], refs[-2], refs[-1]
     lanes = [
         jnp.concatenate([block[i] for block in grads], axis=0)
         for i in range(grads[0].shape[0])
     ]
     every = jnp.concatenate(lanes, axis=1)
-    given = [block[...] for block in queries]
-    ordered = []
-    for place in range(count):
-        chosen = given[0]
-        for m in range(1, count):
-            chosen = jnp.where((me ^ place) == m, given[m], chosen)
-        ordered.append(chosen)
-    both = jnp.concatenate([every] + ordered, axis=0)
+    both = jnp.concatenate([every, queries_ref[...]], axis=0)
     result = dot_nt(both, every)
     half = result.shape[0] // 2
     out_ref[...] = jnp.concatenate([result[:half, :], result[half:, :]], axis=1)
 
 
-def grams(me, grads, queries):
+def grams(grads, queries):
     seqs = len(grads) * grads[0].shape[1]
-    asked = len(queries) * queries[0].shape[0]
-    whole = pl.BlockSpec(memory_space=pltpu.VMEM)
-    return pl.pallas_call(
-        functools.partial(grams_kernel, len(grads)),
-        out_shape=jax.ShapeDtypeStruct(((seqs + asked) // 2, 2 * seqs), jnp.float32),
-        in_specs=[pl.BlockSpec(memory_space=pltpu.SMEM)] + [whole] * (2 * len(grads)),
-        out_specs=whole,
+    return pl.pallas_call(
+        grams_kernel,
+        out_shape=jax.ShapeDtypeStruct(((seqs + queries.shape[0]) // 2, 2 * seqs), jnp.float32),
         compiler_params=pltpu.CompilerParams(vmem_limit_bytes=VMEM_LIMIT),
         name="grams",
-    )(me, *grads, *queries)
+    )(*grads, queries)
 
 
 def scales(count):
@@ -230,7 +233,6 @@
 def solve_kernel(seqs, *refs):
     parts, out_ref = refs[:-1], refs[-1]
     packed = (parts[0][...] + parts[1][...]) + (parts[2][...] + parts[3][...])
-    half = packed.shape[0]
     lane = lax.broadcasted_iota(jnp.int32, packed.shape, 1)
     turned = pltpu.roll(packed, seqs, 1)
     both = jnp.concatenate(
@@ -268,15 +270,23 @@
     )(*parts)
 
 
-def from_partner(value, axis, size, m):
-    return lax.ppermute(value, axis, [(i, i ^ m) for i in range(size)])
-
-
-def from_partners(values, axis, size):
-    taken = [values[0]]
-    for m in range(1, size):
-        taken.append(from_partner(values[m], axis, size, m))
-    return taken
+def move(value, sizes, target):
+    parts, blocks = sizes
+    pairs = []
+    for d in range(blocks):
+        for r in range(parts):
+            to = target(d, r)
+            if to is not None:
+                pairs.append((d * parts + r, to[0] * parts + to[1]))
+    return lax.ppermute(value, ("dp", "tensor"), pairs)
+
+
+def over_blocks(value, sizes, side):
+    came = [
+        move(value, sizes, lambda d, r: (d ^ m, r) if r % 2 == side else None)
+        for m in reversed(range(1, sizes[1]))
+    ]
+    return came + [value]
 
 
 def finish_long(grads, queries, first, seq_dev):
@@ -306,23 +316,25 @@
     me = lax.axis_index("tensor")
     place = lax.axis_index("dp")
     first = place * seq_dev
-    own = rank // parts
+    own = rank // (parts // 2)
     rank_of = me.reshape(1)
-    kept, sent = project(inputs, out_grads, in_proj, out_proj, rank_of, parts)
-    asked = lax.dynamic_slice_in_dim(queries, me * (own * rank), own * rank, 1)
-    weights = token_weights(seq_ids, counts, first)
-    came = from_partner(sent, "tensor", parts, 1)
-    kept, sent = halve(kept, came, rank_of, parts, own)
-    came = from_partner(sent, "tensor", parts, 2)
+    weights = token_weights(seq_ids, counts, first, me % 2)
+    asked = lax.dynamic_slice_in_dim(queries, (me // 2) * (own * rank), own * rank, 1)
+    kept = project(inputs, out_grads, in_proj, out_proj)
+    came = move(kept, sizes, lambda d, r: (d, r + 1) if r % 2 == 0 else None)
+    kept, sent = halve(kept, came, rank_of, own)
+    came = move(sent, sizes, lambda d, r: (d, r ^ 2) if r % 2 == 1 else None)
     grads = gradients(weights, [kept, came], rank)
     if blocks > SMALL:
         return finish_long(grads, asked, first, seq_dev)
-    asked = from_partners([asked] * blocks, "dp", blocks)
-    grads, *asked = lax.optimization_barrier((grads, *asked))
-    grads = from_partners([grads] * blocks, "dp", blocks)
-    partial = grams(place.reshape(1), grads, asked)
-    partial = from_partners([partial] * parts, "tensor", parts)
-    return solve(partial, blocks * seq_dev, blocks * queries.shape[0], seq_dev)
+    sent, asked = lax.optimization_barrier((sent, asked))
+    asked = collect(place.reshape(1), over_blocks(asked, sizes, 0)[::-1])
+    asked = move(asked, sizes, lambda d, r: (d, r + 1) if r % 2 == 0 else None)
+    partial = grams(over_blocks(grads, sizes, 1), asked)
+    partial = [partial] + [
+        move(partial, sizes, lambda d, r: (d, r ^ m) if r % 2 == 1 else None) for m in (2, 3, 1)
+    ]
+    return solve(partial, blocks * seq_dev, asked.shape[0], seq_dev)
 
 
 def solution(mesh):

time: 33.1 us -> 37.7 us (1.14)
  the two profiles are of different devices: /device:TPU:0 before, /device:TPU:1 now
where the time goes in v5:
time: 37.7 us; the launch traced here: 37.3 us
  starting transfers between devices  23.8 us (63%)
  waiting for transfers between devices  8.23 us (22%)
  Pallas kernels  4.85 us (13%)
    ppermute x12, starting transfers between devices, move(): return lax.ppermute(value, ('dp', 'tensor'), pairs)  23.8 us
    ppermute x12, waiting for transfers between devices, move(): return lax.ppermute(value, ('dp', 'tensor'), pairs)  8.23 us
    pallas_call x1, Pallas kernels, project(): pl.pallas_call(project_kernel, out_shape=jax.ShapeDtypeStruct((2 * rank,...  2.15 us
    pallas_call x1, Pallas kernels, solve(): pl.pallas_call(functools.partial(solve_kernel, seqs), out_shape=jax.Shape...  1.81 us
  transfers between devices with their start and end apart: 12, of which 6 were waited for; matrix products, arithmetic and copies ran while one was open for 1% of the time, Pallas kernels for 1%

profile of v5, /device:TPU:1, one launch (start us, length us, event | category | flops | bytes accessed | tf_op | source)
XLA Modules:
  0.0 37.3 jit_solution(5182037567824662357)
XLA Ops:
  0.0 2.1 %project.1.kept_ref = f32[128,256]{1,0:T(8,128)S(1)} custom-call(bf16[2752,256]{1,0:T(8,128)(2,1)} %bitcast.5, bf16[256,1024]{1,0:T(8,128)(2,1)} %g_hbm.1, bf16[64,2752]{1,0:T(8,128)(2,1)} %bitcast.6, bf16[64,1024]{1,0:T(8,128)(2,1)} %bitcast.7), custom_call_target="tpu_custom_call" | custom-call | tf_op jit(solution)/shard_map/project/pallas_call | solution.py:95
  2.2 1.3 %collective-permute-start = (f32[128,256]{1,0:T(8,128)S(1)}, f32[128,256]{1,0:T(8,128)S(1)}, u32[]{:S(2)}, u32[]{:S(2)}) collective-permute-start(f32[128,256]{1,0:T(8,128)S(1)} %project.1.kept_ref), channel_id=1, source_target_pairs={{0,1},{2,3},{4,5},{6,7},{8,9},{10,11},{12,13},{14,15},{16,17},{18,... | collective-permute-start | bytes 393224 | tf_op jit(solution)/shard_map/ppermute | solution.py:281
  3.6 0.1 convert_reduce_fusion
  3.7 1.7 %collective-permute-done.came_ref = f32[128,256]{1,0:T(8,128)S(1)} collective-permute-done((f32[128,256]{1,0:T(8,128)S(1)}, f32[128,256]{1,0:T(8,128)S(1)}, u32[]{:S(2)}, u32[]{:S(2)}) %collective-permute-start) | collective-permute-done | bytes 131104 | tf_op jit(solution)/shard_map/ppermute | solution.py:281
  5.4 0.7 %collective-permute-start.5 = (f32[4,2048]{1,0:T(4,128)S(1)}, f32[4,2048]{1,0:T(4,128)S(1)}, u32[]{:S(2)}, u32[]{:S(2)}) collective-permute-start(f32[4,2048]{1,0:T(4,128)S(1)} %constant_dynamic-slice_fusion.refs_0_), channel_id=1, source_target_pairs={{0,4},{2,6},{4,0},{6,2},{8,12},{10,14},{12,8},{14,10},{16,20},{18,... | collective-permute-start | bytes 98312 | tf_op jit(solution)/shard_map/ppermute | solution.py:281
  6.1 0.7 %collective-permute-start.6 = (f32[4,2048]{1,0:T(4,128)S(1)}, f32[4,2048]{1,0:T(4,128)S(1)}, u32[]{:S(2)}, u32[]{:S(2)}) collective-permute-start(f32[4,2048]{1,0:T(4,128)S(1)} %constant_dynamic-slice_fusion.refs_0_), channel_id=1, source_target_pairs={{0,8},{2,10},{4,12},{6,14},{8,0},{10,2},{12,4},{14,6},{16,24},{18,... | collective-permute-start | bytes 98312 | tf_op jit(solution)/shard_map/ppermute | solution.py:281
  6.8 0.7 %collective-permute-start.7 = (f32[4,2048]{1,0:T(4,128)S(1)}, f32[4,2048]{1,0:T(4,128)S(1)}, u32[]{:S(2)}, u32[]{:S(2)}) collective-permute-start(f32[4,2048]{1,0:T(4,128)S(1)} %constant_dynamic-slice_fusion.refs_0_), channel_id=1, source_target_pairs={{0,12},{2,14},{4,8},{6,10},{8,4},{10,6},{12,0},{14,2},{16,28},{18,... | collective-permute-start | bytes 98312 | tf_op jit(solution)/shard_map/ppermute | solution.py:281
  7.5 3.9 %collective-permute-start.1 = (f32[96,256]{1,0:T(8,128)S(1)}, f32[96,256]{1,0:T(8,128)S(1)}, u32[]{:S(2)}, u32[]{:S(2)}) collective-permute-start(f32[96,256]{1,0:T(8,128)S(1)} %get-tuple-element.9), channel_id=1, source_target_pairs={{1,3},{3,1},{5,7},{7,5},{9,11},{11,9},{13,15},{15,13},{17,19},{19,... | collective-permute-start | bytes 294920 | tf_op jit(solution)/shard_map/ppermute | solution.py:281
  11.4 0.1 fusion.1.weights_ref
  11.5 1.3 %collective-permute-start.8 = (f32[16,2048]{1,0:T(8,128)S(1)}, f32[16,2048]{1,0:T(8,128)S(1)}, u32[]{:S(2)}, u32[]{:S(2)}) collective-permute-start(f32[16,2048]{1,0:T(8,128)S(1)} %collect.1), channel_id=1, source_target_pairs={{0,1},{2,3},{4,5},{6,7},{8,9},{10,11},{12,13},{14,15},{16,17},{18,... | collective-permute-start | bytes 393224 | tf_op jit(solution)/shard_map/ppermute | solution.py:281
  12.8 0.6 %collective-permute-done.1.refs_1_ = f32[96,256]{1,0:T(8,128)S(1)} collective-permute-done((f32[96,256]{1,0:T(8,128)S(1)}, f32[96,256]{1,0:T(8,128)S(1)}, u32[]{:S(2)}, u32[]{:S(2)}) %collective-permute-start.1) | collective-permute-done | bytes 98336 | tf_op jit(solution)/shard_map/ppermute | solution.py:281
  13.4 0.4 gradients.1.refs_3_
  13.8 5.5 %collective-permute-start.2 = (f32[16,16,128]{2,1,0:T(8,128)S(1)}, f32[16,16,128]{2,1,0:T(8,128)S(1)}, u32[]{:S(2)}, u32[]{:S(2)}) collective-permute-start(f32[16,16,128]{2,1,0:T(8,128)S(1)} %gradients.1.refs_3_), channel_id=1, source_target_pairs={{1,13},{3,15},{5,9},{7,11},{9,5},{11,7},{13,1},{15,3},{17,29},{19,... | collective-permute-start | bytes 393224 | tf_op jit(solution)/shard_map/ppermute | solution.py:281
  19.2 1.9 %collective-permute-start.3 = (f32[16,16,128]{2,1,0:T(8,128)S(1)}, f32[16,16,128]{2,1,0:T(8,128)S(1)}, u32[]{:S(2)}, u32[]{:S(2)}) collective-permute-start(f32[16,16,128]{2,1,0:T(8,128)S(1)} %gradients.1.refs_3_), channel_id=1, source_target_pairs={{1,9},{3,11},{5,13},{7,15},{9,1},{11,3},{13,5},{15,7},{17,25},{19,... | collective-permute-start | bytes 393224 | tf_op jit(solution)/shard_map/ppermute | solution.py:281
  21.2 2.2 %collective-permute-start.4 = (f32[16,16,128]{2,1,0:T(8,128)S(1)}, f32[16,16,128]{2,1,0:T(8,128)S(1)}, u32[]{:S(2)}, u32[]{:S(2)}) collective-permute-start(f32[16,16,128]{2,1,0:T(8,128)S(1)} %gradients.1.refs_3_), channel_id=1, source_target_pairs={{1,5},{3,7},{5,1},{7,3},{9,13},{11,15},{13,9},{15,11},{17,21},{19,... | collective-permute-start | bytes 393224 | tf_op jit(solution)/shard_map/ppermute | solution.py:281
  23.4 1.2 %collective-permute-done.8.refs_4_ = f32[16,2048]{1,0:T(8,128)S(1)} collective-permute-done((f32[16,2048]{1,0:T(8,128)S(1)}, f32[16,2048]{1,0:T(8,128)S(1)}, u32[]{:S(2)}, u32[]{:S(2)}) %collective-permute-start.8) | collective-permute-done | bytes 131104 | tf_op jit(solution)/shard_map/ppermute | solution.py:281
  24.6 1.7 %collective-permute-done.3.refs_1_ = f32[16,16,128]{2,1,0:T(8,128)S(1)} collective-permute-done((f32[16,16,128]{2,1,0:T(8,128)S(1)}, f32[16,16,128]{2,1,0:T(8,128)S(1)}, u32[]{:S(2)}, u32[]{:S(2)}) %collective-permute-start.3) | collective-permute-done | bytes 131104 | tf_op jit(solution)/shard_map/ppermute | solution.py:281
  26.3 1.3 %collective-permute-done.4.refs_2_ = f32[16,16,128]{2,1,0:T(8,128)S(1)} collective-permute-done((f32[16,16,128]{2,1,0:T(8,128)S(1)}, f32[16,16,128]{2,1,0:T(8,128)S(1)}, u32[]{:S(2)}, u32[]{:S(2)}) %collective-permute-start.4) | collective-permute-done | bytes 131104 | tf_op jit(solution)/shard_map/ppermute | solution.py:281
  27.7 0.5 %grams.1.refs_0_ = f32[40,128]{1,0:T(8,128)S(1)} custom-call(f32[16,16,128]{2,1,0:T(8,128)S(1)} %collective-permute-done.2.refs_0_, f32[16,16,128]{2,1,0:T(8,128)S(1)} %collective-permute-done.3.refs_1_, f32[16,16,128]{2,1,0:T(8,128)S(1)} %collective-permute-done.4.refs_2_, f32[16,16,128]{2,1,0:T(8,128)S(1)} %gradients.1.refs_3_, ...), custom_call_target="tpu_custom_call" | custom-call | tf_op jit(solution)/shard_map/grams/pallas_call | solution.py:215
  28.1 1.6 %collective-permute-start.10 = (f32[40,128]{1,0:T(8,128)S(1)}, f32[40,128]{1,0:T(8,128)S(1)}, u32[]{:S(2)}, u32[]{:S(2)}) collective-permute-start(f32[40,128]{1,0:T(8,128)S(1)} %grams.1.refs_0_), channel_id=1, source_target_pairs={{1,2},{3,0},{5,6},{7,4},{9,10},{11,8},{13,14},{15,12},{17,18},{19,... | collective-permute-start | bytes 61448 | tf_op jit(solution)/shard_map/ppermute | solution.py:281
  29.7 1.3 %collective-permute-start.11 = (f32[40,128]{1,0:T(8,128)S(1)}, f32[40,128]{1,0:T(8,128)S(1)}, u32[]{:S(2)}, u32[]{:S(2)}) collective-permute-start(f32[40,128]{1,0:T(8,128)S(1)} %grams.1.refs_0_), channel_id=1, source_target_pairs={{1,0},{3,2},{5,4},{7,6},{9,8},{11,10},{13,12},{15,14},{17,16},{19,... | collective-permute-start | bytes 61448 | tf_op jit(solution)/shard_map/ppermute | solution.py:281
  31.0 2.8 %collective-permute-start.9 = (f32[40,128]{1,0:T(8,128)S(1)}, f32[40,128]{1,0:T(8,128)S(1)}, u32[]{:S(2)}, u32[]{:S(2)}) collective-permute-start(f32[40,128]{1,0:T(8,128)S(1)} %grams.1.refs_0_), channel_id=1, source_target_pairs={{1,3},{3,1},{5,7},{7,5},{9,11},{11,9},{13,15},{15,13},{17,19},{19,... | collective-permute-start | bytes 61448 | tf_op jit(solution)/shard_map/ppermute | solution.py:281
  33.9 1.7 %collective-permute-done.9.refs_1_ = f32[40,128]{1,0:T(8,128)S(1)} collective-permute-done((f32[40,128]{1,0:T(8,128)S(1)}, f32[40,128]{1,0:T(8,128)S(1)}, u32[]{:S(2)}, u32[]{:S(2)}) %collective-permute-start.9) | collective-permute-done | bytes 20512 | tf_op jit(solution)/shard_map/ppermute | solution.py:281
  35.5 1.8 %solve.1 = f32[16,16]{1,0:T(8,128)} custom-call(f32[40,128]{1,0:T(8,128)S(1)} %grams.1.refs_0_, f32[40,128]{1,0:T(8,128)S(1)} %collective-permute-done.9.refs_1_, f32[40,128]{1,0:T(8,128)S(1)} %collective-permute-done.10.refs_2_, f32[40,128]{1,0:T(8,128)S(1)} %collective-permute-done.11.refs_3_), custom_call_target="tpu_custom_call" | custom-call | tf_op jit(solution)/shard_map/solve/pallas_call | solution.py:265
  (17 shorter events, 0.1 us)
Async XLA Ops:
  0.0 3.5 %copy-start = (f32[4,4096]{1,0:T(4,128)S(1)}, f32[4,4096]{1,0:T(4,128)}, u32[]{:S(2)}) copy-start(f32[4,4096]{1,0:T(4,128)} %param.13) | copy-start | bytes 196612
  0.0 3.5 %copy-start.1 = (s32[256]{0:T(256)S(1)}, s32[256]{0:T(256)}, u32[]{:S(2)}) copy-start(s32[256]{0:T(256)} %param.11) | copy-start | bytes 3076
  0.0 3.5 %copy-start.2 = (s32[16]{0:T(128)S(1)}, s32[16]{0:T(128)}, u32[]{:S(2)}) copy-start(s32[16]{0:T(128)} %param.12) | copy-start | bytes 196
  2.2 3.2 %collective-permute-start = (f32[128,256]{1,0:T(8,128)S(1)}, f32[128,256]{1,0:T(8,128)S(1)}, u32[]{:S(2)}, u32[]{:S(2)}) collective-permute-start(f32[128,256]{1,0:T(8,128)S(1)} %project.1.kept_ref), channel_id=1, source_target_pairs={{0,1},{2,3},{4,5},{6,7},{8,9},{10,11},{12,13},{14,15},{16,17},{18,... | collective-permute-start | bytes 393224 | tf_op jit(solution)/shard_map/ppermute | solution.py:281
  5.4 6.0 %collective-permute-start.5 = (f32[4,2048]{1,0:T(4,128)S(1)}, f32[4,2048]{1,0:T(4,128)S(1)}, u32[]{:S(2)}, u32[]{:S(2)}) collective-permute-start(f32[4,2048]{1,0:T(4,128)S(1)} %constant_dynamic-slice_fusion.refs_0_), channel_id=1, source_target_pairs={{0,4},{2,6},{4,0},{6,2},{8,12},{10,14},{12,8},{14,10},{16,20},{18,... | collective-permute-start | bytes 98312 | tf_op jit(solution)/shard_map/ppermute | solution.py:281
  6.1 5.4 %collective-permute-start.6 = (f32[4,2048]{1,0:T(4,128)S(1)}, f32[4,2048]{1,0:T(4,128)S(1)}, u32[]{:S(2)}, u32[]{:S(2)}) collective-permute-start(f32[4,2048]{1,0:T(4,128)S(1)} %constant_dynamic-slice_fusion.refs_0_), channel_id=1, source_target_pairs={{0,8},{2,10},{4,12},{6,14},{8,0},{10,2},{12,4},{14,6},{16,24},{18,... | collective-permute-start | bytes 98312 | tf_op jit(solution)/shard_map/ppermute | solution.py:281
  6.8 4.7 %collective-permute-start.7 = (f32[4,2048]{1,0:T(4,128)S(1)}, f32[4,2048]{1,0:T(4,128)S(1)}, u32[]{:S(2)}, u32[]{:S(2)}) collective-permute-start(f32[4,2048]{1,0:T(4,128)S(1)} %constant_dynamic-slice_fusion.refs_0_), channel_id=1, source_target_pairs={{0,12},{2,14},{4,8},{6,10},{8,4},{10,6},{12,0},{14,2},{16,28},{18,... | collective-permute-start | bytes 98312 | tf_op jit(solution)/shard_map/ppermute | solution.py:281
  7.5 5.9 %collective-permute-start.1 = (f32[96,256]{1,0:T(8,128)S(1)}, f32[96,256]{1,0:T(8,128)S(1)}, u32[]{:S(2)}, u32[]{:S(2)}) collective-permute-start(f32[96,256]{1,0:T(8,128)S(1)} %get-tuple-element.9), channel_id=1, source_target_pairs={{1,3},{3,1},{5,7},{7,5},{9,11},{11,9},{13,15},{15,13},{17,19},{19,... | collective-permute-start | bytes 294920 | tf_op jit(solution)/shard_map/ppermute | solution.py:281
  11.5 13.0 %collective-permute-start.8 = (f32[16,2048]{1,0:T(8,128)S(1)}, f32[16,2048]{1,0:T(8,128)S(1)}, u32[]{:S(2)}, u32[]{:S(2)}) collective-permute-start(f32[16,2048]{1,0:T(8,128)S(1)} %collect.1), channel_id=1, source_target_pairs={{0,1},{2,3},{4,5},{6,7},{8,9},{10,11},{12,13},{14,15},{16,17},{18,... | collective-permute-start | bytes 393224 | tf_op jit(solution)/shard_map/ppermute | solution.py:281
  13.8 10.8 %collective-permute-start.2 = (f32[16,16,128]{2,1,0:T(8,128)S(1)}, f32[16,16,128]{2,1,0:T(8,128)S(1)}, u32[]{:S(2)}, u32[]{:S(2)}) collective-permute-start(f32[16,16,128]{2,1,0:T(8,128)S(1)} %gradients.1.refs_3_), channel_id=1, source_target_pairs={{1,13},{3,15},{5,9},{7,11},{9,5},{11,7},{13,1},{15,3},{17,29},{19,... | collective-permute-start | bytes 393224 | tf_op jit(solution)/shard_map/ppermute | solution.py:281
  19.2 7.1 %collective-permute-start.3 = (f32[16,16,128]{2,1,0:T(8,128)S(1)}, f32[16,16,128]{2,1,0:T(8,128)S(1)}, u32[]{:S(2)}, u32[]{:S(2)}) collective-permute-start(f32[16,16,128]{2,1,0:T(8,128)S(1)} %gradients.1.refs_3_), channel_id=1, source_target_pairs={{1,9},{3,11},{5,13},{7,15},{9,1},{11,3},{13,5},{15,7},{17,25},{19,... | collective-permute-start | bytes 393224 | tf_op jit(solution)/shard_map/ppermute | solution.py:281
  21.2 6.5 %collective-permute-start.4 = (f32[16,16,128]{2,1,0:T(8,128)S(1)}, f32[16,16,128]{2,1,0:T(8,128)S(1)}, u32[]{:S(2)}, u32[]{:S(2)}) collective-permute-start(f32[16,16,128]{2,1,0:T(8,128)S(1)} %gradients.1.refs_3_), channel_id=1, source_target_pairs={{1,5},{3,7},{5,1},{7,3},{9,13},{11,15},{13,9},{15,11},{17,21},{19,... | collective-permute-start | bytes 393224 | tf_op jit(solution)/shard_map/ppermute | solution.py:281
  28.1 5.7 %collective-permute-start.10 = (f32[40,128]{1,0:T(8,128)S(1)}, f32[40,128]{1,0:T(8,128)S(1)}, u32[]{:S(2)}, u32[]{:S(2)}) collective-permute-start(f32[40,128]{1,0:T(8,128)S(1)} %grams.1.refs_0_), channel_id=1, source_target_pairs={{1,2},{3,0},{5,6},{7,4},{9,10},{11,8},{13,14},{15,12},{17,18},{19,... | collective-permute-start | bytes 61448 | tf_op jit(solution)/shard_map/ppermute | solution.py:281
  29.7 4.2 %collective-permute-start.11 = (f32[40,128]{1,0:T(8,128)S(1)}, f32[40,128]{1,0:T(8,128)S(1)}, u32[]{:S(2)}, u32[]{:S(2)}) collective-permute-start(f32[40,128]{1,0:T(8,128)S(1)} %grams.1.refs_0_), channel_id=1, source_target_pairs={{1,0},{3,2},{5,4},{7,6},{9,8},{11,10},{13,12},{15,14},{17,16},{19,... | collective-permute-start | bytes 61448 | tf_op jit(solution)/shard_map/ppermute | solution.py:281
  31.0 4.5 %collective-permute-start.9 = (f32[40,128]{1,0:T(8,128)S(1)}, f32[40,128]{1,0:T(8,128)S(1)}, u32[]{:S(2)}, u32[]{:S(2)}) collective-permute-start(f32[40,128]{1,0:T(8,128)S(1)} %grams.1.refs_0_), channel_id=1, source_target_pairs={{1,3},{3,1},{5,7},{7,5},{9,11},{11,9},{13,15},{15,13},{17,19},{19,... | collective-permute-start | bytes 61448 | tf_op jit(solution)/shard_map/ppermute | solution.py:281

commit v6 on v2

--- a/solution.py
+++ b/solution.py
@@ -143,8 +143,7 @@
     )(me, kept, came)
 
 
-def grads_kernel(own, pair, weights_ref, *refs):
-    kept_ref, came_ref, out_ref = refs
+def grads_kernel(own, pair, weights_ref, kept_ref, came_ref, asked_ref, out_ref):
     summed = kept_ref[...] + came_ref[...]
     weights = weights_ref[...]
     seqs = weights.shape[0]
@@ -166,55 +165,61 @@
             )
         )
     left = jnp.concatenate(rows, axis=0)
-    out_ref[...] = dot_nt(left, right).reshape(own // pair, seqs, right.shape[0])
-
-
-def gradients(weights, pieces, rank):
-    own = pieces[0].shape[0] - rank
+    count, lanes = left.shape[0], right.shape[0]
+    out_ref[:count, :] = dot_nt(left, right)
+    asked = asked_ref.shape[0]
+    for i in range(own // pair):
+        start = count + i * asked
+        out_ref[start : start + asked, :] = asked_ref[:, i * lanes : (i + 1) * lanes]
+
+
+def gradients(weights, kept, came, asked, rank):
+    own = kept.shape[0] - rank
     pair = 128 // rank
+    steps = own // pair
+    rows = steps * (weights.shape[0] + asked.shape[0])
     return pl.pallas_call(
         functools.partial(grads_kernel, own, pair),
-        out_shape=jax.ShapeDtypeStruct(
-            (own // pair, weights.shape[0], pair * rank), jnp.float32
-        ),
+        out_shape=jax.ShapeDtypeStruct((rows, pair * rank), jnp.float32),
         compiler_params=pltpu.CompilerParams(vmem_limit_bytes=VMEM_LIMIT),
         name="gradients",
-    )(weights, *pieces)
-
-
-def grams_kernel(count, me_ref, *refs):
-    grads, queries, out_ref = refs[:count], refs[count:-1], refs[-1]
-    me = me_ref[0]
-    lanes = [
-        jnp.concatenate([block[i] for block in grads], axis=0)
-        for i in range(grads[0].shape[0])
-    ]
-    every = jnp.concatenate(lanes, axis=1)
-    given = [block[...] for block in queries]
+    )(weights, kept, came, asked)
+
+
+def grams_kernel(steps, seqs, me_ref, *refs):
+    blocks, out_ref = refs[-2::-1], refs[-1]
+    count = steps * seqs
+    asked = (blocks[0].shape[0] - count) // steps
+    given = [block[count:, :] for block in blocks]
     ordered = []
-    for place in range(count):
+    for place in range(len(blocks)):
         chosen = given[0]
-        for m in range(1, count):
-            chosen = jnp.where((me ^ place) == m, given[m], chosen)
+        for m in range(1, len(blocks)):
+            chosen = jnp.where((me_ref[0] ^ place) == m, given[m], chosen)
         ordered.append(chosen)
-    both = jnp.concatenate([every] + ordered, axis=0)
-    result = dot_nt(both, every)
+    lanes = []
+    for i in range(steps):
+        rows = [block[i * seqs : (i + 1) * seqs, :] for block in blocks]
+        rows += [chosen[i * asked : (i + 1) * asked, :] for chosen in ordered]
+        lanes.append(jnp.concatenate(rows, axis=0))
+    both = jnp.concatenate(lanes, axis=1)
+    result = dot_nt(both, both[: len(blocks) * seqs])
     half = result.shape[0] // 2
     out_ref[...] = jnp.concatenate([result[:half, :], result[half:, :]], axis=1)
 
 
-def grams(me, grads, queries):
-    seqs = len(grads) * grads[0].shape[1]
-    asked = len(queries) * queries[0].shape[0]
+def grams(me, blocks, steps, seqs):
+    asked = blocks[0].shape[0] // steps - seqs
+    total = len(blocks) * seqs
     whole = pl.BlockSpec(memory_space=pltpu.VMEM)
     return pl.pallas_call(
-        functools.partial(grams_kernel, len(grads)),
-        out_shape=jax.ShapeDtypeStruct(((seqs + asked) // 2, 2 * seqs), jnp.float32),
-        in_specs=[pl.BlockSpec(memory_space=pltpu.SMEM)] + [whole] * (2 * len(grads)),
+        functools.partial(grams_kernel, steps, seqs),
+        out_shape=jax.ShapeDtypeStruct(((total + len(blocks) * asked) // 2, 2 * total), jnp.float32),
+        in_specs=[pl.BlockSpec(memory_space=pltpu.SMEM)] + [whole] * len(blocks),
         out_specs=whole,
         compiler_params=pltpu.CompilerParams(vmem_limit_bytes=VMEM_LIMIT),
         name="grams",
-    )(me, *grads, *queries)
+    )(me, *blocks)
 
 
 def scales(count):
@@ -230,7 +235,6 @@
 def solve_kernel(seqs, *refs):
     parts, out_ref = refs[:-1], refs[-1]
     packed = (parts[0][...] + parts[1][...]) + (parts[2][...] + parts[3][...])
-    half = packed.shape[0]
     lane = lax.broadcasted_iota(jnp.int32, packed.shape, 1)
     turned = pltpu.roll(packed, seqs, 1)
     both = jnp.concatenate(
@@ -272,24 +276,26 @@
     return lax.ppermute(value, axis, [(i, i ^ m) for i in range(size)])
 
 
-def from_partners(values, axis, size):
-    taken = [values[0]]
-    for m in range(1, size):
-        taken.append(from_partner(values[m], axis, size, m))
-    return taken
-
-
-def finish_long(grads, queries, first, seq_dev):
-    every = lax.all_gather(grads, "dp", axis=0)
-    steps, seqs, lanes = grads.shape
-    every = every.transpose(0, 2, 1, 3).reshape(-1, steps * lanes)
-    asked = lax.all_gather(queries, "dp", axis=0, tiled=True)
+def from_partners(value, axis, size):
+    return [from_partner(value, axis, size, m) for m in reversed(range(1, size))] + [value]
+
+
+def finish_long(message, steps, first, seq_dev):
+    every = lax.all_gather(message, "dp", axis=0)
+    lanes = message.shape[1]
+
+    def rows_of(block):
+        block = block.reshape(block.shape[0], steps, -1, lanes).transpose(0, 2, 1, 3)
+        return block.reshape(-1, steps * lanes)
+
+    count = steps * seq_dev
+    grads, asked = rows_of(every[:, :count]), rows_of(every[:, count:])
     both = jnp.einsum(
-        "ik,jk->ij", jnp.concatenate([every, asked], axis=0), every,
+        "ik,jk->ij", jnp.concatenate([grads, asked], axis=0), grads,
         precision=lax.Precision.HIGHEST,
     )
     both = lax.psum(both, "tensor")
-    count = every.shape[0]
+    count = grads.shape[0]
     kernel, products = both[:count], both[count:]
     damp = damping * jnp.trace(kernel) / count
     unit = jnp.eye(count, dtype=jnp.float32)
@@ -314,14 +320,12 @@
     came = from_partner(sent, "tensor", parts, 1)
     kept, sent = halve(kept, came, rank_of, parts, own)
     came = from_partner(sent, "tensor", parts, 2)
-    grads = gradients(weights, [kept, came], rank)
+    message = gradients(weights, kept, came, asked, rank)
+    steps = own * rank // message.shape[1]
     if blocks > SMALL:
-        return finish_long(grads, asked, first, seq_dev)
-    asked = from_partners([asked] * blocks, "dp", blocks)
-    grads, *asked = lax.optimization_barrier((grads, *asked))
-    grads = from_partners([grads] * blocks, "dp", blocks)
-    partial = grams(place.reshape(1), grads, asked)
-    partial = from_partners([partial] * parts, "tensor", parts)
+        return finish_long(message, steps, first, seq_dev)
+    partial = grams(place.reshape(1), from_partners(message, "dp", blocks), steps, seq_dev)
+    partial = from_partners(partial, "tensor", parts)
     return solve(partial, blocks * seq_dev, blocks * queries.shape[0], seq_dev)
 
 

time: 33.1 us -> 26.8 us (0.81)
  starting transfers between devices: 14.1 us -> 9.87 us
  waiting for transfers between devices: 13.1 us -> 12 us
  local copies, waits for them, and re-layouts: 0.84 us -> 0.01 us
    ppermute x11 -> x8, starting transfers between devices: 14.1 us -> 9.87 us  [from_partner(): return lax.ppermute(value, axis, [(i, i ^ m) for i in range(size)])]
    ppermute x11 -> x8, waiting for transfers between devices: 13.1 us -> 12 us  [from_partner(): return lax.ppermute(value, axis, [(i, i ^ m) for i in range(size)])]
    unnamed x6, local copies, waits for them, and re-layouts: 0.84 us -> 0.01 us
  transfers between devices with their start and end apart: 11 -> 8, of which waited for: 6 -> 6; matrix products, arithmetic and copies ran while one was open for 1% -> 1% of each run, Pallas kernels for 7% -> 0%
where the time goes in v6:
time: 26.8 us; the launch traced here: 26.7 us
  waiting for transfers between devices  12 us (45%)
  starting transfers between devices  9.87 us (37%)
  Pallas kernels  4.58 us (17%)
    ppermute x8, waiting for transfers between devices, from_partner(): return lax.ppermute(value, axis, [(i, i ^ m) for i in range(size)])  12 us
    ppermute x8, starting transfers between devices, from_partner(): return lax.ppermute(value, axis, [(i, i ^ m) for i in range(size)])  9.87 us
    pallas_call x1, Pallas kernels, project(): pl.pallas_call(functools.partial(project_kernel, parts, own), out_shape=[...  2.15 us
    pallas_call x1, Pallas kernels, solve(): pl.pallas_call(functools.partial(solve_kernel, seqs), out_shape=jax.Shape...  1.82 us
  transfers between devices with their start and end apart: 8, of which 6 were waited for; matrix products, arithmetic and copies ran while one was open for 1% of the time, Pallas kernels for 0%

profile of v6, /device:TPU:0, one launch (start us, length us, event | category | flops | bytes accessed | tf_op | source)
XLA Modules:
  0.0 26.7 jit_solution(11447672608391583742)
XLA Ops:
  0.0 0.0 copy-start
  0.0 2.1 %project.1 = (f32[96,256]{1,0:T(8,128)S(1)}, f32[96,256]{1,0:T(8,128)S(1)}) custom-call(s32[1]{0:T(128)} %bitcast.1.rank_ref, bf16[2752,256]{1,0:T(8,128)(2,1)} %bitcast.5, bf16[256,1024]{1,0:T(8,128)(2,1)} %g_hbm.1, bf16[64,2752]{1,0:T(8,128)(2,1)} %bitcast.6, bf16[64,1024]{1,0:T(8,128)(2,1)} %bitcast.7), custom_call_target="tpu_custom_call" | custom-call | tf_op jit(solution)/shard_map/project/pallas_call | solution.py:104
  2.2 0.5 %collective-permute-start = (f32[96,256]{1,0:T(8,128)S(1)}, f32[96,256]{1,0:T(8,128)S(1)}, u32[]{:S(2)}, u32[]{:S(2)}) collective-permute-start(f32[96,256]{1,0:T(8,128)S(1)} %get-tuple-element.10), channel_id=1, source_target_pairs={{0,1},{1,0},{2,3},{3,2},{4,5},{5,4},{6,7},{7,6},{8,9},{9,8},{10,11... | collective-permute-start | bytes 294920 | tf_op jit(solution)/shard_map/ppermute | solution.py:276
  2.7 0.1 convert_reduce_fusion
  2.8 0.1 fusion.1.weights_ref
  2.9 0.7 %collective-permute-done.came_ref = f32[96,256]{1,0:T(8,128)S(1)} collective-permute-done((f32[96,256]{1,0:T(8,128)S(1)}, f32[96,256]{1,0:T(8,128)S(1)}, u32[]{:S(2)}, u32[]{:S(2)}) %collective-permute-start) | collective-permute-done | bytes 98336 | tf_op jit(solution)/shard_map/ppermute | solution.py:276
  3.7 2.9 %collective-permute-start.1 = (f32[80,256]{1,0:T(8,128)S(1)}, f32[80,256]{1,0:T(8,128)S(1)}, u32[]{:S(2)}, u32[]{:S(2)}) collective-permute-start(f32[80,256]{1,0:T(8,128)S(1)} %get-tuple-element.12), channel_id=1, source_target_pairs={{0,2},{1,3},{2,0},{3,1},{4,6},{5,7},{6,4},{7,5},{8,10},{9,11},{10,... | collective-permute-start | bytes 245768 | tf_op jit(solution)/shard_map/ppermute | solution.py:276
  6.6 0.0 copy-done
  6.6 2.8 %collective-permute-done.1.came_ref = f32[80,256]{1,0:T(8,128)S(1)} collective-permute-done((f32[80,256]{1,0:T(8,128)S(1)}, f32[80,256]{1,0:T(8,128)S(1)}, u32[]{:S(2)}, u32[]{:S(2)}) %collective-permute-start.1) | collective-permute-done | bytes 81952 | tf_op jit(solution)/shard_map/ppermute | solution.py:276
  9.3 0.3 gradients.1.refs_3_
  9.6 3.9 %collective-permute-start.2 = (f32[160,128]{1,0:T(8,128)S(1)}, f32[160,128]{1,0:T(8,128)S(1)}, u32[]{:S(2)}, u32[]{:S(2)}) collective-permute-start(f32[160,128]{1,0:T(8,128)S(1)} %gradients.1.refs_3_), channel_id=1, source_target_pairs={{0,12},{4,8},{8,4},{12,0},{1,13},{5,9},{9,5},{13,1},{2,14},{6,10},... | collective-permute-start | bytes 245768 | tf_op jit(solution)/shard_map/ppermute | solution.py:276
  13.5 0.0 collective-permute-start.3
  13.5 0.6 %collective-permute-start.4 = (f32[160,128]{1,0:T(8,128)S(1)}, f32[160,128]{1,0:T(8,128)S(1)}, u32[]{:S(2)}, u32[]{:S(2)}) collective-permute-start(f32[160,128]{1,0:T(8,128)S(1)} %gradients.1.refs_3_), channel_id=1, source_target_pairs={{0,4},{4,0},{8,12},{12,8},{1,5},{5,1},{9,13},{13,9},{2,6},{6,2},{1... | collective-permute-start | bytes 245768 | tf_op jit(solution)/shard_map/ppermute | solution.py:276
  14.2 2.7 %collective-permute-done.2.refs_0_ = f32[160,128]{1,0:T(8,128)S(1)} collective-permute-done((f32[160,128]{1,0:T(8,128)S(1)}, f32[160,128]{1,0:T(8,128)S(1)}, u32[]{:S(2)}, u32[]{:S(2)}) %collective-permute-start.2) | collective-permute-done | bytes 81952 | tf_op jit(solution)/shard_map/ppermute | solution.py:276
  16.9 3.0 %collective-permute-done.3.refs_1_ = f32[160,128]{1,0:T(8,128)S(1)} collective-permute-done((f32[160,128]{1,0:T(8,128)S(1)}, f32[160,128]{1,0:T(8,128)S(1)}, u32[]{:S(2)}, u32[]{:S(2)}) %collective-permute-start.3) | collective-permute-done | bytes 81952 | tf_op jit(solution)/shard_map/ppermute | solution.py:276
  19.9 0.0 collective-permute-done.4.refs_2_
  19.9 0.3 %grams.1.refs_3_ = f32[40,128]{1,0:T(8,128)S(1)} custom-call(s32[1]{0:T(128)} %bitcast.me_ref, f32[160,128]{1,0:T(8,128)S(1)} %collective-permute-done.2.refs_0_, f32[160,128]{1,0:T(8,128)S(1)} %collective-permute-done.3.refs_1_, f32[160,128]{1,0:T(8,128)S(1)} %collective-permute-done.4.refs_2_, f32[160,128]{1,0:T(8,128)S(1)} %gradients.1.refs_3_), custom_call_target="tpu_custom_call" | custom-call | tf_op jit(solution)/shard_map/grams/pallas_call | solution.py:215
  20.2 0.9 %collective-permute-start.5 = (f32[40,128]{1,0:T(8,128)S(1)}, f32[40,128]{1,0:T(8,128)S(1)}, u32[]{:S(2)}, u32[]{:S(2)}) collective-permute-start(f32[40,128]{1,0:T(8,128)S(1)} %grams.1.refs_3_), channel_id=1, source_target_pairs={{0,3},{1,2},{2,1},{3,0},{4,7},{5,6},{6,5},{7,4},{8,11},{9,10},{10,... | collective-permute-start | bytes 61448 | tf_op jit(solution)/shard_map/ppermute | solution.py:276
  21.1 0.7 %collective-permute-start.6 = (f32[40,128]{1,0:T(8,128)S(1)}, f32[40,128]{1,0:T(8,128)S(1)}, u32[]{:S(2)}, u32[]{:S(2)}) collective-permute-start(f32[40,128]{1,0:T(8,128)S(1)} %grams.1.refs_3_), channel_id=1, source_target_pairs={{0,2},{1,3},{2,0},{3,1},{4,6},{5,7},{6,4},{7,5},{8,10},{9,11},{10,... | collective-permute-start | bytes 61448 | tf_op jit(solution)/shard_map/ppermute | solution.py:276
  21.8 0.3 %collective-permute-start.7 = (f32[40,128]{1,0:T(8,128)S(1)}, f32[40,128]{1,0:T(8,128)S(1)}, u32[]{:S(2)}, u32[]{:S(2)}) collective-permute-start(f32[40,128]{1,0:T(8,128)S(1)} %grams.1.refs_3_), channel_id=1, source_target_pairs={{0,1},{1,0},{2,3},{3,2},{4,5},{5,4},{6,7},{7,6},{8,9},{9,8},{10,11... | collective-permute-start | bytes 61448 | tf_op jit(solution)/shard_map/ppermute | solution.py:276
  22.1 1.5 %collective-permute-done.5.refs_0_ = f32[40,128]{1,0:T(8,128)S(1)} collective-permute-done((f32[40,128]{1,0:T(8,128)S(1)}, f32[40,128]{1,0:T(8,128)S(1)}, u32[]{:S(2)}, u32[]{:S(2)}) %collective-permute-start.5) | collective-permute-done | bytes 20512 | tf_op jit(solution)/shard_map/ppermute | solution.py:276
  23.6 1.3 %collective-permute-done.6.refs_1_ = f32[40,128]{1,0:T(8,128)S(1)} collective-permute-done((f32[40,128]{1,0:T(8,128)S(1)}, f32[40,128]{1,0:T(8,128)S(1)}, u32[]{:S(2)}, u32[]{:S(2)}) %collective-permute-start.6) | collective-permute-done | bytes 20512 | tf_op jit(solution)/shard_map/ppermute | solution.py:276
  24.9 0.0 collective-permute-done.7.refs_2_
  24.9 1.8 %solve.1 = f32[16,16]{1,0:T(8,128)} custom-call(f32[40,128]{1,0:T(8,128)S(1)} %collective-permute-done.5.refs_0_, f32[40,128]{1,0:T(8,128)S(1)} %collective-permute-done.6.refs_1_, f32[40,128]{1,0:T(8,128)S(1)} %collective-permute-done.7.refs_2_, f32[40,128]{1,0:T(8,128)S(1)} %grams.1.refs_3_), custom_call_target="tpu_custom_call" | custom-call | tf_op jit(solution)/shard_map/solve/pallas_call | solution.py:267
  (8 shorter events, 0.0 us)
Async XLA Ops:
  0.0 6.6 %copy-start = (f32[4,4096]{1,0:T(4,128)S(1)}, f32[4,4096]{1,0:T(4,128)}, u32[]{:S(2)}) copy-start(f32[4,4096]{1,0:T(4,128)} %param.13) | copy-start | bytes 196612
  0.0 2.7 %copy-start.1 = (s32[256]{0:T(256)S(1)}, s32[256]{0:T(256)}, u32[]{:S(2)}) copy-start(s32[256]{0:T(256)} %param.11) | copy-start | bytes 3076
  0.0 2.8 %copy-start.2 = (s32[16]{0:T(128)S(1)}, s32[16]{0:T(128)}, u32[]{:S(2)}) copy-start(s32[16]{0:T(128)} %param.12) | copy-start | bytes 196
  2.2 1.5 %collective-permute-start = (f32[96,256]{1,0:T(8,128)S(1)}, f32[96,256]{1,0:T(8,128)S(1)}, u32[]{:S(2)}, u32[]{:S(2)}) collective-permute-start(f32[96,256]{1,0:T(8,128)S(1)} %get-tuple-element.10), channel_id=1, source_target_pairs={{0,1},{1,0},{2,3},{3,2},{4,5},{5,4},{6,7},{7,6},{8,9},{9,8},{10,11... | collective-permute-start | bytes 294920 | tf_op jit(solution)/shard_map/ppermute | solution.py:276
  3.7 5.7 %collective-permute-start.1 = (f32[80,256]{1,0:T(8,128)S(1)}, f32[80,256]{1,0:T(8,128)S(1)}, u32[]{:S(2)}, u32[]{:S(2)}) collective-permute-start(f32[80,256]{1,0:T(8,128)S(1)} %get-tuple-element.12), channel_id=1, source_target_pairs={{0,2},{1,3},{2,0},{3,1},{4,6},{5,7},{6,4},{7,5},{8,10},{9,11},{10,... | collective-permute-start | bytes 245768 | tf_op jit(solution)/shard_map/ppermute | solution.py:276
  9.6 7.3 %collective-permute-start.2 = (f32[160,128]{1,0:T(8,128)S(1)}, f32[160,128]{1,0:T(8,128)S(1)}, u32[]{:S(2)}, u32[]{:S(2)}) collective-permute-start(f32[160,128]{1,0:T(8,128)S(1)} %gradients.1.refs_3_), channel_id=1, source_target_pairs={{0,12},{4,8},{8,4},{12,0},{1,13},{5,9},{9,5},{13,1},{2,14},{6,10},... | collective-permute-start | bytes 245768 | tf_op jit(solution)/shard_map/ppermute | solution.py:276
  13.5 6.3 %collective-permute-start.3 = (f32[160,128]{1,0:T(8,128)S(1)}, f32[160,128]{1,0:T(8,128)S(1)}, u32[]{:S(2)}, u32[]{:S(2)}) collective-permute-start(f32[160,128]{1,0:T(8,128)S(1)} %gradients.1.refs_3_), channel_id=1, source_target_pairs={{0,8},{4,12},{8,0},{12,4},{1,9},{5,13},{9,1},{13,5},{2,10},{6,14},... | collective-permute-start | bytes 245768 | tf_op jit(solution)/shard_map/ppermute | solution.py:276
  13.5 6.3 %collective-permute-start.4 = (f32[160,128]{1,0:T(8,128)S(1)}, f32[160,128]{1,0:T(8,128)S(1)}, u32[]{:S(2)}, u32[]{:S(2)}) collective-permute-start(f32[160,128]{1,0:T(8,128)S(1)} %gradients.1.refs_3_), channel_id=1, source_target_pairs={{0,4},{4,0},{8,12},{12,8},{1,5},{5,1},{9,13},{13,9},{2,6},{6,2},{1... | collective-permute-start | bytes 245768 | tf_op jit(solution)/shard_map/ppermute | solution.py:276
  20.2 3.4 %collective-permute-start.5 = (f32[40,128]{1,0:T(8,128)S(1)}, f32[40,128]{1,0:T(8,128)S(1)}, u32[]{:S(2)}, u32[]{:S(2)}) collective-permute-start(f32[40,128]{1,0:T(8,128)S(1)} %grams.1.refs_3_), channel_id=1, source_target_pairs={{0,3},{1,2},{2,1},{3,0},{4,7},{5,6},{6,5},{7,4},{8,11},{9,10},{10,... | collective-permute-start | bytes 61448 | tf_op jit(solution)/shard_map/ppermute | solution.py:276
  21.1 3.8 %collective-permute-start.6 = (f32[40,128]{1,0:T(8,128)S(1)}, f32[40,128]{1,0:T(8,128)S(1)}, u32[]{:S(2)}, u32[]{:S(2)}) collective-permute-start(f32[40,128]{1,0:T(8,128)S(1)} %grams.1.refs_3_), channel_id=1, source_target_pairs={{0,2},{1,3},{2,0},{3,1},{4,6},{5,7},{6,4},{7,5},{8,10},{9,11},{10,... | collective-permute-start | bytes 61448 | tf_op jit(solution)/shard_map/ppermute | solution.py:276
  21.8 3.1 %collective-permute-start.7 = (f32[40,128]{1,0:T(8,128)S(1)}, f32[40,128]{1,0:T(8,128)S(1)}, u32[]{:S(2)}, u32[]{:S(2)}) collective-permute-start(f32[40,128]{1,0:T(8,128)S(1)} %grams.1.refs_3_), channel_id=1, source_target_pairs={{0,1},{1,0},{2,3},{3,2},{4,5},{5,4},{6,7},{7,6},{8,9},{9,8},{10,11... | collective-permute-start | bytes 61448 | tf_op jit(solution)/shard_map/ppermute | solution.py:276

commit v7 on v6

--- a/solution.py
+++ b/solution.py
@@ -143,7 +143,7 @@
     )(me, kept, came)
 
 
-def grads_kernel(own, pair, weights_ref, kept_ref, came_ref, asked_ref, out_ref):
+def grads_kernel(own, pair, weights_ref, kept_ref, came_ref, out_ref):
     summed = kept_ref[...] + came_ref[...]
     weights = weights_ref[...]
     seqs = weights.shape[0]
@@ -165,61 +165,66 @@
             )
         )
     left = jnp.concatenate(rows, axis=0)
-    count, lanes = left.shape[0], right.shape[0]
-    out_ref[:count, :] = dot_nt(left, right)
-    asked = asked_ref.shape[0]
-    for i in range(own // pair):
-        start = count + i * asked
-        out_ref[start : start + asked, :] = asked_ref[:, i * lanes : (i + 1) * lanes]
-
-
-def gradients(weights, kept, came, asked, rank):
+    out_ref[...] = dot_nt(left, right)
+
+
+def gradients(weights, kept, came, rank):
     own = kept.shape[0] - rank
     pair = 128 // rank
-    steps = own // pair
-    rows = steps * (weights.shape[0] + asked.shape[0])
     return pl.pallas_call(
         functools.partial(grads_kernel, own, pair),
-        out_shape=jax.ShapeDtypeStruct((rows, pair * rank), jnp.float32),
+        out_shape=jax.ShapeDtypeStruct((own // pair * weights.shape[0], pair * rank), jnp.float32),
         compiler_params=pltpu.CompilerParams(vmem_limit_bytes=VMEM_LIMIT),
         name="gradients",
-    )(weights, kept, came, asked)
-
-
-def grams_kernel(steps, seqs, me_ref, *refs):
-    blocks, out_ref = refs[-2::-1], refs[-1]
-    count = steps * seqs
-    asked = (blocks[0].shape[0] - count) // steps
-    given = [block[count:, :] for block in blocks]
+    )(weights, kept, came)
+
+
+def join_kernel(upper_ref, lower_ref, out_ref):
+    out_ref[...] = jnp.concatenate([upper_ref[...], lower_ref[...]], axis=0)
+
+
+def join(upper, lower):
+    return pl.pallas_call(
+        join_kernel,
+        out_shape=jax.ShapeDtypeStruct((2 * upper.shape[0], upper.shape[1]), upper.dtype),
+        compiler_params=pltpu.CompilerParams(vmem_limit_bytes=VMEM_LIMIT),
+        name="join",
+    )(upper, lower)
+
+
+def grams_kernel(seqs, me_ref, *refs):
+    blocks, pairs, out_ref = refs[-4::-1], refs[-3:-1], refs[-1]
+    steps = blocks[0].shape[0] // seqs
+    asked = pairs[0].shape[0] // 2
+    lanes = [
+        jnp.concatenate([block[i * seqs : (i + 1) * seqs, :] for block in blocks], axis=0)
+        for i in range(steps)
+    ]
+    every = jnp.concatenate(lanes, axis=1)
+    given = [pair[at * asked : (at + 1) * asked, :] for at in (0, 1) for pair in pairs]
     ordered = []
     for place in range(len(blocks)):
         chosen = given[0]
         for m in range(1, len(blocks)):
             chosen = jnp.where((me_ref[0] ^ place) == m, given[m], chosen)
         ordered.append(chosen)
-    lanes = []
-    for i in range(steps):
-        rows = [block[i * seqs : (i + 1) * seqs, :] for block in blocks]
-        rows += [chosen[i * asked : (i + 1) * asked, :] for chosen in ordered]
-        lanes.append(jnp.concatenate(rows, axis=0))
-    both = jnp.concatenate(lanes, axis=1)
-    result = dot_nt(both, both[: len(blocks) * seqs])
+    result = dot_nt(jnp.concatenate([every] + ordered, axis=0), every)
     half = result.shape[0] // 2
     out_ref[...] = jnp.concatenate([result[:half, :], result[half:, :]], axis=1)
 
 
-def grams(me, blocks, steps, seqs):
-    asked = blocks[0].shape[0] // steps - seqs
+def grams(me, blocks, seqs, pairs):
     total = len(blocks) * seqs
+    rows = total + 2 * pairs[0].shape[0]
     whole = pl.BlockSpec(memory_space=pltpu.VMEM)
     return pl.pallas_call(
-        functools.partial(grams_kernel, steps, seqs),
-        out_shape=jax.ShapeDtypeStruct(((total + len(blocks) * asked) // 2, 2 * total), jnp.float32),
-        in_specs=[pl.BlockSpec(memory_space=pltpu.SMEM)] + [whole] * len(blocks),
+        functools.partial(grams_kernel, seqs),
+        out_shape=jax.ShapeDtypeStruct((rows // 2, 2 * total), jnp.float32),
+        in_specs=[pl.BlockSpec(memory_space=pltpu.SMEM)] + [whole] * (len(blocks) + 2),
         out_specs=whole,
         compiler_params=pltpu.CompilerParams(vmem_limit_bytes=VMEM_LIMIT),
         name="grams",
-    )(me, *blocks)
+    )(me, *blocks, *pairs)
 
 
 def scales(count):
@@ -280,22 +285,18 @@
     return [from_partner(value, axis, size, m) for m in reversed(range(1, size))] + [value]
 
 
-def finish_long(message, steps, first, seq_dev):
-    every = lax.all_gather(message, "dp", axis=0)
-    lanes = message.shape[1]
-
-    def rows_of(block):
-        block = block.reshape(block.shape[0], steps, -1, lanes).transpose(0, 2, 1, 3)
-        return block.reshape(-1, steps * lanes)
-
-    count = steps * seq_dev
-    grads, asked = rows_of(every[:, :count]), rows_of(every[:, count:])
+def finish_long(grads, asked, first, seq_dev):
+    lanes = grads.shape[1]
+    every = lax.all_gather(grads, "dp", axis=0)
+    every = every.reshape(every.shape[0], -1, seq_dev, lanes).transpose(0, 2, 1, 3)
+    every = every.reshape(-1, asked.shape[1])
+    asked = lax.all_gather(asked, "dp", axis=0, tiled=True)
     both = jnp.einsum(
-        "ik,jk->ij", jnp.concatenate([grads, asked], axis=0), grads,
+        "ik,jk->ij", jnp.concatenate([every, asked], axis=0), every,
         precision=lax.Precision.HIGHEST,
     )
     both = lax.psum(both, "tensor")
-    count = grads.shape[0]
+    count = every.shape[0]
     kernel, products = both[:count], both[count:]
     damp = damping * jnp.trace(kernel) / count
     unit = jnp.eye(count, dtype=jnp.float32)
@@ -316,15 +317,20 @@
     rank_of = me.reshape(1)
     kept, sent = project(inputs, out_grads, in_proj, out_proj, rank_of, parts)
     asked = lax.dynamic_slice_in_dim(queries, me * (own * rank), own * rank, 1)
-    weights = token_weights(seq_ids, counts, first)
     came = from_partner(sent, "tensor", parts, 1)
     kept, sent = halve(kept, came, rank_of, parts, own)
     came = from_partner(sent, "tensor", parts, 2)
-    message = gradients(weights, kept, came, asked, rank)
-    steps = own * rank // message.shape[1]
+    kept, counts = lax.optimization_barrier((kept, counts))
+    weights = token_weights(seq_ids, counts, first)
+    weights, asked = lax.optimization_barrier((weights, asked))
+    if blocks <= SMALL:
+        asked = join(asked, from_partner(asked, "dp", blocks, 2))
+    grads = gradients(weights, kept, came, rank)
     if blocks > SMALL:
-        return finish_long(message, steps, first, seq_dev)
-    partial = grams(place.reshape(1), from_partners(message, "dp", blocks), steps, seq_dev)
+        return finish_long(grads, asked, first, seq_dev)
+    grads, asked = lax.optimization_barrier((grads, asked))
+    pairs = [asked, from_partner(asked, "dp", blocks, 1)]
+    partial = grams(place.reshape(1), from_partners(grads, "dp", blocks), seq_dev, pairs)
     partial = from_partners(partial, "tensor", parts)
     return solve(partial, blocks * seq_dev, blocks * queries.shape[0], seq_dev)
 

time: 26.8 us -> 27 us (level)
  starting transfers between devices: 9.87 us -> 13.6 us
  waiting for transfers between devices: 12 us -> 8.44 us
    ppermute x8 -> x10, starting transfers between devices: 9.87 us -> 13.6 us  [from_partner(): return lax.ppermute(value, axis, [(i, i ^ m) for i in range(size)])]
    ppermute x8 -> x10, waiting for transfers between devices: 12 us -> 8.44 us  [from_partner(): return lax.ppermute(value, axis, [(i, i ^ m) for i in range(size)])]
  transfers between devices with their start and end apart: 8 -> 10, of which waited for: 6 -> 5; matrix products, arithmetic and copies ran while one was open for 1% -> 1% of each run, Pallas kernels for 0% -> 0%
where the time goes in v7:
time: 27 us; the launch traced here: 26.9 us
  starting transfers between devices  13.6 us (50%)
  waiting for transfers between devices  8.44 us (31%)
  Pallas kernels  4.6 us (17%)
    ppermute x10, starting transfers between devices, from_partner(): return lax.ppermute(value, axis, [(i, i ^ m) for i in range(size)])  13.6 us
    ppermute x10, waiting for transfers between devices, from_partner(): return lax.ppermute(value, axis, [(i, i ^ m) for i in range(size)])  8.44 us
    pallas_call x1, Pallas kernels, project(): pl.pallas_call(functools.partial(project_kernel, parts, own), out_shape=[...  2.15 us
    pallas_call x1, Pallas kernels, solve(): pl.pallas_call(functools.partial(solve_kernel, seqs), out_shape=jax.Shape...  1.82 us
  transfers between devices with their start and end apart: 10, of which 5 were waited for; matrix products, arithmetic and copies ran while one was open for 1% of the time, Pallas kernels for 0%

profile of v7, /device:TPU:0, one launch (start us, length us, event | category | flops | bytes accessed | tf_op | source)
XLA Modules:
  0.0 26.9 jit_solution(10630646960303135841)
XLA Ops:
  0.0 2.2 %project.1 = (f32[96,256]{1,0:T(8,128)S(1)}, f32[96,256]{1,0:T(8,128)S(1)}) custom-call(s32[1]{0:T(128)} %bitcast.1.rank_ref, bf16[2752,256]{1,0:T(8,128)(2,1)} %bitcast.5, bf16[256,1024]{1,0:T(8,128)(2,1)} %g_hbm.1, bf16[64,2752]{1,0:T(8,128)(2,1)} %bitcast.6, bf16[64,1024]{1,0:T(8,128)(2,1)} %bitcast.7), custom_call_target="tpu_custom_call" | custom-call | tf_op jit(solution)/shard_map/project/pallas_call | solution.py:104
  2.2 0.5 %collective-permute-start = (f32[96,256]{1,0:T(8,128)S(1)}, f32[96,256]{1,0:T(8,128)S(1)}, u32[]{:S(2)}, u32[]{:S(2)}) collective-permute-start(f32[96,256]{1,0:T(8,128)S(1)} %get-tuple-element.16), channel_id=1, source_target_pairs={{0,1},{1,0},{2,3},{3,2},{4,5},{5,4},{6,7},{7,6},{8,9},{9,8},{10,11... | collective-permute-start | bytes 294920 | tf_op jit(solution)/shard_map/ppermute | solution.py:281
  2.7 0.1 convert_reduce_fusion
  2.8 0.8 %collective-permute-done.came_ref = f32[96,256]{1,0:T(8,128)S(1)} collective-permute-done((f32[96,256]{1,0:T(8,128)S(1)}, f32[96,256]{1,0:T(8,128)S(1)}, u32[]{:S(2)}, u32[]{:S(2)}) %collective-permute-start) | collective-permute-done | bytes 98336 | tf_op jit(solution)/shard_map/ppermute | solution.py:281
  3.7 2.9 %collective-permute-start.1 = (f32[80,256]{1,0:T(8,128)S(1)}, f32[80,256]{1,0:T(8,128)S(1)}, u32[]{:S(2)}, u32[]{:S(2)}) collective-permute-start(f32[80,256]{1,0:T(8,128)S(1)} %get-tuple-element.21), channel_id=1, source_target_pairs={{0,2},{1,3},{2,0},{3,1},{4,6},{5,7},{6,4},{7,5},{8,10},{9,11},{10,... | collective-permute-start | bytes 245768 | tf_op jit(solution)/shard_map/ppermute | solution.py:281
  6.6 0.1 fusion.1.weights_ref
  6.7 2.6 %collective-permute-start.2 = (f32[4,1024]{1,0:T(4,128)S(1)}, f32[4,1024]{1,0:T(4,128)S(1)}, u32[]{:S(2)}, u32[]{:S(2)}) collective-permute-start(f32[4,1024]{1,0:T(4,128)S(1)} %constant_dynamic-slice_fusion.upper_ref), channel_id=1, source_target_pairs={{0,8},{4,12},{8,0},{12,4},{1,9},{5,13},{9,1},{13,5},{2,10},{6,14},... | collective-permute-start | bytes 49160 | tf_op jit(solution)/shard_map/ppermute | solution.py:281
  9.3 2.1 %collective-permute-done.2.lower_ref = f32[4,1024]{1,0:T(4,128)S(1)} collective-permute-done((f32[4,1024]{1,0:T(4,128)S(1)}, f32[4,1024]{1,0:T(4,128)S(1)}, u32[]{:S(2)}, u32[]{:S(2)}) %collective-permute-start.2) | collective-permute-done | bytes 16416 | tf_op jit(solution)/shard_map/ppermute | solution.py:281
  11.4 0.0 collective-permute-done.1.came_ref
  11.4 0.3 gradients.1.refs_3_
  11.7 3.6 %collective-permute-start.3 = (f32[128,128]{1,0:T(8,128)S(1)}, f32[128,128]{1,0:T(8,128)S(1)}, u32[]{:S(2)}, u32[]{:S(2)}) collective-permute-start(f32[128,128]{1,0:T(8,128)S(1)} %gradients.1.refs_3_), channel_id=1, source_target_pairs={{0,12},{4,8},{8,4},{12,0},{1,13},{5,9},{9,5},{13,1},{2,14},{6,10},... | collective-permute-start | bytes 196616 | tf_op jit(solution)/shard_map/ppermute | solution.py:281
  15.3 0.0 collective-permute-start.4
  15.3 0.8 %collective-permute-start.5 = (f32[128,128]{1,0:T(8,128)S(1)}, f32[128,128]{1,0:T(8,128)S(1)}, u32[]{:S(2)}, u32[]{:S(2)}) collective-permute-start(f32[128,128]{1,0:T(8,128)S(1)} %gradients.1.refs_3_), channel_id=1, source_target_pairs={{0,4},{4,0},{8,12},{12,8},{1,5},{5,1},{9,13},{13,9},{2,6},{6,2},{1... | collective-permute-start | bytes 196616 | tf_op jit(solution)/shard_map/ppermute | solution.py:281
  16.1 1.2 %collective-permute-start.6 = (f32[8,1024]{1,0:T(8,128)S(1)}, f32[8,1024]{1,0:T(8,128)S(1)}, u32[]{:S(2)}, u32[]{:S(2)}) collective-permute-start(f32[8,1024]{1,0:T(8,128)S(1)} %join.1.refs_4_), channel_id=1, source_target_pairs={{0,4},{4,0},{8,12},{12,8},{1,5},{5,1},{9,13},{13,9},{2,6},{6,2},{1... | collective-permute-start | bytes 98312 | tf_op jit(solution)/shard_map/ppermute | solution.py:281
  17.3 3.5 %collective-permute-done.6.refs_5_ = f32[8,1024]{1,0:T(8,128)S(1)} collective-permute-done((f32[8,1024]{1,0:T(8,128)S(1)}, f32[8,1024]{1,0:T(8,128)S(1)}, u32[]{:S(2)}, u32[]{:S(2)}) %collective-permute-start.6) | collective-permute-done | bytes 32800 | tf_op jit(solution)/shard_map/ppermute | solution.py:281
  20.8 0.0 collective-permute-done.3.refs_0_
  20.8 0.0 collective-permute-done.4.refs_1_
  20.8 0.4 %grams.1.refs_3_ = f32[40,128]{1,0:T(8,128)S(1)} custom-call(s32[1]{0:T(128)} %bitcast.me_ref, f32[128,128]{1,0:T(8,128)S(1)} %collective-permute-done.3.refs_0_, f32[128,128]{1,0:T(8,128)S(1)} %collective-permute-done.4.refs_1_, f32[128,128]{1,0:T(8,128)S(1)} %collective-permute-done.5.refs_2_, f32[128,128]{1,0:T(8,128)S(1)} %gradients.1.refs_3_, ...), custom_call_target="tpu_custom_call" | custom-call | tf_op jit(solution)/shard_map/grams/pallas_call | solution.py:220
  21.2 0.0 collective-permute-start.7
  21.2 0.6 %collective-permute-start.8 = (f32[40,128]{1,0:T(8,128)S(1)}, f32[40,128]{1,0:T(8,128)S(1)}, u32[]{:S(2)}, u32[]{:S(2)}) collective-permute-start(f32[40,128]{1,0:T(8,128)S(1)} %grams.1.refs_3_), channel_id=1, source_target_pairs={{0,2},{1,3},{2,0},{3,1},{4,6},{5,7},{6,4},{7,5},{8,10},{9,11},{10,... | collective-permute-start | bytes 61448 | tf_op jit(solution)/shard_map/ppermute | solution.py:281
  21.8 1.3 %collective-permute-start.9 = (f32[40,128]{1,0:T(8,128)S(1)}, f32[40,128]{1,0:T(8,128)S(1)}, u32[]{:S(2)}, u32[]{:S(2)}) collective-permute-start(f32[40,128]{1,0:T(8,128)S(1)} %grams.1.refs_3_), channel_id=1, source_target_pairs={{0,1},{1,0},{2,3},{3,2},{4,5},{5,4},{6,7},{7,6},{8,9},{9,8},{10,11... | collective-permute-start | bytes 61448 | tf_op jit(solution)/shard_map/ppermute | solution.py:281
  23.1 1.3 %collective-permute-done.7.refs_0_ = f32[40,128]{1,0:T(8,128)S(1)} collective-permute-done((f32[40,128]{1,0:T(8,128)S(1)}, f32[40,128]{1,0:T(8,128)S(1)}, u32[]{:S(2)}, u32[]{:S(2)}) %collective-permute-start.7) | collective-permute-done | bytes 20512 | tf_op jit(solution)/shard_map/ppermute | solution.py:281
  24.4 0.7 %collective-permute-done.8.refs_1_ = f32[40,128]{1,0:T(8,128)S(1)} collective-permute-done((f32[40,128]{1,0:T(8,128)S(1)}, f32[40,128]{1,0:T(8,128)S(1)}, u32[]{:S(2)}, u32[]{:S(2)}) %collective-permute-start.8) | collective-permute-done | bytes 20512 | tf_op jit(solution)/shard_map/ppermute | solution.py:281
  25.1 1.8 %solve.1 = f32[16,16]{1,0:T(8,128)} custom-call(f32[40,128]{1,0:T(8,128)S(1)} %collective-permute-done.7.refs_0_, f32[40,128]{1,0:T(8,128)S(1)} %collective-permute-done.8.refs_1_, f32[40,128]{1,0:T(8,128)S(1)} %collective-permute-done.9.refs_2_, f32[40,128]{1,0:T(8,128)S(1)} %grams.1.refs_3_), custom_call_target="tpu_custom_call" | custom-call | tf_op jit(solution)/shard_map/solve/pallas_call | solution.py:272
  (13 shorter events, 0.1 us)
Async XLA Ops:
  0.0 2.7 %copy-start = (f32[4,4096]{1,0:T(4,128)S(1)}, f32[4,4096]{1,0:T(4,128)}, u32[]{:S(2)}) copy-start(f32[4,4096]{1,0:T(4,128)} %param.13) | copy-start | bytes 196612
  0.0 2.7 %copy-start.1 = (s32[256]{0:T(256)S(1)}, s32[256]{0:T(256)}, u32[]{:S(2)}) copy-start(s32[256]{0:T(256)} %param.11) | copy-start | bytes 3076
  0.0 3.7 %copy-start.2 = (s32[16]{0:T(128)S(1)}, s32[16]{0:T(128)}, u32[]{:S(2)}) copy-start(s32[16]{0:T(128)} %param.12) | copy-start | bytes 196
  2.2 1.5 %collective-permute-start = (f32[96,256]{1,0:T(8,128)S(1)}, f32[96,256]{1,0:T(8,128)S(1)}, u32[]{:S(2)}, u32[]{:S(2)}) collective-permute-start(f32[96,256]{1,0:T(8,128)S(1)} %get-tuple-element.16), channel_id=1, source_target_pairs={{0,1},{1,0},{2,3},{3,2},{4,5},{5,4},{6,7},{7,6},{8,9},{9,8},{10,11... | collective-permute-start | bytes 294920 | tf_op jit(solution)/shard_map/ppermute | solution.py:281
  3.7 7.7 %collective-permute-start.1 = (f32[80,256]{1,0:T(8,128)S(1)}, f32[80,256]{1,0:T(8,128)S(1)}, u32[]{:S(2)}, u32[]{:S(2)}) collective-permute-start(f32[80,256]{1,0:T(8,128)S(1)} %get-tuple-element.21), channel_id=1, source_target_pairs={{0,2},{1,3},{2,0},{3,1},{4,6},{5,7},{6,4},{7,5},{8,10},{9,11},{10,... | collective-permute-start | bytes 245768 | tf_op jit(solution)/shard_map/ppermute | solution.py:281
  6.7 4.7 %collective-permute-start.2 = (f32[4,1024]{1,0:T(4,128)S(1)}, f32[4,1024]{1,0:T(4,128)S(1)}, u32[]{:S(2)}, u32[]{:S(2)}) collective-permute-start(f32[4,1024]{1,0:T(4,128)S(1)} %constant_dynamic-slice_fusion.upper_ref), channel_id=1, source_target_pairs={{0,8},{4,12},{8,0},{12,4},{1,9},{5,13},{9,1},{13,5},{2,10},{6,14},... | collective-permute-start | bytes 49160 | tf_op jit(solution)/shard_map/ppermute | solution.py:281
  11.7 9.2 %collective-permute-start.3 = (f32[128,128]{1,0:T(8,128)S(1)}, f32[128,128]{1,0:T(8,128)S(1)}, u32[]{:S(2)}, u32[]{:S(2)}) collective-permute-start(f32[128,128]{1,0:T(8,128)S(1)} %gradients.1.refs_3_), channel_id=1, source_target_pairs={{0,12},{4,8},{8,4},{12,0},{1,13},{5,9},{9,5},{13,1},{2,14},{6,10},... | collective-permute-start | bytes 196616 | tf_op jit(solution)/shard_map/ppermute | solution.py:281
  15.3 5.5 %collective-permute-start.4 = (f32[128,128]{1,0:T(8,128)S(1)}, f32[128,128]{1,0:T(8,128)S(1)}, u32[]{:S(2)}, u32[]{:S(2)}) collective-permute-start(f32[128,128]{1,0:T(8,128)S(1)} %gradients.1.refs_3_), channel_id=1, source_target_pairs={{0,8},{4,12},{8,0},{12,4},{1,9},{5,13},{9,1},{13,5},{2,10},{6,14},... | collective-permute-start | bytes 196616 | tf_op jit(solution)/shard_map/ppermute | solution.py:281
  15.3 5.5 %collective-permute-start.5 = (f32[128,128]{1,0:T(8,128)S(1)}, f32[128,128]{1,0:T(8,128)S(1)}, u32[]{:S(2)}, u32[]{:S(2)}) collective-permute-start(f32[128,128]{1,0:T(8,128)S(1)} %gradients.1.refs_3_), channel_id=1, source_target_pairs={{0,4},{4,0},{8,12},{12,8},{1,5},{5,1},{9,13},{13,9},{2,6},{6,2},{1... | collective-permute-start | bytes 196616 | tf_op jit(solution)/shard_map/ppermute | solution.py:281
  16.1 4.7 %collective-permute-start.6 = (f32[8,1024]{1,0:T(8,128)S(1)}, f32[8,1024]{1,0:T(8,128)S(1)}, u32[]{:S(2)}, u32[]{:S(2)}) collective-permute-start(f32[8,1024]{1,0:T(8,128)S(1)} %join.1.refs_4_), channel_id=1, source_target_pairs={{0,4},{4,0},{8,12},{12,8},{1,5},{5,1},{9,13},{13,9},{2,6},{6,2},{1... | collective-permute-start | bytes 98312 | tf_op jit(solution)/shard_map/ppermute | solution.py:281
  21.2 3.2 %collective-permute-start.7 = (f32[40,128]{1,0:T(8,128)S(1)}, f32[40,128]{1,0:T(8,128)S(1)}, u32[]{:S(2)}, u32[]{:S(2)}) collective-permute-start(f32[40,128]{1,0:T(8,128)S(1)} %grams.1.refs_3_), channel_id=1, source_target_pairs={{0,3},{1,2},{2,1},{3,0},{4,7},{5,6},{6,5},{7,4},{8,11},{9,10},{10,... | collective-permute-start | bytes 61448 | tf_op jit(solution)/shard_map/ppermute | solution.py:281
  21.2 3.8 %collective-permute-start.8 = (f32[40,128]{1,0:T(8,128)S(1)}, f32[40,128]{1,0:T(8,128)S(1)}, u32[]{:S(2)}, u32[]{:S(2)}) collective-permute-start(f32[40,128]{1,0:T(8,128)S(1)} %grams.1.refs_3_), channel_id=1, source_target_pairs={{0,2},{1,3},{2,0},{3,1},{4,6},{5,7},{6,4},{7,5},{8,10},{9,11},{10,... | collective-permute-start | bytes 61448 | tf_op jit(solution)/shard_map/ppermute | solution.py:281
  21.8 3.3 %collective-permute-start.9 = (f32[40,128]{1,0:T(8,128)S(1)}, f32[40,128]{1,0:T(8,128)S(1)}, u32[]{:S(2)}, u32[]{:S(2)}) collective-permute-start(f32[40,128]{1,0:T(8,128)S(1)} %grams.1.refs_3_), channel_id=1, source_target_pairs={{0,1},{1,0},{2,3},{3,2},{4,5},{5,4},{6,7},{7,6},{8,9},{9,8},{10,11... | collective-permute-start | bytes 61448 | tf_op jit(solution)/shard_map/ppermute | solution.py:281

commit v8 on v5

--- a/solution.py
+++ b/solution.py
@@ -198,7 +198,7 @@
 
 
 def grams_kernel(*refs):
-    grads, queries_ref, out_ref = refs[-3::-1], refs[-2], refs[-1]
+    queries_ref, grads, out_ref = refs[0], refs[1:-1], refs[-1]
     lanes = [
         jnp.concatenate([block[i] for block in grads], axis=0)
         for i in range(grads[0].shape[0])
@@ -217,7 +217,7 @@
         out_shape=jax.ShapeDtypeStruct(((seqs + queries.shape[0]) // 2, 2 * seqs), jnp.float32),
         compiler_params=pltpu.CompilerParams(vmem_limit_bytes=VMEM_LIMIT),
         name="grams",
-    )(*grads, queries)
+    )(queries, *grads)
 
 
 def scales(count):
@@ -232,7 +232,7 @@
 
 def solve_kernel(seqs, *refs):
     parts, out_ref = refs[:-1], refs[-1]
-    packed = (parts[0][...] + parts[1][...]) + (parts[2][...] + parts[3][...])
+    packed = parts[0][...] + parts[1][...]
     lane = lax.broadcasted_iota(jnp.int32, packed.shape, 1)
     turned = pltpu.roll(packed, seqs, 1)
     both = jnp.concatenate(
@@ -275,15 +275,27 @@
     pairs = []
     for d in range(blocks):
         for r in range(parts):
-            to = target(d, r)
-            if to is not None:
-                pairs.append((d * parts + r, to[0] * parts + to[1]))
+            block, rank = target(d, r)
+            pairs.append((d * parts + r, block * parts + rank))
     return lax.ppermute(value, ("dp", "tensor"), pairs)
+
+
+def add_kernel(left_ref, right_ref, out_ref):
+    out_ref[...] = left_ref[...] + right_ref[...]
+
+
+def add(left, right):
+    return pl.pallas_call(
+        add_kernel,
+        out_shape=jax.ShapeDtypeStruct(left.shape, left.dtype),
+        compiler_params=pltpu.CompilerParams(vmem_limit_bytes=VMEM_LIMIT),
+        name="add",
+    )(left, right)
 
 
 def over_blocks(value, sizes, side):
     came = [
-        move(value, sizes, lambda d, r: (d ^ m, r) if r % 2 == side else None)
+        move(value, sizes, lambda d, r: (d ^ m, r) if r % 2 == side else (d, r))
         for m in reversed(range(1, sizes[1]))
     ]
     return came + [value]
@@ -321,19 +333,22 @@
     weights = token_weights(seq_ids, counts, first, me % 2)
     asked = lax.dynamic_slice_in_dim(queries, (me // 2) * (own * rank), own * rank, 1)
     kept = project(inputs, out_grads, in_proj, out_proj)
-    came = move(kept, sizes, lambda d, r: (d, r + 1) if r % 2 == 0 else None)
+    came = move(kept, sizes, lambda d, r: (d, r ^ 1))
     kept, sent = halve(kept, came, rank_of, own)
-    came = move(sent, sizes, lambda d, r: (d, r ^ 2) if r % 2 == 1 else None)
+    came = move(sent, sizes, lambda d, r: (d, r ^ 2) if r % 2 == 1 else (d, r))
+    if blocks > SMALL:
+        return finish_long(gradients(weights, [kept, came], rank), asked, first, seq_dev)
+    sent, asked = lax.optimization_barrier((sent, asked))
+    asked = over_blocks(asked, sizes, 0)
     grads = gradients(weights, [kept, came], rank)
-    if blocks > SMALL:
-        return finish_long(grads, asked, first, seq_dev)
-    sent, asked = lax.optimization_barrier((sent, asked))
-    asked = collect(place.reshape(1), over_blocks(asked, sizes, 0)[::-1])
-    asked = move(asked, sizes, lambda d, r: (d, r + 1) if r % 2 == 0 else None)
-    partial = grams(over_blocks(grads, sizes, 1), asked)
-    partial = [partial] + [
-        move(partial, sizes, lambda d, r: (d, r ^ m) if r % 2 == 1 else None) for m in (2, 3, 1)
-    ]
+    grads, *asked = lax.optimization_barrier((grads, *asked))
+    grads = over_blocks(grads, sizes, 1)
+    grads[0], *asked = lax.optimization_barrier((grads[0], *asked))
+    asked = collect(place.reshape(1), asked[::-1])
+    asked = move(asked, sizes, lambda d, r: (d, r ^ 1))
+    partial = grams(grads[::-1], asked)
+    partial = add(partial, move(partial, sizes, lambda d, r: (d, r ^ 2) if r % 2 == 1 else (d, r)))
+    partial = [partial, move(partial, sizes, lambda d, r: (d, r ^ 1))]
     return solve(partial, blocks * seq_dev, asked.shape[0], seq_dev)
 
 

time: 37.7 us -> 34.1 us (0.905)
  the two profiles are of different devices: /device:TPU:1 before, /device:TPU:0 now
where the time goes in v8:
time: 34.1 us; the launch traced here: 33.8 us
  starting transfers between devices  22.2 us (65%)
  waiting for transfers between devices  6.35 us (19%)
  Pallas kernels  4.87 us (14%)
    ppermute x11, starting transfers between devices, move(): return lax.ppermute(value, ('dp', 'tensor'), pairs)  22.2 us
    ppermute x11, waiting for transfers between devices, move(): return lax.ppermute(value, ('dp', 'tensor'), pairs)  6.35 us
    pallas_call x1, Pallas kernels, project(): pl.pallas_call(project_kernel, out_shape=jax.ShapeDtypeStruct((2 * rank,...  2.15 us
    pallas_call x1, Pallas kernels, solve(): pl.pallas_call(functools.partial(solve_kernel, seqs), out_shape=jax.Shape...  1.81 us
  transfers between devices with their start and end apart: 11, of which 4 were waited for; matrix products, arithmetic and copies ran while one was open for 1% of the time, Pallas kernels for 1%

profile of v8, /device:TPU:0, one launch (start us, length us, event | category | flops | bytes accessed | tf_op | source)
XLA Modules:
  0.0 33.8 jit_solution(15245338471848327497)
XLA Ops:
  0.0 2.2 %project.1.kept_ref = f32[128,256]{1,0:T(8,128)S(1)} custom-call(bf16[2752,256]{1,0:T(8,128)(2,1)} %bitcast.5, bf16[256,1024]{1,0:T(8,128)(2,1)} %g_hbm.1, bf16[64,2752]{1,0:T(8,128)(2,1)} %bitcast.6, bf16[64,1024]{1,0:T(8,128)(2,1)} %bitcast.7), custom_call_target="tpu_custom_call" | custom-call | tf_op jit(solution)/shard_map/project/pallas_call | solution.py:95
  2.2 0.5 %collective-permute-start = (f32[128,256]{1,0:T(8,128)S(1)}, f32[128,256]{1,0:T(8,128)S(1)}, u32[]{:S(2)}, u32[]{:S(2)}) collective-permute-start(f32[128,256]{1,0:T(8,128)S(1)} %project.1.kept_ref), channel_id=1, source_target_pairs={{0,1},{1,0},{2,3},{3,2},{4,5},{5,4},{6,7},{7,6},{8,9},{9,8},{10,11... | collective-permute-start | bytes 393224 | tf_op jit(solution)/shard_map/ppermute | solution.py:280
  2.7 0.1 convert_reduce_fusion
  2.9 0.8 %collective-permute-done.came_ref = f32[128,256]{1,0:T(8,128)S(1)} collective-permute-done((f32[128,256]{1,0:T(8,128)S(1)}, f32[128,256]{1,0:T(8,128)S(1)}, u32[]{:S(2)}, u32[]{:S(2)}) %collective-permute-start) | collective-permute-done | bytes 131104 | tf_op jit(solution)/shard_map/ppermute | solution.py:280
  3.7 0.7 %collective-permute-start.1 = (f32[96,256]{1,0:T(8,128)S(1)}, f32[96,256]{1,0:T(8,128)S(1)}, u32[]{:S(2)}, u32[]{:S(2)}) collective-permute-start(f32[96,256]{1,0:T(8,128)S(1)} %get-tuple-element.19), channel_id=1, source_target_pairs={{0,0},{1,3},{2,2},{3,1},{4,4},{5,7},{6,6},{7,5},{8,8},{9,11},{10,1... | collective-permute-start | bytes 294920 | tf_op jit(solution)/shard_map/ppermute | solution.py:280
  4.4 6.9 %collective-permute-start.2 = (f32[4,2048]{1,0:T(4,128)S(1)}, f32[4,2048]{1,0:T(4,128)S(1)}, u32[]{:S(2)}, u32[]{:S(2)}) collective-permute-start(f32[4,2048]{1,0:T(4,128)S(1)} %constant_dynamic-slice_fusion.refs_0_), channel_id=1, source_target_pairs={{0,12},{1,1},{2,14},{3,3},{4,8},{5,5},{6,10},{7,7},{8,4},{9,9},{10... | collective-permute-start | bytes 98312 | tf_op jit(solution)/shard_map/ppermute | solution.py:280
  11.3 1.9 %collective-permute-start.3 = (f32[4,2048]{1,0:T(4,128)S(1)}, f32[4,2048]{1,0:T(4,128)S(1)}, u32[]{:S(2)}, u32[]{:S(2)}) collective-permute-start(f32[4,2048]{1,0:T(4,128)S(1)} %constant_dynamic-slice_fusion.refs_0_), channel_id=1, source_target_pairs={{0,8},{1,1},{2,10},{3,3},{4,12},{5,5},{6,14},{7,7},{8,0},{9,9},{10... | collective-permute-start | bytes 98312 | tf_op jit(solution)/shard_map/ppermute | solution.py:280
  13.2 2.5 %collective-permute-start.4 = (f32[4,2048]{1,0:T(4,128)S(1)}, f32[4,2048]{1,0:T(4,128)S(1)}, u32[]{:S(2)}, u32[]{:S(2)}) collective-permute-start(f32[4,2048]{1,0:T(4,128)S(1)} %constant_dynamic-slice_fusion.refs_0_), channel_id=1, source_target_pairs={{0,4},{1,1},{2,6},{3,3},{4,0},{5,5},{6,2},{7,7},{8,12},{9,9},{10,1... | collective-permute-start | bytes 98312 | tf_op jit(solution)/shard_map/ppermute | solution.py:280
  15.7 0.1 fusion.1.weights_ref
  15.7 0.4 %gradients.1.refs_1_ = f32[16,16,128]{2,1,0:T(8,128)S(1)} custom-call(f32[16,256]{1,0:T(8,128)S(1)} %fusion.1.weights_ref, f32[96,256]{1,0:T(8,128)S(1)} %get-tuple-element.18.refs_0_, f32[96,256]{1,0:T(8,128)S(1)} %collective-permute-done.1.refs_1_), custom_call_target="tpu_custom_call" | custom-call | tf_op jit(solution)/shard_map/gradients/pallas_call | solution.py:164
  16.1 0.0 collective-permute-done.2.refs_3_
  16.1 3.4 %collective-permute-done.3.refs_2_ = f32[4,2048]{1,0:T(4,128)S(1)} collective-permute-done((f32[4,2048]{1,0:T(4,128)S(1)}, f32[4,2048]{1,0:T(4,128)S(1)}, u32[]{:S(2)}, u32[]{:S(2)}) %collective-permute-start.3) | collective-permute-done | bytes 32800 | tf_op jit(solution)/shard_map/ppermute | solution.py:280
  19.5 0.7 %collective-permute-start.5 = (f32[16,16,128]{2,1,0:T(8,128)S(1)}, f32[16,16,128]{2,1,0:T(8,128)S(1)}, u32[]{:S(2)}, u32[]{:S(2)}) collective-permute-start(f32[16,16,128]{2,1,0:T(8,128)S(1)} %gradients.1.refs_1_), channel_id=1, source_target_pairs={{0,0},{1,13},{2,2},{3,15},{4,4},{5,9},{6,6},{7,11},{8,8},{9,5},{10... | collective-permute-start | bytes 393224 | tf_op jit(solution)/shard_map/ppermute | solution.py:280
  20.1 0.7 %collective-permute-start.7 = (f32[16,16,128]{2,1,0:T(8,128)S(1)}, f32[16,16,128]{2,1,0:T(8,128)S(1)}, u32[]{:S(2)}, u32[]{:S(2)}) collective-permute-start(f32[16,16,128]{2,1,0:T(8,128)S(1)} %gradients.1.refs_1_), channel_id=1, source_target_pairs={{0,0},{1,5},{2,2},{3,7},{4,4},{5,1},{6,6},{7,3},{8,8},{9,13},{10,1... | collective-permute-start | bytes 393224 | tf_op jit(solution)/shard_map/ppermute | solution.py:280
  20.8 0.7 %collective-permute-start.8 = (f32[16,16,128]{2,1,0:T(8,128)S(1)}, f32[16,16,128]{2,1,0:T(8,128)S(1)}, u32[]{:S(2)}, u32[]{:S(2)}) collective-permute-start(f32[16,16,128]{2,1,0:T(8,128)S(1)} %gradients.1.refs_1_), channel_id=1, source_target_pairs={{0,0},{1,9},{2,2},{3,11},{4,4},{5,13},{6,6},{7,15},{8,8},{9,1},{10... | collective-permute-start | bytes 393224 | tf_op jit(solution)/shard_map/ppermute | solution.py:280
  21.5 0.0 collective-permute-done.5.refs_4_
  21.6 0.1 collective-permute-start.6
  21.6 0.0 collective-permute-done.7.refs_2_
  21.7 1.3 %collective-permute-done.6.refs_0_ = f32[16,2048]{1,0:T(8,128)S(1)} collective-permute-done((f32[16,2048]{1,0:T(8,128)S(1)}, f32[16,2048]{1,0:T(8,128)S(1)}, u32[]{:S(2)}, u32[]{:S(2)}) %collective-permute-start.6) | collective-permute-done | bytes 131104 | tf_op jit(solution)/shard_map/ppermute | solution.py:280
  23.0 0.5 %grams.1.left_ref = f32[40,128]{1,0:T(8,128)S(1)} custom-call(f32[16,2048]{1,0:T(8,128)S(1)} %collective-permute-done.6.refs_0_, f32[16,16,128]{2,1,0:T(8,128)S(1)} %gradients.1.refs_1_, f32[16,16,128]{2,1,0:T(8,128)S(1)} %collective-permute-done.7.refs_2_, f32[16,16,128]{2,1,0:T(8,128)S(1)} %collective-permute-done.8.refs_3_, ...), custom_call_target="tpu_custom_call" | custom-call | tf_op jit(solution)/shard_map/grams/pallas_call | solution.py:215
  23.4 0.7 %collective-permute-start.9 = (f32[40,128]{1,0:T(8,128)S(1)}, f32[40,128]{1,0:T(8,128)S(1)}, u32[]{:S(2)}, u32[]{:S(2)}) collective-permute-start(f32[40,128]{1,0:T(8,128)S(1)} %grams.1.left_ref), channel_id=1, source_target_pairs={{0,0},{1,3},{2,2},{3,1},{4,4},{5,7},{6,6},{7,5},{8,8},{9,11},{10,1... | collective-permute-start | bytes 61448 | tf_op jit(solution)/shard_map/ppermute | solution.py:280
  24.1 7.0 %collective-permute-start.10 = (f32[40,128]{1,0:T(8,128)S(1)}, f32[40,128]{1,0:T(8,128)S(1)}, u32[]{:S(2)}, u32[]{:S(2)}) collective-permute-start(f32[40,128]{1,0:T(8,128)S(1)} %add.11.refs_0_), channel_id=1, source_target_pairs={{0,1},{1,0},{2,3},{3,2},{4,5},{5,4},{6,7},{7,6},{8,9},{9,8},{10,11... | collective-permute-start | bytes 61448 | tf_op jit(solution)/shard_map/ppermute | solution.py:280
  31.2 0.8 %collective-permute-done.10.refs_1_ = f32[40,128]{1,0:T(8,128)S(1)} collective-permute-done((f32[40,128]{1,0:T(8,128)S(1)}, f32[40,128]{1,0:T(8,128)S(1)}, u32[]{:S(2)}, u32[]{:S(2)}) %collective-permute-start.10) | collective-permute-done | bytes 20512 | tf_op jit(solution)/shard_map/ppermute | solution.py:280
  32.0 1.8 %solve.1 = f32[16,16]{1,0:T(8,128)} custom-call(f32[40,128]{1,0:T(8,128)S(1)} %add.11.refs_0_, f32[40,128]{1,0:T(8,128)S(1)} %collective-permute-done.10.refs_1_), custom_call_target="tpu_custom_call" | custom-call | tf_op jit(solution)/shard_map/solve/pallas_call | solution.py:265
  (16 shorter events, 0.1 us)
Async XLA Ops:
  0.0 2.7 %copy-start = (f32[4,4096]{1,0:T(4,128)S(1)}, f32[4,4096]{1,0:T(4,128)}, u32[]{:S(2)}) copy-start(f32[4,4096]{1,0:T(4,128)} %param.13) | copy-start | bytes 196612
  0.0 2.7 %copy-start.1 = (s32[256]{0:T(256)S(1)}, s32[256]{0:T(256)}, u32[]{:S(2)}) copy-start(s32[256]{0:T(256)} %param.11) | copy-start | bytes 3076
  0.0 2.7 %copy-start.2 = (s32[16]{0:T(128)S(1)}, s32[16]{0:T(128)}, u32[]{:S(2)}) copy-start(s32[16]{0:T(128)} %param.12) | copy-start | bytes 196
  2.2 1.5 %collective-permute-start = (f32[128,256]{1,0:T(8,128)S(1)}, f32[128,256]{1,0:T(8,128)S(1)}, u32[]{:S(2)}, u32[]{:S(2)}) collective-permute-start(f32[128,256]{1,0:T(8,128)S(1)} %project.1.kept_ref), channel_id=1, source_target_pairs={{0,1},{1,0},{2,3},{3,2},{4,5},{5,4},{6,7},{7,6},{8,9},{9,8},{10,11... | collective-permute-start | bytes 393224 | tf_op jit(solution)/shard_map/ppermute | solution.py:280
  3.7 12.0 %collective-permute-start.1 = (f32[96,256]{1,0:T(8,128)S(1)}, f32[96,256]{1,0:T(8,128)S(1)}, u32[]{:S(2)}, u32[]{:S(2)}) collective-permute-start(f32[96,256]{1,0:T(8,128)S(1)} %get-tuple-element.19), channel_id=1, source_target_pairs={{0,0},{1,3},{2,2},{3,1},{4,4},{5,7},{6,6},{7,5},{8,8},{9,11},{10,1... | collective-permute-start | bytes 294920 | tf_op jit(solution)/shard_map/ppermute | solution.py:280
  4.4 11.7 %collective-permute-start.2 = (f32[4,2048]{1,0:T(4,128)S(1)}, f32[4,2048]{1,0:T(4,128)S(1)}, u32[]{:S(2)}, u32[]{:S(2)}) collective-permute-start(f32[4,2048]{1,0:T(4,128)S(1)} %constant_dynamic-slice_fusion.refs_0_), channel_id=1, source_target_pairs={{0,12},{1,1},{2,14},{3,3},{4,8},{5,5},{6,10},{7,7},{8,4},{9,9},{10... | collective-permute-start | bytes 98312 | tf_op jit(solution)/shard_map/ppermute | solution.py:280
  11.3 8.2 %collective-permute-start.3 = (f32[4,2048]{1,0:T(4,128)S(1)}, f32[4,2048]{1,0:T(4,128)S(1)}, u32[]{:S(2)}, u32[]{:S(2)}) collective-permute-start(f32[4,2048]{1,0:T(4,128)S(1)} %constant_dynamic-slice_fusion.refs_0_), channel_id=1, source_target_pairs={{0,8},{1,1},{2,10},{3,3},{4,12},{5,5},{6,14},{7,7},{8,0},{9,9},{10... | collective-permute-start | bytes 98312 | tf_op jit(solution)/shard_map/ppermute | solution.py:280
  13.2 6.3 %collective-permute-start.4 = (f32[4,2048]{1,0:T(4,128)S(1)}, f32[4,2048]{1,0:T(4,128)S(1)}, u32[]{:S(2)}, u32[]{:S(2)}) collective-permute-start(f32[4,2048]{1,0:T(4,128)S(1)} %constant_dynamic-slice_fusion.refs_0_), channel_id=1, source_target_pairs={{0,4},{1,1},{2,6},{3,3},{4,0},{5,5},{6,2},{7,7},{8,12},{9,9},{10,1... | collective-permute-start | bytes 98312 | tf_op jit(solution)/shard_map/ppermute | solution.py:280
  19.5 2.0 %collective-permute-start.5 = (f32[16,16,128]{2,1,0:T(8,128)S(1)}, f32[16,16,128]{2,1,0:T(8,128)S(1)}, u32[]{:S(2)}, u32[]{:S(2)}) collective-permute-start(f32[16,16,128]{2,1,0:T(8,128)S(1)} %gradients.1.refs_1_), channel_id=1, source_target_pairs={{0,0},{1,13},{2,2},{3,15},{4,4},{5,9},{6,6},{7,11},{8,8},{9,5},{10... | collective-permute-start | bytes 393224 | tf_op jit(solution)/shard_map/ppermute | solution.py:280
  20.1 1.5 %collective-permute-start.7 = (f32[16,16,128]{2,1,0:T(8,128)S(1)}, f32[16,16,128]{2,1,0:T(8,128)S(1)}, u32[]{:S(2)}, u32[]{:S(2)}) collective-permute-start(f32[16,16,128]{2,1,0:T(8,128)S(1)} %gradients.1.refs_1_), channel_id=1, source_target_pairs={{0,0},{1,5},{2,2},{3,7},{4,4},{5,1},{6,6},{7,3},{8,8},{9,13},{10,1... | collective-permute-start | bytes 393224 | tf_op jit(solution)/shard_map/ppermute | solution.py:280
  20.8 0.8 %collective-permute-start.8 = (f32[16,16,128]{2,1,0:T(8,128)S(1)}, f32[16,16,128]{2,1,0:T(8,128)S(1)}, u32[]{:S(2)}, u32[]{:S(2)}) collective-permute-start(f32[16,16,128]{2,1,0:T(8,128)S(1)} %gradients.1.refs_1_), channel_id=1, source_target_pairs={{0,0},{1,9},{2,2},{3,11},{4,4},{5,13},{6,6},{7,15},{8,8},{9,1},{10... | collective-permute-start | bytes 393224 | tf_op jit(solution)/shard_map/ppermute | solution.py:280
  21.6 1.4 %collective-permute-start.6 = (f32[16,2048]{1,0:T(8,128)S(1)}, f32[16,2048]{1,0:T(8,128)S(1)}, u32[]{:S(2)}, u32[]{:S(2)}) collective-permute-start(f32[16,2048]{1,0:T(8,128)S(1)} %collect.1), channel_id=1, source_target_pairs={{0,1},{1,0},{2,3},{3,2},{4,5},{5,4},{6,7},{7,6},{8,9},{9,8},{10,11... | collective-permute-start | bytes 393224 | tf_op jit(solution)/shard_map/ppermute | solution.py:280
  23.4 0.7 %collective-permute-start.9 = (f32[40,128]{1,0:T(8,128)S(1)}, f32[40,128]{1,0:T(8,128)S(1)}, u32[]{:S(2)}, u32[]{:S(2)}) collective-permute-start(f32[40,128]{1,0:T(8,128)S(1)} %grams.1.left_ref), channel_id=1, source_target_pairs={{0,0},{1,3},{2,2},{3,1},{4,4},{5,7},{6,6},{7,5},{8,8},{9,11},{10,1... | collective-permute-start | bytes 61448 | tf_op jit(solution)/shard_map/ppermute | solution.py:280
  24.1 7.9 %collective-permute-start.10 = (f32[40,128]{1,0:T(8,128)S(1)}, f32[40,128]{1,0:T(8,128)S(1)}, u32[]{:S(2)}, u32[]{:S(2)}) collective-permute-start(f32[40,128]{1,0:T(8,128)S(1)} %add.11.refs_0_), channel_id=1, source_target_pairs={{0,1},{1,0},{2,3},{3,2},{4,5},{5,4},{6,7},{7,6},{8,9},{9,8},{10,11... | collective-permute-start | bytes 61448 | tf_op jit(solution)/shard_map/ppermute | solution.py:280

commit v9 on v7

--- a/solution.py
+++ b/solution.py
@@ -179,52 +179,64 @@
     )(weights, kept, came)
 
 
-def join_kernel(upper_ref, lower_ref, out_ref):
-    out_ref[...] = jnp.concatenate([upper_ref[...], lower_ref[...]], axis=0)
-
-
-def join(upper, lower):
-    return pl.pallas_call(
-        join_kernel,
-        out_shape=jax.ShapeDtypeStruct((2 * upper.shape[0], upper.shape[1]), upper.dtype),
-        compiler_params=pltpu.CompilerParams(vmem_limit_bytes=VMEM_LIMIT),
-        name="join",
-    )(upper, lower)
-
-
-def grams_kernel(seqs, me_ref, *refs):
-    blocks, pairs, out_ref = refs[-4::-1], refs[-3:-1], refs[-1]
-    steps = blocks[0].shape[0] // seqs
-    asked = pairs[0].shape[0] // 2
-    lanes = [
-        jnp.concatenate([block[i * seqs : (i + 1) * seqs, :] for block in blocks], axis=0)
-        for i in range(steps)
-    ]
-    every = jnp.concatenate(lanes, axis=1)
-    given = [pair[at * asked : (at + 1) * asked, :] for at in (0, 1) for pair in pairs]
+def append_kernel(grads_ref, asked_ref, far_ref, out_ref):
+    count, lanes = grads_ref.shape
+    out_ref[:count, :] = grads_ref[...]
+    for queries_ref in (asked_ref, far_ref):
+        rows, columns = queries_ref.shape
+        for at in range(0, columns, lanes):
+            out_ref[count : count + rows, :] = queries_ref[:, at : at + lanes]
+            count += rows
+
+
+def append(grads, asked, far):
+    count, lanes = grads.shape
+    rows = count + 2 * asked.shape[0] * asked.shape[1] // lanes
+    return pl.pallas_call(
+        append_kernel,
+        out_shape=jax.ShapeDtypeStruct((rows, lanes), jnp.float32),
+        compiler_params=pltpu.CompilerParams(vmem_limit_bytes=VMEM_LIMIT),
+        name="append",
+    )(grads, asked, far)
+
+
+def grams_kernel(seqs, me_ref, third_ref, second_ref, first_ref, own_ref, out_ref):
+    blocks = (own_ref, first_ref, second_ref, third_ref)
+    count = second_ref.shape[0]
+    steps = count // seqs
+    size = (own_ref.shape[0] - count) // 2
+    asked = size // steps
+    given = [ref[count + at * size : count + (at + 1) * size, :] for at in (0, 1) for ref in blocks[:2]]
     ordered = []
     for place in range(len(blocks)):
         chosen = given[0]
         for m in range(1, len(blocks)):
             chosen = jnp.where((me_ref[0] ^ place) == m, given[m], chosen)
         ordered.append(chosen)
-    result = dot_nt(jnp.concatenate([every] + ordered, axis=0), every)
+    lanes = []
+    for i in range(steps):
+        rows = [block[i * seqs : (i + 1) * seqs, :] for block in blocks]
+        rows += [chosen[i * asked : (i + 1) * asked, :] for chosen in ordered]
+        lanes.append(jnp.concatenate(rows, axis=0))
+    both = jnp.concatenate(lanes, axis=1)
+    result = dot_nt(both, both[: len(blocks) * seqs])
     half = result.shape[0] // 2
     out_ref[...] = jnp.concatenate([result[:half, :], result[half:, :]], axis=1)
 
 
-def grams(me, blocks, seqs, pairs):
+def grams(me, blocks, seqs):
+    count = blocks[0].shape[0]
     total = len(blocks) * seqs
-    rows = total + 2 * pairs[0].shape[0]
+    rows = total + 2 * (blocks[-1].shape[0] - count) // (count // seqs)
     whole = pl.BlockSpec(memory_space=pltpu.VMEM)
     return pl.pallas_call(
         functools.partial(grams_kernel, seqs),
         out_shape=jax.ShapeDtypeStruct((rows // 2, 2 * total), jnp.float32),
-        in_specs=[pl.BlockSpec(memory_space=pltpu.SMEM)] + [whole] * (len(blocks) + 2),
+        in_specs=[pl.BlockSpec(memory_space=pltpu.SMEM)] + [whole] * len(blocks),
         out_specs=whole,
         compiler_params=pltpu.CompilerParams(vmem_limit_bytes=VMEM_LIMIT),
         name="grams",
-    )(me, *blocks, *pairs)
+    )(me, *blocks)
 
 
 def scales(count):
@@ -323,14 +335,14 @@
     kept, counts = lax.optimization_barrier((kept, counts))
     weights = token_weights(seq_ids, counts, first)
     weights, asked = lax.optimization_barrier((weights, asked))
-    if blocks <= SMALL:
-        asked = join(asked, from_partner(asked, "dp", blocks, 2))
+    far = from_partner(asked, "dp", blocks, 2)
     grads = gradients(weights, kept, came, rank)
     if blocks > SMALL:
         return finish_long(grads, asked, first, seq_dev)
-    grads, asked = lax.optimization_barrier((grads, asked))
-    pairs = [asked, from_partner(asked, "dp", blocks, 1)]
-    partial = grams(place.reshape(1), from_partners(grads, "dp", blocks), seq_dev, pairs)
+    distant = [from_partner(grads, "dp", blocks, m) for m in (3, 2)]
+    near = append(grads, asked, far)
+    grads = distant + [from_partner(near, "dp", blocks, 1), near]
+    partial = grams(place.reshape(1), grads, seq_dev)
     partial = from_partners(partial, "tensor", parts)
     return solve(partial, blocks * seq_dev, blocks * queries.shape[0], seq_dev)
 

time: 27 us -> 27.5 us (1.019)
  waiting for transfers between devices: 8.44 us -> 10.4 us
  starting transfers between devices: 13.6 us -> 12.1 us
    ppermute x10 -> x9, waiting for transfers between devices: 8.44 us -> 10.4 us  [from_partner(): return lax.ppermute(value, axis, [(i, i ^ m) for i in range(size)])]
    ppermute x10 -> x9, starting transfers between devices: 13.6 us -> 12.1 us  [from_partner(): return lax.ppermute(value, axis, [(i, i ^ m) for i in range(size)])]
  transfers between devices with their start and end apart: 10 -> 9, of which waited for: 5 -> 7; matrix products, arithmetic and copies ran while one was open for 1% -> 1% of each run, Pallas kernels for 0% -> 1%
where the time goes in v9:
time: 27.5 us; the launch traced here: 27.4 us
  starting transfers between devices  12.1 us (44%)
  waiting for transfers between devices  10.4 us (38%)
  Pallas kernels  4.6 us (17%)
    ppermute x9, starting transfers between devices, from_partner(): return lax.ppermute(value, axis, [(i, i ^ m) for i in range(size)])  12.1 us
    ppermute x9, waiting for transfers between devices, from_partner(): return lax.ppermute(value, axis, [(i, i ^ m) for i in range(size)])  10.4 us
    pallas_call x1, Pallas kernels, project(): pl.pallas_call(functools.partial(project_kernel, parts, own), out_shape=[...  2.15 us
    pallas_call x1, Pallas kernels, solve(): pl.pallas_call(functools.partial(solve_kernel, seqs), out_shape=jax.Shape...  1.82 us
  transfers between devices with their start and end apart: 9, of which 7 were waited for; matrix products, arithmetic and copies ran while one was open for 1% of the time, Pallas kernels for 1%

profile of v9, /device:TPU:0, one launch (start us, length us, event | category | flops | bytes accessed | tf_op | source)
XLA Modules:
  0.0 27.4 jit_solution(16645551096046728978)
XLA Ops:
  0.0 2.2 %project.1 = (f32[96,256]{1,0:T(8,128)S(1)}, f32[96,256]{1,0:T(8,128)S(1)}) custom-call(s32[1]{0:T(128)} %bitcast.1.rank_ref, bf16[2752,256]{1,0:T(8,128)(2,1)} %bitcast.5, bf16[256,1024]{1,0:T(8,128)(2,1)} %g_hbm.1, bf16[64,2752]{1,0:T(8,128)(2,1)} %bitcast.6, bf16[64,1024]{1,0:T(8,128)(2,1)} %bitcast.7), custom_call_target="tpu_custom_call" | custom-call | tf_op jit(solution)/shard_map/project/pallas_call | solution.py:104
  2.2 0.5 %collective-permute-start = (f32[96,256]{1,0:T(8,128)S(1)}, f32[96,256]{1,0:T(8,128)S(1)}, u32[]{:S(2)}, u32[]{:S(2)}) collective-permute-start(f32[96,256]{1,0:T(8,128)S(1)} %get-tuple-element.14), channel_id=1, source_target_pairs={{0,1},{1,0},{2,3},{3,2},{4,5},{5,4},{6,7},{7,6},{8,9},{9,8},{10,11... | collective-permute-start | bytes 294920 | tf_op jit(solution)/shard_map/ppermute | solution.py:293
  2.7 0.1 convert_reduce_fusion
  2.8 0.8 %collective-permute-done.came_ref = f32[96,256]{1,0:T(8,128)S(1)} collective-permute-done((f32[96,256]{1,0:T(8,128)S(1)}, f32[96,256]{1,0:T(8,128)S(1)}, u32[]{:S(2)}, u32[]{:S(2)}) %collective-permute-start) | collective-permute-done | bytes 98336 | tf_op jit(solution)/shard_map/ppermute | solution.py:293
  3.7 2.9 %collective-permute-start.1 = (f32[80,256]{1,0:T(8,128)S(1)}, f32[80,256]{1,0:T(8,128)S(1)}, u32[]{:S(2)}, u32[]{:S(2)}) collective-permute-start(f32[80,256]{1,0:T(8,128)S(1)} %get-tuple-element.19), channel_id=1, source_target_pairs={{0,2},{1,3},{2,0},{3,1},{4,6},{5,7},{6,4},{7,5},{8,10},{9,11},{10,... | collective-permute-start | bytes 245768 | tf_op jit(solution)/shard_map/ppermute | solution.py:293
  6.6 0.1 fusion.1.weights_ref
  6.7 2.6 %collective-permute-start.4 = (f32[4,1024]{1,0:T(4,128)S(1)}, f32[4,1024]{1,0:T(4,128)S(1)}, u32[]{:S(2)}, u32[]{:S(2)}) collective-permute-start(f32[4,1024]{1,0:T(4,128)S(1)} %constant_dynamic-slice_fusion.asked_ref), channel_id=1, source_target_pairs={{0,8},{4,12},{8,0},{12,4},{1,9},{5,13},{9,1},{13,5},{2,10},{6,14},... | collective-permute-start | bytes 49160 | tf_op jit(solution)/shard_map/ppermute | solution.py:293
  9.3 0.1 collective-permute-done.1.came_ref
  9.4 0.3 gradients.1.grads_ref
  9.6 1.8 %collective-permute-done.4.far_ref = f32[4,1024]{1,0:T(4,128)S(1)} collective-permute-done((f32[4,1024]{1,0:T(4,128)S(1)}, f32[4,1024]{1,0:T(4,128)S(1)}, u32[]{:S(2)}, u32[]{:S(2)}) %collective-permute-start.4) | collective-permute-done | bytes 16416 | tf_op jit(solution)/shard_map/ppermute | solution.py:293
  11.4 1.6 %collective-permute-start.5 = (f32[192,128]{1,0:T(8,128)S(1)}, f32[192,128]{1,0:T(8,128)S(1)}, u32[]{:S(2)}, u32[]{:S(2)}) collective-permute-start(f32[192,128]{1,0:T(8,128)S(1)} %append.1.own_ref), channel_id=1, source_target_pairs={{0,4},{4,0},{8,12},{12,8},{1,5},{5,1},{9,13},{13,9},{2,6},{6,2},{1... | collective-permute-start | bytes 294920 | tf_op jit(solution)/shard_map/ppermute | solution.py:293
  13.0 2.5 %collective-permute-start.2 = (f32[128,128]{1,0:T(8,128)S(1)}, f32[128,128]{1,0:T(8,128)S(1)}, u32[]{:S(2)}, u32[]{:S(2)}) collective-permute-start(f32[128,128]{1,0:T(8,128)S(1)} %gradients.1.grads_ref), channel_id=1, source_target_pairs={{0,12},{4,8},{8,4},{12,0},{1,13},{5,9},{9,5},{13,1},{2,14},{6,10},... | collective-permute-start | bytes 196616 | tf_op jit(solution)/shard_map/ppermute | solution.py:293
  15.4 0.2 collective-permute-start.3
  15.6 3.9 %collective-permute-done.2.third_ref = f32[128,128]{1,0:T(8,128)S(1)} collective-permute-done((f32[128,128]{1,0:T(8,128)S(1)}, f32[128,128]{1,0:T(8,128)S(1)}, u32[]{:S(2)}, u32[]{:S(2)}) %collective-permute-start.2) | collective-permute-done | bytes 65568 | tf_op jit(solution)/shard_map/ppermute | solution.py:293
  19.5 1.8 %collective-permute-done.3.second_ref = f32[128,128]{1,0:T(8,128)S(1)} collective-permute-done((f32[128,128]{1,0:T(8,128)S(1)}, f32[128,128]{1,0:T(8,128)S(1)}, u32[]{:S(2)}, u32[]{:S(2)}) %collective-permute-start.3) | collective-permute-done | bytes 65568 | tf_op jit(solution)/shard_map/ppermute | solution.py:293
  21.3 0.0 collective-permute-done.5.first_ref
  21.3 0.3 %grams.1.refs_3_ = f32[40,128]{1,0:T(8,128)S(1)} custom-call(s32[1]{0:T(128)} %bitcast.me_ref, f32[128,128]{1,0:T(8,128)S(1)} %collective-permute-done.2.third_ref, f32[128,128]{1,0:T(8,128)S(1)} %collective-permute-done.3.second_ref, f32[192,128]{1,0:T(8,128)S(1)} %collective-permute-done.5.first_ref, f32[192,128]{1,0:T(8,128)S(1)} %append.1.own_ref), custom_call_target="tpu_custom_call" | custom-call | tf_op jit(solution)/shard_map/grams/pallas_call | solution.py:232
  21.7 0.0 collective-permute-start.6
  21.7 0.7 %collective-permute-start.7 = (f32[40,128]{1,0:T(8,128)S(1)}, f32[40,128]{1,0:T(8,128)S(1)}, u32[]{:S(2)}, u32[]{:S(2)}) collective-permute-start(f32[40,128]{1,0:T(8,128)S(1)} %grams.1.refs_3_), channel_id=1, source_target_pairs={{0,2},{1,3},{2,0},{3,1},{4,6},{5,7},{6,4},{7,5},{8,10},{9,11},{10,... | collective-permute-start | bytes 61448 | tf_op jit(solution)/shard_map/ppermute | solution.py:293
  22.3 1.2 %collective-permute-start.8 = (f32[40,128]{1,0:T(8,128)S(1)}, f32[40,128]{1,0:T(8,128)S(1)}, u32[]{:S(2)}, u32[]{:S(2)}) collective-permute-start(f32[40,128]{1,0:T(8,128)S(1)} %grams.1.refs_3_), channel_id=1, source_target_pairs={{0,1},{1,0},{2,3},{3,2},{4,5},{5,4},{6,7},{7,6},{8,9},{9,8},{10,11... | collective-permute-start | bytes 61448 | tf_op jit(solution)/shard_map/ppermute | solution.py:293
  23.5 1.3 %collective-permute-done.6.refs_0_ = f32[40,128]{1,0:T(8,128)S(1)} collective-permute-done((f32[40,128]{1,0:T(8,128)S(1)}, f32[40,128]{1,0:T(8,128)S(1)}, u32[]{:S(2)}, u32[]{:S(2)}) %collective-permute-start.6) | collective-permute-done | bytes 20512 | tf_op jit(solution)/shard_map/ppermute | solution.py:293
  24.9 0.7 %collective-permute-done.7.refs_1_ = f32[40,128]{1,0:T(8,128)S(1)} collective-permute-done((f32[40,128]{1,0:T(8,128)S(1)}, f32[40,128]{1,0:T(8,128)S(1)}, u32[]{:S(2)}, u32[]{:S(2)}) %collective-permute-start.7) | collective-permute-done | bytes 20512 | tf_op jit(solution)/shard_map/ppermute | solution.py:293
  25.5 0.0 collective-permute-done.8.refs_2_
  25.5 1.8 %solve.1 = f32[16,16]{1,0:T(8,128)} custom-call(f32[40,128]{1,0:T(8,128)S(1)} %collective-permute-done.6.refs_0_, f32[40,128]{1,0:T(8,128)S(1)} %collective-permute-done.7.refs_1_, f32[40,128]{1,0:T(8,128)S(1)} %collective-permute-done.8.refs_2_, f32[40,128]{1,0:T(8,128)S(1)} %grams.1.refs_3_), custom_call_target="tpu_custom_call" | custom-call | tf_op jit(solution)/shard_map/solve/pallas_call | solution.py:284
  (11 shorter events, 0.1 us)
Async XLA Ops:
  0.0 2.7 %copy-start = (f32[4,4096]{1,0:T(4,128)S(1)}, f32[4,4096]{1,0:T(4,128)}, u32[]{:S(2)}) copy-start(f32[4,4096]{1,0:T(4,128)} %param.13) | copy-start | bytes 196612
  0.0 2.7 %copy-start.1 = (s32[256]{0:T(256)S(1)}, s32[256]{0:T(256)}, u32[]{:S(2)}) copy-start(s32[256]{0:T(256)} %param.11) | copy-start | bytes 3076
  0.0 3.7 %copy-start.2 = (s32[16]{0:T(128)S(1)}, s32[16]{0:T(128)}, u32[]{:S(2)}) copy-start(s32[16]{0:T(128)} %param.12) | copy-start | bytes 196
  2.2 1.5 %collective-permute-start = (f32[96,256]{1,0:T(8,128)S(1)}, f32[96,256]{1,0:T(8,128)S(1)}, u32[]{:S(2)}, u32[]{:S(2)}) collective-permute-start(f32[96,256]{1,0:T(8,128)S(1)} %get-tuple-element.14), channel_id=1, source_target_pairs={{0,1},{1,0},{2,3},{3,2},{4,5},{5,4},{6,7},{7,6},{8,9},{9,8},{10,11... | collective-permute-start | bytes 294920 | tf_op jit(solution)/shard_map/ppermute | solution.py:293
  3.7 5.7 %collective-permute-start.1 = (f32[80,256]{1,0:T(8,128)S(1)}, f32[80,256]{1,0:T(8,128)S(1)}, u32[]{:S(2)}, u32[]{:S(2)}) collective-permute-start(f32[80,256]{1,0:T(8,128)S(1)} %get-tuple-element.19), channel_id=1, source_target_pairs={{0,2},{1,3},{2,0},{3,1},{4,6},{5,7},{6,4},{7,5},{8,10},{9,11},{10,... | collective-permute-start | bytes 245768 | tf_op jit(solution)/shard_map/ppermute | solution.py:293
  6.7 4.7 %collective-permute-start.4 = (f32[4,1024]{1,0:T(4,128)S(1)}, f32[4,1024]{1,0:T(4,128)S(1)}, u32[]{:S(2)}, u32[]{:S(2)}) collective-permute-start(f32[4,1024]{1,0:T(4,128)S(1)} %constant_dynamic-slice_fusion.asked_ref), channel_id=1, source_target_pairs={{0,8},{4,12},{8,0},{12,4},{1,9},{5,13},{9,1},{13,5},{2,10},{6,14},... | collective-permute-start | bytes 49160 | tf_op jit(solution)/shard_map/ppermute | solution.py:293
  11.4 9.9 %collective-permute-start.5 = (f32[192,128]{1,0:T(8,128)S(1)}, f32[192,128]{1,0:T(8,128)S(1)}, u32[]{:S(2)}, u32[]{:S(2)}) collective-permute-start(f32[192,128]{1,0:T(8,128)S(1)} %append.1.own_ref), channel_id=1, source_target_pairs={{0,4},{4,0},{8,12},{12,8},{1,5},{5,1},{9,13},{13,9},{2,6},{6,2},{1... | collective-permute-start | bytes 294920 | tf_op jit(solution)/shard_map/ppermute | solution.py:293
  13.0 6.6 %collective-permute-start.2 = (f32[128,128]{1,0:T(8,128)S(1)}, f32[128,128]{1,0:T(8,128)S(1)}, u32[]{:S(2)}, u32[]{:S(2)}) collective-permute-start(f32[128,128]{1,0:T(8,128)S(1)} %gradients.1.grads_ref), channel_id=1, source_target_pairs={{0,12},{4,8},{8,4},{12,0},{1,13},{5,9},{9,5},{13,1},{2,14},{6,10},... | collective-permute-start | bytes 196616 | tf_op jit(solution)/shard_map/ppermute | solution.py:293
  15.4 5.9 %collective-permute-start.3 = (f32[128,128]{1,0:T(8,128)S(1)}, f32[128,128]{1,0:T(8,128)S(1)}, u32[]{:S(2)}, u32[]{:S(2)}) collective-permute-start(f32[128,128]{1,0:T(8,128)S(1)} %gradients.1.grads_ref), channel_id=1, source_target_pairs={{0,8},{4,12},{8,0},{12,4},{1,9},{5,13},{9,1},{13,5},{2,10},{6,14},... | collective-permute-start | bytes 196616 | tf_op jit(solution)/shard_map/ppermute | solution.py:293
  21.7 3.2 %collective-permute-start.6 = (f32[40,128]{1,0:T(8,128)S(1)}, f32[40,128]{1,0:T(8,128)S(1)}, u32[]{:S(2)}, u32[]{:S(2)}) collective-permute-start(f32[40,128]{1,0:T(8,128)S(1)} %grams.1.refs_3_), channel_id=1, source_target_pairs={{0,3},{1,2},{2,1},{3,0},{4,7},{5,6},{6,5},{7,4},{8,11},{9,10},{10,... | collective-permute-start | bytes 61448 | tf_op jit(solution)/shard_map/ppermute | solution.py:293
  21.7 3.8 %collective-permute-start.7 = (f32[40,128]{1,0:T(8,128)S(1)}, f32[40,128]{1,0:T(8,128)S(1)}, u32[]{:S(2)}, u32[]{:S(2)}) collective-permute-start(f32[40,128]{1,0:T(8,128)S(1)} %grams.1.refs_3_), channel_id=1, source_target_pairs={{0,2},{1,3},{2,0},{3,1},{4,6},{5,7},{6,4},{7,5},{8,10},{9,11},{10,... | collective-permute-start | bytes 61448 | tf_op jit(solution)/shard_map/ppermute | solution.py:293
  22.3 3.2 %collective-permute-start.8 = (f32[40,128]{1,0:T(8,128)S(1)}, f32[40,128]{1,0:T(8,128)S(1)}, u32[]{:S(2)}, u32[]{:S(2)}) collective-permute-start(f32[40,128]{1,0:T(8,128)S(1)} %grams.1.refs_3_), channel_id=1, source_target_pairs={{0,1},{1,0},{2,3},{3,2},{4,5},{5,4},{6,7},{7,6},{8,9},{9,8},{10,11... | collective-permute-start | bytes 61448 | tf_op jit(solution)/shard_map/ppermute | solution.py:293

commit v10 on v6

--- a/solution.py
+++ b/solution.py
@@ -42,9 +42,8 @@
     return mul(lh, rh) + (mul(lh, rl) + mul(ll, rh))
 
 
-def project_kernel(parts, own, rank_ref, x_hbm, g_hbm, wx_hbm, wg_hbm, *rest):
-    outs = rest[:2]
-    x_ref, g_ref, wx_ref, wg_ref, grad_ref, sems = rest[2:]
+def project_kernel(own, rank_ref, x_hbm, g_hbm, wx_hbm, wg_hbm, keep_ref, send_ref, *scratch):
+    x_ref, g_ref, wx_ref, wg_ref, wide_ref, sems = scratch
     copies = []
 
     def fetch(src, dst, index):
@@ -68,42 +67,42 @@
         x_copies.append(fetch(x_hbm.at[rows, :], x_ref.at[rows, :], index))
         index += 1
 
-    def project(w_copy, w_ref, cuts, copies, ref, along):
-        order = 1 if along == 0 else -1
-        total = None
+    half = x_ref.shape[1] // 2
+
+    def project(w_copy, w_ref, cuts, copies, cut, along):
+        totals = [None, None]
         w_copy.wait()
         for (at, size), copy in zip(cuts, copies):
             copy.wait()
-            term = lax.dot_general(
-                w_ref[:, at : at + size],
-                ref[(slice(at, at + size), slice(None))[::order]],
-                (((1,), (along,)), ((), ())),
-                preferred_element_type=jnp.float32,
-            )
-            total = term if total is None else total + term
-        return total
-
-    grad_ref[...] = project(wg_copy, wg_ref, g_cuts, g_copies, g_ref, 1)
-    inputs_t = project(wx_copy, wx_ref, x_cuts, x_copies, x_ref, 0)
-    me = rank_ref[0]
-    for out, side in zip(outs, (me & 1, (me & 1) ^ 1)):
-        for place in range(parts // 2):
-            start = pl.multiple_of((2 * place + side) * own, own)
-            out[place * own : (place + 1) * own, :] = grad_ref[pl.ds(start, own), :]
-        out[parts // 2 * own :, :] = inputs_t
-
-
-def project(inputs, out_grads, in_proj, out_proj, me, parts):
+            for side in (0, 1):
+                term = lax.dot_general(
+                    w_ref[:, at : at + size],
+                    cut(slice(at, at + size), slice(side * half, (side + 1) * half)),
+                    (((1,), (along,)), ((), ())),
+                    preferred_element_type=jnp.float32,
+                )
+                totals[side] = term if totals[side] is None else totals[side] + term
+        return jnp.concatenate(totals, axis=1)
+
+    grads_t = project(wg_copy, wg_ref, g_cuts, g_copies, lambda k, t: g_ref[t, k], 1)
+    wide_ref[...] = project(wx_copy, wx_ref, x_cuts, x_copies, lambda k, t: x_ref[k, t], 0)
+    rank = grads_t.shape[0]
+    side = rank_ref[0] & 1
+    for out, taken in ((keep_ref, side), (send_ref, side ^ 1)):
+        out[:rank, :] = grads_t
+        out[rank:, :] = wide_ref[pl.ds(pl.multiple_of(taken * own, own), own), :]
+
+
+def project(inputs, out_grads, in_proj, out_proj, me, own):
     rank = in_proj.shape[1]
-    own = rank // parts
     tokens, hidden = inputs.shape
     width = out_grads.shape[1]
     copies = 2 + len(cuts_of(width, 512)) + len(cuts_of(hidden, 768))
     arrays = (inputs.T, out_grads, in_proj.T, out_proj.T)
     in_hbm = pl.BlockSpec(memory_space=pltpu.HBM)
     return pl.pallas_call(
-        functools.partial(project_kernel, parts, own),
-        out_shape=[jax.ShapeDtypeStruct((parts // 2 * own + rank, tokens), jnp.float32)] * 2,
+        functools.partial(project_kernel, own),
+        out_shape=[jax.ShapeDtypeStruct((rank + own, tokens), jnp.float32)] * 2,
         in_specs=[pl.BlockSpec(memory_space=pltpu.SMEM)] + [in_hbm] * len(arrays),
         out_specs=[pl.BlockSpec(memory_space=pltpu.VMEM)] * 2,
         scratch_shapes=[
@@ -119,22 +118,20 @@
     )(me, *(pltpu.with_memory_space_constraint(array, pltpu.HBM) for array in arrays))
 
 
-def halve_kernel(parts, own, rank_ref, kept_ref, came_ref, keep_ref, send_ref, sum_ref):
+def halve_kernel(own, rank_ref, kept_ref, came_ref, keep_ref, send_ref, sum_ref):
     sum_ref[...] = kept_ref[...] + came_ref[...]
-    me = rank_ref[0]
-    for out, place in ((keep_ref, me // 2), (send_ref, me // 2 ^ 1)):
-        start = pl.multiple_of(place * own, own)
-        out[:own, :] = sum_ref[pl.ds(start, own), :]
-        out[own:, :] = sum_ref[parts // 2 * own :, :]
-
-
-def halve(kept, came, me, parts, own):
+    place = rank_ref[0] // 2
+    for out, taken in ((keep_ref, place), (send_ref, place ^ 1)):
+        out[:own, :] = sum_ref[pl.ds(pl.multiple_of(taken * own, own), own), :]
+        out[own:, :] = sum_ref[-own:, :]
+
+
+def halve(kept, came, me, own):
     rows, tokens = kept.shape
-    left = rows - (parts // 2 - 1) * own
     whole = pl.BlockSpec(memory_space=pltpu.VMEM)
     return pl.pallas_call(
-        functools.partial(halve_kernel, parts, own),
-        out_shape=[jax.ShapeDtypeStruct((left, tokens), jnp.float32)] * 2,
+        functools.partial(halve_kernel, own),
+        out_shape=[jax.ShapeDtypeStruct((2 * own, tokens), jnp.float32)] * 2,
         in_specs=[pl.BlockSpec(memory_space=pltpu.SMEM), whole, whole],
         out_specs=[whole] * 2,
         scratch_shapes=[pltpu.VMEM((rows, tokens), jnp.float32)],
@@ -143,44 +140,83 @@
     )(me, kept, came)
 
 
-def grads_kernel(own, pair, weights_ref, kept_ref, came_ref, asked_ref, out_ref):
+def pick_kernel(rank, own, rank_ref, queries_ref, out_ref):
+    lanes = out_ref.shape[1]
+    wide = lanes * rank // own
+    steps = own * own // lanes
+    asked = queries_ref.shape[0]
+    me = rank_ref[0]
+    start = (me // 2) * (own * rank)
+    rows = jnp.concatenate(
+        [
+            queries_ref[:, pl.ds(pl.multiple_of(start + i * wide, lanes), wide)]
+            for i in range(steps)
+        ],
+        axis=0,
+    )
+    source = lax.broadcasted_iota(jnp.int32, (wide, lanes), 0)
+    place = lax.broadcasted_iota(jnp.int32, (wide, lanes), 1)
+    wanted = (place // own) * rank + place % own + (me & 1) * own
+    chosen = jnp.where(source == wanted, 1.0, 0.0).astype(jnp.bfloat16)
+    high = rows.astype(jnp.bfloat16)
+    rest = rows - high.astype(jnp.float32)
+    middle = rest.astype(jnp.bfloat16)
+    low = (rest - middle.astype(jnp.float32)).astype(jnp.bfloat16)
+    terms = [
+        jnp.dot(term, chosen, preferred_element_type=jnp.float32) for term in (high, middle, low)
+    ]
+    out_ref[...] = terms[0] + (terms[1] + terms[2])
+
+
+def pick(queries, me, rank, own):
+    lanes = 128
+    rows = queries.shape[0] * own * own // lanes
+    whole = pl.BlockSpec(memory_space=pltpu.VMEM)
+    return pl.pallas_call(
+        functools.partial(pick_kernel, rank, own),
+        out_shape=jax.ShapeDtypeStruct((rows, lanes), jnp.float32),
+        in_specs=[pl.BlockSpec(memory_space=pltpu.SMEM), whole],
+        out_specs=whole,
+        compiler_params=pltpu.CompilerParams(vmem_limit_bytes=VMEM_LIMIT),
+        name="pick",
+    )(me, queries)
+
+
+def grads_kernel(weights_ref, kept_ref, came_ref, asked_ref, out_ref):
     summed = kept_ref[...] + came_ref[...]
     weights = weights_ref[...]
-    seqs = weights.shape[0]
+    own = summed.shape[0] // 2
+    group = out_ref.shape[1] // own
     inputs_t = summed[own:, :]
     zero = jnp.zeros_like(inputs_t)
     right = jnp.concatenate(
         [
-            jnp.concatenate([inputs_t if j == k else zero for k in range(pair)], axis=1)
-            for j in range(pair)
+            jnp.concatenate([inputs_t if j == k else zero for k in range(group)], axis=1)
+            for j in range(group)
         ],
         axis=0,
     )
     rows = []
-    for i in range(own // pair):
+    for i in range(own // group):
         rows.append(
             jnp.concatenate(
-                [weights * summed[pair * i + j : pair * i + j + 1, :] for j in range(pair)],
+                [weights * summed[group * i + j : group * i + j + 1, :] for j in range(group)],
                 axis=1,
             )
         )
     left = jnp.concatenate(rows, axis=0)
-    count, lanes = left.shape[0], right.shape[0]
+    count = left.shape[0]
     out_ref[:count, :] = dot_nt(left, right)
-    asked = asked_ref.shape[0]
-    for i in range(own // pair):
-        start = count + i * asked
-        out_ref[start : start + asked, :] = asked_ref[:, i * lanes : (i + 1) * lanes]
-
-
-def gradients(weights, kept, came, asked, rank):
-    own = kept.shape[0] - rank
-    pair = 128 // rank
-    steps = own // pair
-    rows = steps * (weights.shape[0] + asked.shape[0])
-    return pl.pallas_call(
-        functools.partial(grads_kernel, own, pair),
-        out_shape=jax.ShapeDtypeStruct((rows, pair * rank), jnp.float32),
+    out_ref[count:, :] = asked_ref[...]
+
+
+def gradients(weights, kept, came, asked):
+    lanes = asked.shape[1]
+    own = kept.shape[0] // 2
+    rows = own * own // lanes * weights.shape[0] + asked.shape[0]
+    return pl.pallas_call(
+        grads_kernel,
+        out_shape=jax.ShapeDtypeStruct((rows, lanes), jnp.float32),
         compiler_params=pltpu.CompilerParams(vmem_limit_bytes=VMEM_LIMIT),
         name="gradients",
     )(weights, kept, came, asked)
@@ -253,12 +289,11 @@
         left = jnp.where(left_lanes, high, low).astype(jnp.bfloat16)
         high = high[:seqs].astype(jnp.bfloat16)
         low = low[:seqs].astype(jnp.bfloat16)
-        right = jnp.concatenate([high, high, low, low], axis=0)
         if at + 1 == len(steps):
             left, state = left[seqs:], state[seqs:]
         product = jnp.dot(
-            jnp.concatenate([left, left], axis=1), right, preferred_element_type=jnp.float32
-        )
+            left, jnp.concatenate([high, high], axis=0), preferred_element_type=jnp.float32
+        ) + jnp.dot(left, jnp.concatenate([low, low], axis=0), preferred_element_type=jnp.float32)
         state = step * (2.0 * state - product)
     out_ref[...] = state[:, : out_ref.shape[1]]
 
@@ -312,16 +347,16 @@
     me = lax.axis_index("tensor")
     place = lax.axis_index("dp")
     first = place * seq_dev
-    own = rank // parts
+    own = 2 * rank // parts
     rank_of = me.reshape(1)
-    kept, sent = project(inputs, out_grads, in_proj, out_proj, rank_of, parts)
-    asked = lax.dynamic_slice_in_dim(queries, me * (own * rank), own * rank, 1)
+    kept, sent = project(inputs, out_grads, in_proj, out_proj, rank_of, own)
+    asked = pick(queries, rank_of, rank, own)
     weights = token_weights(seq_ids, counts, first)
     came = from_partner(sent, "tensor", parts, 1)
-    kept, sent = halve(kept, came, rank_of, parts, own)
+    kept, sent = halve(kept, came, rank_of, own)
     came = from_partner(sent, "tensor", parts, 2)
-    message = gradients(weights, kept, came, asked, rank)
-    steps = own * rank // message.shape[1]
+    message = gradients(weights, kept, came, asked)
+    steps = own * own // message.shape[1]
     if blocks > SMALL:
         return finish_long(message, steps, first, seq_dev)
     partial = grams(place.reshape(1), from_partners(message, "dp", blocks), steps, seq_dev)

time: 26.8 us -> 26.7 us (level)
  waiting for transfers between devices: 12 us -> 11.3 us
  Pallas kernels: 4.58 us -> 5.03 us
    ppermute x8, waiting for transfers between devices: 12 us -> 11.3 us  [from_partner(): return lax.ppermute(value, axis, [(i, i ^ m) for i in range(size)])]
    pallas_call x3 -> x4, Pallas kernels: 2.42 us -> 2.75 us  [the longest x1 2.23 us: project(): pl.pallas_call(functools.partial(project_kernel, own), out_shape=[jax.Sha...]
  transfers between devices with their start and end apart: 8 -> 8, of which waited for: 6 -> 6; matrix products, arithmetic and copies ran while one was open for 1% -> 1% of each run, Pallas kernels for 0% -> 1%
where the time goes in v10:
time: 26.7 us; the launch traced here: 26.6 us
  waiting for transfers between devices  11.3 us (42%)
  starting transfers between devices  10 us (37%)
  Pallas kernels  5.03 us (19%)
    ppermute x8, waiting for transfers between devices, from_partner(): return lax.ppermute(value, axis, [(i, i ^ m) for i in range(size)])  11.3 us
    ppermute x8, starting transfers between devices, from_partner(): return lax.ppermute(value, axis, [(i, i ^ m) for i in range(size)])  10 us
    pallas_call x1, Pallas kernels, project(): pl.pallas_call(functools.partial(project_kernel, own), out_shape=[jax.Sha...  2.23 us
    pallas_call x1, Pallas kernels, solve(): pl.pallas_call(functools.partial(solve_kernel, seqs), out_shape=jax.Shape...  1.94 us
  transfers between devices with their start and end apart: 8, of which 6 were waited for; matrix products, arithmetic and copies ran while one was open for 1% of the time, Pallas kernels for 1%

profile of v10, /device:TPU:0, one launch (start us, length us, event | category | flops | bytes accessed | tf_op | source)
XLA Modules:
  0.0 26.6 jit_solution(7963701872912841493)
XLA Ops:
  0.0 2.2 %project.1 = (f32[96,256]{1,0:T(8,128)S(1)}, f32[96,256]{1,0:T(8,128)S(1)}) custom-call(s32[1]{0:T(128)} %bitcast.1.rank_ref, bf16[2752,256]{1,0:T(8,128)(2,1)} %bitcast.5, bf16[256,1024]{1,0:T(8,128)(2,1)} %g_hbm.1, bf16[64,2752]{1,0:T(8,128)(2,1)} %bitcast.6, bf16[64,1024]{1,0:T(8,128)(2,1)} %bitcast.7), custom_call_target="tpu_custom_call" | custom-call | tf_op jit(solution)/shard_map/project/pallas_call | solution.py:103
  2.2 0.5 %collective-permute-start = (f32[96,256]{1,0:T(8,128)S(1)}, f32[96,256]{1,0:T(8,128)S(1)}, u32[]{:S(2)}, u32[]{:S(2)}) collective-permute-start(f32[96,256]{1,0:T(8,128)S(1)} %get-tuple-element.10), channel_id=1, source_target_pairs={{0,1},{1,0},{2,3},{3,2},{4,5},{5,4},{6,7},{7,6},{8,9},{9,8},{10,11... | collective-permute-start | bytes 294920 | tf_op jit(solution)/shard_map/ppermute | solution.py:311
  2.8 0.1 convert_reduce_fusion
  2.9 0.8 %collective-permute-done.came_ref = f32[96,256]{1,0:T(8,128)S(1)} collective-permute-done((f32[96,256]{1,0:T(8,128)S(1)}, f32[96,256]{1,0:T(8,128)S(1)}, u32[]{:S(2)}, u32[]{:S(2)}) %collective-permute-start) | collective-permute-done | bytes 98336 | tf_op jit(solution)/shard_map/ppermute | solution.py:311
  3.8 2.9 %collective-permute-start.1 = (f32[64,256]{1,0:T(8,128)S(1)}, f32[64,256]{1,0:T(8,128)S(1)}, u32[]{:S(2)}, u32[]{:S(2)}) collective-permute-start(f32[64,256]{1,0:T(8,128)S(1)} %get-tuple-element.12), channel_id=1, source_target_pairs={{0,2},{1,3},{2,0},{3,1},{4,6},{5,7},{6,4},{7,5},{8,10},{9,11},{10,... | collective-permute-start | bytes 196616 | tf_op jit(solution)/shard_map/ppermute | solution.py:311
  6.7 0.1 fusion.1.weights_ref
  6.7 0.0 copy-done
  6.7 0.2 pick.1.asked_ref
  6.9 2.2 %collective-permute-done.1.came_ref = f32[64,256]{1,0:T(8,128)S(1)} collective-permute-done((f32[64,256]{1,0:T(8,128)S(1)}, f32[64,256]{1,0:T(8,128)S(1)}, u32[]{:S(2)}, u32[]{:S(2)}) %collective-permute-start.1) | collective-permute-done | bytes 65568 | tf_op jit(solution)/shard_map/ppermute | solution.py:311
  9.1 0.3 %gradients.1.refs_3_ = f32[160,128]{1,0:T(8,128)S(1)} custom-call(f32[16,256]{1,0:T(8,128)S(1)} %fusion.1.weights_ref, f32[64,256]{1,0:T(8,128)S(1)} %get-tuple-element.11.kept_ref, f32[64,256]{1,0:T(8,128)S(1)} %collective-permute-done.1.came_ref, f32[32,128]{1,0:T(8,128)S(1)} %pick.1.asked_ref), custom_call_target="tpu_custom_call" | custom-call | tf_op jit(solution)/shard_map/gradients/pallas_call | solution.py:217
  9.4 4.0 %collective-permute-start.2 = (f32[160,128]{1,0:T(8,128)S(1)}, f32[160,128]{1,0:T(8,128)S(1)}, u32[]{:S(2)}, u32[]{:S(2)}) collective-permute-start(f32[160,128]{1,0:T(8,128)S(1)} %gradients.1.refs_3_), channel_id=1, source_target_pairs={{0,12},{4,8},{8,4},{12,0},{1,13},{5,9},{9,5},{13,1},{2,14},{6,10},... | collective-permute-start | bytes 245768 | tf_op jit(solution)/shard_map/ppermute | solution.py:311
  13.5 0.0 collective-permute-start.3
  13.5 0.6 %collective-permute-start.4 = (f32[160,128]{1,0:T(8,128)S(1)}, f32[160,128]{1,0:T(8,128)S(1)}, u32[]{:S(2)}, u32[]{:S(2)}) collective-permute-start(f32[160,128]{1,0:T(8,128)S(1)} %gradients.1.refs_3_), channel_id=1, source_target_pairs={{0,4},{4,0},{8,12},{12,8},{1,5},{5,1},{9,13},{13,9},{2,6},{6,2},{1... | collective-permute-start | bytes 245768 | tf_op jit(solution)/shard_map/ppermute | solution.py:311
  14.1 2.4 %collective-permute-done.2.refs_0_ = f32[160,128]{1,0:T(8,128)S(1)} collective-permute-done((f32[160,128]{1,0:T(8,128)S(1)}, f32[160,128]{1,0:T(8,128)S(1)}, u32[]{:S(2)}, u32[]{:S(2)}) %collective-permute-start.2) | collective-permute-done | bytes 81952 | tf_op jit(solution)/shard_map/ppermute | solution.py:311
  16.5 3.2 %collective-permute-done.3.refs_1_ = f32[160,128]{1,0:T(8,128)S(1)} collective-permute-done((f32[160,128]{1,0:T(8,128)S(1)}, f32[160,128]{1,0:T(8,128)S(1)}, u32[]{:S(2)}, u32[]{:S(2)}) %collective-permute-start.3) | collective-permute-done | bytes 81952 | tf_op jit(solution)/shard_map/ppermute | solution.py:311
  19.7 0.0 collective-permute-done.4.refs_2_
  19.7 0.3 %grams.1.refs_3_ = f32[40,128]{1,0:T(8,128)S(1)} custom-call(s32[1]{0:T(128)} %bitcast.me_ref, f32[160,128]{1,0:T(8,128)S(1)} %collective-permute-done.2.refs_0_, f32[160,128]{1,0:T(8,128)S(1)} %collective-permute-done.3.refs_1_, f32[160,128]{1,0:T(8,128)S(1)} %collective-permute-done.4.refs_2_, f32[160,128]{1,0:T(8,128)S(1)} %gradients.1.refs_3_), custom_call_target="tpu_custom_call" | custom-call | tf_op jit(solution)/shard_map/grams/pallas_call | solution.py:251
  20.0 0.6 %collective-permute-start.5 = (f32[40,128]{1,0:T(8,128)S(1)}, f32[40,128]{1,0:T(8,128)S(1)}, u32[]{:S(2)}, u32[]{:S(2)}) collective-permute-start(f32[40,128]{1,0:T(8,128)S(1)} %grams.1.refs_3_), channel_id=1, source_target_pairs={{0,3},{1,2},{2,1},{3,0},{4,7},{5,6},{6,5},{7,4},{8,11},{9,10},{10,... | collective-permute-start | bytes 61448 | tf_op jit(solution)/shard_map/ppermute | solution.py:311
  20.7 1.0 %collective-permute-start.6 = (f32[40,128]{1,0:T(8,128)S(1)}, f32[40,128]{1,0:T(8,128)S(1)}, u32[]{:S(2)}, u32[]{:S(2)}) collective-permute-start(f32[40,128]{1,0:T(8,128)S(1)} %grams.1.refs_3_), channel_id=1, source_target_pairs={{0,2},{1,3},{2,0},{3,1},{4,6},{5,7},{6,4},{7,5},{8,10},{9,11},{10,... | collective-permute-start | bytes 61448 | tf_op jit(solution)/shard_map/ppermute | solution.py:311
  21.6 0.3 %collective-permute-start.7 = (f32[40,128]{1,0:T(8,128)S(1)}, f32[40,128]{1,0:T(8,128)S(1)}, u32[]{:S(2)}, u32[]{:S(2)}) collective-permute-start(f32[40,128]{1,0:T(8,128)S(1)} %grams.1.refs_3_), channel_id=1, source_target_pairs={{0,1},{1,0},{2,3},{3,2},{4,5},{5,4},{6,7},{7,6},{8,9},{9,8},{10,11... | collective-permute-start | bytes 61448 | tf_op jit(solution)/shard_map/ppermute | solution.py:311
  21.9 1.5 %collective-permute-done.5.refs_0_ = f32[40,128]{1,0:T(8,128)S(1)} collective-permute-done((f32[40,128]{1,0:T(8,128)S(1)}, f32[40,128]{1,0:T(8,128)S(1)}, u32[]{:S(2)}, u32[]{:S(2)}) %collective-permute-start.5) | collective-permute-done | bytes 20512 | tf_op jit(solution)/shard_map/ppermute | solution.py:311
  23.4 1.2 %collective-permute-done.6.refs_1_ = f32[40,128]{1,0:T(8,128)S(1)} collective-permute-done((f32[40,128]{1,0:T(8,128)S(1)}, f32[40,128]{1,0:T(8,128)S(1)}, u32[]{:S(2)}, u32[]{:S(2)}) %collective-permute-start.6) | collective-permute-done | bytes 20512 | tf_op jit(solution)/shard_map/ppermute | solution.py:311
  24.6 0.0 collective-permute-done.7.refs_2_
  24.6 1.9 %solve.1 = f32[16,16]{1,0:T(8,128)} custom-call(f32[40,128]{1,0:T(8,128)S(1)} %collective-permute-done.5.refs_0_, f32[40,128]{1,0:T(8,128)S(1)} %collective-permute-done.6.refs_1_, f32[40,128]{1,0:T(8,128)S(1)} %collective-permute-done.7.refs_2_, f32[40,128]{1,0:T(8,128)S(1)} %grams.1.refs_3_), custom_call_target="tpu_custom_call" | custom-call | tf_op jit(solution)/shard_map/solve/pallas_call | solution.py:302
  (8 shorter events, 0.0 us)
Async XLA Ops:
  0.0 2.8 %copy-start.2 = (s32[16]{0:T(128)S(1)}, s32[16]{0:T(128)}, u32[]{:S(2)}) copy-start(s32[16]{0:T(128)} %param.12) | copy-start | bytes 196
  0.0 2.8 %copy-start.1 = (s32[256]{0:T(256)S(1)}, s32[256]{0:T(256)}, u32[]{:S(2)}) copy-start(s32[256]{0:T(256)} %param.11) | copy-start | bytes 3076
  0.0 6.7 %copy-start = (f32[4,4096]{1,0:T(4,128)S(1)}, f32[4,4096]{1,0:T(4,128)}, u32[]{:S(2)}) copy-start(f32[4,4096]{1,0:T(4,128)} %queries_ref.1) | copy-start | bytes 196612
  2.2 1.5 %collective-permute-start = (f32[96,256]{1,0:T(8,128)S(1)}, f32[96,256]{1,0:T(8,128)S(1)}, u32[]{:S(2)}, u32[]{:S(2)}) collective-permute-start(f32[96,256]{1,0:T(8,128)S(1)} %get-tuple-element.10), channel_id=1, source_target_pairs={{0,1},{1,0},{2,3},{3,2},{4,5},{5,4},{6,7},{7,6},{8,9},{9,8},{10,11... | collective-permute-start | bytes 294920 | tf_op jit(solution)/shard_map/ppermute | solution.py:311
  3.8 5.3 %collective-permute-start.1 = (f32[64,256]{1,0:T(8,128)S(1)}, f32[64,256]{1,0:T(8,128)S(1)}, u32[]{:S(2)}, u32[]{:S(2)}) collective-permute-start(f32[64,256]{1,0:T(8,128)S(1)} %get-tuple-element.12), channel_id=1, source_target_pairs={{0,2},{1,3},{2,0},{3,1},{4,6},{5,7},{6,4},{7,5},{8,10},{9,11},{10,... | collective-permute-start | bytes 196616 | tf_op jit(solution)/shard_map/ppermute | solution.py:311
  9.4 7.1 %collective-permute-start.2 = (f32[160,128]{1,0:T(8,128)S(1)}, f32[160,128]{1,0:T(8,128)S(1)}, u32[]{:S(2)}, u32[]{:S(2)}) collective-permute-start(f32[160,128]{1,0:T(8,128)S(1)} %gradients.1.refs_3_), channel_id=1, source_target_pairs={{0,12},{4,8},{8,4},{12,0},{1,13},{5,9},{9,5},{13,1},{2,14},{6,10},... | collective-permute-start | bytes 245768 | tf_op jit(solution)/shard_map/ppermute | solution.py:311
  13.5 6.2 %collective-permute-start.3 = (f32[160,128]{1,0:T(8,128)S(1)}, f32[160,128]{1,0:T(8,128)S(1)}, u32[]{:S(2)}, u32[]{:S(2)}) collective-permute-start(f32[160,128]{1,0:T(8,128)S(1)} %gradients.1.refs_3_), channel_id=1, source_target_pairs={{0,8},{4,12},{8,0},{12,4},{1,9},{5,13},{9,1},{13,5},{2,10},{6,14},... | collective-permute-start | bytes 245768 | tf_op jit(solution)/shard_map/ppermute | solution.py:311
  13.5 6.2 %collective-permute-start.4 = (f32[160,128]{1,0:T(8,128)S(1)}, f32[160,128]{1,0:T(8,128)S(1)}, u32[]{:S(2)}, u32[]{:S(2)}) collective-permute-start(f32[160,128]{1,0:T(8,128)S(1)} %gradients.1.refs_3_), channel_id=1, source_target_pairs={{0,4},{4,0},{8,12},{12,8},{1,5},{5,1},{9,13},{13,9},{2,6},{6,2},{1... | collective-permute-start | bytes 245768 | tf_op jit(solution)/shard_map/ppermute | solution.py:311
  20.0 3.4 %collective-permute-start.5 = (f32[40,128]{1,0:T(8,128)S(1)}, f32[40,128]{1,0:T(8,128)S(1)}, u32[]{:S(2)}, u32[]{:S(2)}) collective-permute-start(f32[40,128]{1,0:T(8,128)S(1)} %grams.1.refs_3_), channel_id=1, source_target_pairs={{0,3},{1,2},{2,1},{3,0},{4,7},{5,6},{6,5},{7,4},{8,11},{9,10},{10,... | collective-permute-start | bytes 61448 | tf_op jit(solution)/shard_map/ppermute | solution.py:311
  20.7 4.0 %collective-permute-start.6 = (f32[40,128]{1,0:T(8,128)S(1)}, f32[40,128]{1,0:T(8,128)S(1)}, u32[]{:S(2)}, u32[]{:S(2)}) collective-permute-start(f32[40,128]{1,0:T(8,128)S(1)} %grams.1.refs_3_), channel_id=1, source_target_pairs={{0,2},{1,3},{2,0},{3,1},{4,6},{5,7},{6,4},{7,5},{8,10},{9,11},{10,... | collective-permute-start | bytes 61448 | tf_op jit(solution)/shard_map/ppermute | solution.py:311
  21.6 3.0 %collective-permute-start.7 = (f32[40,128]{1,0:T(8,128)S(1)}, f32[40,128]{1,0:T(8,128)S(1)}, u32[]{:S(2)}, u32[]{:S(2)}) collective-permute-start(f32[40,128]{1,0:T(8,128)S(1)} %grams.1.refs_3_), channel_id=1, source_target_pairs={{0,1},{1,0},{2,3},{3,2},{4,5},{5,4},{6,7},{7,6},{8,9},{9,8},{10,11... | collective-permute-start | bytes 61448 | tf_op jit(solution)/shard_map/ppermute | solution.py:311

commit v11 on v10

--- a/solution.py
+++ b/solution.py
@@ -67,25 +67,23 @@
         x_copies.append(fetch(x_hbm.at[rows, :], x_ref.at[rows, :], index))
         index += 1
 
-    half = x_ref.shape[1] // 2
-
-    def project(w_copy, w_ref, cuts, copies, cut, along):
-        totals = [None, None]
+    def project(w_copy, w_ref, cuts, copies, ref, along):
+        order = 1 if along == 0 else -1
+        total = None
         w_copy.wait()
         for (at, size), copy in zip(cuts, copies):
             copy.wait()
-            for side in (0, 1):
-                term = lax.dot_general(
-                    w_ref[:, at : at + size],
-                    cut(slice(at, at + size), slice(side * half, (side + 1) * half)),
-                    (((1,), (along,)), ((), ())),
-                    preferred_element_type=jnp.float32,
-                )
-                totals[side] = term if totals[side] is None else totals[side] + term
-        return jnp.concatenate(totals, axis=1)
-
-    grads_t = project(wg_copy, wg_ref, g_cuts, g_copies, lambda k, t: g_ref[t, k], 1)
-    wide_ref[...] = project(wx_copy, wx_ref, x_cuts, x_copies, lambda k, t: x_ref[k, t], 0)
+            term = lax.dot_general(
+                w_ref[:, at : at + size],
+                ref[(slice(at, at + size), slice(None))[::order]],
+                (((1,), (along,)), ((), ())),
+                preferred_element_type=jnp.float32,
+            )
+            total = term if total is None else total + term
+        return total
+
+    grads_t = project(wg_copy, wg_ref, g_cuts, g_copies, g_ref, 1)
+    wide_ref[...] = project(wx_copy, wx_ref, x_cuts, x_copies, x_ref, 0)
     rank = grads_t.shape[0]
     side = rank_ref[0] & 1
     for out, taken in ((keep_ref, side), (send_ref, side ^ 1)):
@@ -118,12 +116,13 @@
     )(me, *(pltpu.with_memory_space_constraint(array, pltpu.HBM) for array in arrays))
 
 
-def halve_kernel(own, rank_ref, kept_ref, came_ref, keep_ref, send_ref, sum_ref):
+def halve_kernel(own, rank_ref, kept_ref, came_ref, keep_ref, send_ref, same_ref, sum_ref):
     sum_ref[...] = kept_ref[...] + came_ref[...]
     place = rank_ref[0] // 2
-    for out, taken in ((keep_ref, place), (send_ref, place ^ 1)):
-        out[:own, :] = sum_ref[pl.ds(pl.multiple_of(taken * own, own), own), :]
-        out[own:, :] = sum_ref[-own:, :]
+    keep_ref[:own, :] = sum_ref[pl.ds(pl.multiple_of(place * own, own), own), :]
+    keep_ref[own:, :] = sum_ref[-own:, :]
+    send_ref[...] = sum_ref[pl.ds(pl.multiple_of((place ^ 1) * own, own), own), :]
+    same_ref[...] = sum_ref[-own:, :]
 
 
 def halve(kept, came, me, own):
@@ -131,9 +130,11 @@
     whole = pl.BlockSpec(memory_space=pltpu.VMEM)
     return pl.pallas_call(
         functools.partial(halve_kernel, own),
-        out_shape=[jax.ShapeDtypeStruct((2 * own, tokens), jnp.float32)] * 2,
+        out_shape=[
+            jax.ShapeDtypeStruct((count * own, tokens), jnp.float32) for count in (2, 1, 1)
+        ],
         in_specs=[pl.BlockSpec(memory_space=pltpu.SMEM), whole, whole],
-        out_specs=[whole] * 2,
+        out_specs=[whole] * 3,
         scratch_shapes=[pltpu.VMEM((rows, tokens), jnp.float32)],
         compiler_params=pltpu.CompilerParams(vmem_limit_bytes=VMEM_LIMIT),
         name="halve",
@@ -182,12 +183,12 @@
     )(me, queries)
 
 
-def grads_kernel(weights_ref, kept_ref, came_ref, asked_ref, out_ref):
-    summed = kept_ref[...] + came_ref[...]
+def grads_kernel(weights_ref, kept_ref, grads_ref, inputs_ref, asked_ref, out_ref):
+    own = kept_ref.shape[0] // 2
+    summed = kept_ref[:own, :] + grads_ref[...]
+    inputs_t = kept_ref[own:, :] + inputs_ref[...]
     weights = weights_ref[...]
-    own = summed.shape[0] // 2
     group = out_ref.shape[1] // own
-    inputs_t = summed[own:, :]
     zero = jnp.zeros_like(inputs_t)
     right = jnp.concatenate(
         [
@@ -210,7 +211,7 @@
     out_ref[count:, :] = asked_ref[...]
 
 
-def gradients(weights, kept, came, asked):
+def gradients(weights, kept, grads, inputs, asked):
     lanes = asked.shape[1]
     own = kept.shape[0] // 2
     rows = own * own // lanes * weights.shape[0] + asked.shape[0]
@@ -219,7 +220,7 @@
         out_shape=jax.ShapeDtypeStruct((rows, lanes), jnp.float32),
         compiler_params=pltpu.CompilerParams(vmem_limit_bytes=VMEM_LIMIT),
         name="gradients",
-    )(weights, kept, came, asked)
+    )(weights, kept, grads, inputs, asked)
 
 
 def grams_kernel(steps, seqs, me_ref, *refs):
@@ -289,11 +290,12 @@
         left = jnp.where(left_lanes, high, low).astype(jnp.bfloat16)
         high = high[:seqs].astype(jnp.bfloat16)
         low = low[:seqs].astype(jnp.bfloat16)
+        right = jnp.concatenate([high, high, low, low], axis=0)
         if at + 1 == len(steps):
             left, state = left[seqs:], state[seqs:]
         product = jnp.dot(
-            left, jnp.concatenate([high, high], axis=0), preferred_element_type=jnp.float32
-        ) + jnp.dot(left, jnp.concatenate([low, low], axis=0), preferred_element_type=jnp.float32)
+            jnp.concatenate([left, left], axis=1), right, preferred_element_type=jnp.float32
+        )
         state = step * (2.0 * state - product)
     out_ref[...] = state[:, : out_ref.shape[1]]
 
@@ -353,9 +355,9 @@
     asked = pick(queries, rank_of, rank, own)
     weights = token_weights(seq_ids, counts, first)
     came = from_partner(sent, "tensor", parts, 1)
-    kept, sent = halve(kept, came, rank_of, own)
-    came = from_partner(sent, "tensor", parts, 2)
-    message = gradients(weights, kept, came, asked)
+    kept, *sent = halve(kept, came, rank_of, own)
+    came = [from_partner(rows, "tensor", parts, 2) for rows in sent]
+    message = gradients(weights, kept, *came, asked)
     steps = own * own // message.shape[1]
     if blocks > SMALL:
         return finish_long(message, steps, first, seq_dev)

time: 26.7 us -> 26.9 us (level)
  waiting for transfers between devices: 11.3 us -> 11.8 us
    ppermute x8 -> x9, waiting for transfers between devices: 11.3 us -> 11.8 us  [from_partner(): return lax.ppermute(value, axis, [(i, i ^ m) for i in range(size)])]
    ppermute x8 -> x9, starting transfers between devices: 10 us -> 9.85 us  [from_partner(): return lax.ppermute(value, axis, [(i, i ^ m) for i in range(size)])]
  transfers between devices with their start and end apart: 8 -> 9, of which waited for: 6 -> 7; matrix products, arithmetic and copies ran while one was open for 1% -> 1% of each run, Pallas kernels for 1% -> 1%
where the time goes in v11:
time: 26.9 us; the launch traced here: 26.8 us
  waiting for transfers between devices  11.8 us (44%)
  starting transfers between devices  9.85 us (37%)
  Pallas kernels  4.84 us (18%)
    ppermute x9, waiting for transfers between devices, from_partner(): return lax.ppermute(value, axis, [(i, i ^ m) for i in range(size)])  11.8 us
    ppermute x9, starting transfers between devices, from_partner(): return lax.ppermute(value, axis, [(i, i ^ m) for i in range(size)])  9.85 us
    pallas_call x1, Pallas kernels, project(): pl.pallas_call(functools.partial(project_kernel, own), out_shape=[jax.Sha...  2.16 us
    pallas_call x1, Pallas kernels, solve(): pl.pallas_call(functools.partial(solve_kernel, seqs), out_shape=jax.Shape...  1.82 us
  transfers between devices with their start and end apart: 9, of which 7 were waited for; matrix products, arithmetic and copies ran while one was open for 1% of the time, Pallas kernels for 1%

profile of v11, /device:TPU:0, one launch (start us, length us, event | category | flops | bytes accessed | tf_op | source)
XLA Modules:
  0.0 26.8 jit_solution(11224745376788999873)
XLA Ops:
  0.0 2.2 %project.1 = (f32[96,256]{1,0:T(8,128)S(1)}, f32[96,256]{1,0:T(8,128)S(1)}) custom-call(s32[1]{0:T(128)} %bitcast.1.rank_ref, bf16[2752,256]{1,0:T(8,128)(2,1)} %bitcast.5, bf16[256,1024]{1,0:T(8,128)(2,1)} %g_hbm.1, bf16[64,2752]{1,0:T(8,128)(2,1)} %bitcast.6, bf16[64,1024]{1,0:T(8,128)(2,1)} %bitcast.7), custom_call_target="tpu_custom_call" | custom-call | tf_op jit(solution)/shard_map/project/pallas_call | solution.py:101
  2.2 0.5 %collective-permute-start = (f32[96,256]{1,0:T(8,128)S(1)}, f32[96,256]{1,0:T(8,128)S(1)}, u32[]{:S(2)}, u32[]{:S(2)}) collective-permute-start(f32[96,256]{1,0:T(8,128)S(1)} %get-tuple-element.11), channel_id=1, source_target_pairs={{0,1},{1,0},{2,3},{3,2},{4,5},{5,4},{6,7},{7,6},{8,9},{9,8},{10,11... | collective-permute-start | bytes 294920 | tf_op jit(solution)/shard_map/ppermute | solution.py:313
  2.7 0.1 convert_reduce_fusion
  2.9 0.8 %collective-permute-done.came_ref = f32[96,256]{1,0:T(8,128)S(1)} collective-permute-done((f32[96,256]{1,0:T(8,128)S(1)}, f32[96,256]{1,0:T(8,128)S(1)}, u32[]{:S(2)}, u32[]{:S(2)}) %collective-permute-start) | collective-permute-done | bytes 98336 | tf_op jit(solution)/shard_map/ppermute | solution.py:313
  3.7 2.9 %collective-permute-start.1 = (f32[32,256]{1,0:T(8,128)S(1)}, f32[32,256]{1,0:T(8,128)S(1)}, u32[]{:S(2)}, u32[]{:S(2)}) collective-permute-start(f32[32,256]{1,0:T(8,128)S(1)} %get-tuple-element.13), channel_id=1, source_target_pairs={{0,2},{1,3},{2,0},{3,1},{4,6},{5,7},{6,4},{7,5},{8,10},{9,11},{10,... | collective-permute-start | bytes 98312 | tf_op jit(solution)/shard_map/ppermute | solution.py:313
  6.6 0.1 collective-permute-start.2
  6.7 0.1 fusion.1.weights_ref
  6.7 0.2 pick.1.asked_ref
  6.9 1.6 %collective-permute-done.1.grads_ref = f32[32,256]{1,0:T(8,128)S(1)} collective-permute-done((f32[32,256]{1,0:T(8,128)S(1)}, f32[32,256]{1,0:T(8,128)S(1)}, u32[]{:S(2)}, u32[]{:S(2)}) %collective-permute-start.1) | collective-permute-done | bytes 32800 | tf_op jit(solution)/shard_map/ppermute | solution.py:313
  8.5 2.0 %collective-permute-done.2.inputs_ref = f32[32,256]{1,0:T(8,128)S(1)} collective-permute-done((f32[32,256]{1,0:T(8,128)S(1)}, f32[32,256]{1,0:T(8,128)S(1)}, u32[]{:S(2)}, u32[]{:S(2)}) %collective-permute-start.2) | collective-permute-done | bytes 32800 | tf_op jit(solution)/shard_map/ppermute | solution.py:313
  10.5 0.3 %gradients.1.refs_3_ = f32[160,128]{1,0:T(8,128)S(1)} custom-call(f32[16,256]{1,0:T(8,128)S(1)} %fusion.1.weights_ref, f32[64,256]{1,0:T(8,128)S(1)} %get-tuple-element.12.kept_ref, f32[32,256]{1,0:T(8,128)S(1)} %collective-permute-done.1.grads_ref, f32[32,256]{1,0:T(8,128)S(1)} %collective-permute-done.2.inputs_ref, f32[32,128]{1,0:T(8,128)S(1)} %pick.1.asked_ref), custom_call_target="tpu_custom_call" | custom-call | tf_op jit(solution)/shard_map/gradients/pallas_call | solution.py:218
  10.9 3.7 %collective-permute-start.3 = (f32[160,128]{1,0:T(8,128)S(1)}, f32[160,128]{1,0:T(8,128)S(1)}, u32[]{:S(2)}, u32[]{:S(2)}) collective-permute-start(f32[160,128]{1,0:T(8,128)S(1)} %gradients.1.refs_3_), channel_id=1, source_target_pairs={{0,12},{4,8},{8,4},{12,0},{1,13},{5,9},{9,5},{13,1},{2,14},{6,10},... | collective-permute-start | bytes 245768 | tf_op jit(solution)/shard_map/ppermute | solution.py:313
  14.5 0.0 collective-permute-start.4
  14.5 0.8 %collective-permute-start.5 = (f32[160,128]{1,0:T(8,128)S(1)}, f32[160,128]{1,0:T(8,128)S(1)}, u32[]{:S(2)}, u32[]{:S(2)}) collective-permute-start(f32[160,128]{1,0:T(8,128)S(1)} %gradients.1.refs_3_), channel_id=1, source_target_pairs={{0,4},{4,0},{8,12},{12,8},{1,5},{5,1},{9,13},{13,9},{2,6},{6,2},{1... | collective-permute-start | bytes 245768 | tf_op jit(solution)/shard_map/ppermute | solution.py:313
  15.3 2.0 %collective-permute-done.3.refs_0_ = f32[160,128]{1,0:T(8,128)S(1)} collective-permute-done((f32[160,128]{1,0:T(8,128)S(1)}, f32[160,128]{1,0:T(8,128)S(1)}, u32[]{:S(2)}, u32[]{:S(2)}) %collective-permute-start.3) | collective-permute-done | bytes 81952 | tf_op jit(solution)/shard_map/ppermute | solution.py:313
  17.3 3.4 %collective-permute-done.4.refs_1_ = f32[160,128]{1,0:T(8,128)S(1)} collective-permute-done((f32[160,128]{1,0:T(8,128)S(1)}, f32[160,128]{1,0:T(8,128)S(1)}, u32[]{:S(2)}, u32[]{:S(2)}) %collective-permute-start.4) | collective-permute-done | bytes 81952 | tf_op jit(solution)/shard_map/ppermute | solution.py:313
  20.7 0.3 %grams.1.refs_3_ = f32[40,128]{1,0:T(8,128)S(1)} custom-call(s32[1]{0:T(128)} %bitcast.me_ref, f32[160,128]{1,0:T(8,128)S(1)} %collective-permute-done.3.refs_0_, f32[160,128]{1,0:T(8,128)S(1)} %collective-permute-done.4.refs_1_, f32[160,128]{1,0:T(8,128)S(1)} %collective-permute-done.5.refs_2_, f32[160,128]{1,0:T(8,128)S(1)} %gradients.1.refs_3_), custom_call_target="tpu_custom_call" | custom-call | tf_op jit(solution)/shard_map/grams/pallas_call | solution.py:252
  21.1 0.0 collective-permute-start.6
  21.1 0.9 %collective-permute-start.7 = (f32[40,128]{1,0:T(8,128)S(1)}, f32[40,128]{1,0:T(8,128)S(1)}, u32[]{:S(2)}, u32[]{:S(2)}) collective-permute-start(f32[40,128]{1,0:T(8,128)S(1)} %grams.1.refs_3_), channel_id=1, source_target_pairs={{0,2},{1,3},{2,0},{3,1},{4,6},{5,7},{6,4},{7,5},{8,10},{9,11},{10,... | collective-permute-start | bytes 61448 | tf_op jit(solution)/shard_map/ppermute | solution.py:313
  22.0 0.9 %collective-permute-start.8 = (f32[40,128]{1,0:T(8,128)S(1)}, f32[40,128]{1,0:T(8,128)S(1)}, u32[]{:S(2)}, u32[]{:S(2)}) collective-permute-start(f32[40,128]{1,0:T(8,128)S(1)} %grams.1.refs_3_), channel_id=1, source_target_pairs={{0,1},{1,0},{2,3},{3,2},{4,5},{5,4},{6,7},{7,6},{8,9},{9,8},{10,11... | collective-permute-start | bytes 61448 | tf_op jit(solution)/shard_map/ppermute | solution.py:313
  22.9 1.3 %collective-permute-done.6.refs_0_ = f32[40,128]{1,0:T(8,128)S(1)} collective-permute-done((f32[40,128]{1,0:T(8,128)S(1)}, f32[40,128]{1,0:T(8,128)S(1)}, u32[]{:S(2)}, u32[]{:S(2)}) %collective-permute-start.6) | collective-permute-done | bytes 20512 | tf_op jit(solution)/shard_map/ppermute | solution.py:313
  24.3 0.7 %collective-permute-done.7.refs_1_ = f32[40,128]{1,0:T(8,128)S(1)} collective-permute-done((f32[40,128]{1,0:T(8,128)S(1)}, f32[40,128]{1,0:T(8,128)S(1)}, u32[]{:S(2)}, u32[]{:S(2)}) %collective-permute-start.7) | collective-permute-done | bytes 20512 | tf_op jit(solution)/shard_map/ppermute | solution.py:313
  24.9 0.0 collective-permute-done.8.refs_2_
  24.9 1.8 %solve.1 = f32[16,16]{1,0:T(8,128)} custom-call(f32[40,128]{1,0:T(8,128)S(1)} %collective-permute-done.6.refs_0_, f32[40,128]{1,0:T(8,128)S(1)} %collective-permute-done.7.refs_1_, f32[40,128]{1,0:T(8,128)S(1)} %collective-permute-done.8.refs_2_, f32[40,128]{1,0:T(8,128)S(1)} %grams.1.refs_3_), custom_call_target="tpu_custom_call" | custom-call | tf_op jit(solution)/shard_map/solve/pallas_call | solution.py:304
  (10 shorter events, 0.0 us)
Async XLA Ops:
  0.0 2.7 %copy-start.2 = (s32[16]{0:T(128)S(1)}, s32[16]{0:T(128)}, u32[]{:S(2)}) copy-start(s32[16]{0:T(128)} %param.12) | copy-start | bytes 196
  0.0 2.7 %copy-start.1 = (s32[256]{0:T(256)S(1)}, s32[256]{0:T(256)}, u32[]{:S(2)}) copy-start(s32[256]{0:T(256)} %param.11) | copy-start | bytes 3076
  0.0 6.7 %copy-start = (f32[4,4096]{1,0:T(4,128)S(1)}, f32[4,4096]{1,0:T(4,128)}, u32[]{:S(2)}) copy-start(f32[4,4096]{1,0:T(4,128)} %queries_ref.1) | copy-start | bytes 196612
  2.2 1.5 %collective-permute-start = (f32[96,256]{1,0:T(8,128)S(1)}, f32[96,256]{1,0:T(8,128)S(1)}, u32[]{:S(2)}, u32[]{:S(2)}) collective-permute-start(f32[96,256]{1,0:T(8,128)S(1)} %get-tuple-element.11), channel_id=1, source_target_pairs={{0,1},{1,0},{2,3},{3,2},{4,5},{5,4},{6,7},{7,6},{8,9},{9,8},{10,11... | collective-permute-start | bytes 294920 | tf_op jit(solution)/shard_map/ppermute | solution.py:313
  3.7 4.8 %collective-permute-start.1 = (f32[32,256]{1,0:T(8,128)S(1)}, f32[32,256]{1,0:T(8,128)S(1)}, u32[]{:S(2)}, u32[]{:S(2)}) collective-permute-start(f32[32,256]{1,0:T(8,128)S(1)} %get-tuple-element.13), channel_id=1, source_target_pairs={{0,2},{1,3},{2,0},{3,1},{4,6},{5,7},{6,4},{7,5},{8,10},{9,11},{10,... | collective-permute-start | bytes 98312 | tf_op jit(solution)/shard_map/ppermute | solution.py:313
  6.6 3.9 %collective-permute-start.2 = (f32[32,256]{1,0:T(8,128)S(1)}, f32[32,256]{1,0:T(8,128)S(1)}, u32[]{:S(2)}, u32[]{:S(2)}) collective-permute-start(f32[32,256]{1,0:T(8,128)S(1)} %get-tuple-element.14), channel_id=1, source_target_pairs={{0,2},{1,3},{2,0},{3,1},{4,6},{5,7},{6,4},{7,5},{8,10},{9,11},{10,... | collective-permute-start | bytes 98312 | tf_op jit(solution)/shard_map/ppermute | solution.py:313
  10.9 6.5 %collective-permute-start.3 = (f32[160,128]{1,0:T(8,128)S(1)}, f32[160,128]{1,0:T(8,128)S(1)}, u32[]{:S(2)}, u32[]{:S(2)}) collective-permute-start(f32[160,128]{1,0:T(8,128)S(1)} %gradients.1.refs_3_), channel_id=1, source_target_pairs={{0,12},{4,8},{8,4},{12,0},{1,13},{5,9},{9,5},{13,1},{2,14},{6,10},... | collective-permute-start | bytes 245768 | tf_op jit(solution)/shard_map/ppermute | solution.py:313
  14.5 6.2 %collective-permute-start.4 = (f32[160,128]{1,0:T(8,128)S(1)}, f32[160,128]{1,0:T(8,128)S(1)}, u32[]{:S(2)}, u32[]{:S(2)}) collective-permute-start(f32[160,128]{1,0:T(8,128)S(1)} %gradients.1.refs_3_), channel_id=1, source_target_pairs={{0,8},{4,12},{8,0},{12,4},{1,9},{5,13},{9,1},{13,5},{2,10},{6,14},... | collective-permute-start | bytes 245768 | tf_op jit(solution)/shard_map/ppermute | solution.py:313
  14.5 6.2 %collective-permute-start.5 = (f32[160,128]{1,0:T(8,128)S(1)}, f32[160,128]{1,0:T(8,128)S(1)}, u32[]{:S(2)}, u32[]{:S(2)}) collective-permute-start(f32[160,128]{1,0:T(8,128)S(1)} %gradients.1.refs_3_), channel_id=1, source_target_pairs={{0,4},{4,0},{8,12},{12,8},{1,5},{5,1},{9,13},{13,9},{2,6},{6,2},{1... | collective-permute-start | bytes 245768 | tf_op jit(solution)/shard_map/ppermute | solution.py:313
  21.1 3.2 %collective-permute-start.6 = (f32[40,128]{1,0:T(8,128)S(1)}, f32[40,128]{1,0:T(8,128)S(1)}, u32[]{:S(2)}, u32[]{:S(2)}) collective-permute-start(f32[40,128]{1,0:T(8,128)S(1)} %grams.1.refs_3_), channel_id=1, source_target_pairs={{0,3},{1,2},{2,1},{3,0},{4,7},{5,6},{6,5},{7,4},{8,11},{9,10},{10,... | collective-permute-start | bytes 61448 | tf_op jit(solution)/shard_map/ppermute | solution.py:313
  21.1 3.8 %collective-permute-start.7 = (f32[40,128]{1,0:T(8,128)S(1)}, f32[40,128]{1,0:T(8,128)S(1)}, u32[]{:S(2)}, u32[]{:S(2)}) collective-permute-start(f32[40,128]{1,0:T(8,128)S(1)} %grams.1.refs_3_), channel_id=1, source_target_pairs={{0,2},{1,3},{2,0},{3,1},{4,6},{5,7},{6,4},{7,5},{8,10},{9,11},{10,... | collective-permute-start | bytes 61448 | tf_op jit(solution)/shard_map/ppermute | solution.py:313
  22.0 2.9 %collective-permute-start.8 = (f32[40,128]{1,0:T(8,128)S(1)}, f32[40,128]{1,0:T(8,128)S(1)}, u32[]{:S(2)}, u32[]{:S(2)}) collective-permute-start(f32[40,128]{1,0:T(8,128)S(1)} %grams.1.refs_3_), channel_id=1, source_target_pairs={{0,1},{1,0},{2,3},{3,2},{4,5},{5,4},{6,7},{7,6},{8,9},{9,8},{10,11... | collective-permute-start | bytes 61448 | tf_op jit(solution)/shard_map/ppermute | solution.py:313

commit v12 on v10

--- a/solution.py
+++ b/solution.py
@@ -33,13 +33,16 @@
 
 
 def dot_nt(left, right):
-    dims = (((1,), (1,)), ((), ()))
+    rows = left.shape[0]
     lh, ll = two_terms(left)
     rh, rl = two_terms(right)
     mul = functools.partial(
-        lax.dot_general, dimension_numbers=dims, preferred_element_type=jnp.float32
-    )
-    return mul(lh, rh) + (mul(lh, rl) + mul(ll, rh))
+        lax.dot_general,
+        dimension_numbers=(((1,), (1,)), ((), ())),
+        preferred_element_type=jnp.float32,
+    )
+    both = mul(jnp.concatenate([lh, ll], axis=0), rh)
+    return both[:rows] + (mul(lh, rl) + both[rows:])
 
 
 def project_kernel(own, rank_ref, x_hbm, g_hbm, wx_hbm, wg_hbm, keep_ref, send_ref, *scratch):
@@ -51,8 +54,8 @@
         copy.start()
         return copy
 
-    g_cuts = cuts_of(g_ref.shape[1], 512)
-    x_cuts = cuts_of(x_ref.shape[0], 768)
+    g_cuts = cuts_of(g_ref.shape[1], 1024)
+    x_cuts = cuts_of(x_ref.shape[0], 1024)
     wg_copy = fetch(wg_hbm, wg_ref, 0)
     index = 2
     g_copies = []
@@ -67,25 +70,23 @@
         x_copies.append(fetch(x_hbm.at[rows, :], x_ref.at[rows, :], index))
         index += 1
 
-    half = x_ref.shape[1] // 2
-
-    def project(w_copy, w_ref, cuts, copies, cut, along):
-        totals = [None, None]
+    def project(w_copy, w_ref, cuts, copies, ref, along):
+        order = 1 if along == 0 else -1
+        total = None
         w_copy.wait()
         for (at, size), copy in zip(cuts, copies):
             copy.wait()
-            for side in (0, 1):
-                term = lax.dot_general(
-                    w_ref[:, at : at + size],
-                    cut(slice(at, at + size), slice(side * half, (side + 1) * half)),
-                    (((1,), (along,)), ((), ())),
-                    preferred_element_type=jnp.float32,
-                )
-                totals[side] = term if totals[side] is None else totals[side] + term
-        return jnp.concatenate(totals, axis=1)
-
-    grads_t = project(wg_copy, wg_ref, g_cuts, g_copies, lambda k, t: g_ref[t, k], 1)
-    wide_ref[...] = project(wx_copy, wx_ref, x_cuts, x_copies, lambda k, t: x_ref[k, t], 0)
+            term = lax.dot_general(
+                w_ref[:, at : at + size],
+                ref[(slice(at, at + size), slice(None))[::order]],
+                (((1,), (along,)), ((), ())),
+                preferred_element_type=jnp.float32,
+            )
+            total = term if total is None else total + term
+        return total
+
+    grads_t = project(wg_copy, wg_ref, g_cuts, g_copies, g_ref, 1)
+    wide_ref[...] = project(wx_copy, wx_ref, x_cuts, x_copies, x_ref, 0)
     rank = grads_t.shape[0]
     side = rank_ref[0] & 1
     for out, taken in ((keep_ref, side), (send_ref, side ^ 1)):
@@ -97,7 +98,7 @@
     rank = in_proj.shape[1]
     tokens, hidden = inputs.shape
     width = out_grads.shape[1]
-    copies = 2 + len(cuts_of(width, 512)) + len(cuts_of(hidden, 768))
+    copies = 2 + len(cuts_of(width, 1024)) + len(cuts_of(hidden, 1024))
     arrays = (inputs.T, out_grads, in_proj.T, out_proj.T)
     in_hbm = pl.BlockSpec(memory_space=pltpu.HBM)
     return pl.pallas_call(
@@ -188,25 +189,12 @@
     own = summed.shape[0] // 2
     group = out_ref.shape[1] // own
     inputs_t = summed[own:, :]
-    zero = jnp.zeros_like(inputs_t)
-    right = jnp.concatenate(
-        [
-            jnp.concatenate([inputs_t if j == k else zero for k in range(group)], axis=1)
-            for j in range(group)
-        ],
-        axis=0,
-    )
-    rows = []
-    for i in range(own // group):
-        rows.append(
-            jnp.concatenate(
-                [weights * summed[group * i + j : group * i + j + 1, :] for j in range(group)],
-                axis=1,
-            )
-        )
-    left = jnp.concatenate(rows, axis=0)
-    count = left.shape[0]
-    out_ref[:count, :] = dot_nt(left, right)
+    made = []
+    for j in range(group):
+        left = [weights * summed[i + j : i + j + 1, :] for i in range(0, own, group)]
+        made.append(dot_nt(jnp.concatenate(left, axis=0), inputs_t))
+    count = made[0].shape[0]
+    out_ref[:count, :] = jnp.concatenate(made, axis=1)
     out_ref[count:, :] = asked_ref[...]
 
 
@@ -289,11 +277,12 @@
         left = jnp.where(left_lanes, high, low).astype(jnp.bfloat16)
         high = high[:seqs].astype(jnp.bfloat16)
         low = low[:seqs].astype(jnp.bfloat16)
+        right = jnp.concatenate([high, high, low, low], axis=0)
         if at + 1 == len(steps):
             left, state = left[seqs:], state[seqs:]
         product = jnp.dot(
-            left, jnp.concatenate([high, high], axis=0), preferred_element_type=jnp.float32
-        ) + jnp.dot(left, jnp.concatenate([low, low], axis=0), preferred_element_type=jnp.float32)
+            jnp.concatenate([left, left], axis=1), right, preferred_element_type=jnp.float32
+        )
         state = step * (2.0 * state - product)
     out_ref[...] = state[:, : out_ref.shape[1]]
 

time: 26.7 us -> 26.6 us (level)
  no operation moved by 1% of the time
where the time goes in v12:
time: 26.6 us; the launch traced here: 26.4 us
  waiting for transfers between devices  11.3 us (42%)
  starting transfers between devices  10 us (38%)
  Pallas kernels  4.9 us (18%)
    ppermute x8, waiting for transfers between devices, from_partner(): return lax.ppermute(value, axis, [(i, i ^ m) for i in range(size)])  11.3 us
    ppermute x8, starting transfers between devices, from_partner(): return lax.ppermute(value, axis, [(i, i ^ m) for i in range(size)])  10 us
    pallas_call x1, Pallas kernels, project(): pl.pallas_call(functools.partial(project_kernel, own), out_shape=[jax.Sha...  2.16 us
    pallas_call x1, Pallas kernels, solve(): pl.pallas_call(functools.partial(solve_kernel, seqs), out_shape=jax.Shape...  1.82 us
  transfers between devices with their start and end apart: 8, of which 6 were waited for; matrix products, arithmetic and copies ran while one was open for 1% of the time, Pallas kernels for 1%

profile of v12, /device:TPU:0, one launch (start us, length us, event | category | flops | bytes accessed | tf_op | source)
XLA Modules:
  0.0 26.4 jit_solution(8715023567041395919)
XLA Ops:
  0.0 2.2 %project.1 = (f32[96,256]{1,0:T(8,128)S(1)}, f32[96,256]{1,0:T(8,128)S(1)}) custom-call(s32[1]{0:T(128)} %bitcast.1.rank_ref, bf16[2752,256]{1,0:T(8,128)(2,1)} %bitcast.5, bf16[256,1024]{1,0:T(8,128)(2,1)} %g_hbm.1, bf16[64,2752]{1,0:T(8,128)(2,1)} %bitcast.6, bf16[64,1024]{1,0:T(8,128)(2,1)} %bitcast.7), custom_call_target="tpu_custom_call" | custom-call | tf_op jit(solution)/shard_map/project/pallas_call | solution.py:104
  2.2 0.5 %collective-permute-start = (f32[96,256]{1,0:T(8,128)S(1)}, f32[96,256]{1,0:T(8,128)S(1)}, u32[]{:S(2)}, u32[]{:S(2)}) collective-permute-start(f32[96,256]{1,0:T(8,128)S(1)} %get-tuple-element.10), channel_id=1, source_target_pairs={{0,1},{1,0},{2,3},{3,2},{4,5},{5,4},{6,7},{7,6},{8,9},{9,8},{10,11... | collective-permute-start | bytes 294920 | tf_op jit(solution)/shard_map/ppermute | solution.py:300
  2.7 0.0 copy-done.2
  2.7 0.1 convert_reduce_fusion
  2.8 0.8 %collective-permute-done.came_ref = f32[96,256]{1,0:T(8,128)S(1)} collective-permute-done((f32[96,256]{1,0:T(8,128)S(1)}, f32[96,256]{1,0:T(8,128)S(1)}, u32[]{:S(2)}, u32[]{:S(2)}) %collective-permute-start) | collective-permute-done | bytes 98336 | tf_op jit(solution)/shard_map/ppermute | solution.py:300
  3.7 2.9 %collective-permute-start.1 = (f32[64,256]{1,0:T(8,128)S(1)}, f32[64,256]{1,0:T(8,128)S(1)}, u32[]{:S(2)}, u32[]{:S(2)}) collective-permute-start(f32[64,256]{1,0:T(8,128)S(1)} %get-tuple-element.12), channel_id=1, source_target_pairs={{0,2},{1,3},{2,0},{3,1},{4,6},{5,7},{6,4},{7,5},{8,10},{9,11},{10,... | collective-permute-start | bytes 196616 | tf_op jit(solution)/shard_map/ppermute | solution.py:300
  6.6 0.1 fusion.1.weights_ref
  6.7 0.2 pick.1.asked_ref
  6.8 2.2 %collective-permute-done.1.came_ref = f32[64,256]{1,0:T(8,128)S(1)} collective-permute-done((f32[64,256]{1,0:T(8,128)S(1)}, f32[64,256]{1,0:T(8,128)S(1)}, u32[]{:S(2)}, u32[]{:S(2)}) %collective-permute-start.1) | collective-permute-done | bytes 65568 | tf_op jit(solution)/shard_map/ppermute | solution.py:300
  9.0 0.4 %gradients.1.refs_3_ = f32[160,128]{1,0:T(8,128)S(1)} custom-call(f32[16,256]{1,0:T(8,128)S(1)} %fusion.1.weights_ref, f32[64,256]{1,0:T(8,128)S(1)} %get-tuple-element.11.kept_ref, f32[64,256]{1,0:T(8,128)S(1)} %collective-permute-done.1.came_ref, f32[32,128]{1,0:T(8,128)S(1)} %pick.1.asked_ref), custom_call_target="tpu_custom_call" | custom-call | tf_op jit(solution)/shard_map/gradients/pallas_call | solution.py:205
  9.4 4.0 %collective-permute-start.2 = (f32[160,128]{1,0:T(8,128)S(1)}, f32[160,128]{1,0:T(8,128)S(1)}, u32[]{:S(2)}, u32[]{:S(2)}) collective-permute-start(f32[160,128]{1,0:T(8,128)S(1)} %gradients.1.refs_3_), channel_id=1, source_target_pairs={{0,12},{4,8},{8,4},{12,0},{1,13},{5,9},{9,5},{13,1},{2,14},{6,10},... | collective-permute-start | bytes 245768 | tf_op jit(solution)/shard_map/ppermute | solution.py:300
  13.5 0.0 collective-permute-start.3
  13.5 0.6 %collective-permute-start.4 = (f32[160,128]{1,0:T(8,128)S(1)}, f32[160,128]{1,0:T(8,128)S(1)}, u32[]{:S(2)}, u32[]{:S(2)}) collective-permute-start(f32[160,128]{1,0:T(8,128)S(1)} %gradients.1.refs_3_), channel_id=1, source_target_pairs={{0,4},{4,0},{8,12},{12,8},{1,5},{5,1},{9,13},{13,9},{2,6},{6,2},{1... | collective-permute-start | bytes 245768 | tf_op jit(solution)/shard_map/ppermute | solution.py:300
  14.1 2.4 %collective-permute-done.2.refs_0_ = f32[160,128]{1,0:T(8,128)S(1)} collective-permute-done((f32[160,128]{1,0:T(8,128)S(1)}, f32[160,128]{1,0:T(8,128)S(1)}, u32[]{:S(2)}, u32[]{:S(2)}) %collective-permute-start.2) | collective-permute-done | bytes 81952 | tf_op jit(solution)/shard_map/ppermute | solution.py:300
  16.5 3.2 %collective-permute-done.3.refs_1_ = f32[160,128]{1,0:T(8,128)S(1)} collective-permute-done((f32[160,128]{1,0:T(8,128)S(1)}, f32[160,128]{1,0:T(8,128)S(1)}, u32[]{:S(2)}, u32[]{:S(2)}) %collective-permute-start.3) | collective-permute-done | bytes 81952 | tf_op jit(solution)/shard_map/ppermute | solution.py:300
  19.7 0.0 collective-permute-done.4.refs_2_
  19.7 0.3 %grams.1.refs_3_ = f32[40,128]{1,0:T(8,128)S(1)} custom-call(s32[1]{0:T(128)} %bitcast.me_ref, f32[160,128]{1,0:T(8,128)S(1)} %collective-permute-done.2.refs_0_, f32[160,128]{1,0:T(8,128)S(1)} %collective-permute-done.3.refs_1_, f32[160,128]{1,0:T(8,128)S(1)} %collective-permute-done.4.refs_2_, f32[160,128]{1,0:T(8,128)S(1)} %gradients.1.refs_3_), custom_call_target="tpu_custom_call" | custom-call | tf_op jit(solution)/shard_map/grams/pallas_call | solution.py:239
  20.0 0.6 %collective-permute-start.5 = (f32[40,128]{1,0:T(8,128)S(1)}, f32[40,128]{1,0:T(8,128)S(1)}, u32[]{:S(2)}, u32[]{:S(2)}) collective-permute-start(f32[40,128]{1,0:T(8,128)S(1)} %grams.1.refs_3_), channel_id=1, source_target_pairs={{0,3},{1,2},{2,1},{3,0},{4,7},{5,6},{6,5},{7,4},{8,11},{9,10},{10,... | collective-permute-start | bytes 61448 | tf_op jit(solution)/shard_map/ppermute | solution.py:300
  20.7 1.0 %collective-permute-start.6 = (f32[40,128]{1,0:T(8,128)S(1)}, f32[40,128]{1,0:T(8,128)S(1)}, u32[]{:S(2)}, u32[]{:S(2)}) collective-permute-start(f32[40,128]{1,0:T(8,128)S(1)} %grams.1.refs_3_), channel_id=1, source_target_pairs={{0,2},{1,3},{2,0},{3,1},{4,6},{5,7},{6,4},{7,5},{8,10},{9,11},{10,... | collective-permute-start | bytes 61448 | tf_op jit(solution)/shard_map/ppermute | solution.py:300
  21.6 0.3 %collective-permute-start.7 = (f32[40,128]{1,0:T(8,128)S(1)}, f32[40,128]{1,0:T(8,128)S(1)}, u32[]{:S(2)}, u32[]{:S(2)}) collective-permute-start(f32[40,128]{1,0:T(8,128)S(1)} %grams.1.refs_3_), channel_id=1, source_target_pairs={{0,1},{1,0},{2,3},{3,2},{4,5},{5,4},{6,7},{7,6},{8,9},{9,8},{10,11... | collective-permute-start | bytes 61448 | tf_op jit(solution)/shard_map/ppermute | solution.py:300
  21.9 1.5 %collective-permute-done.5.refs_0_ = f32[40,128]{1,0:T(8,128)S(1)} collective-permute-done((f32[40,128]{1,0:T(8,128)S(1)}, f32[40,128]{1,0:T(8,128)S(1)}, u32[]{:S(2)}, u32[]{:S(2)}) %collective-permute-start.5) | collective-permute-done | bytes 20512 | tf_op jit(solution)/shard_map/ppermute | solution.py:300
  23.4 1.2 %collective-permute-done.6.refs_1_ = f32[40,128]{1,0:T(8,128)S(1)} collective-permute-done((f32[40,128]{1,0:T(8,128)S(1)}, f32[40,128]{1,0:T(8,128)S(1)}, u32[]{:S(2)}, u32[]{:S(2)}) %collective-permute-start.6) | collective-permute-done | bytes 20512 | tf_op jit(solution)/shard_map/ppermute | solution.py:300
  24.6 0.0 collective-permute-done.7.refs_2_
  24.6 1.8 %solve.1 = f32[16,16]{1,0:T(8,128)} custom-call(f32[40,128]{1,0:T(8,128)S(1)} %collective-permute-done.5.refs_0_, f32[40,128]{1,0:T(8,128)S(1)} %collective-permute-done.6.refs_1_, f32[40,128]{1,0:T(8,128)S(1)} %collective-permute-done.7.refs_2_, f32[40,128]{1,0:T(8,128)S(1)} %grams.1.refs_3_), custom_call_target="tpu_custom_call" | custom-call | tf_op jit(solution)/shard_map/solve/pallas_call | solution.py:291
  (8 shorter events, 0.0 us)
Async XLA Ops:
  0.0 2.7 %copy-start.2 = (s32[16]{0:T(128)S(1)}, s32[16]{0:T(128)}, u32[]{:S(2)}) copy-start(s32[16]{0:T(128)} %param.12) | copy-start | bytes 196
  0.0 2.7 %copy-start.1 = (s32[256]{0:T(256)S(1)}, s32[256]{0:T(256)}, u32[]{:S(2)}) copy-start(s32[256]{0:T(256)} %param.11) | copy-start | bytes 3076
  0.0 6.7 %copy-start = (f32[4,4096]{1,0:T(4,128)S(1)}, f32[4,4096]{1,0:T(4,128)}, u32[]{:S(2)}) copy-start(f32[4,4096]{1,0:T(4,128)} %queries_ref.1) | copy-start | bytes 196612
  2.2 1.5 %collective-permute-start = (f32[96,256]{1,0:T(8,128)S(1)}, f32[96,256]{1,0:T(8,128)S(1)}, u32[]{:S(2)}, u32[]{:S(2)}) collective-permute-start(f32[96,256]{1,0:T(8,128)S(1)} %get-tuple-element.10), channel_id=1, source_target_pairs={{0,1},{1,0},{2,3},{3,2},{4,5},{5,4},{6,7},{7,6},{8,9},{9,8},{10,11... | collective-permute-start | bytes 294920 | tf_op jit(solution)/shard_map/ppermute | solution.py:300
  3.7 5.3 %collective-permute-start.1 = (f32[64,256]{1,0:T(8,128)S(1)}, f32[64,256]{1,0:T(8,128)S(1)}, u32[]{:S(2)}, u32[]{:S(2)}) collective-permute-start(f32[64,256]{1,0:T(8,128)S(1)} %get-tuple-element.12), channel_id=1, source_target_pairs={{0,2},{1,3},{2,0},{3,1},{4,6},{5,7},{6,4},{7,5},{8,10},{9,11},{10,... | collective-permute-start | bytes 196616 | tf_op jit(solution)/shard_map/ppermute | solution.py:300
  9.4 7.1 %collective-permute-start.2 = (f32[160,128]{1,0:T(8,128)S(1)}, f32[160,128]{1,0:T(8,128)S(1)}, u32[]{:S(2)}, u32[]{:S(2)}) collective-permute-start(f32[160,128]{1,0:T(8,128)S(1)} %gradients.1.refs_3_), channel_id=1, source_target_pairs={{0,12},{4,8},{8,4},{12,0},{1,13},{5,9},{9,5},{13,1},{2,14},{6,10},... | collective-permute-start | bytes 245768 | tf_op jit(solution)/shard_map/ppermute | solution.py:300
  13.5 6.2 %collective-permute-start.3 = (f32[160,128]{1,0:T(8,128)S(1)}, f32[160,128]{1,0:T(8,128)S(1)}, u32[]{:S(2)}, u32[]{:S(2)}) collective-permute-start(f32[160,128]{1,0:T(8,128)S(1)} %gradients.1.refs_3_), channel_id=1, source_target_pairs={{0,8},{4,12},{8,0},{12,4},{1,9},{5,13},{9,1},{13,5},{2,10},{6,14},... | collective-permute-start | bytes 245768 | tf_op jit(solution)/shard_map/ppermute | solution.py:300
  13.5 6.2 %collective-permute-start.4 = (f32[160,128]{1,0:T(8,128)S(1)}, f32[160,128]{1,0:T(8,128)S(1)}, u32[]{:S(2)}, u32[]{:S(2)}) collective-permute-start(f32[160,128]{1,0:T(8,128)S(1)} %gradients.1.refs_3_), channel_id=1, source_target_pairs={{0,4},{4,0},{8,12},{12,8},{1,5},{5,1},{9,13},{13,9},{2,6},{6,2},{1... | collective-permute-start | bytes 245768 | tf_op jit(solution)/shard_map/ppermute | solution.py:300
  20.0 3.4 %collective-permute-start.5 = (f32[40,128]{1,0:T(8,128)S(1)}, f32[40,128]{1,0:T(8,128)S(1)}, u32[]{:S(2)}, u32[]{:S(2)}) collective-permute-start(f32[40,128]{1,0:T(8,128)S(1)} %grams.1.refs_3_), channel_id=1, source_target_pairs={{0,3},{1,2},{2,1},{3,0},{4,7},{5,6},{6,5},{7,4},{8,11},{9,10},{10,... | collective-permute-start | bytes 61448 | tf_op jit(solution)/shard_map/ppermute | solution.py:300
  20.7 4.0 %collective-permute-start.6 = (f32[40,128]{1,0:T(8,128)S(1)}, f32[40,128]{1,0:T(8,128)S(1)}, u32[]{:S(2)}, u32[]{:S(2)}) collective-permute-start(f32[40,128]{1,0:T(8,128)S(1)} %grams.1.refs_3_), channel_id=1, source_target_pairs={{0,2},{1,3},{2,0},{3,1},{4,6},{5,7},{6,4},{7,5},{8,10},{9,11},{10,... | collective-permute-start | bytes 61448 | tf_op jit(solution)/shard_map/ppermute | solution.py:300
  21.6 3.0 %collective-permute-start.7 = (f32[40,128]{1,0:T(8,128)S(1)}, f32[40,128]{1,0:T(8,128)S(1)}, u32[]{:S(2)}, u32[]{:S(2)}) collective-permute-start(f32[40,128]{1,0:T(8,128)S(1)} %grams.1.refs_3_), channel_id=1, source_target_pairs={{0,1},{1,0},{2,3},{3,2},{4,5},{5,4},{6,7},{7,6},{8,9},{9,8},{10,11... | collective-permute-start | bytes 61448 | tf_op jit(solution)/shard_map/ppermute | solution.py:300

commit v13 on v12

--- a/solution.py
+++ b/solution.py
@@ -70,23 +70,27 @@
         x_copies.append(fetch(x_hbm.at[rows, :], x_ref.at[rows, :], index))
         index += 1
 
-    def project(w_copy, w_ref, cuts, copies, ref, along):
-        order = 1 if along == 0 else -1
+    def product(copies, terms):
         total = None
-        w_copy.wait()
-        for (at, size), copy in zip(cuts, copies):
+        for copy, (left, right, along) in zip(copies, terms):
             copy.wait()
             term = lax.dot_general(
-                w_ref[:, at : at + size],
-                ref[(slice(at, at + size), slice(None))[::order]],
-                (((1,), (along,)), ((), ())),
-                preferred_element_type=jnp.float32,
+                left(), right(), (((1,), (along,)), ((), ())), preferred_element_type=jnp.float32
             )
             total = term if total is None else total + term
         return total
 
-    grads_t = project(wg_copy, wg_ref, g_cuts, g_copies, g_ref, 1)
-    wide_ref[...] = project(wx_copy, wx_ref, x_cuts, x_copies, x_ref, 0)
+    def cut(ref, at, size, along):
+        return lambda: ref[at : at + size, :] if along == 0 else ref[:, at : at + size]
+
+    wg_copy.wait()
+    grads_t = product(
+        g_copies, [(cut(g_ref, at, size, 1), cut(wg_ref, at, size, 1), 1) for at, size in g_cuts]
+    ).T
+    wx_copy.wait()
+    wide_ref[...] = product(
+        x_copies, [(cut(wx_ref, at, size, 1), cut(x_ref, at, size, 0), 0) for at, size in x_cuts]
+    )
     rank = grads_t.shape[0]
     side = rank_ref[0] & 1
     for out, taken in ((keep_ref, side), (send_ref, side ^ 1)):
@@ -189,12 +193,25 @@
     own = summed.shape[0] // 2
     group = out_ref.shape[1] // own
     inputs_t = summed[own:, :]
-    made = []
-    for j in range(group):
-        left = [weights * summed[i + j : i + j + 1, :] for i in range(0, own, group)]
-        made.append(dot_nt(jnp.concatenate(left, axis=0), inputs_t))
-    count = made[0].shape[0]
-    out_ref[:count, :] = jnp.concatenate(made, axis=1)
+    zero = jnp.zeros_like(inputs_t)
+    right = jnp.concatenate(
+        [
+            jnp.concatenate([inputs_t if j == k else zero for k in range(group)], axis=1)
+            for j in range(group)
+        ],
+        axis=0,
+    )
+    rows = []
+    for i in range(own // group):
+        rows.append(
+            jnp.concatenate(
+                [weights * summed[group * i + j : group * i + j + 1, :] for j in range(group)],
+                axis=1,
+            )
+        )
+    left = jnp.concatenate(rows, axis=0)
+    count = left.shape[0]
+    out_ref[:count, :] = dot_nt(left, right)
     out_ref[count:, :] = asked_ref[...]
 
 

time: 26.6 us -> 26.6 us (level)
  no operation moved by 1% of the time
where the time goes in v13:
time: 26.6 us; the launch traced here: 26.4 us
  waiting for transfers between devices  11.3 us (42%)
  starting transfers between devices  9.99 us (38%)
  Pallas kernels  4.87 us (18%)
    ppermute x8, waiting for transfers between devices, from_partner(): return lax.ppermute(value, axis, [(i, i ^ m) for i in range(size)])  11.3 us
    ppermute x8, starting transfers between devices, from_partner(): return lax.ppermute(value, axis, [(i, i ^ m) for i in range(size)])  9.99 us
    pallas_call x1, Pallas kernels, project(): pl.pallas_call(functools.partial(project_kernel, own), out_shape=[jax.Sha...  2.19 us
    pallas_call x1, Pallas kernels, solve(): pl.pallas_call(functools.partial(solve_kernel, seqs), out_shape=jax.Shape...  1.82 us
  transfers between devices with their start and end apart: 8, of which 6 were waited for; matrix products, arithmetic and copies ran while one was open for 1% of the time, Pallas kernels for 1%

profile of v13, /device:TPU:0, one launch (start us, length us, event | category | flops | bytes accessed | tf_op | source)
XLA Modules:
  0.0 26.4 jit_solution(3993849945419914260)
XLA Ops:
  0.0 2.2 %project.1 = (f32[96,256]{1,0:T(8,128)S(1)}, f32[96,256]{1,0:T(8,128)S(1)}) custom-call(s32[1]{0:T(128)} %bitcast.1.rank_ref, bf16[2752,256]{1,0:T(8,128)(2,1)} %bitcast.5, bf16[256,1024]{1,0:T(8,128)(2,1)} %g_hbm.1, bf16[64,2752]{1,0:T(8,128)(2,1)} %bitcast.6, bf16[64,1024]{1,0:T(8,128)(2,1)} %bitcast.7), custom_call_target="tpu_custom_call" | custom-call | tf_op jit(solution)/shard_map/project/pallas_call | solution.py:108
  2.2 0.5 %collective-permute-start = (f32[96,256]{1,0:T(8,128)S(1)}, f32[96,256]{1,0:T(8,128)S(1)}, u32[]{:S(2)}, u32[]{:S(2)}) collective-permute-start(f32[96,256]{1,0:T(8,128)S(1)} %get-tuple-element.10), channel_id=1, source_target_pairs={{0,1},{1,0},{2,3},{3,2},{4,5},{5,4},{6,7},{7,6},{8,9},{9,8},{10,11... | collective-permute-start | bytes 294920 | tf_op jit(solution)/shard_map/ppermute | solution.py:317
  2.7 0.0 copy-done.2
  2.8 0.1 convert_reduce_fusion
  2.9 0.8 %collective-permute-done.came_ref = f32[96,256]{1,0:T(8,128)S(1)} collective-permute-done((f32[96,256]{1,0:T(8,128)S(1)}, f32[96,256]{1,0:T(8,128)S(1)}, u32[]{:S(2)}, u32[]{:S(2)}) %collective-permute-start) | collective-permute-done | bytes 98336 | tf_op jit(solution)/shard_map/ppermute | solution.py:317
  3.7 2.9 %collective-permute-start.1 = (f32[64,256]{1,0:T(8,128)S(1)}, f32[64,256]{1,0:T(8,128)S(1)}, u32[]{:S(2)}, u32[]{:S(2)}) collective-permute-start(f32[64,256]{1,0:T(8,128)S(1)} %get-tuple-element.12), channel_id=1, source_target_pairs={{0,2},{1,3},{2,0},{3,1},{4,6},{5,7},{6,4},{7,5},{8,10},{9,11},{10,... | collective-permute-start | bytes 196616 | tf_op jit(solution)/shard_map/ppermute | solution.py:317
  6.6 0.1 fusion.1.weights_ref
  6.7 0.2 pick.1.asked_ref
  6.8 2.2 %collective-permute-done.1.came_ref = f32[64,256]{1,0:T(8,128)S(1)} collective-permute-done((f32[64,256]{1,0:T(8,128)S(1)}, f32[64,256]{1,0:T(8,128)S(1)}, u32[]{:S(2)}, u32[]{:S(2)}) %collective-permute-start.1) | collective-permute-done | bytes 65568 | tf_op jit(solution)/shard_map/ppermute | solution.py:317
  9.0 0.4 %gradients.1.refs_3_ = f32[160,128]{1,0:T(8,128)S(1)} custom-call(f32[16,256]{1,0:T(8,128)S(1)} %fusion.1.weights_ref, f32[64,256]{1,0:T(8,128)S(1)} %get-tuple-element.11.kept_ref, f32[64,256]{1,0:T(8,128)S(1)} %collective-permute-done.1.came_ref, f32[32,128]{1,0:T(8,128)S(1)} %pick.1.asked_ref), custom_call_target="tpu_custom_call" | custom-call | tf_op jit(solution)/shard_map/gradients/pallas_call | solution.py:222
  9.4 4.0 %collective-permute-start.2 = (f32[160,128]{1,0:T(8,128)S(1)}, f32[160,128]{1,0:T(8,128)S(1)}, u32[]{:S(2)}, u32[]{:S(2)}) collective-permute-start(f32[160,128]{1,0:T(8,128)S(1)} %gradients.1.refs_3_), channel_id=1, source_target_pairs={{0,12},{4,8},{8,4},{12,0},{1,13},{5,9},{9,5},{13,1},{2,14},{6,10},... | collective-permute-start | bytes 245768 | tf_op jit(solution)/shard_map/ppermute | solution.py:317
  13.4 0.0 collective-permute-start.3
  13.4 0.6 %collective-permute-start.4 = (f32[160,128]{1,0:T(8,128)S(1)}, f32[160,128]{1,0:T(8,128)S(1)}, u32[]{:S(2)}, u32[]{:S(2)}) collective-permute-start(f32[160,128]{1,0:T(8,128)S(1)} %gradients.1.refs_3_), channel_id=1, source_target_pairs={{0,4},{4,0},{8,12},{12,8},{1,5},{5,1},{9,13},{13,9},{2,6},{6,2},{1... | collective-permute-start | bytes 245768 | tf_op jit(solution)/shard_map/ppermute | solution.py:317
  14.1 2.4 %collective-permute-done.2.refs_0_ = f32[160,128]{1,0:T(8,128)S(1)} collective-permute-done((f32[160,128]{1,0:T(8,128)S(1)}, f32[160,128]{1,0:T(8,128)S(1)}, u32[]{:S(2)}, u32[]{:S(2)}) %collective-permute-start.2) | collective-permute-done | bytes 81952 | tf_op jit(solution)/shard_map/ppermute | solution.py:317
  16.5 3.2 %collective-permute-done.3.refs_1_ = f32[160,128]{1,0:T(8,128)S(1)} collective-permute-done((f32[160,128]{1,0:T(8,128)S(1)}, f32[160,128]{1,0:T(8,128)S(1)}, u32[]{:S(2)}, u32[]{:S(2)}) %collective-permute-start.3) | collective-permute-done | bytes 81952 | tf_op jit(solution)/shard_map/ppermute | solution.py:317
  19.7 0.0 collective-permute-done.4.refs_2_
  19.7 0.3 %grams.1.refs_3_ = f32[40,128]{1,0:T(8,128)S(1)} custom-call(s32[1]{0:T(128)} %bitcast.me_ref, f32[160,128]{1,0:T(8,128)S(1)} %collective-permute-done.2.refs_0_, f32[160,128]{1,0:T(8,128)S(1)} %collective-permute-done.3.refs_1_, f32[160,128]{1,0:T(8,128)S(1)} %collective-permute-done.4.refs_2_, f32[160,128]{1,0:T(8,128)S(1)} %gradients.1.refs_3_), custom_call_target="tpu_custom_call" | custom-call | tf_op jit(solution)/shard_map/grams/pallas_call | solution.py:256
  20.0 0.6 %collective-permute-start.5 = (f32[40,128]{1,0:T(8,128)S(1)}, f32[40,128]{1,0:T(8,128)S(1)}, u32[]{:S(2)}, u32[]{:S(2)}) collective-permute-start(f32[40,128]{1,0:T(8,128)S(1)} %grams.1.refs_3_), channel_id=1, source_target_pairs={{0,3},{1,2},{2,1},{3,0},{4,7},{5,6},{6,5},{7,4},{8,11},{9,10},{10,... | collective-permute-start | bytes 61448 | tf_op jit(solution)/shard_map/ppermute | solution.py:317
  20.6 1.0 %collective-permute-start.6 = (f32[40,128]{1,0:T(8,128)S(1)}, f32[40,128]{1,0:T(8,128)S(1)}, u32[]{:S(2)}, u32[]{:S(2)}) collective-permute-start(f32[40,128]{1,0:T(8,128)S(1)} %grams.1.refs_3_), channel_id=1, source_target_pairs={{0,2},{1,3},{2,0},{3,1},{4,6},{5,7},{6,4},{7,5},{8,10},{9,11},{10,... | collective-permute-start | bytes 61448 | tf_op jit(solution)/shard_map/ppermute | solution.py:317
  21.6 0.3 %collective-permute-start.7 = (f32[40,128]{1,0:T(8,128)S(1)}, f32[40,128]{1,0:T(8,128)S(1)}, u32[]{:S(2)}, u32[]{:S(2)}) collective-permute-start(f32[40,128]{1,0:T(8,128)S(1)} %grams.1.refs_3_), channel_id=1, source_target_pairs={{0,1},{1,0},{2,3},{3,2},{4,5},{5,4},{6,7},{7,6},{8,9},{9,8},{10,11... | collective-permute-start | bytes 61448 | tf_op jit(solution)/shard_map/ppermute | solution.py:317
  21.9 1.5 %collective-permute-done.5.refs_0_ = f32[40,128]{1,0:T(8,128)S(1)} collective-permute-done((f32[40,128]{1,0:T(8,128)S(1)}, f32[40,128]{1,0:T(8,128)S(1)}, u32[]{:S(2)}, u32[]{:S(2)}) %collective-permute-start.5) | collective-permute-done | bytes 20512 | tf_op jit(solution)/shard_map/ppermute | solution.py:317
  23.4 1.2 %collective-permute-done.6.refs_1_ = f32[40,128]{1,0:T(8,128)S(1)} collective-permute-done((f32[40,128]{1,0:T(8,128)S(1)}, f32[40,128]{1,0:T(8,128)S(1)}, u32[]{:S(2)}, u32[]{:S(2)}) %collective-permute-start.6) | collective-permute-done | bytes 20512 | tf_op jit(solution)/shard_map/ppermute | solution.py:317
  24.6 0.0 collective-permute-done.7.refs_2_
  24.6 1.8 %solve.1 = f32[16,16]{1,0:T(8,128)} custom-call(f32[40,128]{1,0:T(8,128)S(1)} %collective-permute-done.5.refs_0_, f32[40,128]{1,0:T(8,128)S(1)} %collective-permute-done.6.refs_1_, f32[40,128]{1,0:T(8,128)S(1)} %collective-permute-done.7.refs_2_, f32[40,128]{1,0:T(8,128)S(1)} %grams.1.refs_3_), custom_call_target="tpu_custom_call" | custom-call | tf_op jit(solution)/shard_map/solve/pallas_call | solution.py:308
  (8 shorter events, 0.0 us)
Async XLA Ops:
  0.0 2.7 %copy-start.2 = (s32[16]{0:T(128)S(1)}, s32[16]{0:T(128)}, u32[]{:S(2)}) copy-start(s32[16]{0:T(128)} %param.12) | copy-start | bytes 196
  0.0 2.8 %copy-start.1 = (s32[256]{0:T(256)S(1)}, s32[256]{0:T(256)}, u32[]{:S(2)}) copy-start(s32[256]{0:T(256)} %param.11) | copy-start | bytes 3076
  0.0 6.7 %copy-start = (f32[4,4096]{1,0:T(4,128)S(1)}, f32[4,4096]{1,0:T(4,128)}, u32[]{:S(2)}) copy-start(f32[4,4096]{1,0:T(4,128)} %queries_ref.1) | copy-start | bytes 196612
  2.2 1.5 %collective-permute-start = (f32[96,256]{1,0:T(8,128)S(1)}, f32[96,256]{1,0:T(8,128)S(1)}, u32[]{:S(2)}, u32[]{:S(2)}) collective-permute-start(f32[96,256]{1,0:T(8,128)S(1)} %get-tuple-element.10), channel_id=1, source_target_pairs={{0,1},{1,0},{2,3},{3,2},{4,5},{5,4},{6,7},{7,6},{8,9},{9,8},{10,11... | collective-permute-start | bytes 294920 | tf_op jit(solution)/shard_map/ppermute | solution.py:317
  3.7 5.3 %collective-permute-start.1 = (f32[64,256]{1,0:T(8,128)S(1)}, f32[64,256]{1,0:T(8,128)S(1)}, u32[]{:S(2)}, u32[]{:S(2)}) collective-permute-start(f32[64,256]{1,0:T(8,128)S(1)} %get-tuple-element.12), channel_id=1, source_target_pairs={{0,2},{1,3},{2,0},{3,1},{4,6},{5,7},{6,4},{7,5},{8,10},{9,11},{10,... | collective-permute-start | bytes 196616 | tf_op jit(solution)/shard_map/ppermute | solution.py:317
  9.4 7.1 %collective-permute-start.2 = (f32[160,128]{1,0:T(8,128)S(1)}, f32[160,128]{1,0:T(8,128)S(1)}, u32[]{:S(2)}, u32[]{:S(2)}) collective-permute-start(f32[160,128]{1,0:T(8,128)S(1)} %gradients.1.refs_3_), channel_id=1, source_target_pairs={{0,12},{4,8},{8,4},{12,0},{1,13},{5,9},{9,5},{13,1},{2,14},{6,10},... | collective-permute-start | bytes 245768 | tf_op jit(solution)/shard_map/ppermute | solution.py:317
  13.4 6.2 %collective-permute-start.3 = (f32[160,128]{1,0:T(8,128)S(1)}, f32[160,128]{1,0:T(8,128)S(1)}, u32[]{:S(2)}, u32[]{:S(2)}) collective-permute-start(f32[160,128]{1,0:T(8,128)S(1)} %gradients.1.refs_3_), channel_id=1, source_target_pairs={{0,8},{4,12},{8,0},{12,4},{1,9},{5,13},{9,1},{13,5},{2,10},{6,14},... | collective-permute-start | bytes 245768 | tf_op jit(solution)/shard_map/ppermute | solution.py:317
  13.4 6.2 %collective-permute-start.4 = (f32[160,128]{1,0:T(8,128)S(1)}, f32[160,128]{1,0:T(8,128)S(1)}, u32[]{:S(2)}, u32[]{:S(2)}) collective-permute-start(f32[160,128]{1,0:T(8,128)S(1)} %gradients.1.refs_3_), channel_id=1, source_target_pairs={{0,4},{4,0},{8,12},{12,8},{1,5},{5,1},{9,13},{13,9},{2,6},{6,2},{1... | collective-permute-start | bytes 245768 | tf_op jit(solution)/shard_map/ppermute | solution.py:317
  20.0 3.4 %collective-permute-start.5 = (f32[40,128]{1,0:T(8,128)S(1)}, f32[40,128]{1,0:T(8,128)S(1)}, u32[]{:S(2)}, u32[]{:S(2)}) collective-permute-start(f32[40,128]{1,0:T(8,128)S(1)} %grams.1.refs_3_), channel_id=1, source_target_pairs={{0,3},{1,2},{2,1},{3,0},{4,7},{5,6},{6,5},{7,4},{8,11},{9,10},{10,... | collective-permute-start | bytes 61448 | tf_op jit(solution)/shard_map/ppermute | solution.py:317
  20.6 4.0 %collective-permute-start.6 = (f32[40,128]{1,0:T(8,128)S(1)}, f32[40,128]{1,0:T(8,128)S(1)}, u32[]{:S(2)}, u32[]{:S(2)}) collective-permute-start(f32[40,128]{1,0:T(8,128)S(1)} %grams.1.refs_3_), channel_id=1, source_target_pairs={{0,2},{1,3},{2,0},{3,1},{4,6},{5,7},{6,4},{7,5},{8,10},{9,11},{10,... | collective-permute-start | bytes 61448 | tf_op jit(solution)/shard_map/ppermute | solution.py:317
  21.6 3.0 %collective-permute-start.7 = (f32[40,128]{1,0:T(8,128)S(1)}, f32[40,128]{1,0:T(8,128)S(1)}, u32[]{:S(2)}, u32[]{:S(2)}) collective-permute-start(f32[40,128]{1,0:T(8,128)S(1)} %grams.1.refs_3_), channel_id=1, source_target_pairs={{0,1},{1,0},{2,3},{3,2},{4,5},{5,4},{6,7},{7,6},{8,9},{9,8},{10,11... | collective-permute-start | bytes 61448 | tf_op jit(solution)/shard_map/ppermute | solution.py:317

commit v14 on v13

--- a/solution.py
+++ b/solution.py
@@ -236,7 +236,8 @@
     for place in range(len(blocks)):
         chosen = given[0]
         for m in range(1, len(blocks)):
-            chosen = jnp.where((me_ref[0] ^ place) == m, given[m], chosen)
+            ahead = lax.rem(place - me_ref[0] + len(blocks), len(blocks))
+            chosen = jnp.where(ahead == m, given[m], chosen)
         ordered.append(chosen)
     lanes = []
     for i in range(steps):
@@ -321,6 +322,11 @@
     return [from_partner(value, axis, size, m) for m in reversed(range(1, size))] + [value]
 
 
+def from_all(value, axis, size):
+    shifts = [[(i, (i + s) % size) for i in range(size)] for s in range(1, size)]
+    return [lax.ppermute(value, axis, shift) for shift in shifts] + [value]
+
+
 def finish_long(message, steps, first, seq_dev):
     every = lax.all_gather(message, "dp", axis=0)
     lanes = message.shape[1]
@@ -365,7 +371,7 @@
     steps = own * own // message.shape[1]
     if blocks > SMALL:
         return finish_long(message, steps, first, seq_dev)
-    partial = grams(place.reshape(1), from_partners(message, "dp", blocks), steps, seq_dev)
+    partial = grams(place.reshape(1), from_all(message, "dp", blocks), steps, seq_dev)
     partial = from_partners(partial, "tensor", parts)
     return solve(partial, blocks * seq_dev, blocks * queries.shape[0], seq_dev)
 

time: 26.6 us -> 25.3 us (0.951)
  waiting for transfers between devices: 11.3 us -> 8.79 us
  starting transfers between devices: 9.99 us -> 11.2 us
    ppermute x8 -> x5, waiting for transfers between devices: 11.3 us -> 4.99 us  [from_partner(): return lax.ppermute(value, axis, [(i, i ^ m) for i in range(size)])]
    ppermute x0 -> x3, starting transfers between devices: none -> 5.93 us  [from_all(): return [lax.ppermute(value, axis, shift) for shift in shifts] + [value]]
    ppermute x8 -> x5, starting transfers between devices: 9.99 us -> 5.31 us  [from_partner(): return lax.ppermute(value, axis, [(i, i ^ m) for i in range(size)])]
    ppermute x0 -> x3, waiting for transfers between devices: none -> 3.8 us  [from_all(): return [lax.ppermute(value, axis, shift) for shift in shifts] + [value]]
  transfers between devices with their start and end apart: 8 -> 8, of which waited for: 6 -> 7; matrix products, arithmetic and copies ran while one was open for 1% -> 1% of each run, Pallas kernels for 1% -> 1%
where the time goes in v14:
time: 25.3 us; the launch traced here: 25.2 us
  starting transfers between devices  11.2 us (44%)
  waiting for transfers between devices  8.79 us (35%)
  Pallas kernels  4.88 us (19%)
    ppermute x3, starting transfers between devices, from_all(): return [lax.ppermute(value, axis, shift) for shift in shifts] + [value]  5.93 us
    ppermute x5, starting transfers between devices, from_partner(): return lax.ppermute(value, axis, [(i, i ^ m) for i in range(size)])  5.31 us
    ppermute x5, waiting for transfers between devices, from_partner(): return lax.ppermute(value, axis, [(i, i ^ m) for i in range(size)])  4.99 us
    ppermute x3, waiting for transfers between devices, from_all(): return [lax.ppermute(value, axis, shift) for shift in shifts] + [value]  3.8 us
    pallas_call x1, Pallas kernels, project(): pl.pallas_call(functools.partial(project_kernel, own), out_shape=[jax.Sha...  2.19 us
    pallas_call x1, Pallas kernels, solve(): pl.pallas_call(functools.partial(solve_kernel, seqs), out_shape=jax.Shape...  1.82 us
  transfers between devices with their start and end apart: 8, of which 7 were waited for; matrix products, arithmetic and copies ran while one was open for 1% of the time, Pallas kernels for 1%

profile of v14, /device:TPU:0, one launch (start us, length us, event | category | flops | bytes accessed | tf_op | source)
XLA Modules:
  0.0 25.2 jit_solution(13916765034208615564)
XLA Ops:
  0.0 2.2 %project.1 = (f32[96,256]{1,0:T(8,128)S(1)}, f32[96,256]{1,0:T(8,128)S(1)}) custom-call(s32[1]{0:T(128)} %bitcast.1.rank_ref, bf16[2752,256]{1,0:T(8,128)(2,1)} %bitcast.5, bf16[256,1024]{1,0:T(8,128)(2,1)} %g_hbm.1, bf16[64,2752]{1,0:T(8,128)(2,1)} %bitcast.6, bf16[64,1024]{1,0:T(8,128)(2,1)} %bitcast.7), custom_call_target="tpu_custom_call" | custom-call | tf_op jit(solution)/shard_map/project/pallas_call | solution.py:108
  2.2 0.5 %collective-permute-start = (f32[96,256]{1,0:T(8,128)S(1)}, f32[96,256]{1,0:T(8,128)S(1)}, u32[]{:S(2)}, u32[]{:S(2)}) collective-permute-start(f32[96,256]{1,0:T(8,128)S(1)} %get-tuple-element.10), channel_id=1, source_target_pairs={{0,1},{1,0},{2,3},{3,2},{4,5},{5,4},{6,7},{7,6},{8,9},{9,8},{10,11... | collective-permute-start | bytes 294920 | tf_op jit(solution)/shard_map/ppermute | solution.py:318
  2.7 0.0 copy-done.2
  2.8 0.1 convert_reduce_fusion
  2.9 0.8 %collective-permute-done.came_ref = f32[96,256]{1,0:T(8,128)S(1)} collective-permute-done((f32[96,256]{1,0:T(8,128)S(1)}, f32[96,256]{1,0:T(8,128)S(1)}, u32[]{:S(2)}, u32[]{:S(2)}) %collective-permute-start) | collective-permute-done | bytes 98336 | tf_op jit(solution)/shard_map/ppermute | solution.py:318
  3.7 2.9 %collective-permute-start.1 = (f32[64,256]{1,0:T(8,128)S(1)}, f32[64,256]{1,0:T(8,128)S(1)}, u32[]{:S(2)}, u32[]{:S(2)}) collective-permute-start(f32[64,256]{1,0:T(8,128)S(1)} %get-tuple-element.12), channel_id=1, source_target_pairs={{0,2},{1,3},{2,0},{3,1},{4,6},{5,7},{6,4},{7,5},{8,10},{9,11},{10,... | collective-permute-start | bytes 196616 | tf_op jit(solution)/shard_map/ppermute | solution.py:318
  6.6 0.1 fusion.1.weights_ref
  6.7 0.2 pick.1.asked_ref
  6.8 2.2 %collective-permute-done.1.came_ref = f32[64,256]{1,0:T(8,128)S(1)} collective-permute-done((f32[64,256]{1,0:T(8,128)S(1)}, f32[64,256]{1,0:T(8,128)S(1)}, u32[]{:S(2)}, u32[]{:S(2)}) %collective-permute-start.1) | collective-permute-done | bytes 65568 | tf_op jit(solution)/shard_map/ppermute | solution.py:318
  9.0 0.4 %gradients.1.refs_3_ = f32[160,128]{1,0:T(8,128)S(1)} custom-call(f32[16,256]{1,0:T(8,128)S(1)} %fusion.1.weights_ref, f32[64,256]{1,0:T(8,128)S(1)} %get-tuple-element.11.kept_ref, f32[64,256]{1,0:T(8,128)S(1)} %collective-permute-done.1.came_ref, f32[32,128]{1,0:T(8,128)S(1)} %pick.1.asked_ref), custom_call_target="tpu_custom_call" | custom-call | tf_op jit(solution)/shard_map/gradients/pallas_call | solution.py:222
  9.4 2.0 %collective-permute-start.2 = (f32[160,128]{1,0:T(8,128)S(1)}, f32[160,128]{1,0:T(8,128)S(1)}, u32[]{:S(2)}, u32[]{:S(2)}) collective-permute-start(f32[160,128]{1,0:T(8,128)S(1)} %gradients.1.refs_3_), channel_id=1, source_target_pairs={{0,4},{4,8},{8,12},{12,0},{1,5},{5,9},{9,13},{13,1},{2,6},{6,10},{... | collective-permute-start | bytes 245768 | tf_op jit(solution)/shard_map/ppermute | solution.py:327
  11.4 2.6 %collective-permute-start.3 = (f32[160,128]{1,0:T(8,128)S(1)}, f32[160,128]{1,0:T(8,128)S(1)}, u32[]{:S(2)}, u32[]{:S(2)}) collective-permute-start(f32[160,128]{1,0:T(8,128)S(1)} %gradients.1.refs_3_), channel_id=1, source_target_pairs={{0,8},{4,12},{8,0},{12,4},{1,9},{5,13},{9,1},{13,5},{2,10},{6,14},... | collective-permute-start | bytes 245768 | tf_op jit(solution)/shard_map/ppermute | solution.py:327
  14.0 1.3 %collective-permute-start.4 = (f32[160,128]{1,0:T(8,128)S(1)}, f32[160,128]{1,0:T(8,128)S(1)}, u32[]{:S(2)}, u32[]{:S(2)}) collective-permute-start(f32[160,128]{1,0:T(8,128)S(1)} %gradients.1.refs_3_), channel_id=1, source_target_pairs={{0,12},{4,0},{8,4},{12,8},{1,13},{5,1},{9,5},{13,9},{2,14},{6,2},{... | collective-permute-start | bytes 245768 | tf_op jit(solution)/shard_map/ppermute | solution.py:327
  15.3 1.5 %collective-permute-done.2.refs_0_ = f32[160,128]{1,0:T(8,128)S(1)} collective-permute-done((f32[160,128]{1,0:T(8,128)S(1)}, f32[160,128]{1,0:T(8,128)S(1)}, u32[]{:S(2)}, u32[]{:S(2)}) %collective-permute-start.2) | collective-permute-done | bytes 81952 | tf_op jit(solution)/shard_map/ppermute | solution.py:327
  16.8 2.2 %collective-permute-done.3.refs_1_ = f32[160,128]{1,0:T(8,128)S(1)} collective-permute-done((f32[160,128]{1,0:T(8,128)S(1)}, f32[160,128]{1,0:T(8,128)S(1)}, u32[]{:S(2)}, u32[]{:S(2)}) %collective-permute-start.3) | collective-permute-done | bytes 81952 | tf_op jit(solution)/shard_map/ppermute | solution.py:327
  19.0 0.1 collective-permute-done.4.refs_2_
  19.1 0.3 %grams.1.refs_3_ = f32[40,128]{1,0:T(8,128)S(1)} custom-call(s32[1]{0:T(128)} %bitcast.me_ref, f32[160,128]{1,0:T(8,128)S(1)} %collective-permute-done.2.refs_0_, f32[160,128]{1,0:T(8,128)S(1)} %collective-permute-done.3.refs_1_, f32[160,128]{1,0:T(8,128)S(1)} %collective-permute-done.4.refs_2_, f32[160,128]{1,0:T(8,128)S(1)} %gradients.1.refs_3_), custom_call_target="tpu_custom_call" | custom-call | tf_op jit(solution)/shard_map/grams/pallas_call | solution.py:257
  19.5 0.0 collective-permute-start.5
  19.5 1.5 %collective-permute-start.6 = (f32[40,128]{1,0:T(8,128)S(1)}, f32[40,128]{1,0:T(8,128)S(1)}, u32[]{:S(2)}, u32[]{:S(2)}) collective-permute-start(f32[40,128]{1,0:T(8,128)S(1)} %grams.1.refs_3_), channel_id=1, source_target_pairs={{0,2},{1,3},{2,0},{3,1},{4,6},{5,7},{6,4},{7,5},{8,10},{9,11},{10,... | collective-permute-start | bytes 61448 | tf_op jit(solution)/shard_map/ppermute | solution.py:318
  21.0 0.3 %collective-permute-start.7 = (f32[40,128]{1,0:T(8,128)S(1)}, f32[40,128]{1,0:T(8,128)S(1)}, u32[]{:S(2)}, u32[]{:S(2)}) collective-permute-start(f32[40,128]{1,0:T(8,128)S(1)} %grams.1.refs_3_), channel_id=1, source_target_pairs={{0,1},{1,0},{2,3},{3,2},{4,5},{5,4},{6,7},{7,6},{8,9},{9,8},{10,11... | collective-permute-start | bytes 61448 | tf_op jit(solution)/shard_map/ppermute | solution.py:318
  21.3 1.6 %collective-permute-done.5.refs_0_ = f32[40,128]{1,0:T(8,128)S(1)} collective-permute-done((f32[40,128]{1,0:T(8,128)S(1)}, f32[40,128]{1,0:T(8,128)S(1)}, u32[]{:S(2)}, u32[]{:S(2)}) %collective-permute-start.5) | collective-permute-done | bytes 20512 | tf_op jit(solution)/shard_map/ppermute | solution.py:318
  22.9 0.4 %collective-permute-done.6.refs_1_ = f32[40,128]{1,0:T(8,128)S(1)} collective-permute-done((f32[40,128]{1,0:T(8,128)S(1)}, f32[40,128]{1,0:T(8,128)S(1)}, u32[]{:S(2)}, u32[]{:S(2)}) %collective-permute-start.6) | collective-permute-done | bytes 20512 | tf_op jit(solution)/shard_map/ppermute | solution.py:318
  23.3 0.0 collective-permute-done.7.refs_2_
  23.3 1.8 %solve.1 = f32[16,16]{1,0:T(8,128)} custom-call(f32[40,128]{1,0:T(8,128)S(1)} %collective-permute-done.5.refs_0_, f32[40,128]{1,0:T(8,128)S(1)} %collective-permute-done.6.refs_1_, f32[40,128]{1,0:T(8,128)S(1)} %collective-permute-done.7.refs_2_, f32[40,128]{1,0:T(8,128)S(1)} %grams.1.refs_3_), custom_call_target="tpu_custom_call" | custom-call | tf_op jit(solution)/shard_map/solve/pallas_call | solution.py:309
  (8 shorter events, 0.0 us)
Async XLA Ops:
  0.0 2.7 %copy-start.2 = (s32[16]{0:T(128)S(1)}, s32[16]{0:T(128)}, u32[]{:S(2)}) copy-start(s32[16]{0:T(128)} %param.12) | copy-start | bytes 196
  0.0 2.8 %copy-start.1 = (s32[256]{0:T(256)S(1)}, s32[256]{0:T(256)}, u32[]{:S(2)}) copy-start(s32[256]{0:T(256)} %param.11) | copy-start | bytes 3076
  0.0 6.7 %copy-start = (f32[4,4096]{1,0:T(4,128)S(1)}, f32[4,4096]{1,0:T(4,128)}, u32[]{:S(2)}) copy-start(f32[4,4096]{1,0:T(4,128)} %queries_ref.1) | copy-start | bytes 196612
  2.2 1.5 %collective-permute-start = (f32[96,256]{1,0:T(8,128)S(1)}, f32[96,256]{1,0:T(8,128)S(1)}, u32[]{:S(2)}, u32[]{:S(2)}) collective-permute-start(f32[96,256]{1,0:T(8,128)S(1)} %get-tuple-element.10), channel_id=1, source_target_pairs={{0,1},{1,0},{2,3},{3,2},{4,5},{5,4},{6,7},{7,6},{8,9},{9,8},{10,11... | collective-permute-start | bytes 294920 | tf_op jit(solution)/shard_map/ppermute | solution.py:318
  3.7 5.3 %collective-permute-start.1 = (f32[64,256]{1,0:T(8,128)S(1)}, f32[64,256]{1,0:T(8,128)S(1)}, u32[]{:S(2)}, u32[]{:S(2)}) collective-permute-start(f32[64,256]{1,0:T(8,128)S(1)} %get-tuple-element.12), channel_id=1, source_target_pairs={{0,2},{1,3},{2,0},{3,1},{4,6},{5,7},{6,4},{7,5},{8,10},{9,11},{10,... | collective-permute-start | bytes 196616 | tf_op jit(solution)/shard_map/ppermute | solution.py:318
  9.4 7.4 %collective-permute-start.2 = (f32[160,128]{1,0:T(8,128)S(1)}, f32[160,128]{1,0:T(8,128)S(1)}, u32[]{:S(2)}, u32[]{:S(2)}) collective-permute-start(f32[160,128]{1,0:T(8,128)S(1)} %gradients.1.refs_3_), channel_id=1, source_target_pairs={{0,4},{4,8},{8,12},{12,0},{1,5},{5,9},{9,13},{13,1},{2,6},{6,10},{... | collective-permute-start | bytes 245768 | tf_op jit(solution)/shard_map/ppermute | solution.py:327
  11.4 7.6 %collective-permute-start.3 = (f32[160,128]{1,0:T(8,128)S(1)}, f32[160,128]{1,0:T(8,128)S(1)}, u32[]{:S(2)}, u32[]{:S(2)}) collective-permute-start(f32[160,128]{1,0:T(8,128)S(1)} %gradients.1.refs_3_), channel_id=1, source_target_pairs={{0,8},{4,12},{8,0},{12,4},{1,9},{5,13},{9,1},{13,5},{2,10},{6,14},... | collective-permute-start | bytes 245768 | tf_op jit(solution)/shard_map/ppermute | solution.py:327
  14.0 5.1 %collective-permute-start.4 = (f32[160,128]{1,0:T(8,128)S(1)}, f32[160,128]{1,0:T(8,128)S(1)}, u32[]{:S(2)}, u32[]{:S(2)}) collective-permute-start(f32[160,128]{1,0:T(8,128)S(1)} %gradients.1.refs_3_), channel_id=1, source_target_pairs={{0,12},{4,0},{8,4},{12,8},{1,13},{5,1},{9,5},{13,9},{2,14},{6,2},{... | collective-permute-start | bytes 245768 | tf_op jit(solution)/shard_map/ppermute | solution.py:327
  19.5 3.4 %collective-permute-start.5 = (f32[40,128]{1,0:T(8,128)S(1)}, f32[40,128]{1,0:T(8,128)S(1)}, u32[]{:S(2)}, u32[]{:S(2)}) collective-permute-start(f32[40,128]{1,0:T(8,128)S(1)} %grams.1.refs_3_), channel_id=1, source_target_pairs={{0,3},{1,2},{2,1},{3,0},{4,7},{5,6},{6,5},{7,4},{8,11},{9,10},{10,... | collective-permute-start | bytes 61448 | tf_op jit(solution)/shard_map/ppermute | solution.py:318
  19.5 3.8 %collective-permute-start.6 = (f32[40,128]{1,0:T(8,128)S(1)}, f32[40,128]{1,0:T(8,128)S(1)}, u32[]{:S(2)}, u32[]{:S(2)}) collective-permute-start(f32[40,128]{1,0:T(8,128)S(1)} %grams.1.refs_3_), channel_id=1, source_target_pairs={{0,2},{1,3},{2,0},{3,1},{4,6},{5,7},{6,4},{7,5},{8,10},{9,11},{10,... | collective-permute-start | bytes 61448 | tf_op jit(solution)/shard_map/ppermute | solution.py:318
  21.0 2.3 %collective-permute-start.7 = (f32[40,128]{1,0:T(8,128)S(1)}, f32[40,128]{1,0:T(8,128)S(1)}, u32[]{:S(2)}, u32[]{:S(2)}) collective-permute-start(f32[40,128]{1,0:T(8,128)S(1)} %grams.1.refs_3_), channel_id=1, source_target_pairs={{0,1},{1,0},{2,3},{3,2},{4,5},{5,4},{6,7},{7,6},{8,9},{9,8},{10,11... | collective-permute-start | bytes 61448 | tf_op jit(solution)/shard_map/ppermute | solution.py:318

commit v15 on v14

--- a/solution.py
+++ b/solution.py
@@ -10,6 +10,7 @@
 damping = 0.5
 VMEM_LIMIT = 32 * 1024 * 1024
 SMALL = 4
+SHIFTS = {1: (), 2: (1,), 4: (2, 1, 3)}
 
 
 def token_weights(seq_ids, counts, first):
@@ -228,7 +229,9 @@
 
 
 def grams_kernel(steps, seqs, me_ref, *refs):
-    blocks, out_ref = refs[-2::-1], refs[-1]
+    blocks, out_ref = refs[:-1], refs[-1]
+    shifts = (*SHIFTS[len(blocks)], 0)
+    blocks = [blocks[shifts.index(-m % len(blocks))] for m in range(len(blocks))]
     count = steps * seqs
     asked = (blocks[0].shape[0] - count) // steps
     given = [block[count:, :] for block in blocks]
@@ -323,7 +326,7 @@
 
 
 def from_all(value, axis, size):
-    shifts = [[(i, (i + s) % size) for i in range(size)] for s in range(1, size)]
+    shifts = [[(i, (i + s) % size) for i in range(size)] for s in SHIFTS[size]]
     return [lax.ppermute(value, axis, shift) for shift in shifts] + [value]
 
 

time: 25.3 us -> 25.5 us (level)
  starting transfers between devices: 11.2 us -> 12.1 us
  waiting for transfers between devices: 8.79 us -> 8.06 us
    ppermute x3, starting transfers between devices: 5.93 us -> 6.84 us  [from_all(): return [lax.ppermute(value, axis, shift) for shift in shifts] + [value]]
    ppermute x3, waiting for transfers between devices: 3.8 us -> 3.07 us  [from_all(): return [lax.ppermute(value, axis, shift) for shift in shifts] + [value]]
where the time goes in v15:
time: 25.5 us; the launch traced here: 25.3 us
  starting transfers between devices  12.1 us (47%)
  waiting for transfers between devices  8.06 us (32%)
  Pallas kernels  4.88 us (19%)
    ppermute x3, starting transfers between devices, from_all(): return [lax.ppermute(value, axis, shift) for shift in shifts] + [value]  6.84 us
    ppermute x5, starting transfers between devices, from_partner(): return lax.ppermute(value, axis, [(i, i ^ m) for i in range(size)])  5.31 us
    ppermute x5, waiting for transfers between devices, from_partner(): return lax.ppermute(value, axis, [(i, i ^ m) for i in range(size)])  4.99 us
    ppermute x3, waiting for transfers between devices, from_all(): return [lax.ppermute(value, axis, shift) for shift in shifts] + [value]  3.07 us
    pallas_call x1, Pallas kernels, project(): pl.pallas_call(functools.partial(project_kernel, own), out_shape=[jax.Sha...  2.19 us
    pallas_call x1, Pallas kernels, solve(): pl.pallas_call(functools.partial(solve_kernel, seqs), out_shape=jax.Shape...  1.82 us
  transfers between devices with their start and end apart: 8, of which 7 were waited for; matrix products, arithmetic and copies ran while one was open for 1% of the time, Pallas kernels for 1%

profile of v15, /device:TPU:0, one launch (start us, length us, event | category | flops | bytes accessed | tf_op | source)
XLA Modules:
  0.0 25.3 jit_solution(1142025731606968366)
XLA Ops:
  0.0 2.2 %project.1 = (f32[96,256]{1,0:T(8,128)S(1)}, f32[96,256]{1,0:T(8,128)S(1)}) custom-call(s32[1]{0:T(128)} %bitcast.1.rank_ref, bf16[2752,256]{1,0:T(8,128)(2,1)} %bitcast.5, bf16[256,1024]{1,0:T(8,128)(2,1)} %g_hbm.1, bf16[64,2752]{1,0:T(8,128)(2,1)} %bitcast.6, bf16[64,1024]{1,0:T(8,128)(2,1)} %bitcast.7), custom_call_target="tpu_custom_call" | custom-call | tf_op jit(solution)/shard_map/project/pallas_call | solution.py:109
  2.2 0.5 %collective-permute-start = (f32[96,256]{1,0:T(8,128)S(1)}, f32[96,256]{1,0:T(8,128)S(1)}, u32[]{:S(2)}, u32[]{:S(2)}) collective-permute-start(f32[96,256]{1,0:T(8,128)S(1)} %get-tuple-element.10), channel_id=1, source_target_pairs={{0,1},{1,0},{2,3},{3,2},{4,5},{5,4},{6,7},{7,6},{8,9},{9,8},{10,11... | collective-permute-start | bytes 294920 | tf_op jit(solution)/shard_map/ppermute | solution.py:321
  2.7 0.0 copy-done.2
  2.8 0.1 convert_reduce_fusion
  2.9 0.8 %collective-permute-done.came_ref = f32[96,256]{1,0:T(8,128)S(1)} collective-permute-done((f32[96,256]{1,0:T(8,128)S(1)}, f32[96,256]{1,0:T(8,128)S(1)}, u32[]{:S(2)}, u32[]{:S(2)}) %collective-permute-start) | collective-permute-done | bytes 98336 | tf_op jit(solution)/shard_map/ppermute | solution.py:321
  3.7 2.9 %collective-permute-start.1 = (f32[64,256]{1,0:T(8,128)S(1)}, f32[64,256]{1,0:T(8,128)S(1)}, u32[]{:S(2)}, u32[]{:S(2)}) collective-permute-start(f32[64,256]{1,0:T(8,128)S(1)} %get-tuple-element.12), channel_id=1, source_target_pairs={{0,2},{1,3},{2,0},{3,1},{4,6},{5,7},{6,4},{7,5},{8,10},{9,11},{10,... | collective-permute-start | bytes 196616 | tf_op jit(solution)/shard_map/ppermute | solution.py:321
  6.6 0.1 fusion.1.weights_ref
  6.7 0.2 pick.1.asked_ref
  6.8 2.2 %collective-permute-done.1.came_ref = f32[64,256]{1,0:T(8,128)S(1)} collective-permute-done((f32[64,256]{1,0:T(8,128)S(1)}, f32[64,256]{1,0:T(8,128)S(1)}, u32[]{:S(2)}, u32[]{:S(2)}) %collective-permute-start.1) | collective-permute-done | bytes 65568 | tf_op jit(solution)/shard_map/ppermute | solution.py:321
  9.0 0.4 %gradients.1.refs_3_ = f32[160,128]{1,0:T(8,128)S(1)} custom-call(f32[16,256]{1,0:T(8,128)S(1)} %fusion.1.weights_ref, f32[64,256]{1,0:T(8,128)S(1)} %get-tuple-element.11.kept_ref, f32[64,256]{1,0:T(8,128)S(1)} %collective-permute-done.1.came_ref, f32[32,128]{1,0:T(8,128)S(1)} %pick.1.asked_ref), custom_call_target="tpu_custom_call" | custom-call | tf_op jit(solution)/shard_map/gradients/pallas_call | solution.py:223
  9.4 3.0 %collective-permute-start.2 = (f32[160,128]{1,0:T(8,128)S(1)}, f32[160,128]{1,0:T(8,128)S(1)}, u32[]{:S(2)}, u32[]{:S(2)}) collective-permute-start(f32[160,128]{1,0:T(8,128)S(1)} %gradients.1.refs_3_), channel_id=1, source_target_pairs={{0,8},{4,12},{8,0},{12,4},{1,9},{5,13},{9,1},{13,5},{2,10},{6,14},... | collective-permute-start | bytes 245768 | tf_op jit(solution)/shard_map/ppermute | solution.py:330
  12.4 1.6 %collective-permute-start.3 = (f32[160,128]{1,0:T(8,128)S(1)}, f32[160,128]{1,0:T(8,128)S(1)}, u32[]{:S(2)}, u32[]{:S(2)}) collective-permute-start(f32[160,128]{1,0:T(8,128)S(1)} %gradients.1.refs_3_), channel_id=1, source_target_pairs={{0,4},{4,8},{8,12},{12,0},{1,5},{5,9},{9,13},{13,1},{2,6},{6,10},{... | collective-permute-start | bytes 245768 | tf_op jit(solution)/shard_map/ppermute | solution.py:330
  14.0 2.2 %collective-permute-start.4 = (f32[160,128]{1,0:T(8,128)S(1)}, f32[160,128]{1,0:T(8,128)S(1)}, u32[]{:S(2)}, u32[]{:S(2)}) collective-permute-start(f32[160,128]{1,0:T(8,128)S(1)} %gradients.1.refs_3_), channel_id=1, source_target_pairs={{0,12},{4,0},{8,4},{12,8},{1,13},{5,1},{9,5},{13,9},{2,14},{6,2},{... | collective-permute-start | bytes 245768 | tf_op jit(solution)/shard_map/ppermute | solution.py:330
  16.2 1.3 %collective-permute-done.2.refs_0_ = f32[160,128]{1,0:T(8,128)S(1)} collective-permute-done((f32[160,128]{1,0:T(8,128)S(1)}, f32[160,128]{1,0:T(8,128)S(1)}, u32[]{:S(2)}, u32[]{:S(2)}) %collective-permute-start.2) | collective-permute-done | bytes 81952 | tf_op jit(solution)/shard_map/ppermute | solution.py:330
  17.5 1.5 %collective-permute-done.3.refs_1_ = f32[160,128]{1,0:T(8,128)S(1)} collective-permute-done((f32[160,128]{1,0:T(8,128)S(1)}, f32[160,128]{1,0:T(8,128)S(1)}, u32[]{:S(2)}, u32[]{:S(2)}) %collective-permute-start.3) | collective-permute-done | bytes 81952 | tf_op jit(solution)/shard_map/ppermute | solution.py:330
  19.0 0.3 %collective-permute-done.4.refs_2_ = f32[160,128]{1,0:T(8,128)S(1)} collective-permute-done((f32[160,128]{1,0:T(8,128)S(1)}, f32[160,128]{1,0:T(8,128)S(1)}, u32[]{:S(2)}, u32[]{:S(2)}) %collective-permute-start.4) | collective-permute-done | bytes 81952 | tf_op jit(solution)/shard_map/ppermute | solution.py:330
  19.3 0.3 %grams.1.refs_3_ = f32[40,128]{1,0:T(8,128)S(1)} custom-call(s32[1]{0:T(128)} %bitcast.me_ref, f32[160,128]{1,0:T(8,128)S(1)} %collective-permute-done.2.refs_0_, f32[160,128]{1,0:T(8,128)S(1)} %collective-permute-done.3.refs_1_, f32[160,128]{1,0:T(8,128)S(1)} %collective-permute-done.4.refs_2_, f32[160,128]{1,0:T(8,128)S(1)} %gradients.1.refs_3_), custom_call_target="tpu_custom_call" | custom-call | tf_op jit(solution)/shard_map/grams/pallas_call | solution.py:260
  19.6 0.0 collective-permute-start.5
  19.7 1.6 %collective-permute-start.6 = (f32[40,128]{1,0:T(8,128)S(1)}, f32[40,128]{1,0:T(8,128)S(1)}, u32[]{:S(2)}, u32[]{:S(2)}) collective-permute-start(f32[40,128]{1,0:T(8,128)S(1)} %grams.1.refs_3_), channel_id=1, source_target_pairs={{0,2},{1,3},{2,0},{3,1},{4,6},{5,7},{6,4},{7,5},{8,10},{9,11},{10,... | collective-permute-start | bytes 61448 | tf_op jit(solution)/shard_map/ppermute | solution.py:321
  21.2 0.3 %collective-permute-start.7 = (f32[40,128]{1,0:T(8,128)S(1)}, f32[40,128]{1,0:T(8,128)S(1)}, u32[]{:S(2)}, u32[]{:S(2)}) collective-permute-start(f32[40,128]{1,0:T(8,128)S(1)} %grams.1.refs_3_), channel_id=1, source_target_pairs={{0,1},{1,0},{2,3},{3,2},{4,5},{5,4},{6,7},{7,6},{8,9},{9,8},{10,11... | collective-permute-start | bytes 61448 | tf_op jit(solution)/shard_map/ppermute | solution.py:321
  21.5 1.5 %collective-permute-done.5.refs_0_ = f32[40,128]{1,0:T(8,128)S(1)} collective-permute-done((f32[40,128]{1,0:T(8,128)S(1)}, f32[40,128]{1,0:T(8,128)S(1)}, u32[]{:S(2)}, u32[]{:S(2)}) %collective-permute-start.5) | collective-permute-done | bytes 20512 | tf_op jit(solution)/shard_map/ppermute | solution.py:321
  23.0 0.5 %collective-permute-done.6.refs_1_ = f32[40,128]{1,0:T(8,128)S(1)} collective-permute-done((f32[40,128]{1,0:T(8,128)S(1)}, f32[40,128]{1,0:T(8,128)S(1)}, u32[]{:S(2)}, u32[]{:S(2)}) %collective-permute-start.6) | collective-permute-done | bytes 20512 | tf_op jit(solution)/shard_map/ppermute | solution.py:321
  23.5 0.0 collective-permute-done.7.refs_2_
  23.5 1.8 %solve.1 = f32[16,16]{1,0:T(8,128)} custom-call(f32[40,128]{1,0:T(8,128)S(1)} %collective-permute-done.5.refs_0_, f32[40,128]{1,0:T(8,128)S(1)} %collective-permute-done.6.refs_1_, f32[40,128]{1,0:T(8,128)S(1)} %collective-permute-done.7.refs_2_, f32[40,128]{1,0:T(8,128)S(1)} %grams.1.refs_3_), custom_call_target="tpu_custom_call" | custom-call | tf_op jit(solution)/shard_map/solve/pallas_call | solution.py:312
  (8 shorter events, 0.0 us)
Async XLA Ops:
  0.0 2.7 %copy-start.2 = (s32[16]{0:T(128)S(1)}, s32[16]{0:T(128)}, u32[]{:S(2)}) copy-start(s32[16]{0:T(128)} %param.12) | copy-start | bytes 196
  0.0 2.8 %copy-start.1 = (s32[256]{0:T(256)S(1)}, s32[256]{0:T(256)}, u32[]{:S(2)}) copy-start(s32[256]{0:T(256)} %param.11) | copy-start | bytes 3076
  0.0 6.7 %copy-start = (f32[4,4096]{1,0:T(4,128)S(1)}, f32[4,4096]{1,0:T(4,128)}, u32[]{:S(2)}) copy-start(f32[4,4096]{1,0:T(4,128)} %queries_ref.1) | copy-start | bytes 196612
  2.2 1.5 %collective-permute-start = (f32[96,256]{1,0:T(8,128)S(1)}, f32[96,256]{1,0:T(8,128)S(1)}, u32[]{:S(2)}, u32[]{:S(2)}) collective-permute-start(f32[96,256]{1,0:T(8,128)S(1)} %get-tuple-element.10), channel_id=1, source_target_pairs={{0,1},{1,0},{2,3},{3,2},{4,5},{5,4},{6,7},{7,6},{8,9},{9,8},{10,11... | collective-permute-start | bytes 294920 | tf_op jit(solution)/shard_map/ppermute | solution.py:321
  3.7 5.3 %collective-permute-start.1 = (f32[64,256]{1,0:T(8,128)S(1)}, f32[64,256]{1,0:T(8,128)S(1)}, u32[]{:S(2)}, u32[]{:S(2)}) collective-permute-start(f32[64,256]{1,0:T(8,128)S(1)} %get-tuple-element.12), channel_id=1, source_target_pairs={{0,2},{1,3},{2,0},{3,1},{4,6},{5,7},{6,4},{7,5},{8,10},{9,11},{10,... | collective-permute-start | bytes 196616 | tf_op jit(solution)/shard_map/ppermute | solution.py:321
  9.4 8.1 %collective-permute-start.2 = (f32[160,128]{1,0:T(8,128)S(1)}, f32[160,128]{1,0:T(8,128)S(1)}, u32[]{:S(2)}, u32[]{:S(2)}) collective-permute-start(f32[160,128]{1,0:T(8,128)S(1)} %gradients.1.refs_3_), channel_id=1, source_target_pairs={{0,8},{4,12},{8,0},{12,4},{1,9},{5,13},{9,1},{13,5},{2,10},{6,14},... | collective-permute-start | bytes 245768 | tf_op jit(solution)/shard_map/ppermute | solution.py:330
  12.4 6.6 %collective-permute-start.3 = (f32[160,128]{1,0:T(8,128)S(1)}, f32[160,128]{1,0:T(8,128)S(1)}, u32[]{:S(2)}, u32[]{:S(2)}) collective-permute-start(f32[160,128]{1,0:T(8,128)S(1)} %gradients.1.refs_3_), channel_id=1, source_target_pairs={{0,4},{4,8},{8,12},{12,0},{1,5},{5,9},{9,13},{13,1},{2,6},{6,10},{... | collective-permute-start | bytes 245768 | tf_op jit(solution)/shard_map/ppermute | solution.py:330
  14.0 5.3 %collective-permute-start.4 = (f32[160,128]{1,0:T(8,128)S(1)}, f32[160,128]{1,0:T(8,128)S(1)}, u32[]{:S(2)}, u32[]{:S(2)}) collective-permute-start(f32[160,128]{1,0:T(8,128)S(1)} %gradients.1.refs_3_), channel_id=1, source_target_pairs={{0,12},{4,0},{8,4},{12,8},{1,13},{5,1},{9,5},{13,9},{2,14},{6,2},{... | collective-permute-start | bytes 245768 | tf_op jit(solution)/shard_map/ppermute | solution.py:330
  19.6 3.4 %collective-permute-start.5 = (f32[40,128]{1,0:T(8,128)S(1)}, f32[40,128]{1,0:T(8,128)S(1)}, u32[]{:S(2)}, u32[]{:S(2)}) collective-permute-start(f32[40,128]{1,0:T(8,128)S(1)} %grams.1.refs_3_), channel_id=1, source_target_pairs={{0,3},{1,2},{2,1},{3,0},{4,7},{5,6},{6,5},{7,4},{8,11},{9,10},{10,... | collective-permute-start | bytes 61448 | tf_op jit(solution)/shard_map/ppermute | solution.py:321
  19.7 3.8 %collective-permute-start.6 = (f32[40,128]{1,0:T(8,128)S(1)}, f32[40,128]{1,0:T(8,128)S(1)}, u32[]{:S(2)}, u32[]{:S(2)}) collective-permute-start(f32[40,128]{1,0:T(8,128)S(1)} %grams.1.refs_3_), channel_id=1, source_target_pairs={{0,2},{1,3},{2,0},{3,1},{4,6},{5,7},{6,4},{7,5},{8,10},{9,11},{10,... | collective-permute-start | bytes 61448 | tf_op jit(solution)/shard_map/ppermute | solution.py:321
  21.2 2.3 %collective-permute-start.7 = (f32[40,128]{1,0:T(8,128)S(1)}, f32[40,128]{1,0:T(8,128)S(1)}, u32[]{:S(2)}, u32[]{:S(2)}) collective-permute-start(f32[40,128]{1,0:T(8,128)S(1)} %grams.1.refs_3_), channel_id=1, source_target_pairs={{0,1},{1,0},{2,3},{3,2},{4,5},{5,4},{6,7},{7,6},{8,9},{9,8},{10,11... | collective-permute-start | bytes 61448 | tf_op jit(solution)/shard_map/ppermute | solution.py:321

commit v16 on v14

--- a/solution.py
+++ b/solution.py
@@ -49,13 +49,13 @@
     x_ref, g_ref, wx_ref, wg_ref, wide_ref, sems = scratch
     copies = []
 
-    def fetch(src, dst, index):
+    def fetch(src, dst, index, priority=1):
         copy = pltpu.make_async_copy(src, dst, sems.at[index])
-        copy.start()
+        copy.start(priority=priority)
         return copy
 
-    g_cuts = cuts_of(g_ref.shape[1], 1024)
-    x_cuts = cuts_of(x_ref.shape[0], 1024)
+    g_cuts = cuts_of(g_ref.shape[1], 512)
+    x_cuts = cuts_of(x_ref.shape[0], 512)
     wg_copy = fetch(wg_hbm, wg_ref, 0)
     index = 2
     g_copies = []
@@ -67,7 +67,7 @@
     x_copies = []
     for at, size in x_cuts:
         rows = pl.ds(at, size)
-        x_copies.append(fetch(x_hbm.at[rows, :], x_ref.at[rows, :], index))
+        x_copies.append(fetch(x_hbm.at[rows, :], x_ref.at[rows, :], index, int(at < 1024)))
         index += 1
 
     def product(copies, terms):
@@ -102,7 +102,7 @@
     rank = in_proj.shape[1]
     tokens, hidden = inputs.shape
     width = out_grads.shape[1]
-    copies = 2 + len(cuts_of(width, 1024)) + len(cuts_of(hidden, 1024))
+    copies = 2 + len(cuts_of(width, 512)) + len(cuts_of(hidden, 512))
     arrays = (inputs.T, out_grads, in_proj.T, out_proj.T)
     in_hbm = pl.BlockSpec(memory_space=pltpu.HBM)
     return pl.pallas_call(
@@ -293,14 +293,14 @@
         high = state.astype(jnp.bfloat16).astype(jnp.float32)
         low = state - high
         left = jnp.where(left_lanes, high, low).astype(jnp.bfloat16)
+        lead = high[:, :seqs].astype(jnp.bfloat16)
         high = high[:seqs].astype(jnp.bfloat16)
         low = low[:seqs].astype(jnp.bfloat16)
-        right = jnp.concatenate([high, high, low, low], axis=0)
         if at + 1 == len(steps):
-            left, state = left[seqs:], state[seqs:]
+            left, lead, state = left[seqs:], lead[seqs:], state[seqs:]
         product = jnp.dot(
-            jnp.concatenate([left, left], axis=1), right, preferred_element_type=jnp.float32
-        )
+            left, jnp.concatenate([high, high], axis=0), preferred_element_type=jnp.float32
+        ) + jnp.dot(lead, low, preferred_element_type=jnp.float32)
         state = step * (2.0 * state - product)
     out_ref[...] = state[:, : out_ref.shape[1]]
 

time: 25.3 us -> 25.8 us (1.020)
  Pallas kernels: 4.88 us -> 5.42 us
    pallas_call x1, Pallas kernels: 2.19 us -> 2.65 us  [project(): pl.pallas_call(functools.partial(project_kernel, own), out_shape=[jax.Sha...]
where the time goes in v16:
time: 25.8 us; the launch traced here: 25.7 us
  starting transfers between devices  11.2 us (43%)
  waiting for transfers between devices  8.78 us (34%)
  Pallas kernels  5.42 us (21%)
    ppermute x3, starting transfers between devices, from_all(): return [lax.ppermute(value, axis, shift) for shift in shifts] + [value]  5.92 us
    ppermute x5, starting transfers between devices, from_partner(): return lax.ppermute(value, axis, [(i, i ^ m) for i in range(size)])  5.32 us
    ppermute x5, waiting for transfers between devices, from_partner(): return lax.ppermute(value, axis, [(i, i ^ m) for i in range(size)])  4.99 us
    ppermute x3, waiting for transfers between devices, from_all(): return [lax.ppermute(value, axis, shift) for shift in shifts] + [value]  3.8 us
    pallas_call x1, Pallas kernels, project(): pl.pallas_call(functools.partial(project_kernel, own), out_shape=[jax.Sha...  2.65 us
    pallas_call x1, Pallas kernels, solve(): pl.pallas_call(functools.partial(solve_kernel, seqs), out_shape=jax.Shape...  1.89 us
  transfers between devices with their start and end apart: 8, of which 7 were waited for; matrix products, arithmetic and copies ran while one was open for 1% of the time, Pallas kernels for 1%

profile of v16, /device:TPU:0, one launch (start us, length us, event | category | flops | bytes accessed | tf_op | source)
XLA Modules:
  0.0 25.7 jit_solution(10451859394797275260)
XLA Ops:
  0.0 2.7 %project.1 = (f32[96,256]{1,0:T(8,128)S(1)}, f32[96,256]{1,0:T(8,128)S(1)}) custom-call(s32[1]{0:T(128)} %bitcast.1.rank_ref, bf16[2752,256]{1,0:T(8,128)(2,1)} %bitcast.5, bf16[256,1024]{1,0:T(8,128)(2,1)} %g_hbm.1, bf16[64,2752]{1,0:T(8,128)(2,1)} %bitcast.6, bf16[64,1024]{1,0:T(8,128)(2,1)} %bitcast.7), custom_call_target="tpu_custom_call" | custom-call | tf_op jit(solution)/shard_map/project/pallas_call | solution.py:108
  2.7 0.5 %collective-permute-start = (f32[96,256]{1,0:T(8,128)S(1)}, f32[96,256]{1,0:T(8,128)S(1)}, u32[]{:S(2)}, u32[]{:S(2)}) collective-permute-start(f32[96,256]{1,0:T(8,128)S(1)} %get-tuple-element.10), channel_id=1, source_target_pairs={{0,1},{1,0},{2,3},{3,2},{4,5},{5,4},{6,7},{7,6},{8,9},{9,8},{10,11... | collective-permute-start | bytes 294920 | tf_op jit(solution)/shard_map/ppermute | solution.py:318
  3.2 0.1 convert_reduce_fusion
  3.4 0.8 %collective-permute-done.came_ref = f32[96,256]{1,0:T(8,128)S(1)} collective-permute-done((f32[96,256]{1,0:T(8,128)S(1)}, f32[96,256]{1,0:T(8,128)S(1)}, u32[]{:S(2)}, u32[]{:S(2)}) %collective-permute-start) | collective-permute-done | bytes 98336 | tf_op jit(solution)/shard_map/ppermute | solution.py:318
  4.2 2.9 %collective-permute-start.1 = (f32[64,256]{1,0:T(8,128)S(1)}, f32[64,256]{1,0:T(8,128)S(1)}, u32[]{:S(2)}, u32[]{:S(2)}) collective-permute-start(f32[64,256]{1,0:T(8,128)S(1)} %get-tuple-element.12), channel_id=1, source_target_pairs={{0,2},{1,3},{2,0},{3,1},{4,6},{5,7},{6,4},{7,5},{8,10},{9,11},{10,... | collective-permute-start | bytes 196616 | tf_op jit(solution)/shard_map/ppermute | solution.py:318
  7.1 0.1 fusion.1.weights_ref
  7.2 0.0 copy-done
  7.2 0.2 pick.1.asked_ref
  7.3 2.2 %collective-permute-done.1.came_ref = f32[64,256]{1,0:T(8,128)S(1)} collective-permute-done((f32[64,256]{1,0:T(8,128)S(1)}, f32[64,256]{1,0:T(8,128)S(1)}, u32[]{:S(2)}, u32[]{:S(2)}) %collective-permute-start.1) | collective-permute-done | bytes 65568 | tf_op jit(solution)/shard_map/ppermute | solution.py:318
  9.5 0.4 %gradients.1.refs_3_ = f32[160,128]{1,0:T(8,128)S(1)} custom-call(f32[16,256]{1,0:T(8,128)S(1)} %fusion.1.weights_ref, f32[64,256]{1,0:T(8,128)S(1)} %get-tuple-element.11.kept_ref, f32[64,256]{1,0:T(8,128)S(1)} %collective-permute-done.1.came_ref, f32[32,128]{1,0:T(8,128)S(1)} %pick.1.asked_ref), custom_call_target="tpu_custom_call" | custom-call | tf_op jit(solution)/shard_map/gradients/pallas_call | solution.py:222
  9.9 2.0 %collective-permute-start.2 = (f32[160,128]{1,0:T(8,128)S(1)}, f32[160,128]{1,0:T(8,128)S(1)}, u32[]{:S(2)}, u32[]{:S(2)}) collective-permute-start(f32[160,128]{1,0:T(8,128)S(1)} %gradients.1.refs_3_), channel_id=1, source_target_pairs={{0,4},{4,8},{8,12},{12,0},{1,5},{5,9},{9,13},{13,1},{2,6},{6,10},{... | collective-permute-start | bytes 245768 | tf_op jit(solution)/shard_map/ppermute | solution.py:327
  11.9 2.6 %collective-permute-start.3 = (f32[160,128]{1,0:T(8,128)S(1)}, f32[160,128]{1,0:T(8,128)S(1)}, u32[]{:S(2)}, u32[]{:S(2)}) collective-permute-start(f32[160,128]{1,0:T(8,128)S(1)} %gradients.1.refs_3_), channel_id=1, source_target_pairs={{0,8},{4,12},{8,0},{12,4},{1,9},{5,13},{9,1},{13,5},{2,10},{6,14},... | collective-permute-start | bytes 245768 | tf_op jit(solution)/shard_map/ppermute | solution.py:327
  14.4 1.3 %collective-permute-start.4 = (f32[160,128]{1,0:T(8,128)S(1)}, f32[160,128]{1,0:T(8,128)S(1)}, u32[]{:S(2)}, u32[]{:S(2)}) collective-permute-start(f32[160,128]{1,0:T(8,128)S(1)} %gradients.1.refs_3_), channel_id=1, source_target_pairs={{0,12},{4,0},{8,4},{12,8},{1,13},{5,1},{9,5},{13,9},{2,14},{6,2},{... | collective-permute-start | bytes 245768 | tf_op jit(solution)/shard_map/ppermute | solution.py:327
  15.8 1.5 %collective-permute-done.2.refs_0_ = f32[160,128]{1,0:T(8,128)S(1)} collective-permute-done((f32[160,128]{1,0:T(8,128)S(1)}, f32[160,128]{1,0:T(8,128)S(1)}, u32[]{:S(2)}, u32[]{:S(2)}) %collective-permute-start.2) | collective-permute-done | bytes 81952 | tf_op jit(solution)/shard_map/ppermute | solution.py:327
  17.3 2.2 %collective-permute-done.3.refs_1_ = f32[160,128]{1,0:T(8,128)S(1)} collective-permute-done((f32[160,128]{1,0:T(8,128)S(1)}, f32[160,128]{1,0:T(8,128)S(1)}, u32[]{:S(2)}, u32[]{:S(2)}) %collective-permute-start.3) | collective-permute-done | bytes 81952 | tf_op jit(solution)/shard_map/ppermute | solution.py:327
  19.5 0.1 collective-permute-done.4.refs_2_
  19.6 0.3 %grams.1.refs_3_ = f32[40,128]{1,0:T(8,128)S(1)} custom-call(s32[1]{0:T(128)} %bitcast.me_ref, f32[160,128]{1,0:T(8,128)S(1)} %collective-permute-done.2.refs_0_, f32[160,128]{1,0:T(8,128)S(1)} %collective-permute-done.3.refs_1_, f32[160,128]{1,0:T(8,128)S(1)} %collective-permute-done.4.refs_2_, f32[160,128]{1,0:T(8,128)S(1)} %gradients.1.refs_3_), custom_call_target="tpu_custom_call" | custom-call | tf_op jit(solution)/shard_map/grams/pallas_call | solution.py:257
  19.9 0.0 collective-permute-start.5
  20.0 1.5 %collective-permute-start.6 = (f32[40,128]{1,0:T(8,128)S(1)}, f32[40,128]{1,0:T(8,128)S(1)}, u32[]{:S(2)}, u32[]{:S(2)}) collective-permute-start(f32[40,128]{1,0:T(8,128)S(1)} %grams.1.refs_3_), channel_id=1, source_target_pairs={{0,2},{1,3},{2,0},{3,1},{4,6},{5,7},{6,4},{7,5},{8,10},{9,11},{10,... | collective-permute-start | bytes 61448 | tf_op jit(solution)/shard_map/ppermute | solution.py:318
  21.5 0.3 %collective-permute-start.7 = (f32[40,128]{1,0:T(8,128)S(1)}, f32[40,128]{1,0:T(8,128)S(1)}, u32[]{:S(2)}, u32[]{:S(2)}) collective-permute-start(f32[40,128]{1,0:T(8,128)S(1)} %grams.1.refs_3_), channel_id=1, source_target_pairs={{0,1},{1,0},{2,3},{3,2},{4,5},{5,4},{6,7},{7,6},{8,9},{9,8},{10,11... | collective-permute-start | bytes 61448 | tf_op jit(solution)/shard_map/ppermute | solution.py:318
  21.8 1.6 %collective-permute-done.5.refs_0_ = f32[40,128]{1,0:T(8,128)S(1)} collective-permute-done((f32[40,128]{1,0:T(8,128)S(1)}, f32[40,128]{1,0:T(8,128)S(1)}, u32[]{:S(2)}, u32[]{:S(2)}) %collective-permute-start.5) | collective-permute-done | bytes 20512 | tf_op jit(solution)/shard_map/ppermute | solution.py:318
  23.4 0.4 %collective-permute-done.6.refs_1_ = f32[40,128]{1,0:T(8,128)S(1)} collective-permute-done((f32[40,128]{1,0:T(8,128)S(1)}, f32[40,128]{1,0:T(8,128)S(1)}, u32[]{:S(2)}, u32[]{:S(2)}) %collective-permute-start.6) | collective-permute-done | bytes 20512 | tf_op jit(solution)/shard_map/ppermute | solution.py:318
  23.8 0.0 collective-permute-done.7.refs_2_
  23.8 1.9 %solve.1 = f32[16,16]{1,0:T(8,128)} custom-call(f32[40,128]{1,0:T(8,128)S(1)} %collective-permute-done.5.refs_0_, f32[40,128]{1,0:T(8,128)S(1)} %collective-permute-done.6.refs_1_, f32[40,128]{1,0:T(8,128)S(1)} %collective-permute-done.7.refs_2_, f32[40,128]{1,0:T(8,128)S(1)} %grams.1.refs_3_), custom_call_target="tpu_custom_call" | custom-call | tf_op jit(solution)/shard_map/solve/pallas_call | solution.py:309
  (8 shorter events, 0.0 us)
Async XLA Ops:
  0.0 3.2 %copy-start.2 = (s32[16]{0:T(128)S(1)}, s32[16]{0:T(128)}, u32[]{:S(2)}) copy-start(s32[16]{0:T(128)} %param.12) | copy-start | bytes 196
  0.0 3.2 %copy-start.1 = (s32[256]{0:T(256)S(1)}, s32[256]{0:T(256)}, u32[]{:S(2)}) copy-start(s32[256]{0:T(256)} %param.11) | copy-start | bytes 3076
  0.0 7.2 %copy-start = (f32[4,4096]{1,0:T(4,128)S(1)}, f32[4,4096]{1,0:T(4,128)}, u32[]{:S(2)}) copy-start(f32[4,4096]{1,0:T(4,128)} %queries_ref.1) | copy-start | bytes 196612
  2.7 1.5 %collective-permute-start = (f32[96,256]{1,0:T(8,128)S(1)}, f32[96,256]{1,0:T(8,128)S(1)}, u32[]{:S(2)}, u32[]{:S(2)}) collective-permute-start(f32[96,256]{1,0:T(8,128)S(1)} %get-tuple-element.10), channel_id=1, source_target_pairs={{0,1},{1,0},{2,3},{3,2},{4,5},{5,4},{6,7},{7,6},{8,9},{9,8},{10,11... | collective-permute-start | bytes 294920 | tf_op jit(solution)/shard_map/ppermute | solution.py:318
  4.2 5.3 %collective-permute-start.1 = (f32[64,256]{1,0:T(8,128)S(1)}, f32[64,256]{1,0:T(8,128)S(1)}, u32[]{:S(2)}, u32[]{:S(2)}) collective-permute-start(f32[64,256]{1,0:T(8,128)S(1)} %get-tuple-element.12), channel_id=1, source_target_pairs={{0,2},{1,3},{2,0},{3,1},{4,6},{5,7},{6,4},{7,5},{8,10},{9,11},{10,... | collective-permute-start | bytes 196616 | tf_op jit(solution)/shard_map/ppermute | solution.py:318
  9.9 7.4 %collective-permute-start.2 = (f32[160,128]{1,0:T(8,128)S(1)}, f32[160,128]{1,0:T(8,128)S(1)}, u32[]{:S(2)}, u32[]{:S(2)}) collective-permute-start(f32[160,128]{1,0:T(8,128)S(1)} %gradients.1.refs_3_), channel_id=1, source_target_pairs={{0,4},{4,8},{8,12},{12,0},{1,5},{5,9},{9,13},{13,1},{2,6},{6,10},{... | collective-permute-start | bytes 245768 | tf_op jit(solution)/shard_map/ppermute | solution.py:327
  11.9 7.6 %collective-permute-start.3 = (f32[160,128]{1,0:T(8,128)S(1)}, f32[160,128]{1,0:T(8,128)S(1)}, u32[]{:S(2)}, u32[]{:S(2)}) collective-permute-start(f32[160,128]{1,0:T(8,128)S(1)} %gradients.1.refs_3_), channel_id=1, source_target_pairs={{0,8},{4,12},{8,0},{12,4},{1,9},{5,13},{9,1},{13,5},{2,10},{6,14},... | collective-permute-start | bytes 245768 | tf_op jit(solution)/shard_map/ppermute | solution.py:327
  14.4 5.1 %collective-permute-start.4 = (f32[160,128]{1,0:T(8,128)S(1)}, f32[160,128]{1,0:T(8,128)S(1)}, u32[]{:S(2)}, u32[]{:S(2)}) collective-permute-start(f32[160,128]{1,0:T(8,128)S(1)} %gradients.1.refs_3_), channel_id=1, source_target_pairs={{0,12},{4,0},{8,4},{12,8},{1,13},{5,1},{9,5},{13,9},{2,14},{6,2},{... | collective-permute-start | bytes 245768 | tf_op jit(solution)/shard_map/ppermute | solution.py:327
  19.9 3.4 %collective-permute-start.5 = (f32[40,128]{1,0:T(8,128)S(1)}, f32[40,128]{1,0:T(8,128)S(1)}, u32[]{:S(2)}, u32[]{:S(2)}) collective-permute-start(f32[40,128]{1,0:T(8,128)S(1)} %grams.1.refs_3_), channel_id=1, source_target_pairs={{0,3},{1,2},{2,1},{3,0},{4,7},{5,6},{6,5},{7,4},{8,11},{9,10},{10,... | collective-permute-start | bytes 61448 | tf_op jit(solution)/shard_map/ppermute | solution.py:318
  20.0 3.8 %collective-permute-start.6 = (f32[40,128]{1,0:T(8,128)S(1)}, f32[40,128]{1,0:T(8,128)S(1)}, u32[]{:S(2)}, u32[]{:S(2)}) collective-permute-start(f32[40,128]{1,0:T(8,128)S(1)} %grams.1.refs_3_), channel_id=1, source_target_pairs={{0,2},{1,3},{2,0},{3,1},{4,6},{5,7},{6,4},{7,5},{8,10},{9,11},{10,... | collective-permute-start | bytes 61448 | tf_op jit(solution)/shard_map/ppermute | solution.py:318
  21.5 2.3 %collective-permute-start.7 = (f32[40,128]{1,0:T(8,128)S(1)}, f32[40,128]{1,0:T(8,128)S(1)}, u32[]{:S(2)}, u32[]{:S(2)}) collective-permute-start(f32[40,128]{1,0:T(8,128)S(1)} %grams.1.refs_3_), channel_id=1, source_target_pairs={{0,1},{1,0},{2,3},{3,2},{4,5},{5,4},{6,7},{7,6},{8,9},{9,8},{10,11... | collective-permute-start | bytes 61448 | tf_op jit(solution)/shard_map/ppermute | solution.py:318

commit v17 on v15

--- a/solution.py
+++ b/solution.py
@@ -10,7 +10,7 @@
 damping = 0.5
 VMEM_LIMIT = 32 * 1024 * 1024
 SMALL = 4
-SHIFTS = {1: (), 2: (1,), 4: (2, 1, 3)}
+SHIFTS = {1: (), 2: (1,), 4: (3, 2, 1)}
 
 
 def token_weights(seq_ids, counts, first):
@@ -55,8 +55,8 @@
         copy.start()
         return copy
 
-    g_cuts = cuts_of(g_ref.shape[1], 1024)
-    x_cuts = cuts_of(x_ref.shape[0], 1024)
+    g_cuts = cuts_of(g_ref.shape[1], 512)
+    x_cuts = cuts_of(x_ref.shape[0], 768)
     wg_copy = fetch(wg_hbm, wg_ref, 0)
     index = 2
     g_copies = []
@@ -103,7 +103,7 @@
     rank = in_proj.shape[1]
     tokens, hidden = inputs.shape
     width = out_grads.shape[1]
-    copies = 2 + len(cuts_of(width, 1024)) + len(cuts_of(hidden, 1024))
+    copies = 2 + len(cuts_of(width, 512)) + len(cuts_of(hidden, 768))
     arrays = (inputs.T, out_grads, in_proj.T, out_proj.T)
     in_hbm = pl.BlockSpec(memory_space=pltpu.HBM)
     return pl.pallas_call(

time: 25.5 us -> 27.4 us (1.075)
  waiting for transfers between devices: 8.06 us -> 11.8 us
  starting transfers between devices: 12.1 us -> 10.4 us
    ppermute x3, waiting for transfers between devices: 3.07 us -> 6.02 us  [from_all(): return [lax.ppermute(value, axis, shift) for shift in shifts] + [value]]
    ppermute x3, starting transfers between devices: 6.84 us -> 5.03 us  [from_all(): return [lax.ppermute(value, axis, shift) for shift in shifts] + [value]]
    ppermute x5, waiting for transfers between devices: 4.99 us -> 5.76 us  [from_partner(): return lax.ppermute(value, axis, [(i, i ^ m) for i in range(size)])]
  transfers between devices with their start and end apart: 8 -> 8, of which waited for: 7 -> 6; matrix products, arithmetic and copies ran while one was open for 1% -> 1% of each run, Pallas kernels for 1% -> 1%
where the time goes in v17:
time: 27.4 us; the launch traced here: 27.3 us
  waiting for transfers between devices  11.8 us (43%)
  starting transfers between devices  10.4 us (38%)
  Pallas kernels  4.88 us (18%)
    ppermute x3, waiting for transfers between devices, from_all(): return [lax.ppermute(value, axis, shift) for shift in shifts] + [value]  6.02 us
    ppermute x5, waiting for transfers between devices, from_partner(): return lax.ppermute(value, axis, [(i, i ^ m) for i in range(size)])  5.76 us
    ppermute x5, starting transfers between devices, from_partner(): return lax.ppermute(value, axis, [(i, i ^ m) for i in range(size)])  5.32 us
    ppermute x3, starting transfers between devices, from_all(): return [lax.ppermute(value, axis, shift) for shift in shifts] + [value]  5.03 us
    pallas_call x1, Pallas kernels, project(): pl.pallas_call(functools.partial(project_kernel, own), out_shape=[jax.Sha...  2.19 us
    pallas_call x1, Pallas kernels, solve(): pl.pallas_call(functools.partial(solve_kernel, seqs), out_shape=jax.Shape...  1.82 us
  transfers between devices with their start and end apart: 8, of which 6 were waited for; matrix products, arithmetic and copies ran while one was open for 1% of the time, Pallas kernels for 1%

profile of v17, /device:TPU:0, one launch (start us, length us, event | category | flops | bytes accessed | tf_op | source)
XLA Modules:
  0.0 27.3 jit_solution(17638528877753036202)
XLA Ops:
  0.0 2.2 %project.1 = (f32[96,256]{1,0:T(8,128)S(1)}, f32[96,256]{1,0:T(8,128)S(1)}) custom-call(s32[1]{0:T(128)} %bitcast.1.rank_ref, bf16[2752,256]{1,0:T(8,128)(2,1)} %bitcast.5, bf16[256,1024]{1,0:T(8,128)(2,1)} %g_hbm.1, bf16[64,2752]{1,0:T(8,128)(2,1)} %bitcast.6, bf16[64,1024]{1,0:T(8,128)(2,1)} %bitcast.7), custom_call_target="tpu_custom_call" | custom-call | tf_op jit(solution)/shard_map/project/pallas_call | solution.py:109
  2.2 0.5 %collective-permute-start = (f32[96,256]{1,0:T(8,128)S(1)}, f32[96,256]{1,0:T(8,128)S(1)}, u32[]{:S(2)}, u32[]{:S(2)}) collective-permute-start(f32[96,256]{1,0:T(8,128)S(1)} %get-tuple-element.10), channel_id=1, source_target_pairs={{0,1},{1,0},{2,3},{3,2},{4,5},{5,4},{6,7},{7,6},{8,9},{9,8},{10,11... | collective-permute-start | bytes 294920 | tf_op jit(solution)/shard_map/ppermute | solution.py:321
  2.7 0.0 copy-done.2
  2.8 0.1 convert_reduce_fusion
  2.9 0.8 %collective-permute-done.came_ref = f32[96,256]{1,0:T(8,128)S(1)} collective-permute-done((f32[96,256]{1,0:T(8,128)S(1)}, f32[96,256]{1,0:T(8,128)S(1)}, u32[]{:S(2)}, u32[]{:S(2)}) %collective-permute-start) | collective-permute-done | bytes 98336 | tf_op jit(solution)/shard_map/ppermute | solution.py:321
  3.7 2.9 %collective-permute-start.1 = (f32[64,256]{1,0:T(8,128)S(1)}, f32[64,256]{1,0:T(8,128)S(1)}, u32[]{:S(2)}, u32[]{:S(2)}) collective-permute-start(f32[64,256]{1,0:T(8,128)S(1)} %get-tuple-element.12), channel_id=1, source_target_pairs={{0,2},{1,3},{2,0},{3,1},{4,6},{5,7},{6,4},{7,5},{8,10},{9,11},{10,... | collective-permute-start | bytes 196616 | tf_op jit(solution)/shard_map/ppermute | solution.py:321
  6.6 0.1 fusion.1.weights_ref
  6.7 0.2 pick.1.asked_ref
  6.9 2.2 %collective-permute-done.1.came_ref = f32[64,256]{1,0:T(8,128)S(1)} collective-permute-done((f32[64,256]{1,0:T(8,128)S(1)}, f32[64,256]{1,0:T(8,128)S(1)}, u32[]{:S(2)}, u32[]{:S(2)}) %collective-permute-start.1) | collective-permute-done | bytes 65568 | tf_op jit(solution)/shard_map/ppermute | solution.py:321
  9.0 0.4 %gradients.1.refs_3_ = f32[160,128]{1,0:T(8,128)S(1)} custom-call(f32[16,256]{1,0:T(8,128)S(1)} %fusion.1.weights_ref, f32[64,256]{1,0:T(8,128)S(1)} %get-tuple-element.11.kept_ref, f32[64,256]{1,0:T(8,128)S(1)} %collective-permute-done.1.came_ref, f32[32,128]{1,0:T(8,128)S(1)} %pick.1.asked_ref), custom_call_target="tpu_custom_call" | custom-call | tf_op jit(solution)/shard_map/gradients/pallas_call | solution.py:223
  9.4 4.0 %collective-permute-start.2 = (f32[160,128]{1,0:T(8,128)S(1)}, f32[160,128]{1,0:T(8,128)S(1)}, u32[]{:S(2)}, u32[]{:S(2)}) collective-permute-start(f32[160,128]{1,0:T(8,128)S(1)} %gradients.1.refs_3_), channel_id=1, source_target_pairs={{0,12},{4,0},{8,4},{12,8},{1,13},{5,1},{9,5},{13,9},{2,14},{6,2},{... | collective-permute-start | bytes 245768 | tf_op jit(solution)/shard_map/ppermute | solution.py:330
  13.4 0.0 collective-permute-start.3
  13.4 1.0 %collective-permute-start.4 = (f32[160,128]{1,0:T(8,128)S(1)}, f32[160,128]{1,0:T(8,128)S(1)}, u32[]{:S(2)}, u32[]{:S(2)}) collective-permute-start(f32[160,128]{1,0:T(8,128)S(1)} %gradients.1.refs_3_), channel_id=1, source_target_pairs={{0,4},{4,8},{8,12},{12,0},{1,5},{5,9},{9,13},{13,1},{2,6},{6,10},{... | collective-permute-start | bytes 245768 | tf_op jit(solution)/shard_map/ppermute | solution.py:330
  14.4 1.6 %collective-permute-done.2.refs_0_ = f32[160,128]{1,0:T(8,128)S(1)} collective-permute-done((f32[160,128]{1,0:T(8,128)S(1)}, f32[160,128]{1,0:T(8,128)S(1)}, u32[]{:S(2)}, u32[]{:S(2)}) %collective-permute-start.2) | collective-permute-done | bytes 81952 | tf_op jit(solution)/shard_map/ppermute | solution.py:330
  16.1 4.4 %collective-permute-done.3.refs_1_ = f32[160,128]{1,0:T(8,128)S(1)} collective-permute-done((f32[160,128]{1,0:T(8,128)S(1)}, f32[160,128]{1,0:T(8,128)S(1)}, u32[]{:S(2)}, u32[]{:S(2)}) %collective-permute-start.3) | collective-permute-done | bytes 81952 | tf_op jit(solution)/shard_map/ppermute | solution.py:330
  20.5 0.0 collective-permute-done.4.refs_2_
  20.5 0.3 %grams.1.refs_3_ = f32[40,128]{1,0:T(8,128)S(1)} custom-call(s32[1]{0:T(128)} %bitcast.me_ref, f32[160,128]{1,0:T(8,128)S(1)} %collective-permute-done.2.refs_0_, f32[160,128]{1,0:T(8,128)S(1)} %collective-permute-done.3.refs_1_, f32[160,128]{1,0:T(8,128)S(1)} %collective-permute-done.4.refs_2_, f32[160,128]{1,0:T(8,128)S(1)} %gradients.1.refs_3_), custom_call_target="tpu_custom_call" | custom-call | tf_op jit(solution)/shard_map/grams/pallas_call | solution.py:260
  20.8 0.8 %collective-permute-start.5 = (f32[40,128]{1,0:T(8,128)S(1)}, f32[40,128]{1,0:T(8,128)S(1)}, u32[]{:S(2)}, u32[]{:S(2)}) collective-permute-start(f32[40,128]{1,0:T(8,128)S(1)} %grams.1.refs_3_), channel_id=1, source_target_pairs={{0,3},{1,2},{2,1},{3,0},{4,7},{5,6},{6,5},{7,4},{8,11},{9,10},{10,... | collective-permute-start | bytes 61448 | tf_op jit(solution)/shard_map/ppermute | solution.py:321
  21.6 0.8 %collective-permute-start.6 = (f32[40,128]{1,0:T(8,128)S(1)}, f32[40,128]{1,0:T(8,128)S(1)}, u32[]{:S(2)}, u32[]{:S(2)}) collective-permute-start(f32[40,128]{1,0:T(8,128)S(1)} %grams.1.refs_3_), channel_id=1, source_target_pairs={{0,2},{1,3},{2,0},{3,1},{4,6},{5,7},{6,4},{7,5},{8,10},{9,11},{10,... | collective-permute-start | bytes 61448 | tf_op jit(solution)/shard_map/ppermute | solution.py:321
  22.4 0.3 %collective-permute-start.7 = (f32[40,128]{1,0:T(8,128)S(1)}, f32[40,128]{1,0:T(8,128)S(1)}, u32[]{:S(2)}, u32[]{:S(2)}) collective-permute-start(f32[40,128]{1,0:T(8,128)S(1)} %grams.1.refs_3_), channel_id=1, source_target_pairs={{0,1},{1,0},{2,3},{3,2},{4,5},{5,4},{6,7},{7,6},{8,9},{9,8},{10,11... | collective-permute-start | bytes 61448 | tf_op jit(solution)/shard_map/ppermute | solution.py:321
  22.7 1.5 %collective-permute-done.5.refs_0_ = f32[40,128]{1,0:T(8,128)S(1)} collective-permute-done((f32[40,128]{1,0:T(8,128)S(1)}, f32[40,128]{1,0:T(8,128)S(1)}, u32[]{:S(2)}, u32[]{:S(2)}) %collective-permute-start.5) | collective-permute-done | bytes 20512 | tf_op jit(solution)/shard_map/ppermute | solution.py:321
  24.2 1.3 %collective-permute-done.6.refs_1_ = f32[40,128]{1,0:T(8,128)S(1)} collective-permute-done((f32[40,128]{1,0:T(8,128)S(1)}, f32[40,128]{1,0:T(8,128)S(1)}, u32[]{:S(2)}, u32[]{:S(2)}) %collective-permute-start.6) | collective-permute-done | bytes 20512 | tf_op jit(solution)/shard_map/ppermute | solution.py:321
  25.5 0.0 collective-permute-done.7.refs_2_
  25.5 1.8 %solve.1 = f32[16,16]{1,0:T(8,128)} custom-call(f32[40,128]{1,0:T(8,128)S(1)} %collective-permute-done.5.refs_0_, f32[40,128]{1,0:T(8,128)S(1)} %collective-permute-done.6.refs_1_, f32[40,128]{1,0:T(8,128)S(1)} %collective-permute-done.7.refs_2_, f32[40,128]{1,0:T(8,128)S(1)} %grams.1.refs_3_), custom_call_target="tpu_custom_call" | custom-call | tf_op jit(solution)/shard_map/solve/pallas_call | solution.py:312
  (8 shorter events, 0.0 us)
Async XLA Ops:
  0.0 2.8 %copy-start.2 = (s32[16]{0:T(128)S(1)}, s32[16]{0:T(128)}, u32[]{:S(2)}) copy-start(s32[16]{0:T(128)} %param.12) | copy-start | bytes 196
  0.0 2.8 %copy-start.1 = (s32[256]{0:T(256)S(1)}, s32[256]{0:T(256)}, u32[]{:S(2)}) copy-start(s32[256]{0:T(256)} %param.11) | copy-start | bytes 3076
  0.0 6.7 %copy-start = (f32[4,4096]{1,0:T(4,128)S(1)}, f32[4,4096]{1,0:T(4,128)}, u32[]{:S(2)}) copy-start(f32[4,4096]{1,0:T(4,128)} %queries_ref.1) | copy-start | bytes 196612
  2.2 1.5 %collective-permute-start = (f32[96,256]{1,0:T(8,128)S(1)}, f32[96,256]{1,0:T(8,128)S(1)}, u32[]{:S(2)}, u32[]{:S(2)}) collective-permute-start(f32[96,256]{1,0:T(8,128)S(1)} %get-tuple-element.10), channel_id=1, source_target_pairs={{0,1},{1,0},{2,3},{3,2},{4,5},{5,4},{6,7},{7,6},{8,9},{9,8},{10,11... | collective-permute-start | bytes 294920 | tf_op jit(solution)/shard_map/ppermute | solution.py:321
  3.7 5.3 %collective-permute-start.1 = (f32[64,256]{1,0:T(8,128)S(1)}, f32[64,256]{1,0:T(8,128)S(1)}, u32[]{:S(2)}, u32[]{:S(2)}) collective-permute-start(f32[64,256]{1,0:T(8,128)S(1)} %get-tuple-element.12), channel_id=1, source_target_pairs={{0,2},{1,3},{2,0},{3,1},{4,6},{5,7},{6,4},{7,5},{8,10},{9,11},{10,... | collective-permute-start | bytes 196616 | tf_op jit(solution)/shard_map/ppermute | solution.py:321
  9.4 6.7 %collective-permute-start.2 = (f32[160,128]{1,0:T(8,128)S(1)}, f32[160,128]{1,0:T(8,128)S(1)}, u32[]{:S(2)}, u32[]{:S(2)}) collective-permute-start(f32[160,128]{1,0:T(8,128)S(1)} %gradients.1.refs_3_), channel_id=1, source_target_pairs={{0,12},{4,0},{8,4},{12,8},{1,13},{5,1},{9,5},{13,9},{2,14},{6,2},{... | collective-permute-start | bytes 245768 | tf_op jit(solution)/shard_map/ppermute | solution.py:330
  13.4 7.0 %collective-permute-start.3 = (f32[160,128]{1,0:T(8,128)S(1)}, f32[160,128]{1,0:T(8,128)S(1)}, u32[]{:S(2)}, u32[]{:S(2)}) collective-permute-start(f32[160,128]{1,0:T(8,128)S(1)} %gradients.1.refs_3_), channel_id=1, source_target_pairs={{0,8},{4,12},{8,0},{12,4},{1,9},{5,13},{9,1},{13,5},{2,10},{6,14},... | collective-permute-start | bytes 245768 | tf_op jit(solution)/shard_map/ppermute | solution.py:330
  13.4 7.0 %collective-permute-start.4 = (f32[160,128]{1,0:T(8,128)S(1)}, f32[160,128]{1,0:T(8,128)S(1)}, u32[]{:S(2)}, u32[]{:S(2)}) collective-permute-start(f32[160,128]{1,0:T(8,128)S(1)} %gradients.1.refs_3_), channel_id=1, source_target_pairs={{0,4},{4,8},{8,12},{12,0},{1,5},{5,9},{9,13},{13,1},{2,6},{6,10},{... | collective-permute-start | bytes 245768 | tf_op jit(solution)/shard_map/ppermute | solution.py:330
  20.8 3.4 %collective-permute-start.5 = (f32[40,128]{1,0:T(8,128)S(1)}, f32[40,128]{1,0:T(8,128)S(1)}, u32[]{:S(2)}, u32[]{:S(2)}) collective-permute-start(f32[40,128]{1,0:T(8,128)S(1)} %grams.1.refs_3_), channel_id=1, source_target_pairs={{0,3},{1,2},{2,1},{3,0},{4,7},{5,6},{6,5},{7,4},{8,11},{9,10},{10,... | collective-permute-start | bytes 61448 | tf_op jit(solution)/shard_map/ppermute | solution.py:321
  21.6 3.8 %collective-permute-start.6 = (f32[40,128]{1,0:T(8,128)S(1)}, f32[40,128]{1,0:T(8,128)S(1)}, u32[]{:S(2)}, u32[]{:S(2)}) collective-permute-start(f32[40,128]{1,0:T(8,128)S(1)} %grams.1.refs_3_), channel_id=1, source_target_pairs={{0,2},{1,3},{2,0},{3,1},{4,6},{5,7},{6,4},{7,5},{8,10},{9,11},{10,... | collective-permute-start | bytes 61448 | tf_op jit(solution)/shard_map/ppermute | solution.py:321
  22.4 3.1 %collective-permute-start.7 = (f32[40,128]{1,0:T(8,128)S(1)}, f32[40,128]{1,0:T(8,128)S(1)}, u32[]{:S(2)}, u32[]{:S(2)}) collective-permute-start(f32[40,128]{1,0:T(8,128)S(1)} %grams.1.refs_3_), channel_id=1, source_target_pairs={{0,1},{1,0},{2,3},{3,2},{4,5},{5,4},{6,7},{7,6},{8,9},{9,8},{10,11... | collective-permute-start | bytes 61448 | tf_op jit(solution)/shard_map/ppermute | solution.py:321

commit v18 on v14

--- a/solution.py
+++ b/solution.py
@@ -276,7 +276,7 @@
 
 def solve_kernel(seqs, *refs):
     parts, out_ref = refs[:-1], refs[-1]
-    packed = (parts[0][...] + parts[1][...]) + (parts[2][...] + parts[3][...])
+    packed = (parts[1][...] + parts[3][...]) + (parts[0][...] + parts[2][...])
     lane = lax.broadcasted_iota(jnp.int32, packed.shape, 1)
     turned = pltpu.roll(packed, seqs, 1)
     both = jnp.concatenate(
@@ -318,10 +318,6 @@
     return lax.ppermute(value, axis, [(i, i ^ m) for i in range(size)])
 
 
-def from_partners(value, axis, size):
-    return [from_partner(value, axis, size, m) for m in reversed(range(1, size))] + [value]
-
-
 def from_all(value, axis, size):
     shifts = [[(i, (i + s) % size) for i in range(size)] for s in range(1, size)]
     return [lax.ppermute(value, axis, shift) for shift in shifts] + [value]
@@ -372,7 +368,7 @@
     if blocks > SMALL:
         return finish_long(message, steps, first, seq_dev)
     partial = grams(place.reshape(1), from_all(message, "dp", blocks), steps, seq_dev)
-    partial = from_partners(partial, "tensor", parts)
+    partial = from_all(partial, "tensor", parts)
     return solve(partial, blocks * seq_dev, blocks * queries.shape[0], seq_dev)
 
 

time: 25.3 us -> 26 us (1.028)
  starting transfers between devices: 11.2 us -> 12.3 us
  waiting for transfers between devices: 8.79 us -> 8.27 us
    ppermute x3 -> x6, starting transfers between devices: 5.93 us -> 8.83 us  [from_all(): return [lax.ppermute(value, axis, shift) for shift in shifts] + [value]]
    ppermute x5 -> x2, waiting for transfers between devices: 4.99 us -> 2.99 us  [from_partner(): return lax.ppermute(value, axis, [(i, i ^ m) for i in range(size)])]
    ppermute x5 -> x2, starting transfers between devices: 5.31 us -> 3.44 us  [from_partner(): return lax.ppermute(value, axis, [(i, i ^ m) for i in range(size)])]
    ppermute x3 -> x6, waiting for transfers between devices: 3.8 us -> 5.28 us  [from_all(): return [lax.ppermute(value, axis, shift) for shift in shifts] + [value]]
  transfers between devices with their start and end apart: 8 -> 8, of which waited for: 7 -> 8; matrix products, arithmetic and copies ran while one was open for 1% -> 1% of each run, Pallas kernels for 1% -> 1%
where the time goes in v18:
time: 26 us; the launch traced here: 25.7 us
  starting transfers between devices  12.3 us (47%)
  waiting for transfers between devices  8.27 us (32%)
  Pallas kernels  4.88 us (19%)
    ppermute x6, starting transfers between devices, from_all(): return [lax.ppermute(value, axis, shift) for shift in shifts] + [value]  8.83 us
    ppermute x6, waiting for transfers between devices, from_all(): return [lax.ppermute(value, axis, shift) for shift in shifts] + [value]  5.28 us
    ppermute x2, starting transfers between devices, from_partner(): return lax.ppermute(value, axis, [(i, i ^ m) for i in range(size)])  3.44 us
    ppermute x2, waiting for transfers between devices, from_partner(): return lax.ppermute(value, axis, [(i, i ^ m) for i in range(size)])  2.99 us
    pallas_call x1, Pallas kernels, project(): pl.pallas_call(functools.partial(project_kernel, own), out_shape=[jax.Sha...  2.19 us
    pallas_call x1, Pallas kernels, solve(): pl.pallas_call(functools.partial(solve_kernel, seqs), out_shape=jax.Shape...  1.81 us
  transfers between devices with their start and end apart: 8, of which 8 were waited for; matrix products, arithmetic and copies ran while one was open for 1% of the time, Pallas kernels for 1%

profile of v18, /device:TPU:0, one launch (start us, length us, event | category | flops | bytes accessed | tf_op | source)
XLA Modules:
  0.0 25.7 jit_solution(2925914390615414785)
XLA Ops:
  0.0 2.2 %project.1 = (f32[96,256]{1,0:T(8,128)S(1)}, f32[96,256]{1,0:T(8,128)S(1)}) custom-call(s32[1]{0:T(128)} %bitcast.1.rank_ref, bf16[2752,256]{1,0:T(8,128)(2,1)} %bitcast.5, bf16[256,1024]{1,0:T(8,128)(2,1)} %g_hbm.1, bf16[64,2752]{1,0:T(8,128)(2,1)} %bitcast.6, bf16[64,1024]{1,0:T(8,128)(2,1)} %bitcast.7), custom_call_target="tpu_custom_call" | custom-call | tf_op jit(solution)/shard_map/project/pallas_call | solution.py:108
  2.2 0.5 %collective-permute-start = (f32[96,256]{1,0:T(8,128)S(1)}, f32[96,256]{1,0:T(8,128)S(1)}, u32[]{:S(2)}, u32[]{:S(2)}) collective-permute-start(f32[96,256]{1,0:T(8,128)S(1)} %get-tuple-element.10), channel_id=1, source_target_pairs={{0,1},{1,0},{2,3},{3,2},{4,5},{5,4},{6,7},{7,6},{8,9},{9,8},{10,11... | collective-permute-start | bytes 294920 | tf_op jit(solution)/shard_map/ppermute | solution.py:318
  2.7 0.0 copy-done.2
  2.8 0.1 convert_reduce_fusion
  2.9 0.8 %collective-permute-done.came_ref = f32[96,256]{1,0:T(8,128)S(1)} collective-permute-done((f32[96,256]{1,0:T(8,128)S(1)}, f32[96,256]{1,0:T(8,128)S(1)}, u32[]{:S(2)}, u32[]{:S(2)}) %collective-permute-start) | collective-permute-done | bytes 98336 | tf_op jit(solution)/shard_map/ppermute | solution.py:318
  3.7 2.9 %collective-permute-start.1 = (f32[64,256]{1,0:T(8,128)S(1)}, f32[64,256]{1,0:T(8,128)S(1)}, u32[]{:S(2)}, u32[]{:S(2)}) collective-permute-start(f32[64,256]{1,0:T(8,128)S(1)} %get-tuple-element.12), channel_id=1, source_target_pairs={{0,2},{1,3},{2,0},{3,1},{4,6},{5,7},{6,4},{7,5},{8,10},{9,11},{10,... | collective-permute-start | bytes 196616 | tf_op jit(solution)/shard_map/ppermute | solution.py:318
  6.6 0.1 fusion.1.weights_ref
  6.7 0.2 pick.1.asked_ref
  6.8 2.2 %collective-permute-done.1.came_ref = f32[64,256]{1,0:T(8,128)S(1)} collective-permute-done((f32[64,256]{1,0:T(8,128)S(1)}, f32[64,256]{1,0:T(8,128)S(1)}, u32[]{:S(2)}, u32[]{:S(2)}) %collective-permute-start.1) | collective-permute-done | bytes 65568 | tf_op jit(solution)/shard_map/ppermute | solution.py:318
  9.0 0.4 %gradients.1.refs_3_ = f32[160,128]{1,0:T(8,128)S(1)} custom-call(f32[16,256]{1,0:T(8,128)S(1)} %fusion.1.weights_ref, f32[64,256]{1,0:T(8,128)S(1)} %get-tuple-element.11.kept_ref, f32[64,256]{1,0:T(8,128)S(1)} %collective-permute-done.1.came_ref, f32[32,128]{1,0:T(8,128)S(1)} %pick.1.asked_ref), custom_call_target="tpu_custom_call" | custom-call | tf_op jit(solution)/shard_map/gradients/pallas_call | solution.py:222
  9.4 2.0 %collective-permute-start.2 = (f32[160,128]{1,0:T(8,128)S(1)}, f32[160,128]{1,0:T(8,128)S(1)}, u32[]{:S(2)}, u32[]{:S(2)}) collective-permute-start(f32[160,128]{1,0:T(8,128)S(1)} %gradients.1.refs_3_), channel_id=1, source_target_pairs={{0,4},{4,8},{8,12},{12,0},{1,5},{5,9},{9,13},{13,1},{2,6},{6,10},{... | collective-permute-start | bytes 245768 | tf_op jit(solution)/shard_map/ppermute | solution.py:323
  11.4 2.6 %collective-permute-start.3 = (f32[160,128]{1,0:T(8,128)S(1)}, f32[160,128]{1,0:T(8,128)S(1)}, u32[]{:S(2)}, u32[]{:S(2)}) collective-permute-start(f32[160,128]{1,0:T(8,128)S(1)} %gradients.1.refs_3_), channel_id=1, source_target_pairs={{0,8},{4,12},{8,0},{12,4},{1,9},{5,13},{9,1},{13,5},{2,10},{6,14},... | collective-permute-start | bytes 245768 | tf_op jit(solution)/shard_map/ppermute | solution.py:323
  14.0 1.3 %collective-permute-start.4 = (f32[160,128]{1,0:T(8,128)S(1)}, f32[160,128]{1,0:T(8,128)S(1)}, u32[]{:S(2)}, u32[]{:S(2)}) collective-permute-start(f32[160,128]{1,0:T(8,128)S(1)} %gradients.1.refs_3_), channel_id=1, source_target_pairs={{0,12},{4,0},{8,4},{12,8},{1,13},{5,1},{9,5},{13,9},{2,14},{6,2},{... | collective-permute-start | bytes 245768 | tf_op jit(solution)/shard_map/ppermute | solution.py:323
  15.3 1.5 %collective-permute-done.2.refs_0_ = f32[160,128]{1,0:T(8,128)S(1)} collective-permute-done((f32[160,128]{1,0:T(8,128)S(1)}, f32[160,128]{1,0:T(8,128)S(1)}, u32[]{:S(2)}, u32[]{:S(2)}) %collective-permute-start.2) | collective-permute-done | bytes 81952 | tf_op jit(solution)/shard_map/ppermute | solution.py:323
  16.8 2.2 %collective-permute-done.3.refs_1_ = f32[160,128]{1,0:T(8,128)S(1)} collective-permute-done((f32[160,128]{1,0:T(8,128)S(1)}, f32[160,128]{1,0:T(8,128)S(1)}, u32[]{:S(2)}, u32[]{:S(2)}) %collective-permute-start.3) | collective-permute-done | bytes 81952 | tf_op jit(solution)/shard_map/ppermute | solution.py:323
  19.0 0.1 collective-permute-done.4.refs_2_
  19.1 0.3 %grams.1.refs_3_ = f32[40,128]{1,0:T(8,128)S(1)} custom-call(s32[1]{0:T(128)} %bitcast.me_ref, f32[160,128]{1,0:T(8,128)S(1)} %collective-permute-done.2.refs_0_, f32[160,128]{1,0:T(8,128)S(1)} %collective-permute-done.3.refs_1_, f32[160,128]{1,0:T(8,128)S(1)} %collective-permute-done.4.refs_2_, f32[160,128]{1,0:T(8,128)S(1)} %gradients.1.refs_3_), custom_call_target="tpu_custom_call" | custom-call | tf_op jit(solution)/shard_map/grams/pallas_call | solution.py:257
  19.5 0.0 collective-permute-start.5
  19.5 1.5 %collective-permute-start.6 = (f32[40,128]{1,0:T(8,128)S(1)}, f32[40,128]{1,0:T(8,128)S(1)}, u32[]{:S(2)}, u32[]{:S(2)}) collective-permute-start(f32[40,128]{1,0:T(8,128)S(1)} %grams.1.refs_3_), channel_id=1, source_target_pairs={{0,2},{1,3},{2,0},{3,1},{4,6},{5,7},{6,4},{7,5},{8,10},{9,11},{10,... | collective-permute-start | bytes 61448 | tf_op jit(solution)/shard_map/ppermute | solution.py:323
  21.0 1.4 %collective-permute-start.7 = (f32[40,128]{1,0:T(8,128)S(1)}, f32[40,128]{1,0:T(8,128)S(1)}, u32[]{:S(2)}, u32[]{:S(2)}) collective-permute-start(f32[40,128]{1,0:T(8,128)S(1)} %grams.1.refs_3_), channel_id=1, source_target_pairs={{0,3},{1,0},{2,1},{3,2},{4,7},{5,4},{6,5},{7,6},{8,11},{9,8},{10,9... | collective-permute-start | bytes 61448 | tf_op jit(solution)/shard_map/ppermute | solution.py:323
  22.4 0.3 %collective-permute-done.5.refs_0_ = f32[40,128]{1,0:T(8,128)S(1)} collective-permute-done((f32[40,128]{1,0:T(8,128)S(1)}, f32[40,128]{1,0:T(8,128)S(1)}, u32[]{:S(2)}, u32[]{:S(2)}) %collective-permute-start.5) | collective-permute-done | bytes 20512 | tf_op jit(solution)/shard_map/ppermute | solution.py:323
  22.7 0.6 %collective-permute-done.6.refs_1_ = f32[40,128]{1,0:T(8,128)S(1)} collective-permute-done((f32[40,128]{1,0:T(8,128)S(1)}, f32[40,128]{1,0:T(8,128)S(1)}, u32[]{:S(2)}, u32[]{:S(2)}) %collective-permute-start.6) | collective-permute-done | bytes 20512 | tf_op jit(solution)/shard_map/ppermute | solution.py:323
  23.3 0.5 %collective-permute-done.7.refs_2_ = f32[40,128]{1,0:T(8,128)S(1)} collective-permute-done((f32[40,128]{1,0:T(8,128)S(1)}, f32[40,128]{1,0:T(8,128)S(1)}, u32[]{:S(2)}, u32[]{:S(2)}) %collective-permute-start.7) | collective-permute-done | bytes 20512 | tf_op jit(solution)/shard_map/ppermute | solution.py:323
  23.9 1.8 %solve.1 = f32[16,16]{1,0:T(8,128)} custom-call(f32[40,128]{1,0:T(8,128)S(1)} %collective-permute-done.5.refs_0_, f32[40,128]{1,0:T(8,128)S(1)} %collective-permute-done.6.refs_1_, f32[40,128]{1,0:T(8,128)S(1)} %collective-permute-done.7.refs_2_, f32[40,128]{1,0:T(8,128)S(1)} %grams.1.refs_3_), custom_call_target="tpu_custom_call" | custom-call | tf_op jit(solution)/shard_map/solve/pallas_call | solution.py:309
  (8 shorter events, 0.0 us)
Async XLA Ops:
  0.0 2.7 %copy-start.2 = (s32[16]{0:T(128)S(1)}, s32[16]{0:T(128)}, u32[]{:S(2)}) copy-start(s32[16]{0:T(128)} %param.12) | copy-start | bytes 196
  0.0 2.8 %copy-start.1 = (s32[256]{0:T(256)S(1)}, s32[256]{0:T(256)}, u32[]{:S(2)}) copy-start(s32[256]{0:T(256)} %param.11) | copy-start | bytes 3076
  0.0 6.7 %copy-start = (f32[4,4096]{1,0:T(4,128)S(1)}, f32[4,4096]{1,0:T(4,128)}, u32[]{:S(2)}) copy-start(f32[4,4096]{1,0:T(4,128)} %queries_ref.1) | copy-start | bytes 196612
  2.2 1.5 %collective-permute-start = (f32[96,256]{1,0:T(8,128)S(1)}, f32[96,256]{1,0:T(8,128)S(1)}, u32[]{:S(2)}, u32[]{:S(2)}) collective-permute-start(f32[96,256]{1,0:T(8,128)S(1)} %get-tuple-element.10), channel_id=1, source_target_pairs={{0,1},{1,0},{2,3},{3,2},{4,5},{5,4},{6,7},{7,6},{8,9},{9,8},{10,11... | collective-permute-start | bytes 294920 | tf_op jit(solution)/shard_map/ppermute | solution.py:318
  3.7 5.3 %collective-permute-start.1 = (f32[64,256]{1,0:T(8,128)S(1)}, f32[64,256]{1,0:T(8,128)S(1)}, u32[]{:S(2)}, u32[]{:S(2)}) collective-permute-start(f32[64,256]{1,0:T(8,128)S(1)} %get-tuple-element.12), channel_id=1, source_target_pairs={{0,2},{1,3},{2,0},{3,1},{4,6},{5,7},{6,4},{7,5},{8,10},{9,11},{10,... | collective-permute-start | bytes 196616 | tf_op jit(solution)/shard_map/ppermute | solution.py:318
  9.4 7.4 %collective-permute-start.2 = (f32[160,128]{1,0:T(8,128)S(1)}, f32[160,128]{1,0:T(8,128)S(1)}, u32[]{:S(2)}, u32[]{:S(2)}) collective-permute-start(f32[160,128]{1,0:T(8,128)S(1)} %gradients.1.refs_3_), channel_id=1, source_target_pairs={{0,4},{4,8},{8,12},{12,0},{1,5},{5,9},{9,13},{13,1},{2,6},{6,10},{... | collective-permute-start | bytes 245768 | tf_op jit(solution)/shard_map/ppermute | solution.py:323
  11.4 7.6 %collective-permute-start.3 = (f32[160,128]{1,0:T(8,128)S(1)}, f32[160,128]{1,0:T(8,128)S(1)}, u32[]{:S(2)}, u32[]{:S(2)}) collective-permute-start(f32[160,128]{1,0:T(8,128)S(1)} %gradients.1.refs_3_), channel_id=1, source_target_pairs={{0,8},{4,12},{8,0},{12,4},{1,9},{5,13},{9,1},{13,5},{2,10},{6,14},... | collective-permute-start | bytes 245768 | tf_op jit(solution)/shard_map/ppermute | solution.py:323
  14.0 5.1 %collective-permute-start.4 = (f32[160,128]{1,0:T(8,128)S(1)}, f32[160,128]{1,0:T(8,128)S(1)}, u32[]{:S(2)}, u32[]{:S(2)}) collective-permute-start(f32[160,128]{1,0:T(8,128)S(1)} %gradients.1.refs_3_), channel_id=1, source_target_pairs={{0,12},{4,0},{8,4},{12,8},{1,13},{5,1},{9,5},{13,9},{2,14},{6,2},{... | collective-permute-start | bytes 245768 | tf_op jit(solution)/shard_map/ppermute | solution.py:323
  19.5 3.2 %collective-permute-start.5 = (f32[40,128]{1,0:T(8,128)S(1)}, f32[40,128]{1,0:T(8,128)S(1)}, u32[]{:S(2)}, u32[]{:S(2)}) collective-permute-start(f32[40,128]{1,0:T(8,128)S(1)} %grams.1.refs_3_), channel_id=1, source_target_pairs={{0,1},{1,2},{2,3},{3,0},{4,5},{5,6},{6,7},{7,4},{8,9},{9,10},{10,1... | collective-permute-start | bytes 61448 | tf_op jit(solution)/shard_map/ppermute | solution.py:323
  19.5 3.8 %collective-permute-start.6 = (f32[40,128]{1,0:T(8,128)S(1)}, f32[40,128]{1,0:T(8,128)S(1)}, u32[]{:S(2)}, u32[]{:S(2)}) collective-permute-start(f32[40,128]{1,0:T(8,128)S(1)} %grams.1.refs_3_), channel_id=1, source_target_pairs={{0,2},{1,3},{2,0},{3,1},{4,6},{5,7},{6,4},{7,5},{8,10},{9,11},{10,... | collective-permute-start | bytes 61448 | tf_op jit(solution)/shard_map/ppermute | solution.py:323
  21.0 2.9 %collective-permute-start.7 = (f32[40,128]{1,0:T(8,128)S(1)}, f32[40,128]{1,0:T(8,128)S(1)}, u32[]{:S(2)}, u32[]{:S(2)}) collective-permute-start(f32[40,128]{1,0:T(8,128)S(1)} %grams.1.refs_3_), channel_id=1, source_target_pairs={{0,3},{1,0},{2,1},{3,2},{4,7},{5,4},{6,5},{7,6},{8,11},{9,8},{10,9... | collective-permute-start | bytes 61448 | tf_op jit(solution)/shard_map/ppermute | solution.py:323

commit v19 on v14

--- a/solution.py
+++ b/solution.py
@@ -19,7 +19,8 @@
     starts = jnp.sum((local_ids[None, :] < slots[:, None]).astype(jnp.int32), axis=1)
     offset = jnp.arange(seq_ids.shape[0], dtype=jnp.int32)[None, :] - starts[:, None]
     scale = 1.0 / counts.astype(jnp.float32)
-    return jnp.where(member & (offset < counts[:, None]), scale[:, None], 0.0)
+    scale = jnp.sum(jnp.where(member, scale[:, None], 0.0), axis=0, keepdims=True)
+    return jnp.where(member & (offset < counts[:, None]), 1.0, 0.0).astype(jnp.bfloat16), scale
 
 
 def cuts_of(extent, step):
@@ -33,9 +34,11 @@
 
 
 def dot_nt(left, right):
-    rows = left.shape[0]
-    lh, ll = two_terms(left)
-    rh, rl = two_terms(right)
+    return product_nt(*two_terms(left), *two_terms(right))
+
+
+def product_nt(lh, ll, rh, rl):
+    rows = lh.shape[0]
     mul = functools.partial(
         lax.dot_general,
         dimension_numbers=(((1,), (1,)), ((), ())),
@@ -187,44 +190,46 @@
     )(me, queries)
 
 
-def grads_kernel(weights_ref, kept_ref, came_ref, asked_ref, out_ref):
+def grads_kernel(member_ref, scale_ref, kept_ref, came_ref, asked_ref, out_ref):
     summed = kept_ref[...] + came_ref[...]
-    weights = weights_ref[...]
+    member = member_ref[...]
     own = summed.shape[0] // 2
     group = out_ref.shape[1] // own
-    inputs_t = summed[own:, :]
-    zero = jnp.zeros_like(inputs_t)
-    right = jnp.concatenate(
-        [
-            jnp.concatenate([inputs_t if j == k else zero for k in range(group)], axis=1)
+    inputs_t = summed[own:, :] * scale_ref[...]
+    zero = jnp.zeros(inputs_t.shape, jnp.bfloat16)
+
+    def diagonal(term):
+        rows = [
+            jnp.concatenate([term if j == k else zero for k in range(group)], axis=1)
             for j in range(group)
-        ],
-        axis=0,
-    )
-    rows = []
-    for i in range(own // group):
-        rows.append(
-            jnp.concatenate(
-                [weights * summed[group * i + j : group * i + j + 1, :] for j in range(group)],
-                axis=1,
-            )
-        )
-    left = jnp.concatenate(rows, axis=0)
-    count = left.shape[0]
-    out_ref[:count, :] = dot_nt(left, right)
+        ]
+        return jnp.concatenate(rows, axis=0)
+
+    def spread(term):
+        rows = [
+            jnp.concatenate([member * term[i + j : i + j + 1, :] for j in range(group)], axis=1)
+            for i in range(0, own, group)
+        ]
+        return jnp.concatenate(rows, axis=0)
+
+    lh, ll = (spread(term) for term in two_terms(summed[:own, :]))
+    rh, rl = (diagonal(term) for term in two_terms(inputs_t))
+    made = product_nt(lh, ll, rh, rl)
+    count = made.shape[0]
+    out_ref[:count, :] = made
     out_ref[count:, :] = asked_ref[...]
 
 
 def gradients(weights, kept, came, asked):
     lanes = asked.shape[1]
     own = kept.shape[0] // 2
-    rows = own * own // lanes * weights.shape[0] + asked.shape[0]
+    rows = own * own // lanes * weights[0].shape[0] + asked.shape[0]
     return pl.pallas_call(
         grads_kernel,
         out_shape=jax.ShapeDtypeStruct((rows, lanes), jnp.float32),
         compiler_params=pltpu.CompilerParams(vmem_limit_bytes=VMEM_LIMIT),
         name="gradients",
-    )(weights, kept, came, asked)
+    )(*weights, kept, came, asked)
 
 
 def grams_kernel(steps, seqs, me_ref, *refs):
@@ -293,14 +298,13 @@
         high = state.astype(jnp.bfloat16).astype(jnp.float32)
         low = state - high
         left = jnp.where(left_lanes, high, low).astype(jnp.bfloat16)
+        left = jnp.concatenate([left, high[:, :seqs].astype(jnp.bfloat16)], axis=1)
         high = high[:seqs].astype(jnp.bfloat16)
         low = low[:seqs].astype(jnp.bfloat16)
-        right = jnp.concatenate([high, high, low, low], axis=0)
+        right = jnp.concatenate([high, high, low], axis=0)
         if at + 1 == len(steps):
             left, state = left[seqs:], state[seqs:]
-        product = jnp.dot(
-            jnp.concatenate([left, left], axis=1), right, preferred_element_type=jnp.float32
-        )
+        product = jnp.dot(left, right, preferred_element_type=jnp.float32)
         state = step * (2.0 * state - product)
     out_ref[...] = state[:, : out_ref.shape[1]]
 

time: 25.3 us -> 25.3 us (level)
  no operation moved by 1% of the time
where the time goes in v19:
time: 25.3 us; the launch traced here: 25.2 us
  starting transfers between devices  11.2 us (44%)
  waiting for transfers between devices  8.76 us (35%)
  Pallas kernels  4.9 us (19%)
    ppermute x3, starting transfers between devices, from_all(): return [lax.ppermute(value, axis, shift) for shift in shifts] + [value]  5.93 us
    ppermute x5, starting transfers between devices, from_partner(): return lax.ppermute(value, axis, [(i, i ^ m) for i in range(size)])  5.31 us
    ppermute x5, waiting for transfers between devices, from_partner(): return lax.ppermute(value, axis, [(i, i ^ m) for i in range(size)])  4.97 us
    ppermute x3, waiting for transfers between devices, from_all(): return [lax.ppermute(value, axis, shift) for shift in shifts] + [value]  3.79 us
    pallas_call x1, Pallas kernels, project(): pl.pallas_call(functools.partial(project_kernel, own), out_shape=[jax.Sha...  2.19 us
    pallas_call x1, Pallas kernels, solve(): pl.pallas_call(functools.partial(solve_kernel, seqs), out_shape=jax.Shape...  1.84 us
  transfers between devices with their start and end apart: 8, of which 7 were waited for; matrix products, arithmetic and copies ran while one was open for 1% of the time, Pallas kernels for 1%

profile of v19, /device:TPU:0, one launch (start us, length us, event | category | flops | bytes accessed | tf_op | source)
XLA Modules:
  0.0 25.2 jit_solution(2066900295291374219)
XLA Ops:
  0.0 2.2 %project.1 = (f32[96,256]{1,0:T(8,128)S(1)}, f32[96,256]{1,0:T(8,128)S(1)}) custom-call(s32[1]{0:T(128)} %bitcast.2.rank_ref, bf16[2752,256]{1,0:T(8,128)(2,1)} %bitcast.7, bf16[256,1024]{1,0:T(8,128)(2,1)} %g_hbm.1, bf16[64,2752]{1,0:T(8,128)(2,1)} %bitcast.8, bf16[64,1024]{1,0:T(8,128)(2,1)} %bitcast.9), custom_call_target="tpu_custom_call" | custom-call | tf_op jit(solution)/shard_map/project/pallas_call | solution.py:111
  2.2 0.5 %collective-permute-start = (f32[96,256]{1,0:T(8,128)S(1)}, f32[96,256]{1,0:T(8,128)S(1)}, u32[]{:S(2)}, u32[]{:S(2)}) collective-permute-start(f32[96,256]{1,0:T(8,128)S(1)} %get-tuple-element.10), channel_id=1, source_target_pairs={{0,1},{1,0},{2,3},{3,2},{4,5},{5,4},{6,7},{7,6},{8,9},{9,8},{10,11... | collective-permute-start | bytes 294920 | tf_op jit(solution)/shard_map/ppermute | solution.py:322
  2.7 0.0 copy-done.2
  2.8 0.1 convert_reduce_fusion
  2.9 0.8 %collective-permute-done.came_ref = f32[96,256]{1,0:T(8,128)S(1)} collective-permute-done((f32[96,256]{1,0:T(8,128)S(1)}, f32[96,256]{1,0:T(8,128)S(1)}, u32[]{:S(2)}, u32[]{:S(2)}) %collective-permute-start) | collective-permute-done | bytes 98336 | tf_op jit(solution)/shard_map/ppermute | solution.py:322
  3.7 2.9 %collective-permute-start.1 = (f32[64,256]{1,0:T(8,128)S(1)}, f32[64,256]{1,0:T(8,128)S(1)}, u32[]{:S(2)}, u32[]{:S(2)}) collective-permute-start(f32[64,256]{1,0:T(8,128)S(1)} %get-tuple-element.12), channel_id=1, source_target_pairs={{0,2},{1,3},{2,0},{3,1},{4,6},{5,7},{6,4},{7,5},{8,10},{9,11},{10,... | collective-permute-start | bytes 196616 | tf_op jit(solution)/shard_map/ppermute | solution.py:322
  6.6 0.1 select_reduce_fusion
  6.7 0.2 pick.1.asked_ref
  6.9 2.2 %collective-permute-done.1.came_ref = f32[64,256]{1,0:T(8,128)S(1)} collective-permute-done((f32[64,256]{1,0:T(8,128)S(1)}, f32[64,256]{1,0:T(8,128)S(1)}, u32[]{:S(2)}, u32[]{:S(2)}) %collective-permute-start.1) | collective-permute-done | bytes 65568 | tf_op jit(solution)/shard_map/ppermute | solution.py:322
  9.0 0.4 %gradients.1.refs_3_ = f32[160,128]{1,0:T(8,128)S(1)} custom-call(bf16[16,256]{1,0:T(8,128)(2,1)S(1)} %get-tuple-element.14.member_ref, f32[1,256]{1,0:T(1,128)S(1)} %bitcast.6, f32[64,256]{1,0:T(8,128)S(1)} %get-tuple-element.11.kept_ref, f32[64,256]{1,0:T(8,128)S(1)} %collective-permute-done.1.came_ref, f32[32,128]{1,0:T(8,128)S(1)} %pick.1.asked_ref), custom_call_target="tpu_custom_call" | custom-call | tf_op jit(solution)/shard_map/gradients/pallas_call | solution.py:227
  9.4 2.0 %collective-permute-start.2 = (f32[160,128]{1,0:T(8,128)S(1)}, f32[160,128]{1,0:T(8,128)S(1)}, u32[]{:S(2)}, u32[]{:S(2)}) collective-permute-start(f32[160,128]{1,0:T(8,128)S(1)} %gradients.1.refs_3_), channel_id=1, source_target_pairs={{0,4},{4,8},{8,12},{12,0},{1,5},{5,9},{9,13},{13,1},{2,6},{6,10},{... | collective-permute-start | bytes 245768 | tf_op jit(solution)/shard_map/ppermute | solution.py:331
  11.4 2.6 %collective-permute-start.3 = (f32[160,128]{1,0:T(8,128)S(1)}, f32[160,128]{1,0:T(8,128)S(1)}, u32[]{:S(2)}, u32[]{:S(2)}) collective-permute-start(f32[160,128]{1,0:T(8,128)S(1)} %gradients.1.refs_3_), channel_id=1, source_target_pairs={{0,8},{4,12},{8,0},{12,4},{1,9},{5,13},{9,1},{13,5},{2,10},{6,14},... | collective-permute-start | bytes 245768 | tf_op jit(solution)/shard_map/ppermute | solution.py:331
  14.0 1.4 %collective-permute-start.4 = (f32[160,128]{1,0:T(8,128)S(1)}, f32[160,128]{1,0:T(8,128)S(1)}, u32[]{:S(2)}, u32[]{:S(2)}) collective-permute-start(f32[160,128]{1,0:T(8,128)S(1)} %gradients.1.refs_3_), channel_id=1, source_target_pairs={{0,12},{4,0},{8,4},{12,8},{1,13},{5,1},{9,5},{13,9},{2,14},{6,2},{... | collective-permute-start | bytes 245768 | tf_op jit(solution)/shard_map/ppermute | solution.py:331
  15.3 1.5 %collective-permute-done.2.refs_0_ = f32[160,128]{1,0:T(8,128)S(1)} collective-permute-done((f32[160,128]{1,0:T(8,128)S(1)}, f32[160,128]{1,0:T(8,128)S(1)}, u32[]{:S(2)}, u32[]{:S(2)}) %collective-permute-start.2) | collective-permute-done | bytes 81952 | tf_op jit(solution)/shard_map/ppermute | solution.py:331
  16.8 2.2 %collective-permute-done.3.refs_1_ = f32[160,128]{1,0:T(8,128)S(1)} collective-permute-done((f32[160,128]{1,0:T(8,128)S(1)}, f32[160,128]{1,0:T(8,128)S(1)}, u32[]{:S(2)}, u32[]{:S(2)}) %collective-permute-start.3) | collective-permute-done | bytes 81952 | tf_op jit(solution)/shard_map/ppermute | solution.py:331
  19.0 0.1 collective-permute-done.4.refs_2_
  19.1 0.3 %grams.1.refs_3_ = f32[40,128]{1,0:T(8,128)S(1)} custom-call(s32[1]{0:T(128)} %bitcast.me_ref, f32[160,128]{1,0:T(8,128)S(1)} %collective-permute-done.2.refs_0_, f32[160,128]{1,0:T(8,128)S(1)} %collective-permute-done.3.refs_1_, f32[160,128]{1,0:T(8,128)S(1)} %collective-permute-done.4.refs_2_, f32[160,128]{1,0:T(8,128)S(1)} %gradients.1.refs_3_), custom_call_target="tpu_custom_call" | custom-call | tf_op jit(solution)/shard_map/grams/pallas_call | solution.py:262
  19.5 0.0 collective-permute-start.5
  19.5 1.5 %collective-permute-start.6 = (f32[40,128]{1,0:T(8,128)S(1)}, f32[40,128]{1,0:T(8,128)S(1)}, u32[]{:S(2)}, u32[]{:S(2)}) collective-permute-start(f32[40,128]{1,0:T(8,128)S(1)} %grams.1.refs_3_), channel_id=1, source_target_pairs={{0,2},{1,3},{2,0},{3,1},{4,6},{5,7},{6,4},{7,5},{8,10},{9,11},{10,... | collective-permute-start | bytes 61448 | tf_op jit(solution)/shard_map/ppermute | solution.py:322
  21.0 0.3 %collective-permute-start.7 = (f32[40,128]{1,0:T(8,128)S(1)}, f32[40,128]{1,0:T(8,128)S(1)}, u32[]{:S(2)}, u32[]{:S(2)}) collective-permute-start(f32[40,128]{1,0:T(8,128)S(1)} %grams.1.refs_3_), channel_id=1, source_target_pairs={{0,1},{1,0},{2,3},{3,2},{4,5},{5,4},{6,7},{7,6},{8,9},{9,8},{10,11... | collective-permute-start | bytes 61448 | tf_op jit(solution)/shard_map/ppermute | solution.py:322
  21.3 1.6 %collective-permute-done.5.refs_0_ = f32[40,128]{1,0:T(8,128)S(1)} collective-permute-done((f32[40,128]{1,0:T(8,128)S(1)}, f32[40,128]{1,0:T(8,128)S(1)}, u32[]{:S(2)}, u32[]{:S(2)}) %collective-permute-start.5) | collective-permute-done | bytes 20512 | tf_op jit(solution)/shard_map/ppermute | solution.py:322
  22.9 0.4 %collective-permute-done.6.refs_1_ = f32[40,128]{1,0:T(8,128)S(1)} collective-permute-done((f32[40,128]{1,0:T(8,128)S(1)}, f32[40,128]{1,0:T(8,128)S(1)}, u32[]{:S(2)}, u32[]{:S(2)}) %collective-permute-start.6) | collective-permute-done | bytes 20512 | tf_op jit(solution)/shard_map/ppermute | solution.py:322
  23.3 0.0 collective-permute-done.7.refs_2_
  23.3 1.8 %solve.1 = f32[16,16]{1,0:T(8,128)} custom-call(f32[40,128]{1,0:T(8,128)S(1)} %collective-permute-done.5.refs_0_, f32[40,128]{1,0:T(8,128)S(1)} %collective-permute-done.6.refs_1_, f32[40,128]{1,0:T(8,128)S(1)} %collective-permute-done.7.refs_2_, f32[40,128]{1,0:T(8,128)S(1)} %grams.1.refs_3_), custom_call_target="tpu_custom_call" | custom-call | tf_op jit(solution)/shard_map/solve/pallas_call | solution.py:313
  (8 shorter events, 0.0 us)
Async XLA Ops:
  0.0 2.7 %copy-start.2 = (s32[16]{0:T(128)S(1)}, s32[16]{0:T(128)}, u32[]{:S(2)}) copy-start(s32[16]{0:T(128)} %param.12) | copy-start | bytes 196
  0.0 2.8 %copy-start.1 = (s32[256]{0:T(256)S(1)}, s32[256]{0:T(256)}, u32[]{:S(2)}) copy-start(s32[256]{0:T(256)} %param.11) | copy-start | bytes 3076
  0.0 6.7 %copy-start = (f32[4,4096]{1,0:T(4,128)S(1)}, f32[4,4096]{1,0:T(4,128)}, u32[]{:S(2)}) copy-start(f32[4,4096]{1,0:T(4,128)} %queries_ref.1) | copy-start | bytes 196612
  2.2 1.5 %collective-permute-start = (f32[96,256]{1,0:T(8,128)S(1)}, f32[96,256]{1,0:T(8,128)S(1)}, u32[]{:S(2)}, u32[]{:S(2)}) collective-permute-start(f32[96,256]{1,0:T(8,128)S(1)} %get-tuple-element.10), channel_id=1, source_target_pairs={{0,1},{1,0},{2,3},{3,2},{4,5},{5,4},{6,7},{7,6},{8,9},{9,8},{10,11... | collective-permute-start | bytes 294920 | tf_op jit(solution)/shard_map/ppermute | solution.py:322
  3.7 5.3 %collective-permute-start.1 = (f32[64,256]{1,0:T(8,128)S(1)}, f32[64,256]{1,0:T(8,128)S(1)}, u32[]{:S(2)}, u32[]{:S(2)}) collective-permute-start(f32[64,256]{1,0:T(8,128)S(1)} %get-tuple-element.12), channel_id=1, source_target_pairs={{0,2},{1,3},{2,0},{3,1},{4,6},{5,7},{6,4},{7,5},{8,10},{9,11},{10,... | collective-permute-start | bytes 196616 | tf_op jit(solution)/shard_map/ppermute | solution.py:322
  9.4 7.4 %collective-permute-start.2 = (f32[160,128]{1,0:T(8,128)S(1)}, f32[160,128]{1,0:T(8,128)S(1)}, u32[]{:S(2)}, u32[]{:S(2)}) collective-permute-start(f32[160,128]{1,0:T(8,128)S(1)} %gradients.1.refs_3_), channel_id=1, source_target_pairs={{0,4},{4,8},{8,12},{12,0},{1,5},{5,9},{9,13},{13,1},{2,6},{6,10},{... | collective-permute-start | bytes 245768 | tf_op jit(solution)/shard_map/ppermute | solution.py:331
  11.4 7.6 %collective-permute-start.3 = (f32[160,128]{1,0:T(8,128)S(1)}, f32[160,128]{1,0:T(8,128)S(1)}, u32[]{:S(2)}, u32[]{:S(2)}) collective-permute-start(f32[160,128]{1,0:T(8,128)S(1)} %gradients.1.refs_3_), channel_id=1, source_target_pairs={{0,8},{4,12},{8,0},{12,4},{1,9},{5,13},{9,1},{13,5},{2,10},{6,14},... | collective-permute-start | bytes 245768 | tf_op jit(solution)/shard_map/ppermute | solution.py:331
  14.0 5.1 %collective-permute-start.4 = (f32[160,128]{1,0:T(8,128)S(1)}, f32[160,128]{1,0:T(8,128)S(1)}, u32[]{:S(2)}, u32[]{:S(2)}) collective-permute-start(f32[160,128]{1,0:T(8,128)S(1)} %gradients.1.refs_3_), channel_id=1, source_target_pairs={{0,12},{4,0},{8,4},{12,8},{1,13},{5,1},{9,5},{13,9},{2,14},{6,2},{... | collective-permute-start | bytes 245768 | tf_op jit(solution)/shard_map/ppermute | solution.py:331
  19.5 3.4 %collective-permute-start.5 = (f32[40,128]{1,0:T(8,128)S(1)}, f32[40,128]{1,0:T(8,128)S(1)}, u32[]{:S(2)}, u32[]{:S(2)}) collective-permute-start(f32[40,128]{1,0:T(8,128)S(1)} %grams.1.refs_3_), channel_id=1, source_target_pairs={{0,3},{1,2},{2,1},{3,0},{4,7},{5,6},{6,5},{7,4},{8,11},{9,10},{10,... | collective-permute-start | bytes 61448 | tf_op jit(solution)/shard_map/ppermute | solution.py:322
  19.5 3.8 %collective-permute-start.6 = (f32[40,128]{1,0:T(8,128)S(1)}, f32[40,128]{1,0:T(8,128)S(1)}, u32[]{:S(2)}, u32[]{:S(2)}) collective-permute-start(f32[40,128]{1,0:T(8,128)S(1)} %grams.1.refs_3_), channel_id=1, source_target_pairs={{0,2},{1,3},{2,0},{3,1},{4,6},{5,7},{6,4},{7,5},{8,10},{9,11},{10,... | collective-permute-start | bytes 61448 | tf_op jit(solution)/shard_map/ppermute | solution.py:322
  21.0 2.3 %collective-permute-start.7 = (f32[40,128]{1,0:T(8,128)S(1)}, f32[40,128]{1,0:T(8,128)S(1)}, u32[]{:S(2)}, u32[]{:S(2)}) collective-permute-start(f32[40,128]{1,0:T(8,128)S(1)} %grams.1.refs_3_), channel_id=1, source_target_pairs={{0,1},{1,0},{2,3},{3,2},{4,5},{5,4},{6,7},{7,6},{8,9},{9,8},{10,11... | collective-permute-start | bytes 61448 | tf_op jit(solution)/shard_map/ppermute | solution.py:322

commit v20 on v14

--- a/solution.py
+++ b/solution.py
@@ -10,6 +10,7 @@
 damping = 0.5
 VMEM_LIMIT = 32 * 1024 * 1024
 SMALL = 4
+SOURCES = {1: (), 2: ((1, 0),), 4: ((3, 2, 1, 0), (2, 0, 3, 1), (1, 3, 0, 2))}
 
 
 def token_weights(seq_ids, counts, first):
@@ -228,16 +229,16 @@
 
 
 def grams_kernel(steps, seqs, me_ref, *refs):
-    blocks, out_ref = refs[-2::-1], refs[-1]
+    blocks, out_ref = (refs[-2], *refs[:-2]), refs[-1]
     count = steps * seqs
     asked = (blocks[0].shape[0] - count) // steps
     given = [block[count:, :] for block in blocks]
     ordered = []
     for place in range(len(blocks)):
         chosen = given[0]
-        for m in range(1, len(blocks)):
-            ahead = lax.rem(place - me_ref[0] + len(blocks), len(blocks))
-            chosen = jnp.where(ahead == m, given[m], chosen)
+        for m, sources in enumerate(SOURCES[len(blocks)]):
+            source = sum(jnp.where(me_ref[0] == i, j, 0) for i, j in enumerate(sources))
+            chosen = jnp.where(source == place, given[m + 1], chosen)
         ordered.append(chosen)
     lanes = []
     for i in range(steps):
@@ -323,8 +324,8 @@
 
 
 def from_all(value, axis, size):
-    shifts = [[(i, (i + s) % size) for i in range(size)] for s in range(1, size)]
-    return [lax.ppermute(value, axis, shift) for shift in shifts] + [value]
+    swaps = [[(source, i) for i, source in enumerate(sources)] for sources in SOURCES[size]]
+    return [lax.ppermute(value, axis, swap) for swap in swaps] + [value]
 
 
 def finish_long(message, steps, first, seq_dev):

time: 25.3 us -> 25.9 us (1.024)
  starting transfers between devices: 11.2 us -> 12.3 us
  waiting for transfers between devices: 8.79 us -> 8.3 us
    ppermute x3, starting transfers between devices: 5.93 us -> 6.95 us  [from_all(): return [lax.ppermute(value, axis, swap) for swap in swaps] + [value]]
    ppermute x3, waiting for transfers between devices: 3.8 us -> 3.31 us  [from_all(): return [lax.ppermute(value, axis, swap) for swap in swaps] + [value]]
  transfers between devices with their start and end apart: 8 -> 8, of which waited for: 7 -> 6; matrix products, arithmetic and copies ran while one was open for 1% -> 1% of each run, Pallas kernels for 1% -> 1%
where the time goes in v20:
time: 25.9 us; the launch traced here: 25.7 us
  starting transfers between devices  12.3 us (47%)
  waiting for transfers between devices  8.3 us (32%)
  Pallas kernels  4.88 us (19%)
    ppermute x3, starting transfers between devices, from_all(): return [lax.ppermute(value, axis, swap) for swap in swaps] + [value]  6.95 us
    ppermute x5, starting transfers between devices, from_partner(): return lax.ppermute(value, axis, [(i, i ^ m) for i in range(size)])  5.31 us
    ppermute x5, waiting for transfers between devices, from_partner(): return lax.ppermute(value, axis, [(i, i ^ m) for i in range(size)])  4.99 us
    ppermute x3, waiting for transfers between devices, from_all(): return [lax.ppermute(value, axis, swap) for swap in swaps] + [value]  3.31 us
    pallas_call x1, Pallas kernels, project(): pl.pallas_call(functools.partial(project_kernel, own), out_shape=[jax.Sha...  2.19 us
    pallas_call x1, Pallas kernels, solve(): pl.pallas_call(functools.partial(solve_kernel, seqs), out_shape=jax.Shape...  1.82 us
  transfers between devices with their start and end apart: 8, of which 6 were waited for; matrix products, arithmetic and copies ran while one was open for 1% of the time, Pallas kernels for 1%

profile of v20, /device:TPU:0, one launch (start us, length us, event | category | flops | bytes accessed | tf_op | source)
XLA Modules:
  0.0 25.7 jit_solution(4134051911053257307)
XLA Ops:
  0.0 2.2 %project.1 = (f32[96,256]{1,0:T(8,128)S(1)}, f32[96,256]{1,0:T(8,128)S(1)}) custom-call(s32[1]{0:T(128)} %bitcast.1.rank_ref, bf16[2752,256]{1,0:T(8,128)(2,1)} %bitcast.5, bf16[256,1024]{1,0:T(8,128)(2,1)} %g_hbm.1, bf16[64,2752]{1,0:T(8,128)(2,1)} %bitcast.6, bf16[64,1024]{1,0:T(8,128)(2,1)} %bitcast.7), custom_call_target="tpu_custom_call" | custom-call | tf_op jit(solution)/shard_map/project/pallas_call | solution.py:109
  2.2 0.5 %collective-permute-start = (f32[96,256]{1,0:T(8,128)S(1)}, f32[96,256]{1,0:T(8,128)S(1)}, u32[]{:S(2)}, u32[]{:S(2)}) collective-permute-start(f32[96,256]{1,0:T(8,128)S(1)} %get-tuple-element.10), channel_id=1, source_target_pairs={{0,1},{1,0},{2,3},{3,2},{4,5},{5,4},{6,7},{7,6},{8,9},{9,8},{10,11... | collective-permute-start | bytes 294920 | tf_op jit(solution)/shard_map/ppermute | solution.py:319
  2.7 0.0 copy-done.2
  2.8 0.1 convert_reduce_fusion
  2.9 0.8 %collective-permute-done.came_ref = f32[96,256]{1,0:T(8,128)S(1)} collective-permute-done((f32[96,256]{1,0:T(8,128)S(1)}, f32[96,256]{1,0:T(8,128)S(1)}, u32[]{:S(2)}, u32[]{:S(2)}) %collective-permute-start) | collective-permute-done | bytes 98336 | tf_op jit(solution)/shard_map/ppermute | solution.py:319
  3.7 2.9 %collective-permute-start.1 = (f32[64,256]{1,0:T(8,128)S(1)}, f32[64,256]{1,0:T(8,128)S(1)}, u32[]{:S(2)}, u32[]{:S(2)}) collective-permute-start(f32[64,256]{1,0:T(8,128)S(1)} %get-tuple-element.12), channel_id=1, source_target_pairs={{0,2},{1,3},{2,0},{3,1},{4,6},{5,7},{6,4},{7,5},{8,10},{9,11},{10,... | collective-permute-start | bytes 196616 | tf_op jit(solution)/shard_map/ppermute | solution.py:319
  6.6 0.1 fusion.1.weights_ref
  6.7 0.2 pick.1.asked_ref
  6.8 2.2 %collective-permute-done.1.came_ref = f32[64,256]{1,0:T(8,128)S(1)} collective-permute-done((f32[64,256]{1,0:T(8,128)S(1)}, f32[64,256]{1,0:T(8,128)S(1)}, u32[]{:S(2)}, u32[]{:S(2)}) %collective-permute-start.1) | collective-permute-done | bytes 65568 | tf_op jit(solution)/shard_map/ppermute | solution.py:319
  9.0 0.4 %gradients.1.refs_3_ = f32[160,128]{1,0:T(8,128)S(1)} custom-call(f32[16,256]{1,0:T(8,128)S(1)} %fusion.1.weights_ref, f32[64,256]{1,0:T(8,128)S(1)} %get-tuple-element.11.kept_ref, f32[64,256]{1,0:T(8,128)S(1)} %collective-permute-done.1.came_ref, f32[32,128]{1,0:T(8,128)S(1)} %pick.1.asked_ref), custom_call_target="tpu_custom_call" | custom-call | tf_op jit(solution)/shard_map/gradients/pallas_call | solution.py:223
  9.4 4.0 %collective-permute-start.2 = (f32[160,128]{1,0:T(8,128)S(1)}, f32[160,128]{1,0:T(8,128)S(1)}, u32[]{:S(2)}, u32[]{:S(2)}) collective-permute-start(f32[160,128]{1,0:T(8,128)S(1)} %gradients.1.refs_3_), channel_id=1, source_target_pairs={{12,0},{8,4},{4,8},{0,12},{13,1},{9,5},{5,9},{1,13},{14,2},{10,6},... | collective-permute-start | bytes 245768 | tf_op jit(solution)/shard_map/ppermute | solution.py:328
  13.4 0.0 collective-permute-start.3
  13.4 2.9 %collective-permute-start.4 = (f32[160,128]{1,0:T(8,128)S(1)}, f32[160,128]{1,0:T(8,128)S(1)}, u32[]{:S(2)}, u32[]{:S(2)}) collective-permute-start(f32[160,128]{1,0:T(8,128)S(1)} %gradients.1.refs_3_), channel_id=1, source_target_pairs={{4,0},{12,4},{0,8},{8,12},{5,1},{13,5},{1,9},{9,13},{6,2},{14,6},{... | collective-permute-start | bytes 245768 | tf_op jit(solution)/shard_map/ppermute | solution.py:328
  16.3 0.2 collective-permute-done.2.refs_0_
  16.5 3.2 %collective-permute-done.3.refs_1_ = f32[160,128]{1,0:T(8,128)S(1)} collective-permute-done((f32[160,128]{1,0:T(8,128)S(1)}, f32[160,128]{1,0:T(8,128)S(1)}, u32[]{:S(2)}, u32[]{:S(2)}) %collective-permute-start.3) | collective-permute-done | bytes 81952 | tf_op jit(solution)/shard_map/ppermute | solution.py:328
  19.7 0.0 collective-permute-done.4.refs_2_
  19.7 0.4 %grams.1.refs_3_ = f32[40,128]{1,0:T(8,128)S(1)} custom-call(s32[1]{0:T(128)} %bitcast.me_ref, f32[160,128]{1,0:T(8,128)S(1)} %collective-permute-done.2.refs_0_, f32[160,128]{1,0:T(8,128)S(1)} %collective-permute-done.3.refs_1_, f32[160,128]{1,0:T(8,128)S(1)} %collective-permute-done.4.refs_2_, f32[160,128]{1,0:T(8,128)S(1)} %gradients.1.refs_3_), custom_call_target="tpu_custom_call" | custom-call | tf_op jit(solution)/shard_map/grams/pallas_call | solution.py:258
  20.0 0.0 collective-permute-start.5
  20.0 1.6 %collective-permute-start.6 = (f32[40,128]{1,0:T(8,128)S(1)}, f32[40,128]{1,0:T(8,128)S(1)}, u32[]{:S(2)}, u32[]{:S(2)}) collective-permute-start(f32[40,128]{1,0:T(8,128)S(1)} %grams.1.refs_3_), channel_id=1, source_target_pairs={{0,2},{1,3},{2,0},{3,1},{4,6},{5,7},{6,4},{7,5},{8,10},{9,11},{10,... | collective-permute-start | bytes 61448 | tf_op jit(solution)/shard_map/ppermute | solution.py:319
  21.6 0.3 %collective-permute-start.7 = (f32[40,128]{1,0:T(8,128)S(1)}, f32[40,128]{1,0:T(8,128)S(1)}, u32[]{:S(2)}, u32[]{:S(2)}) collective-permute-start(f32[40,128]{1,0:T(8,128)S(1)} %grams.1.refs_3_), channel_id=1, source_target_pairs={{0,1},{1,0},{2,3},{3,2},{4,5},{5,4},{6,7},{7,6},{8,9},{9,8},{10,11... | collective-permute-start | bytes 61448 | tf_op jit(solution)/shard_map/ppermute | solution.py:319
  21.9 1.5 %collective-permute-done.5.refs_0_ = f32[40,128]{1,0:T(8,128)S(1)} collective-permute-done((f32[40,128]{1,0:T(8,128)S(1)}, f32[40,128]{1,0:T(8,128)S(1)}, u32[]{:S(2)}, u32[]{:S(2)}) %collective-permute-start.5) | collective-permute-done | bytes 20512 | tf_op jit(solution)/shard_map/ppermute | solution.py:319
  23.4 0.5 %collective-permute-done.6.refs_1_ = f32[40,128]{1,0:T(8,128)S(1)} collective-permute-done((f32[40,128]{1,0:T(8,128)S(1)}, f32[40,128]{1,0:T(8,128)S(1)}, u32[]{:S(2)}, u32[]{:S(2)}) %collective-permute-start.6) | collective-permute-done | bytes 20512 | tf_op jit(solution)/shard_map/ppermute | solution.py:319
  23.9 0.0 collective-permute-done.7.refs_2_
  23.9 1.8 %solve.1 = f32[16,16]{1,0:T(8,128)} custom-call(f32[40,128]{1,0:T(8,128)S(1)} %collective-permute-done.5.refs_0_, f32[40,128]{1,0:T(8,128)S(1)} %collective-permute-done.6.refs_1_, f32[40,128]{1,0:T(8,128)S(1)} %collective-permute-done.7.refs_2_, f32[40,128]{1,0:T(8,128)S(1)} %grams.1.refs_3_), custom_call_target="tpu_custom_call" | custom-call | tf_op jit(solution)/shard_map/solve/pallas_call | solution.py:310
  (8 shorter events, 0.0 us)
Async XLA Ops:
  0.0 2.7 %copy-start.2 = (s32[16]{0:T(128)S(1)}, s32[16]{0:T(128)}, u32[]{:S(2)}) copy-start(s32[16]{0:T(128)} %param.12) | copy-start | bytes 196
  0.0 2.8 %copy-start.1 = (s32[256]{0:T(256)S(1)}, s32[256]{0:T(256)}, u32[]{:S(2)}) copy-start(s32[256]{0:T(256)} %param.11) | copy-start | bytes 3076
  0.0 6.7 %copy-start = (f32[4,4096]{1,0:T(4,128)S(1)}, f32[4,4096]{1,0:T(4,128)}, u32[]{:S(2)}) copy-start(f32[4,4096]{1,0:T(4,128)} %queries_ref.1) | copy-start | bytes 196612
  2.2 1.5 %collective-permute-start = (f32[96,256]{1,0:T(8,128)S(1)}, f32[96,256]{1,0:T(8,128)S(1)}, u32[]{:S(2)}, u32[]{:S(2)}) collective-permute-start(f32[96,256]{1,0:T(8,128)S(1)} %get-tuple-element.10), channel_id=1, source_target_pairs={{0,1},{1,0},{2,3},{3,2},{4,5},{5,4},{6,7},{7,6},{8,9},{9,8},{10,11... | collective-permute-start | bytes 294920 | tf_op jit(solution)/shard_map/ppermute | solution.py:319
  3.7 5.3 %collective-permute-start.1 = (f32[64,256]{1,0:T(8,128)S(1)}, f32[64,256]{1,0:T(8,128)S(1)}, u32[]{:S(2)}, u32[]{:S(2)}) collective-permute-start(f32[64,256]{1,0:T(8,128)S(1)} %get-tuple-element.12), channel_id=1, source_target_pairs={{0,2},{1,3},{2,0},{3,1},{4,6},{5,7},{6,4},{7,5},{8,10},{9,11},{10,... | collective-permute-start | bytes 196616 | tf_op jit(solution)/shard_map/ppermute | solution.py:319
  9.4 7.1 %collective-permute-start.2 = (f32[160,128]{1,0:T(8,128)S(1)}, f32[160,128]{1,0:T(8,128)S(1)}, u32[]{:S(2)}, u32[]{:S(2)}) collective-permute-start(f32[160,128]{1,0:T(8,128)S(1)} %gradients.1.refs_3_), channel_id=1, source_target_pairs={{12,0},{8,4},{4,8},{0,12},{13,1},{9,5},{5,9},{1,13},{14,2},{10,6},... | collective-permute-start | bytes 245768 | tf_op jit(solution)/shard_map/ppermute | solution.py:328
  13.4 6.2 %collective-permute-start.3 = (f32[160,128]{1,0:T(8,128)S(1)}, f32[160,128]{1,0:T(8,128)S(1)}, u32[]{:S(2)}, u32[]{:S(2)}) collective-permute-start(f32[160,128]{1,0:T(8,128)S(1)} %gradients.1.refs_3_), channel_id=1, source_target_pairs={{8,0},{0,4},{12,8},{4,12},{9,1},{1,5},{13,9},{5,13},{10,2},{2,6},{... | collective-permute-start | bytes 245768 | tf_op jit(solution)/shard_map/ppermute | solution.py:328
  13.4 6.2 %collective-permute-start.4 = (f32[160,128]{1,0:T(8,128)S(1)}, f32[160,128]{1,0:T(8,128)S(1)}, u32[]{:S(2)}, u32[]{:S(2)}) collective-permute-start(f32[160,128]{1,0:T(8,128)S(1)} %gradients.1.refs_3_), channel_id=1, source_target_pairs={{4,0},{12,4},{0,8},{8,12},{5,1},{13,5},{1,9},{9,13},{6,2},{14,6},{... | collective-permute-start | bytes 245768 | tf_op jit(solution)/shard_map/ppermute | solution.py:328
  20.0 3.4 %collective-permute-start.5 = (f32[40,128]{1,0:T(8,128)S(1)}, f32[40,128]{1,0:T(8,128)S(1)}, u32[]{:S(2)}, u32[]{:S(2)}) collective-permute-start(f32[40,128]{1,0:T(8,128)S(1)} %grams.1.refs_3_), channel_id=1, source_target_pairs={{0,3},{1,2},{2,1},{3,0},{4,7},{5,6},{6,5},{7,4},{8,11},{9,10},{10,... | collective-permute-start | bytes 61448 | tf_op jit(solution)/shard_map/ppermute | solution.py:319
  20.0 3.8 %collective-permute-start.6 = (f32[40,128]{1,0:T(8,128)S(1)}, f32[40,128]{1,0:T(8,128)S(1)}, u32[]{:S(2)}, u32[]{:S(2)}) collective-permute-start(f32[40,128]{1,0:T(8,128)S(1)} %grams.1.refs_3_), channel_id=1, source_target_pairs={{0,2},{1,3},{2,0},{3,1},{4,6},{5,7},{6,4},{7,5},{8,10},{9,11},{10,... | collective-permute-start | bytes 61448 | tf_op jit(solution)/shard_map/ppermute | solution.py:319
  21.6 2.3 %collective-permute-start.7 = (f32[40,128]{1,0:T(8,128)S(1)}, f32[40,128]{1,0:T(8,128)S(1)}, u32[]{:S(2)}, u32[]{:S(2)}) collective-permute-start(f32[40,128]{1,0:T(8,128)S(1)} %grams.1.refs_3_), channel_id=1, source_target_pairs={{0,1},{1,0},{2,3},{3,2},{4,5},{5,4},{6,7},{7,6},{8,9},{9,8},{10,11... | collective-permute-start | bytes 61448 | tf_op jit(solution)/shard_map/ppermute | solution.py:319

commit v21 on v20

--- a/solution.py
+++ b/solution.py
@@ -10,7 +10,7 @@
 damping = 0.5
 VMEM_LIMIT = 32 * 1024 * 1024
 SMALL = 4
-SOURCES = {1: (), 2: ((1, 0),), 4: ((3, 2, 1, 0), (2, 0, 3, 1), (1, 3, 0, 2))}
+SOURCES = {1: (), 2: ((1, 0),), 4: ((2, 0, 3, 1), (3, 2, 1, 0), (1, 3, 0, 2))}
 
 
 def token_weights(seq_ids, counts, first):

time: 25.9 us -> 25.4 us (0.981)
  starting transfers between devices: 12.3 us -> 11.4 us
    ppermute x3, starting transfers between devices: 6.95 us -> 6.04 us  [from_all(): return [lax.ppermute(value, axis, swap) for swap in swaps] + [value]]
  transfers between devices with their start and end apart: 8 -> 8, of which waited for: 6 -> 7; matrix products, arithmetic and copies ran while one was open for 1% -> 1% of each run, Pallas kernels for 1% -> 1%
where the time goes in v21:
time: 25.4 us; the launch traced here: 25 us
  starting transfers between devices  11.4 us (45%)
  waiting for transfers between devices  8.46 us (33%)
  Pallas kernels  4.88 us (19%)
    ppermute x3, starting transfers between devices, from_all(): return [lax.ppermute(value, axis, swap) for swap in swaps] + [value]  6.04 us
    ppermute x5, starting transfers between devices, from_partner(): return lax.ppermute(value, axis, [(i, i ^ m) for i in range(size)])  5.35 us
    ppermute x5, waiting for transfers between devices, from_partner(): return lax.ppermute(value, axis, [(i, i ^ m) for i in range(size)])  4.95 us
    ppermute x3, waiting for transfers between devices, from_all(): return [lax.ppermute(value, axis, swap) for swap in swaps] + [value]  3.51 us
    pallas_call x1, Pallas kernels, project(): pl.pallas_call(functools.partial(project_kernel, own), out_shape=[jax.Sha...  2.19 us
    pallas_call x1, Pallas kernels, solve(): pl.pallas_call(functools.partial(solve_kernel, seqs), out_shape=jax.Shape...  1.82 us
  transfers between devices with their start and end apart: 8, of which 7 were waited for; matrix products, arithmetic and copies ran while one was open for 1% of the time, Pallas kernels for 1%

profile of v21, /device:TPU:0, one launch (start us, length us, event | category | flops | bytes accessed | tf_op | source)
XLA Modules:
  0.0 25.0 jit_solution(17738945139171609155)
XLA Ops:
  0.0 2.2 %project.1 = (f32[96,256]{1,0:T(8,128)S(1)}, f32[96,256]{1,0:T(8,128)S(1)}) custom-call(s32[1]{0:T(128)} %bitcast.1.rank_ref, bf16[2752,256]{1,0:T(8,128)(2,1)} %bitcast.5, bf16[256,1024]{1,0:T(8,128)(2,1)} %g_hbm.1, bf16[64,2752]{1,0:T(8,128)(2,1)} %bitcast.6, bf16[64,1024]{1,0:T(8,128)(2,1)} %bitcast.7), custom_call_target="tpu_custom_call" | custom-call | tf_op jit(solution)/shard_map/project/pallas_call | solution.py:109
  2.2 0.5 %collective-permute-start = (f32[96,256]{1,0:T(8,128)S(1)}, f32[96,256]{1,0:T(8,128)S(1)}, u32[]{:S(2)}, u32[]{:S(2)}) collective-permute-start(f32[96,256]{1,0:T(8,128)S(1)} %get-tuple-element.10), channel_id=1, source_target_pairs={{0,1},{1,0},{2,3},{3,2},{4,5},{5,4},{6,7},{7,6},{8,9},{9,8},{10,11... | collective-permute-start | bytes 294920 | tf_op jit(solution)/shard_map/ppermute | solution.py:319
  2.7 0.0 copy-done.2
  2.8 0.1 convert_reduce_fusion
  2.9 0.8 %collective-permute-done.came_ref = f32[96,256]{1,0:T(8,128)S(1)} collective-permute-done((f32[96,256]{1,0:T(8,128)S(1)}, f32[96,256]{1,0:T(8,128)S(1)}, u32[]{:S(2)}, u32[]{:S(2)}) %collective-permute-start) | collective-permute-done | bytes 98336 | tf_op jit(solution)/shard_map/ppermute | solution.py:319
  3.7 2.9 %collective-permute-start.1 = (f32[64,256]{1,0:T(8,128)S(1)}, f32[64,256]{1,0:T(8,128)S(1)}, u32[]{:S(2)}, u32[]{:S(2)}) collective-permute-start(f32[64,256]{1,0:T(8,128)S(1)} %get-tuple-element.12), channel_id=1, source_target_pairs={{0,2},{1,3},{2,0},{3,1},{4,6},{5,7},{6,4},{7,5},{8,10},{9,11},{10,... | collective-permute-start | bytes 196616 | tf_op jit(solution)/shard_map/ppermute | solution.py:319
  6.6 0.1 fusion.1.weights_ref
  6.7 0.2 pick.1.asked_ref
  6.8 2.2 %collective-permute-done.1.came_ref = f32[64,256]{1,0:T(8,128)S(1)} collective-permute-done((f32[64,256]{1,0:T(8,128)S(1)}, f32[64,256]{1,0:T(8,128)S(1)}, u32[]{:S(2)}, u32[]{:S(2)}) %collective-permute-start.1) | collective-permute-done | bytes 65568 | tf_op jit(solution)/shard_map/ppermute | solution.py:319
  9.0 0.4 %gradients.1.refs_3_ = f32[160,128]{1,0:T(8,128)S(1)} custom-call(f32[16,256]{1,0:T(8,128)S(1)} %fusion.1.weights_ref, f32[64,256]{1,0:T(8,128)S(1)} %get-tuple-element.11.kept_ref, f32[64,256]{1,0:T(8,128)S(1)} %collective-permute-done.1.came_ref, f32[32,128]{1,0:T(8,128)S(1)} %pick.1.asked_ref), custom_call_target="tpu_custom_call" | custom-call | tf_op jit(solution)/shard_map/gradients/pallas_call | solution.py:223
  9.4 2.0 %collective-permute-start.2 = (f32[160,128]{1,0:T(8,128)S(1)}, f32[160,128]{1,0:T(8,128)S(1)}, u32[]{:S(2)}, u32[]{:S(2)}) collective-permute-start(f32[160,128]{1,0:T(8,128)S(1)} %gradients.1.refs_3_), channel_id=1, source_target_pairs={{8,0},{0,4},{12,8},{4,12},{9,1},{1,5},{13,9},{5,13},{10,2},{2,6},{... | collective-permute-start | bytes 245768 | tf_op jit(solution)/shard_map/ppermute | solution.py:328
  11.4 2.5 %collective-permute-start.3 = (f32[160,128]{1,0:T(8,128)S(1)}, f32[160,128]{1,0:T(8,128)S(1)}, u32[]{:S(2)}, u32[]{:S(2)}) collective-permute-start(f32[160,128]{1,0:T(8,128)S(1)} %gradients.1.refs_3_), channel_id=1, source_target_pairs={{12,0},{8,4},{4,8},{0,12},{13,1},{9,5},{5,9},{1,13},{14,2},{10,6},... | collective-permute-start | bytes 245768 | tf_op jit(solution)/shard_map/ppermute | solution.py:328
  13.9 1.6 %collective-permute-start.4 = (f32[160,128]{1,0:T(8,128)S(1)}, f32[160,128]{1,0:T(8,128)S(1)}, u32[]{:S(2)}, u32[]{:S(2)}) collective-permute-start(f32[160,128]{1,0:T(8,128)S(1)} %gradients.1.refs_3_), channel_id=1, source_target_pairs={{4,0},{12,4},{0,8},{8,12},{5,1},{13,5},{1,9},{9,13},{6,2},{14,6},{... | collective-permute-start | bytes 245768 | tf_op jit(solution)/shard_map/ppermute | solution.py:328
  15.4 0.8 %collective-permute-done.2.refs_0_ = f32[160,128]{1,0:T(8,128)S(1)} collective-permute-done((f32[160,128]{1,0:T(8,128)S(1)}, f32[160,128]{1,0:T(8,128)S(1)}, u32[]{:S(2)}, u32[]{:S(2)}) %collective-permute-start.2) | collective-permute-done | bytes 81952 | tf_op jit(solution)/shard_map/ppermute | solution.py:328
  16.3 1.9 %collective-permute-done.3.refs_1_ = f32[160,128]{1,0:T(8,128)S(1)} collective-permute-done((f32[160,128]{1,0:T(8,128)S(1)}, f32[160,128]{1,0:T(8,128)S(1)}, u32[]{:S(2)}, u32[]{:S(2)}) %collective-permute-start.3) | collective-permute-done | bytes 81952 | tf_op jit(solution)/shard_map/ppermute | solution.py:328
  18.2 0.8 %collective-permute-done.4.refs_2_ = f32[160,128]{1,0:T(8,128)S(1)} collective-permute-done((f32[160,128]{1,0:T(8,128)S(1)}, f32[160,128]{1,0:T(8,128)S(1)}, u32[]{:S(2)}, u32[]{:S(2)}) %collective-permute-start.4) | collective-permute-done | bytes 81952 | tf_op jit(solution)/shard_map/ppermute | solution.py:328
  18.9 0.3 %grams.1.refs_3_ = f32[40,128]{1,0:T(8,128)S(1)} custom-call(s32[1]{0:T(128)} %bitcast.me_ref, f32[160,128]{1,0:T(8,128)S(1)} %collective-permute-done.2.refs_0_, f32[160,128]{1,0:T(8,128)S(1)} %collective-permute-done.3.refs_1_, f32[160,128]{1,0:T(8,128)S(1)} %collective-permute-done.4.refs_2_, f32[160,128]{1,0:T(8,128)S(1)} %gradients.1.refs_3_), custom_call_target="tpu_custom_call" | custom-call | tf_op jit(solution)/shard_map/grams/pallas_call | solution.py:258
  19.3 0.0 collective-permute-start.5
  19.3 1.8 %collective-permute-start.6 = (f32[40,128]{1,0:T(8,128)S(1)}, f32[40,128]{1,0:T(8,128)S(1)}, u32[]{:S(2)}, u32[]{:S(2)}) collective-permute-start(f32[40,128]{1,0:T(8,128)S(1)} %grams.1.refs_3_), channel_id=1, source_target_pairs={{0,2},{1,3},{2,0},{3,1},{4,6},{5,7},{6,4},{7,5},{8,10},{9,11},{10,... | collective-permute-start | bytes 61448 | tf_op jit(solution)/shard_map/ppermute | solution.py:319
  21.1 0.1 collective-permute-start.7
  21.2 1.3 %collective-permute-done.5.refs_0_ = f32[40,128]{1,0:T(8,128)S(1)} collective-permute-done((f32[40,128]{1,0:T(8,128)S(1)}, f32[40,128]{1,0:T(8,128)S(1)}, u32[]{:S(2)}, u32[]{:S(2)}) %collective-permute-start.5) | collective-permute-done | bytes 20512 | tf_op jit(solution)/shard_map/ppermute | solution.py:319
  22.5 0.7 %collective-permute-done.6.refs_1_ = f32[40,128]{1,0:T(8,128)S(1)} collective-permute-done((f32[40,128]{1,0:T(8,128)S(1)}, f32[40,128]{1,0:T(8,128)S(1)}, u32[]{:S(2)}, u32[]{:S(2)}) %collective-permute-start.6) | collective-permute-done | bytes 20512 | tf_op jit(solution)/shard_map/ppermute | solution.py:319
  23.2 0.0 collective-permute-done.7.refs_2_
  23.2 1.8 %solve.1 = f32[16,16]{1,0:T(8,128)} custom-call(f32[40,128]{1,0:T(8,128)S(1)} %collective-permute-done.5.refs_0_, f32[40,128]{1,0:T(8,128)S(1)} %collective-permute-done.6.refs_1_, f32[40,128]{1,0:T(8,128)S(1)} %collective-permute-done.7.refs_2_, f32[40,128]{1,0:T(8,128)S(1)} %grams.1.refs_3_), custom_call_target="tpu_custom_call" | custom-call | tf_op jit(solution)/shard_map/solve/pallas_call | solution.py:310
  (8 shorter events, 0.0 us)
Async XLA Ops:
  0.0 2.7 %copy-start.2 = (s32[16]{0:T(128)S(1)}, s32[16]{0:T(128)}, u32[]{:S(2)}) copy-start(s32[16]{0:T(128)} %param.12) | copy-start | bytes 196
  0.0 2.8 %copy-start.1 = (s32[256]{0:T(256)S(1)}, s32[256]{0:T(256)}, u32[]{:S(2)}) copy-start(s32[256]{0:T(256)} %param.11) | copy-start | bytes 3076
  0.0 6.7 %copy-start = (f32[4,4096]{1,0:T(4,128)S(1)}, f32[4,4096]{1,0:T(4,128)}, u32[]{:S(2)}) copy-start(f32[4,4096]{1,0:T(4,128)} %queries_ref.1) | copy-start | bytes 196612
  2.2 1.5 %collective-permute-start = (f32[96,256]{1,0:T(8,128)S(1)}, f32[96,256]{1,0:T(8,128)S(1)}, u32[]{:S(2)}, u32[]{:S(2)}) collective-permute-start(f32[96,256]{1,0:T(8,128)S(1)} %get-tuple-element.10), channel_id=1, source_target_pairs={{0,1},{1,0},{2,3},{3,2},{4,5},{5,4},{6,7},{7,6},{8,9},{9,8},{10,11... | collective-permute-start | bytes 294920 | tf_op jit(solution)/shard_map/ppermute | solution.py:319
  3.7 5.3 %collective-permute-start.1 = (f32[64,256]{1,0:T(8,128)S(1)}, f32[64,256]{1,0:T(8,128)S(1)}, u32[]{:S(2)}, u32[]{:S(2)}) collective-permute-start(f32[64,256]{1,0:T(8,128)S(1)} %get-tuple-element.12), channel_id=1, source_target_pairs={{0,2},{1,3},{2,0},{3,1},{4,6},{5,7},{6,4},{7,5},{8,10},{9,11},{10,... | collective-permute-start | bytes 196616 | tf_op jit(solution)/shard_map/ppermute | solution.py:319
  9.4 6.9 %collective-permute-start.2 = (f32[160,128]{1,0:T(8,128)S(1)}, f32[160,128]{1,0:T(8,128)S(1)}, u32[]{:S(2)}, u32[]{:S(2)}) collective-permute-start(f32[160,128]{1,0:T(8,128)S(1)} %gradients.1.refs_3_), channel_id=1, source_target_pairs={{8,0},{0,4},{12,8},{4,12},{9,1},{1,5},{13,9},{5,13},{10,2},{2,6},{... | collective-permute-start | bytes 245768 | tf_op jit(solution)/shard_map/ppermute | solution.py:328
  11.4 6.8 %collective-permute-start.3 = (f32[160,128]{1,0:T(8,128)S(1)}, f32[160,128]{1,0:T(8,128)S(1)}, u32[]{:S(2)}, u32[]{:S(2)}) collective-permute-start(f32[160,128]{1,0:T(8,128)S(1)} %gradients.1.refs_3_), channel_id=1, source_target_pairs={{12,0},{8,4},{4,8},{0,12},{13,1},{9,5},{5,9},{1,13},{14,2},{10,6},... | collective-permute-start | bytes 245768 | tf_op jit(solution)/shard_map/ppermute | solution.py:328
  13.9 5.1 %collective-permute-start.4 = (f32[160,128]{1,0:T(8,128)S(1)}, f32[160,128]{1,0:T(8,128)S(1)}, u32[]{:S(2)}, u32[]{:S(2)}) collective-permute-start(f32[160,128]{1,0:T(8,128)S(1)} %gradients.1.refs_3_), channel_id=1, source_target_pairs={{4,0},{12,4},{0,8},{8,12},{5,1},{13,5},{1,9},{9,13},{6,2},{14,6},{... | collective-permute-start | bytes 245768 | tf_op jit(solution)/shard_map/ppermute | solution.py:328
  19.3 3.2 %collective-permute-start.5 = (f32[40,128]{1,0:T(8,128)S(1)}, f32[40,128]{1,0:T(8,128)S(1)}, u32[]{:S(2)}, u32[]{:S(2)}) collective-permute-start(f32[40,128]{1,0:T(8,128)S(1)} %grams.1.refs_3_), channel_id=1, source_target_pairs={{0,3},{1,2},{2,1},{3,0},{4,7},{5,6},{6,5},{7,4},{8,11},{9,10},{10,... | collective-permute-start | bytes 61448 | tf_op jit(solution)/shard_map/ppermute | solution.py:319
  19.3 3.8 %collective-permute-start.6 = (f32[40,128]{1,0:T(8,128)S(1)}, f32[40,128]{1,0:T(8,128)S(1)}, u32[]{:S(2)}, u32[]{:S(2)}) collective-permute-start(f32[40,128]{1,0:T(8,128)S(1)} %grams.1.refs_3_), channel_id=1, source_target_pairs={{0,2},{1,3},{2,0},{3,1},{4,6},{5,7},{6,4},{7,5},{8,10},{9,11},{10,... | collective-permute-start | bytes 61448 | tf_op jit(solution)/shard_map/ppermute | solution.py:319
  21.1 2.0 %collective-permute-start.7 = (f32[40,128]{1,0:T(8,128)S(1)}, f32[40,128]{1,0:T(8,128)S(1)}, u32[]{:S(2)}, u32[]{:S(2)}) collective-permute-start(f32[40,128]{1,0:T(8,128)S(1)} %grams.1.refs_3_), channel_id=1, source_target_pairs={{0,1},{1,0},{2,3},{3,2},{4,5},{5,4},{6,7},{7,6},{8,9},{9,8},{10,11... | collective-permute-start | bytes 61448 | tf_op jit(solution)/shard_map/ppermute | solution.py:319

commit v22 on v21

--- a/solution.py
+++ b/solution.py
@@ -229,7 +229,7 @@
 
 
 def grams_kernel(steps, seqs, me_ref, *refs):
-    blocks, out_ref = (refs[-2], *refs[:-2]), refs[-1]
+    blocks, out_ref = (refs[0], *refs[-3:0:-1]), refs[-1]
     count = steps * seqs
     asked = (blocks[0].shape[0] - count) // steps
     given = [block[count:, :] for block in blocks]
@@ -251,18 +251,18 @@
     out_ref[...] = jnp.concatenate([result[:half, :], result[half:, :]], axis=1)
 
 
-def grams(me, blocks, steps, seqs):
+def grams(me, level, blocks, steps, seqs):
     asked = blocks[0].shape[0] // steps - seqs
     total = len(blocks) * seqs
     whole = pl.BlockSpec(memory_space=pltpu.VMEM)
     return pl.pallas_call(
         functools.partial(grams_kernel, steps, seqs),
         out_shape=jax.ShapeDtypeStruct(((total + len(blocks) * asked) // 2, 2 * total), jnp.float32),
-        in_specs=[pl.BlockSpec(memory_space=pltpu.SMEM)] + [whole] * len(blocks),
+        in_specs=[pl.BlockSpec(memory_space=pltpu.SMEM)] + [whole] * (len(blocks) + 1),
         out_specs=whole,
         compiler_params=pltpu.CompilerParams(vmem_limit_bytes=VMEM_LIMIT),
         name="grams",
-    )(me, *blocks)
+    )(me, *blocks[::-1], level)
 
 
 def scales(count):
@@ -372,8 +372,9 @@
     steps = own * own // message.shape[1]
     if blocks > SMALL:
         return finish_long(message, steps, first, seq_dev)
-    partial = grams(place.reshape(1), from_all(message, "dp", blocks), steps, seq_dev)
-    partial = from_partners(partial, "tensor", parts)
+    level = from_partner(message, "tensor", parts, 1)
+    partial = grams(place.reshape(1), level, from_all(message, "dp", blocks), steps, seq_dev)
+    partial = from_partners(partial, "tensor", parts)[::-1]
     return solve(partial, blocks * seq_dev, blocks * queries.shape[0], seq_dev)
 
 

time: 25.4 us -> 26.8 us (1.055); the launches traced: 25 us -> 26.7 us
  waiting for transfers between devices: 8.46 us -> 10.1 us
    ppermute x5 -> x6, waiting for transfers between devices: 4.95 us -> 5.77 us  [from_partner(): return lax.ppermute(value, axis, [(i, i ^ m) for i in range(size)])]
    ppermute x3, waiting for transfers between devices: 3.51 us -> 4.33 us  [from_all(): return [lax.ppermute(value, axis, swap) for swap in swaps] + [value]]
    ppermute x5 -> x6, starting transfers between devices: 5.35 us -> 5.39 us  [from_partner(): return lax.ppermute(value, axis, [(i, i ^ m) for i in range(size)])]
  transfers between devices with their start and end apart: 8 -> 9, of which waited for: 7 -> 6; matrix products, arithmetic and copies ran while one was open for 1% -> 1% of each run, Pallas kernels for 1% -> 1%
where the time goes in v22:
time: 26.8 us; the launch traced here: 26.7 us
  starting transfers between devices  11.4 us (43%)
  waiting for transfers between devices  10.1 us (38%)
  Pallas kernels  4.88 us (18%)
    ppermute x3, starting transfers between devices, from_all(): return [lax.ppermute(value, axis, swap) for swap in swaps] + [value]  6.04 us
    ppermute x6, waiting for transfers between devices, from_partner(): return lax.ppermute(value, axis, [(i, i ^ m) for i in range(size)])  5.77 us
    ppermute x6, starting transfers between devices, from_partner(): return lax.ppermute(value, axis, [(i, i ^ m) for i in range(size)])  5.39 us
    ppermute x3, waiting for transfers between devices, from_all(): return [lax.ppermute(value, axis, swap) for swap in swaps] + [value]  4.33 us
    pallas_call x1, Pallas kernels, project(): pl.pallas_call(functools.partial(project_kernel, own), out_shape=[jax.Sha...  2.19 us
    pallas_call x1, Pallas kernels, solve(): pl.pallas_call(functools.partial(solve_kernel, seqs), out_shape=jax.Shape...  1.82 us
  transfers between devices with their start and end apart: 9, of which 6 were waited for; matrix products, arithmetic and copies ran while one was open for 1% of the time, Pallas kernels for 1%

profile of v22, /device:TPU:0, one launch (start us, length us, event | category | flops | bytes accessed | tf_op | source)
XLA Modules:
  0.0 26.7 jit_solution(71245034205345170)
XLA Ops:
  0.0 2.2 %project.1 = (f32[96,256]{1,0:T(8,128)S(1)}, f32[96,256]{1,0:T(8,128)S(1)}) custom-call(s32[1]{0:T(128)} %bitcast.1.rank_ref, bf16[2752,256]{1,0:T(8,128)(2,1)} %bitcast.5, bf16[256,1024]{1,0:T(8,128)(2,1)} %g_hbm.1, bf16[64,2752]{1,0:T(8,128)(2,1)} %bitcast.6, bf16[64,1024]{1,0:T(8,128)(2,1)} %bitcast.7), custom_call_target="tpu_custom_call" | custom-call | tf_op jit(solution)/shard_map/project/pallas_call | solution.py:109
  2.2 0.5 %collective-permute-start = (f32[96,256]{1,0:T(8,128)S(1)}, f32[96,256]{1,0:T(8,128)S(1)}, u32[]{:S(2)}, u32[]{:S(2)}) collective-permute-start(f32[96,256]{1,0:T(8,128)S(1)} %get-tuple-element.10), channel_id=1, source_target_pairs={{0,1},{1,0},{2,3},{3,2},{4,5},{5,4},{6,7},{7,6},{8,9},{9,8},{10,11... | collective-permute-start | bytes 294920 | tf_op jit(solution)/shard_map/ppermute | solution.py:319
  2.8 0.1 convert_reduce_fusion
  2.9 0.8 %collective-permute-done.came_ref = f32[96,256]{1,0:T(8,128)S(1)} collective-permute-done((f32[96,256]{1,0:T(8,128)S(1)}, f32[96,256]{1,0:T(8,128)S(1)}, u32[]{:S(2)}, u32[]{:S(2)}) %collective-permute-start) | collective-permute-done | bytes 98336 | tf_op jit(solution)/shard_map/ppermute | solution.py:319
  3.7 2.9 %collective-permute-start.1 = (f32[64,256]{1,0:T(8,128)S(1)}, f32[64,256]{1,0:T(8,128)S(1)}, u32[]{:S(2)}, u32[]{:S(2)}) collective-permute-start(f32[64,256]{1,0:T(8,128)S(1)} %get-tuple-element.12), channel_id=1, source_target_pairs={{0,2},{1,3},{2,0},{3,1},{4,6},{5,7},{6,4},{7,5},{8,10},{9,11},{10,... | collective-permute-start | bytes 196616 | tf_op jit(solution)/shard_map/ppermute | solution.py:319
  6.6 0.1 fusion.1.weights_ref
  6.7 0.2 pick.1.asked_ref
  6.8 2.2 %collective-permute-done.1.came_ref = f32[64,256]{1,0:T(8,128)S(1)} collective-permute-done((f32[64,256]{1,0:T(8,128)S(1)}, f32[64,256]{1,0:T(8,128)S(1)}, u32[]{:S(2)}, u32[]{:S(2)}) %collective-permute-start.1) | collective-permute-done | bytes 65568 | tf_op jit(solution)/shard_map/ppermute | solution.py:319
  9.0 0.4 %gradients.1.refs_0_ = f32[160,128]{1,0:T(8,128)S(1)} custom-call(f32[16,256]{1,0:T(8,128)S(1)} %fusion.1.weights_ref, f32[64,256]{1,0:T(8,128)S(1)} %get-tuple-element.11.kept_ref, f32[64,256]{1,0:T(8,128)S(1)} %collective-permute-done.1.came_ref, f32[32,128]{1,0:T(8,128)S(1)} %pick.1.asked_ref), custom_call_target="tpu_custom_call" | custom-call | tf_op jit(solution)/shard_map/gradients/pallas_call | solution.py:223
  9.4 0.1 collective-permute-start.5
  9.5 2.0 %collective-permute-start.4 = (f32[160,128]{1,0:T(8,128)S(1)}, f32[160,128]{1,0:T(8,128)S(1)}, u32[]{:S(2)}, u32[]{:S(2)}) collective-permute-start(f32[160,128]{1,0:T(8,128)S(1)} %gradients.1.refs_0_), channel_id=1, source_target_pairs={{8,0},{0,4},{12,8},{4,12},{9,1},{1,5},{13,9},{5,13},{10,2},{2,6},{... | collective-permute-start | bytes 245768 | tf_op jit(solution)/shard_map/ppermute | solution.py:328
  11.5 2.5 %collective-permute-start.3 = (f32[160,128]{1,0:T(8,128)S(1)}, f32[160,128]{1,0:T(8,128)S(1)}, u32[]{:S(2)}, u32[]{:S(2)}) collective-permute-start(f32[160,128]{1,0:T(8,128)S(1)} %gradients.1.refs_0_), channel_id=1, source_target_pairs={{12,0},{8,4},{4,8},{0,12},{13,1},{9,5},{5,9},{1,13},{14,2},{10,6},... | collective-permute-start | bytes 245768 | tf_op jit(solution)/shard_map/ppermute | solution.py:328
  13.9 1.6 %collective-permute-start.2 = (f32[160,128]{1,0:T(8,128)S(1)}, f32[160,128]{1,0:T(8,128)S(1)}, u32[]{:S(2)}, u32[]{:S(2)}) collective-permute-start(f32[160,128]{1,0:T(8,128)S(1)} %gradients.1.refs_0_), channel_id=1, source_target_pairs={{4,0},{12,4},{0,8},{8,12},{5,1},{13,5},{1,9},{9,13},{6,2},{14,6},{... | collective-permute-start | bytes 245768 | tf_op jit(solution)/shard_map/ppermute | solution.py:328
  15.5 0.0 collective-permute-done.5.refs_4_
  15.5 0.0 collective-permute-done.4.refs_3_
  15.5 3.5 %collective-permute-done.3.refs_2_ = f32[160,128]{1,0:T(8,128)S(1)} collective-permute-done((f32[160,128]{1,0:T(8,128)S(1)}, f32[160,128]{1,0:T(8,128)S(1)}, u32[]{:S(2)}, u32[]{:S(2)}) %collective-permute-start.3) | collective-permute-done | bytes 81952 | tf_op jit(solution)/shard_map/ppermute | solution.py:328
  19.0 0.8 %collective-permute-done.2.refs_1_ = f32[160,128]{1,0:T(8,128)S(1)} collective-permute-done((f32[160,128]{1,0:T(8,128)S(1)}, f32[160,128]{1,0:T(8,128)S(1)}, u32[]{:S(2)}, u32[]{:S(2)}) %collective-permute-start.2) | collective-permute-done | bytes 81952 | tf_op jit(solution)/shard_map/ppermute | solution.py:328
  19.8 0.3 %grams.1.refs_0_ = f32[40,128]{1,0:T(8,128)S(1)} custom-call(s32[1]{0:T(128)} %bitcast.me_ref, f32[160,128]{1,0:T(8,128)S(1)} %gradients.1.refs_0_, f32[160,128]{1,0:T(8,128)S(1)} %collective-permute-done.2.refs_1_, f32[160,128]{1,0:T(8,128)S(1)} %collective-permute-done.3.refs_2_, f32[160,128]{1,0:T(8,128)S(1)} %collective-permute-done.4.refs_3_, ...), custom_call_target="tpu_custom_call" | custom-call | tf_op jit(solution)/shard_map/grams/pallas_call | solution.py:258
  20.2 0.7 %collective-permute-start.8 = (f32[40,128]{1,0:T(8,128)S(1)}, f32[40,128]{1,0:T(8,128)S(1)}, u32[]{:S(2)}, u32[]{:S(2)}) collective-permute-start(f32[40,128]{1,0:T(8,128)S(1)} %grams.1.refs_0_), channel_id=1, source_target_pairs={{0,3},{1,2},{2,1},{3,0},{4,7},{5,6},{6,5},{7,4},{8,11},{9,10},{10,... | collective-permute-start | bytes 61448 | tf_op jit(solution)/shard_map/ppermute | solution.py:319
  20.9 0.9 %collective-permute-start.7 = (f32[40,128]{1,0:T(8,128)S(1)}, f32[40,128]{1,0:T(8,128)S(1)}, u32[]{:S(2)}, u32[]{:S(2)}) collective-permute-start(f32[40,128]{1,0:T(8,128)S(1)} %grams.1.refs_0_), channel_id=1, source_target_pairs={{0,2},{1,3},{2,0},{3,1},{4,6},{5,7},{6,4},{7,5},{8,10},{9,11},{10,... | collective-permute-start | bytes 61448 | tf_op jit(solution)/shard_map/ppermute | solution.py:319
  21.8 0.3 %collective-permute-start.6 = (f32[40,128]{1,0:T(8,128)S(1)}, f32[40,128]{1,0:T(8,128)S(1)}, u32[]{:S(2)}, u32[]{:S(2)}) collective-permute-start(f32[40,128]{1,0:T(8,128)S(1)} %grams.1.refs_0_), channel_id=1, source_target_pairs={{0,1},{1,0},{2,3},{3,2},{4,5},{5,4},{6,7},{7,6},{8,9},{9,8},{10,11... | collective-permute-start | bytes 61448 | tf_op jit(solution)/shard_map/ppermute | solution.py:319
  22.1 1.5 %collective-permute-done.8.refs_3_ = f32[40,128]{1,0:T(8,128)S(1)} collective-permute-done((f32[40,128]{1,0:T(8,128)S(1)}, f32[40,128]{1,0:T(8,128)S(1)}, u32[]{:S(2)}, u32[]{:S(2)}) %collective-permute-start.8) | collective-permute-done | bytes 20512 | tf_op jit(solution)/shard_map/ppermute | solution.py:319
  23.6 1.3 %collective-permute-done.7.refs_2_ = f32[40,128]{1,0:T(8,128)S(1)} collective-permute-done((f32[40,128]{1,0:T(8,128)S(1)}, f32[40,128]{1,0:T(8,128)S(1)}, u32[]{:S(2)}, u32[]{:S(2)}) %collective-permute-start.7) | collective-permute-done | bytes 20512 | tf_op jit(solution)/shard_map/ppermute | solution.py:319
  24.8 1.8 %solve.1 = f32[16,16]{1,0:T(8,128)} custom-call(f32[40,128]{1,0:T(8,128)S(1)} %grams.1.refs_0_, f32[40,128]{1,0:T(8,128)S(1)} %collective-permute-done.6.refs_1_, f32[40,128]{1,0:T(8,128)S(1)} %collective-permute-done.7.refs_2_, f32[40,128]{1,0:T(8,128)S(1)} %collective-permute-done.8.refs_3_), custom_call_target="tpu_custom_call" | custom-call | tf_op jit(solution)/shard_map/solve/pallas_call | solution.py:310
  (10 shorter events, 0.0 us)
Async XLA Ops:
  0.0 2.7 %copy-start.2 = (s32[16]{0:T(128)S(1)}, s32[16]{0:T(128)}, u32[]{:S(2)}) copy-start(s32[16]{0:T(128)} %param.12) | copy-start | bytes 196
  0.0 2.8 %copy-start.1 = (s32[256]{0:T(256)S(1)}, s32[256]{0:T(256)}, u32[]{:S(2)}) copy-start(s32[256]{0:T(256)} %param.11) | copy-start | bytes 3076
  0.0 6.7 %copy-start = (f32[4,4096]{1,0:T(4,128)S(1)}, f32[4,4096]{1,0:T(4,128)}, u32[]{:S(2)}) copy-start(f32[4,4096]{1,0:T(4,128)} %queries_ref.1) | copy-start | bytes 196612
  2.2 1.5 %collective-permute-start = (f32[96,256]{1,0:T(8,128)S(1)}, f32[96,256]{1,0:T(8,128)S(1)}, u32[]{:S(2)}, u32[]{:S(2)}) collective-permute-start(f32[96,256]{1,0:T(8,128)S(1)} %get-tuple-element.10), channel_id=1, source_target_pairs={{0,1},{1,0},{2,3},{3,2},{4,5},{5,4},{6,7},{7,6},{8,9},{9,8},{10,11... | collective-permute-start | bytes 294920 | tf_op jit(solution)/shard_map/ppermute | solution.py:319
  3.7 5.3 %collective-permute-start.1 = (f32[64,256]{1,0:T(8,128)S(1)}, f32[64,256]{1,0:T(8,128)S(1)}, u32[]{:S(2)}, u32[]{:S(2)}) collective-permute-start(f32[64,256]{1,0:T(8,128)S(1)} %get-tuple-element.12), channel_id=1, source_target_pairs={{0,2},{1,3},{2,0},{3,1},{4,6},{5,7},{6,4},{7,5},{8,10},{9,11},{10,... | collective-permute-start | bytes 196616 | tf_op jit(solution)/shard_map/ppermute | solution.py:319
  9.4 6.1 %collective-permute-start.5 = (f32[160,128]{1,0:T(8,128)S(1)}, f32[160,128]{1,0:T(8,128)S(1)}, u32[]{:S(2)}, u32[]{:S(2)}) collective-permute-start(f32[160,128]{1,0:T(8,128)S(1)} %gradients.1.refs_0_), channel_id=1, source_target_pairs={{0,1},{1,0},{2,3},{3,2},{4,5},{5,4},{6,7},{7,6},{8,9},{9,8},{10,11... | collective-permute-start | bytes 245768 | tf_op jit(solution)/shard_map/ppermute | solution.py:319
  9.5 6.1 %collective-permute-start.4 = (f32[160,128]{1,0:T(8,128)S(1)}, f32[160,128]{1,0:T(8,128)S(1)}, u32[]{:S(2)}, u32[]{:S(2)}) collective-permute-start(f32[160,128]{1,0:T(8,128)S(1)} %gradients.1.refs_0_), channel_id=1, source_target_pairs={{8,0},{0,4},{12,8},{4,12},{9,1},{1,5},{13,9},{5,13},{10,2},{2,6},{... | collective-permute-start | bytes 245768 | tf_op jit(solution)/shard_map/ppermute | solution.py:328
  11.5 7.6 %collective-permute-start.3 = (f32[160,128]{1,0:T(8,128)S(1)}, f32[160,128]{1,0:T(8,128)S(1)}, u32[]{:S(2)}, u32[]{:S(2)}) collective-permute-start(f32[160,128]{1,0:T(8,128)S(1)} %gradients.1.refs_0_), channel_id=1, source_target_pairs={{12,0},{8,4},{4,8},{0,12},{13,1},{9,5},{5,9},{1,13},{14,2},{10,6},... | collective-permute-start | bytes 245768 | tf_op jit(solution)/shard_map/ppermute | solution.py:328
  13.9 5.9 %collective-permute-start.2 = (f32[160,128]{1,0:T(8,128)S(1)}, f32[160,128]{1,0:T(8,128)S(1)}, u32[]{:S(2)}, u32[]{:S(2)}) collective-permute-start(f32[160,128]{1,0:T(8,128)S(1)} %gradients.1.refs_0_), channel_id=1, source_target_pairs={{4,0},{12,4},{0,8},{8,12},{5,1},{13,5},{1,9},{9,13},{6,2},{14,6},{... | collective-permute-start | bytes 245768 | tf_op jit(solution)/shard_map/ppermute | solution.py:328
  20.2 3.4 %collective-permute-start.8 = (f32[40,128]{1,0:T(8,128)S(1)}, f32[40,128]{1,0:T(8,128)S(1)}, u32[]{:S(2)}, u32[]{:S(2)}) collective-permute-start(f32[40,128]{1,0:T(8,128)S(1)} %grams.1.refs_0_), channel_id=1, source_target_pairs={{0,3},{1,2},{2,1},{3,0},{4,7},{5,6},{6,5},{7,4},{8,11},{9,10},{10,... | collective-permute-start | bytes 61448 | tf_op jit(solution)/shard_map/ppermute | solution.py:319
  20.9 3.9 %collective-permute-start.7 = (f32[40,128]{1,0:T(8,128)S(1)}, f32[40,128]{1,0:T(8,128)S(1)}, u32[]{:S(2)}, u32[]{:S(2)}) collective-permute-start(f32[40,128]{1,0:T(8,128)S(1)} %grams.1.refs_0_), channel_id=1, source_target_pairs={{0,2},{1,3},{2,0},{3,1},{4,6},{5,7},{6,4},{7,5},{8,10},{9,11},{10,... | collective-permute-start | bytes 61448 | tf_op jit(solution)/shard_map/ppermute | solution.py:319
  21.8 3.1 %collective-permute-start.6 = (f32[40,128]{1,0:T(8,128)S(1)}, f32[40,128]{1,0:T(8,128)S(1)}, u32[]{:S(2)}, u32[]{:S(2)}) collective-permute-start(f32[40,128]{1,0:T(8,128)S(1)} %grams.1.refs_0_), channel_id=1, source_target_pairs={{0,1},{1,0},{2,3},{3,2},{4,5},{5,4},{6,7},{7,6},{8,9},{9,8},{10,11... | collective-permute-start | bytes 61448 | tf_op jit(solution)/shard_map/ppermute | solution.py:319

commit v23 on v21

--- a/solution.py
+++ b/solution.py
@@ -10,7 +10,7 @@
 damping = 0.5
 VMEM_LIMIT = 32 * 1024 * 1024
 SMALL = 4
-SOURCES = {1: (), 2: ((1, 0),), 4: ((2, 0, 3, 1), (3, 2, 1, 0), (1, 3, 0, 2))}
+SOURCES = {1: (), 2: ((1, 0),), 4: ((2, 0, 3, 1), (1, 3, 0, 2), (3, 2, 1, 0))}
 
 
 def token_weights(seq_ids, counts, first):

time: 25.4 us -> 26.1 us (1.028)
  starting transfers between devices: 11.4 us -> 12.3 us
    ppermute x3, starting transfers between devices: 6.04 us -> 6.94 us  [from_all(): return [lax.ppermute(value, axis, swap) for swap in swaps] + [value]]
  transfers between devices with their start and end apart: 8 -> 8, of which waited for: 7 -> 6; matrix products, arithmetic and copies ran while one was open for 1% -> 1% of each run, Pallas kernels for 1% -> 1%
where the time goes in v23:
time: 26.1 us; the launch traced here: 25.9 us
  starting transfers between devices  12.3 us (47%)
  waiting for transfers between devices  8.54 us (33%)
  Pallas kernels  4.88 us (19%)
    ppermute x3, starting transfers between devices, from_all(): return [lax.ppermute(value, axis, swap) for swap in swaps] + [value]  6.94 us
    ppermute x5, starting transfers between devices, from_partner(): return lax.ppermute(value, axis, [(i, i ^ m) for i in range(size)])  5.31 us
    ppermute x5, waiting for transfers between devices, from_partner(): return lax.ppermute(value, axis, [(i, i ^ m) for i in range(size)])  4.99 us
    ppermute x3, waiting for transfers between devices, from_all(): return [lax.ppermute(value, axis, swap) for swap in swaps] + [value]  3.55 us
    pallas_call x1, Pallas kernels, project(): pl.pallas_call(functools.partial(project_kernel, own), out_shape=[jax.Sha...  2.19 us
    pallas_call x1, Pallas kernels, solve(): pl.pallas_call(functools.partial(solve_kernel, seqs), out_shape=jax.Shape...  1.82 us
  transfers between devices with their start and end apart: 8, of which 6 were waited for; matrix products, arithmetic and copies ran while one was open for 1% of the time, Pallas kernels for 1%

profile of v23, /device:TPU:0, one launch (start us, length us, event | category | flops | bytes accessed | tf_op | source)
XLA Modules:
  0.0 25.9 jit_solution(12762638876384493579)
XLA Ops:
  0.0 2.2 %project.1 = (f32[96,256]{1,0:T(8,128)S(1)}, f32[96,256]{1,0:T(8,128)S(1)}) custom-call(s32[1]{0:T(128)} %bitcast.1.rank_ref, bf16[2752,256]{1,0:T(8,128)(2,1)} %bitcast.5, bf16[256,1024]{1,0:T(8,128)(2,1)} %g_hbm.1, bf16[64,2752]{1,0:T(8,128)(2,1)} %bitcast.6, bf16[64,1024]{1,0:T(8,128)(2,1)} %bitcast.7), custom_call_target="tpu_custom_call" | custom-call | tf_op jit(solution)/shard_map/project/pallas_call | solution.py:109
  2.2 0.5 %collective-permute-start = (f32[96,256]{1,0:T(8,128)S(1)}, f32[96,256]{1,0:T(8,128)S(1)}, u32[]{:S(2)}, u32[]{:S(2)}) collective-permute-start(f32[96,256]{1,0:T(8,128)S(1)} %get-tuple-element.10), channel_id=1, source_target_pairs={{0,1},{1,0},{2,3},{3,2},{4,5},{5,4},{6,7},{7,6},{8,9},{9,8},{10,11... | collective-permute-start | bytes 294920 | tf_op jit(solution)/shard_map/ppermute | solution.py:319
  2.8 0.1 convert_reduce_fusion
  2.9 0.8 %collective-permute-done.came_ref = f32[96,256]{1,0:T(8,128)S(1)} collective-permute-done((f32[96,256]{1,0:T(8,128)S(1)}, f32[96,256]{1,0:T(8,128)S(1)}, u32[]{:S(2)}, u32[]{:S(2)}) %collective-permute-start) | collective-permute-done | bytes 98336 | tf_op jit(solution)/shard_map/ppermute | solution.py:319
  3.7 2.9 %collective-permute-start.1 = (f32[64,256]{1,0:T(8,128)S(1)}, f32[64,256]{1,0:T(8,128)S(1)}, u32[]{:S(2)}, u32[]{:S(2)}) collective-permute-start(f32[64,256]{1,0:T(8,128)S(1)} %get-tuple-element.12), channel_id=1, source_target_pairs={{0,2},{1,3},{2,0},{3,1},{4,6},{5,7},{6,4},{7,5},{8,10},{9,11},{10,... | collective-permute-start | bytes 196616 | tf_op jit(solution)/shard_map/ppermute | solution.py:319
  6.6 0.1 fusion.1.weights_ref
  6.7 0.0 copy-done
  6.7 0.2 pick.1.asked_ref
  6.8 2.2 %collective-permute-done.1.came_ref = f32[64,256]{1,0:T(8,128)S(1)} collective-permute-done((f32[64,256]{1,0:T(8,128)S(1)}, f32[64,256]{1,0:T(8,128)S(1)}, u32[]{:S(2)}, u32[]{:S(2)}) %collective-permute-start.1) | collective-permute-done | bytes 65568 | tf_op jit(solution)/shard_map/ppermute | solution.py:319
  9.0 0.4 %gradients.1.refs_3_ = f32[160,128]{1,0:T(8,128)S(1)} custom-call(f32[16,256]{1,0:T(8,128)S(1)} %fusion.1.weights_ref, f32[64,256]{1,0:T(8,128)S(1)} %get-tuple-element.11.kept_ref, f32[64,256]{1,0:T(8,128)S(1)} %collective-permute-done.1.came_ref, f32[32,128]{1,0:T(8,128)S(1)} %pick.1.asked_ref), custom_call_target="tpu_custom_call" | custom-call | tf_op jit(solution)/shard_map/gradients/pallas_call | solution.py:223
  9.4 2.0 %collective-permute-start.2 = (f32[160,128]{1,0:T(8,128)S(1)}, f32[160,128]{1,0:T(8,128)S(1)}, u32[]{:S(2)}, u32[]{:S(2)}) collective-permute-start(f32[160,128]{1,0:T(8,128)S(1)} %gradients.1.refs_3_), channel_id=1, source_target_pairs={{8,0},{0,4},{12,8},{4,12},{9,1},{1,5},{13,9},{5,13},{10,2},{2,6},{... | collective-permute-start | bytes 245768 | tf_op jit(solution)/shard_map/ppermute | solution.py:328
  11.4 1.1 %collective-permute-start.3 = (f32[160,128]{1,0:T(8,128)S(1)}, f32[160,128]{1,0:T(8,128)S(1)}, u32[]{:S(2)}, u32[]{:S(2)}) collective-permute-start(f32[160,128]{1,0:T(8,128)S(1)} %gradients.1.refs_3_), channel_id=1, source_target_pairs={{4,0},{12,4},{0,8},{8,12},{5,1},{13,5},{1,9},{9,13},{6,2},{14,6},{... | collective-permute-start | bytes 245768 | tf_op jit(solution)/shard_map/ppermute | solution.py:328
  12.5 3.9 %collective-permute-start.4 = (f32[160,128]{1,0:T(8,128)S(1)}, f32[160,128]{1,0:T(8,128)S(1)}, u32[]{:S(2)}, u32[]{:S(2)}) collective-permute-start(f32[160,128]{1,0:T(8,128)S(1)} %gradients.1.refs_3_), channel_id=1, source_target_pairs={{12,0},{8,4},{4,8},{0,12},{13,1},{9,5},{5,9},{1,13},{14,2},{10,6},... | collective-permute-start | bytes 245768 | tf_op jit(solution)/shard_map/ppermute | solution.py:328
  16.3 0.0 collective-permute-done.2.refs_0_
  16.3 0.1 collective-permute-done.3.refs_1_
  16.4 3.5 %collective-permute-done.4.refs_2_ = f32[160,128]{1,0:T(8,128)S(1)} collective-permute-done((f32[160,128]{1,0:T(8,128)S(1)}, f32[160,128]{1,0:T(8,128)S(1)}, u32[]{:S(2)}, u32[]{:S(2)}) %collective-permute-start.4) | collective-permute-done | bytes 81952 | tf_op jit(solution)/shard_map/ppermute | solution.py:328
  19.9 0.3 %grams.1.refs_3_ = f32[40,128]{1,0:T(8,128)S(1)} custom-call(s32[1]{0:T(128)} %bitcast.me_ref, f32[160,128]{1,0:T(8,128)S(1)} %collective-permute-done.2.refs_0_, f32[160,128]{1,0:T(8,128)S(1)} %collective-permute-done.3.refs_1_, f32[160,128]{1,0:T(8,128)S(1)} %collective-permute-done.4.refs_2_, f32[160,128]{1,0:T(8,128)S(1)} %gradients.1.refs_3_), custom_call_target="tpu_custom_call" | custom-call | tf_op jit(solution)/shard_map/grams/pallas_call | solution.py:258
  20.2 0.0 collective-permute-start.5
  20.3 1.6 %collective-permute-start.6 = (f32[40,128]{1,0:T(8,128)S(1)}, f32[40,128]{1,0:T(8,128)S(1)}, u32[]{:S(2)}, u32[]{:S(2)}) collective-permute-start(f32[40,128]{1,0:T(8,128)S(1)} %grams.1.refs_3_), channel_id=1, source_target_pairs={{0,2},{1,3},{2,0},{3,1},{4,6},{5,7},{6,4},{7,5},{8,10},{9,11},{10,... | collective-permute-start | bytes 61448 | tf_op jit(solution)/shard_map/ppermute | solution.py:319
  21.8 0.3 %collective-permute-start.7 = (f32[40,128]{1,0:T(8,128)S(1)}, f32[40,128]{1,0:T(8,128)S(1)}, u32[]{:S(2)}, u32[]{:S(2)}) collective-permute-start(f32[40,128]{1,0:T(8,128)S(1)} %grams.1.refs_3_), channel_id=1, source_target_pairs={{0,1},{1,0},{2,3},{3,2},{4,5},{5,4},{6,7},{7,6},{8,9},{9,8},{10,11... | collective-permute-start | bytes 61448 | tf_op jit(solution)/shard_map/ppermute | solution.py:319
  22.1 1.5 %collective-permute-done.5.refs_0_ = f32[40,128]{1,0:T(8,128)S(1)} collective-permute-done((f32[40,128]{1,0:T(8,128)S(1)}, f32[40,128]{1,0:T(8,128)S(1)}, u32[]{:S(2)}, u32[]{:S(2)}) %collective-permute-start.5) | collective-permute-done | bytes 20512 | tf_op jit(solution)/shard_map/ppermute | solution.py:319
  23.6 0.5 %collective-permute-done.6.refs_1_ = f32[40,128]{1,0:T(8,128)S(1)} collective-permute-done((f32[40,128]{1,0:T(8,128)S(1)}, f32[40,128]{1,0:T(8,128)S(1)}, u32[]{:S(2)}, u32[]{:S(2)}) %collective-permute-start.6) | collective-permute-done | bytes 20512 | tf_op jit(solution)/shard_map/ppermute | solution.py:319
  24.1 0.0 collective-permute-done.7.refs_2_
  24.1 1.8 %solve.1 = f32[16,16]{1,0:T(8,128)} custom-call(f32[40,128]{1,0:T(8,128)S(1)} %collective-permute-done.5.refs_0_, f32[40,128]{1,0:T(8,128)S(1)} %collective-permute-done.6.refs_1_, f32[40,128]{1,0:T(8,128)S(1)} %collective-permute-done.7.refs_2_, f32[40,128]{1,0:T(8,128)S(1)} %grams.1.refs_3_), custom_call_target="tpu_custom_call" | custom-call | tf_op jit(solution)/shard_map/solve/pallas_call | solution.py:310
  (8 shorter events, 0.0 us)
Async XLA Ops:
  0.0 2.7 %copy-start.2 = (s32[16]{0:T(128)S(1)}, s32[16]{0:T(128)}, u32[]{:S(2)}) copy-start(s32[16]{0:T(128)} %param.12) | copy-start | bytes 196
  0.0 2.8 %copy-start.1 = (s32[256]{0:T(256)S(1)}, s32[256]{0:T(256)}, u32[]{:S(2)}) copy-start(s32[256]{0:T(256)} %param.11) | copy-start | bytes 3076
  0.0 6.7 %copy-start = (f32[4,4096]{1,0:T(4,128)S(1)}, f32[4,4096]{1,0:T(4,128)}, u32[]{:S(2)}) copy-start(f32[4,4096]{1,0:T(4,128)} %queries_ref.1) | copy-start | bytes 196612
  2.2 1.5 %collective-permute-start = (f32[96,256]{1,0:T(8,128)S(1)}, f32[96,256]{1,0:T(8,128)S(1)}, u32[]{:S(2)}, u32[]{:S(2)}) collective-permute-start(f32[96,256]{1,0:T(8,128)S(1)} %get-tuple-element.10), channel_id=1, source_target_pairs={{0,1},{1,0},{2,3},{3,2},{4,5},{5,4},{6,7},{7,6},{8,9},{9,8},{10,11... | collective-permute-start | bytes 294920 | tf_op jit(solution)/shard_map/ppermute | solution.py:319
  3.7 5.3 %collective-permute-start.1 = (f32[64,256]{1,0:T(8,128)S(1)}, f32[64,256]{1,0:T(8,128)S(1)}, u32[]{:S(2)}, u32[]{:S(2)}) collective-permute-start(f32[64,256]{1,0:T(8,128)S(1)} %get-tuple-element.12), channel_id=1, source_target_pairs={{0,2},{1,3},{2,0},{3,1},{4,6},{5,7},{6,4},{7,5},{8,10},{9,11},{10,... | collective-permute-start | bytes 196616 | tf_op jit(solution)/shard_map/ppermute | solution.py:319
  9.4 6.9 %collective-permute-start.2 = (f32[160,128]{1,0:T(8,128)S(1)}, f32[160,128]{1,0:T(8,128)S(1)}, u32[]{:S(2)}, u32[]{:S(2)}) collective-permute-start(f32[160,128]{1,0:T(8,128)S(1)} %gradients.1.refs_3_), channel_id=1, source_target_pairs={{8,0},{0,4},{12,8},{4,12},{9,1},{1,5},{13,9},{5,13},{10,2},{2,6},{... | collective-permute-start | bytes 245768 | tf_op jit(solution)/shard_map/ppermute | solution.py:328
  11.4 5.0 %collective-permute-start.3 = (f32[160,128]{1,0:T(8,128)S(1)}, f32[160,128]{1,0:T(8,128)S(1)}, u32[]{:S(2)}, u32[]{:S(2)}) collective-permute-start(f32[160,128]{1,0:T(8,128)S(1)} %gradients.1.refs_3_), channel_id=1, source_target_pairs={{4,0},{12,4},{0,8},{8,12},{5,1},{13,5},{1,9},{9,13},{6,2},{14,6},{... | collective-permute-start | bytes 245768 | tf_op jit(solution)/shard_map/ppermute | solution.py:328
  12.5 7.4 %collective-permute-start.4 = (f32[160,128]{1,0:T(8,128)S(1)}, f32[160,128]{1,0:T(8,128)S(1)}, u32[]{:S(2)}, u32[]{:S(2)}) collective-permute-start(f32[160,128]{1,0:T(8,128)S(1)} %gradients.1.refs_3_), channel_id=1, source_target_pairs={{12,0},{8,4},{4,8},{0,12},{13,1},{9,5},{5,9},{1,13},{14,2},{10,6},... | collective-permute-start | bytes 245768 | tf_op jit(solution)/shard_map/ppermute | solution.py:328
  20.2 3.4 %collective-permute-start.5 = (f32[40,128]{1,0:T(8,128)S(1)}, f32[40,128]{1,0:T(8,128)S(1)}, u32[]{:S(2)}, u32[]{:S(2)}) collective-permute-start(f32[40,128]{1,0:T(8,128)S(1)} %grams.1.refs_3_), channel_id=1, source_target_pairs={{0,3},{1,2},{2,1},{3,0},{4,7},{5,6},{6,5},{7,4},{8,11},{9,10},{10,... | collective-permute-start | bytes 61448 | tf_op jit(solution)/shard_map/ppermute | solution.py:319
  20.3 3.8 %collective-permute-start.6 = (f32[40,128]{1,0:T(8,128)S(1)}, f32[40,128]{1,0:T(8,128)S(1)}, u32[]{:S(2)}, u32[]{:S(2)}) collective-permute-start(f32[40,128]{1,0:T(8,128)S(1)} %grams.1.refs_3_), channel_id=1, source_target_pairs={{0,2},{1,3},{2,0},{3,1},{4,6},{5,7},{6,4},{7,5},{8,10},{9,11},{10,... | collective-permute-start | bytes 61448 | tf_op jit(solution)/shard_map/ppermute | solution.py:319
  21.8 2.3 %collective-permute-start.7 = (f32[40,128]{1,0:T(8,128)S(1)}, f32[40,128]{1,0:T(8,128)S(1)}, u32[]{:S(2)}, u32[]{:S(2)}) collective-permute-start(f32[40,128]{1,0:T(8,128)S(1)} %grams.1.refs_3_), channel_id=1, source_target_pairs={{0,1},{1,0},{2,3},{3,2},{4,5},{5,4},{6,7},{7,6},{8,9},{9,8},{10,11... | collective-permute-start | bytes 61448 | tf_op jit(solution)/shard_map/ppermute | solution.py:319

commit v24 on v15

--- a/solution.py
+++ b/solution.py
@@ -10,7 +10,7 @@
 damping = 0.5
 VMEM_LIMIT = 32 * 1024 * 1024
 SMALL = 4
-SHIFTS = {1: (), 2: (1,), 4: (2, 1, 3)}
+SHIFTS = {1: (), 2: (1,), 4: (1, 3, 2)}
 
 
 def token_weights(seq_ids, counts, first):

time: 25.5 us -> 26.8 us (1.051)
  waiting for transfers between devices: 8.06 us -> 11.2 us
  starting transfers between devices: 12.1 us -> 10.3 us
    ppermute x3, waiting for transfers between devices: 3.07 us -> 6.25 us  [from_all(): return [lax.ppermute(value, axis, shift) for shift in shifts] + [value]]
    ppermute x3, starting transfers between devices: 6.84 us -> 5.03 us  [from_all(): return [lax.ppermute(value, axis, shift) for shift in shifts] + [value]]
where the time goes in v24:
time: 26.8 us; the launch traced here: 26.7 us
  waiting for transfers between devices  11.2 us (42%)
  starting transfers between devices  10.3 us (38%)
  Pallas kernels  4.88 us (18%)
    ppermute x3, waiting for transfers between devices, from_all(): return [lax.ppermute(value, axis, shift) for shift in shifts] + [value]  6.25 us
    ppermute x5, starting transfers between devices, from_partner(): return lax.ppermute(value, axis, [(i, i ^ m) for i in range(size)])  5.31 us
    ppermute x3, starting transfers between devices, from_all(): return [lax.ppermute(value, axis, shift) for shift in shifts] + [value]  5.03 us
    ppermute x5, waiting for transfers between devices, from_partner(): return lax.ppermute(value, axis, [(i, i ^ m) for i in range(size)])  4.99 us
    pallas_call x1, Pallas kernels, project(): pl.pallas_call(functools.partial(project_kernel, own), out_shape=[jax.Sha...  2.19 us
    pallas_call x1, Pallas kernels, solve(): pl.pallas_call(functools.partial(solve_kernel, seqs), out_shape=jax.Shape...  1.82 us
  transfers between devices with their start and end apart: 8, of which 7 were waited for; matrix products, arithmetic and copies ran while one was open for 1% of the time, Pallas kernels for 1%

profile of v24, /device:TPU:0, one launch (start us, length us, event | category | flops | bytes accessed | tf_op | source)
XLA Modules:
  0.0 26.7 jit_solution(15036861595299880807)
XLA Ops:
  0.0 2.2 %project.1 = (f32[96,256]{1,0:T(8,128)S(1)}, f32[96,256]{1,0:T(8,128)S(1)}) custom-call(s32[1]{0:T(128)} %bitcast.1.rank_ref, bf16[2752,256]{1,0:T(8,128)(2,1)} %bitcast.5, bf16[256,1024]{1,0:T(8,128)(2,1)} %g_hbm.1, bf16[64,2752]{1,0:T(8,128)(2,1)} %bitcast.6, bf16[64,1024]{1,0:T(8,128)(2,1)} %bitcast.7), custom_call_target="tpu_custom_call" | custom-call | tf_op jit(solution)/shard_map/project/pallas_call | solution.py:109
  2.2 0.5 %collective-permute-start = (f32[96,256]{1,0:T(8,128)S(1)}, f32[96,256]{1,0:T(8,128)S(1)}, u32[]{:S(2)}, u32[]{:S(2)}) collective-permute-start(f32[96,256]{1,0:T(8,128)S(1)} %get-tuple-element.10), channel_id=1, source_target_pairs={{0,1},{1,0},{2,3},{3,2},{4,5},{5,4},{6,7},{7,6},{8,9},{9,8},{10,11... | collective-permute-start | bytes 294920 | tf_op jit(solution)/shard_map/ppermute | solution.py:321
  2.7 0.0 copy-done.2
  2.8 0.1 convert_reduce_fusion
  2.9 0.8 %collective-permute-done.came_ref = f32[96,256]{1,0:T(8,128)S(1)} collective-permute-done((f32[96,256]{1,0:T(8,128)S(1)}, f32[96,256]{1,0:T(8,128)S(1)}, u32[]{:S(2)}, u32[]{:S(2)}) %collective-permute-start) | collective-permute-done | bytes 98336 | tf_op jit(solution)/shard_map/ppermute | solution.py:321
  3.7 2.9 %collective-permute-start.1 = (f32[64,256]{1,0:T(8,128)S(1)}, f32[64,256]{1,0:T(8,128)S(1)}, u32[]{:S(2)}, u32[]{:S(2)}) collective-permute-start(f32[64,256]{1,0:T(8,128)S(1)} %get-tuple-element.12), channel_id=1, source_target_pairs={{0,2},{1,3},{2,0},{3,1},{4,6},{5,7},{6,4},{7,5},{8,10},{9,11},{10,... | collective-permute-start | bytes 196616 | tf_op jit(solution)/shard_map/ppermute | solution.py:321
  6.6 0.1 fusion.1.weights_ref
  6.7 0.2 pick.1.asked_ref
  6.8 2.2 %collective-permute-done.1.came_ref = f32[64,256]{1,0:T(8,128)S(1)} collective-permute-done((f32[64,256]{1,0:T(8,128)S(1)}, f32[64,256]{1,0:T(8,128)S(1)}, u32[]{:S(2)}, u32[]{:S(2)}) %collective-permute-start.1) | collective-permute-done | bytes 65568 | tf_op jit(solution)/shard_map/ppermute | solution.py:321
  9.0 0.4 %gradients.1.refs_3_ = f32[160,128]{1,0:T(8,128)S(1)} custom-call(f32[16,256]{1,0:T(8,128)S(1)} %fusion.1.weights_ref, f32[64,256]{1,0:T(8,128)S(1)} %get-tuple-element.11.kept_ref, f32[64,256]{1,0:T(8,128)S(1)} %collective-permute-done.1.came_ref, f32[32,128]{1,0:T(8,128)S(1)} %pick.1.asked_ref), custom_call_target="tpu_custom_call" | custom-call | tf_op jit(solution)/shard_map/gradients/pallas_call | solution.py:223
  9.4 2.0 %collective-permute-start.2 = (f32[160,128]{1,0:T(8,128)S(1)}, f32[160,128]{1,0:T(8,128)S(1)}, u32[]{:S(2)}, u32[]{:S(2)}) collective-permute-start(f32[160,128]{1,0:T(8,128)S(1)} %gradients.1.refs_3_), channel_id=1, source_target_pairs={{0,4},{4,8},{8,12},{12,0},{1,5},{5,9},{9,13},{13,1},{2,6},{6,10},{... | collective-permute-start | bytes 245768 | tf_op jit(solution)/shard_map/ppermute | solution.py:330
  11.4 2.1 %collective-permute-start.3 = (f32[160,128]{1,0:T(8,128)S(1)}, f32[160,128]{1,0:T(8,128)S(1)}, u32[]{:S(2)}, u32[]{:S(2)}) collective-permute-start(f32[160,128]{1,0:T(8,128)S(1)} %gradients.1.refs_3_), channel_id=1, source_target_pairs={{0,12},{4,0},{8,4},{12,8},{1,13},{5,1},{9,5},{13,9},{2,14},{6,2},{... | collective-permute-start | bytes 245768 | tf_op jit(solution)/shard_map/ppermute | solution.py:330
  13.5 0.9 %collective-permute-start.4 = (f32[160,128]{1,0:T(8,128)S(1)}, f32[160,128]{1,0:T(8,128)S(1)}, u32[]{:S(2)}, u32[]{:S(2)}) collective-permute-start(f32[160,128]{1,0:T(8,128)S(1)} %gradients.1.refs_3_), channel_id=1, source_target_pairs={{0,8},{4,12},{8,0},{12,4},{1,9},{5,13},{9,1},{13,5},{2,10},{6,14},... | collective-permute-start | bytes 245768 | tf_op jit(solution)/shard_map/ppermute | solution.py:330
  14.4 2.4 %collective-permute-done.2.refs_0_ = f32[160,128]{1,0:T(8,128)S(1)} collective-permute-done((f32[160,128]{1,0:T(8,128)S(1)}, f32[160,128]{1,0:T(8,128)S(1)}, u32[]{:S(2)}, u32[]{:S(2)}) %collective-permute-start.2) | collective-permute-done | bytes 81952 | tf_op jit(solution)/shard_map/ppermute | solution.py:330
  16.8 0.1 collective-permute-done.3.refs_1_
  16.9 3.8 %collective-permute-done.4.refs_2_ = f32[160,128]{1,0:T(8,128)S(1)} collective-permute-done((f32[160,128]{1,0:T(8,128)S(1)}, f32[160,128]{1,0:T(8,128)S(1)}, u32[]{:S(2)}, u32[]{:S(2)}) %collective-permute-start.4) | collective-permute-done | bytes 81952 | tf_op jit(solution)/shard_map/ppermute | solution.py:330
  20.7 0.3 %grams.1.refs_3_ = f32[40,128]{1,0:T(8,128)S(1)} custom-call(s32[1]{0:T(128)} %bitcast.me_ref, f32[160,128]{1,0:T(8,128)S(1)} %collective-permute-done.2.refs_0_, f32[160,128]{1,0:T(8,128)S(1)} %collective-permute-done.3.refs_1_, f32[160,128]{1,0:T(8,128)S(1)} %collective-permute-done.4.refs_2_, f32[160,128]{1,0:T(8,128)S(1)} %gradients.1.refs_3_), custom_call_target="tpu_custom_call" | custom-call | tf_op jit(solution)/shard_map/grams/pallas_call | solution.py:260
  21.0 0.0 collective-permute-start.5
  21.0 1.5 %collective-permute-start.6 = (f32[40,128]{1,0:T(8,128)S(1)}, f32[40,128]{1,0:T(8,128)S(1)}, u32[]{:S(2)}, u32[]{:S(2)}) collective-permute-start(f32[40,128]{1,0:T(8,128)S(1)} %grams.1.refs_3_), channel_id=1, source_target_pairs={{0,2},{1,3},{2,0},{3,1},{4,6},{5,7},{6,4},{7,5},{8,10},{9,11},{10,... | collective-permute-start | bytes 61448 | tf_op jit(solution)/shard_map/ppermute | solution.py:321
  22.6 0.3 %collective-permute-start.7 = (f32[40,128]{1,0:T(8,128)S(1)}, f32[40,128]{1,0:T(8,128)S(1)}, u32[]{:S(2)}, u32[]{:S(2)}) collective-permute-start(f32[40,128]{1,0:T(8,128)S(1)} %grams.1.refs_3_), channel_id=1, source_target_pairs={{0,1},{1,0},{2,3},{3,2},{4,5},{5,4},{6,7},{7,6},{8,9},{9,8},{10,11... | collective-permute-start | bytes 61448 | tf_op jit(solution)/shard_map/ppermute | solution.py:321
  22.9 1.5 %collective-permute-done.5.refs_0_ = f32[40,128]{1,0:T(8,128)S(1)} collective-permute-done((f32[40,128]{1,0:T(8,128)S(1)}, f32[40,128]{1,0:T(8,128)S(1)}, u32[]{:S(2)}, u32[]{:S(2)}) %collective-permute-start.5) | collective-permute-done | bytes 20512 | tf_op jit(solution)/shard_map/ppermute | solution.py:321
  24.4 0.5 %collective-permute-done.6.refs_1_ = f32[40,128]{1,0:T(8,128)S(1)} collective-permute-done((f32[40,128]{1,0:T(8,128)S(1)}, f32[40,128]{1,0:T(8,128)S(1)}, u32[]{:S(2)}, u32[]{:S(2)}) %collective-permute-start.6) | collective-permute-done | bytes 20512 | tf_op jit(solution)/shard_map/ppermute | solution.py:321
  24.9 0.0 collective-permute-done.7.refs_2_
  24.9 1.8 %solve.1 = f32[16,16]{1,0:T(8,128)} custom-call(f32[40,128]{1,0:T(8,128)S(1)} %collective-permute-done.5.refs_0_, f32[40,128]{1,0:T(8,128)S(1)} %collective-permute-done.6.refs_1_, f32[40,128]{1,0:T(8,128)S(1)} %collective-permute-done.7.refs_2_, f32[40,128]{1,0:T(8,128)S(1)} %grams.1.refs_3_), custom_call_target="tpu_custom_call" | custom-call | tf_op jit(solution)/shard_map/solve/pallas_call | solution.py:312
  (8 shorter events, 0.0 us)
Async XLA Ops:
  0.0 2.7 %copy-start.2 = (s32[16]{0:T(128)S(1)}, s32[16]{0:T(128)}, u32[]{:S(2)}) copy-start(s32[16]{0:T(128)} %param.12) | copy-start | bytes 196
  0.0 2.8 %copy-start.1 = (s32[256]{0:T(256)S(1)}, s32[256]{0:T(256)}, u32[]{:S(2)}) copy-start(s32[256]{0:T(256)} %param.11) | copy-start | bytes 3076
  0.0 6.7 %copy-start = (f32[4,4096]{1,0:T(4,128)S(1)}, f32[4,4096]{1,0:T(4,128)}, u32[]{:S(2)}) copy-start(f32[4,4096]{1,0:T(4,128)} %queries_ref.1) | copy-start | bytes 196612
  2.2 1.5 %collective-permute-start = (f32[96,256]{1,0:T(8,128)S(1)}, f32[96,256]{1,0:T(8,128)S(1)}, u32[]{:S(2)}, u32[]{:S(2)}) collective-permute-start(f32[96,256]{1,0:T(8,128)S(1)} %get-tuple-element.10), channel_id=1, source_target_pairs={{0,1},{1,0},{2,3},{3,2},{4,5},{5,4},{6,7},{7,6},{8,9},{9,8},{10,11... | collective-permute-start | bytes 294920 | tf_op jit(solution)/shard_map/ppermute | solution.py:321
  3.7 5.3 %collective-permute-start.1 = (f32[64,256]{1,0:T(8,128)S(1)}, f32[64,256]{1,0:T(8,128)S(1)}, u32[]{:S(2)}, u32[]{:S(2)}) collective-permute-start(f32[64,256]{1,0:T(8,128)S(1)} %get-tuple-element.12), channel_id=1, source_target_pairs={{0,2},{1,3},{2,0},{3,1},{4,6},{5,7},{6,4},{7,5},{8,10},{9,11},{10,... | collective-permute-start | bytes 196616 | tf_op jit(solution)/shard_map/ppermute | solution.py:321
  9.4 7.4 %collective-permute-start.2 = (f32[160,128]{1,0:T(8,128)S(1)}, f32[160,128]{1,0:T(8,128)S(1)}, u32[]{:S(2)}, u32[]{:S(2)}) collective-permute-start(f32[160,128]{1,0:T(8,128)S(1)} %gradients.1.refs_3_), channel_id=1, source_target_pairs={{0,4},{4,8},{8,12},{12,0},{1,5},{5,9},{9,13},{13,1},{2,6},{6,10},{... | collective-permute-start | bytes 245768 | tf_op jit(solution)/shard_map/ppermute | solution.py:330
  11.4 5.5 %collective-permute-start.3 = (f32[160,128]{1,0:T(8,128)S(1)}, f32[160,128]{1,0:T(8,128)S(1)}, u32[]{:S(2)}, u32[]{:S(2)}) collective-permute-start(f32[160,128]{1,0:T(8,128)S(1)} %gradients.1.refs_3_), channel_id=1, source_target_pairs={{0,12},{4,0},{8,4},{12,8},{1,13},{5,1},{9,5},{13,9},{2,14},{6,2},{... | collective-permute-start | bytes 245768 | tf_op jit(solution)/shard_map/ppermute | solution.py:330
  13.5 7.2 %collective-permute-start.4 = (f32[160,128]{1,0:T(8,128)S(1)}, f32[160,128]{1,0:T(8,128)S(1)}, u32[]{:S(2)}, u32[]{:S(2)}) collective-permute-start(f32[160,128]{1,0:T(8,128)S(1)} %gradients.1.refs_3_), channel_id=1, source_target_pairs={{0,8},{4,12},{8,0},{12,4},{1,9},{5,13},{9,1},{13,5},{2,10},{6,14},... | collective-permute-start | bytes 245768 | tf_op jit(solution)/shard_map/ppermute | solution.py:330
  21.0 3.4 %collective-permute-start.5 = (f32[40,128]{1,0:T(8,128)S(1)}, f32[40,128]{1,0:T(8,128)S(1)}, u32[]{:S(2)}, u32[]{:S(2)}) collective-permute-start(f32[40,128]{1,0:T(8,128)S(1)} %grams.1.refs_3_), channel_id=1, source_target_pairs={{0,3},{1,2},{2,1},{3,0},{4,7},{5,6},{6,5},{7,4},{8,11},{9,10},{10,... | collective-permute-start | bytes 61448 | tf_op jit(solution)/shard_map/ppermute | solution.py:321
  21.0 3.8 %collective-permute-start.6 = (f32[40,128]{1,0:T(8,128)S(1)}, f32[40,128]{1,0:T(8,128)S(1)}, u32[]{:S(2)}, u32[]{:S(2)}) collective-permute-start(f32[40,128]{1,0:T(8,128)S(1)} %grams.1.refs_3_), channel_id=1, source_target_pairs={{0,2},{1,3},{2,0},{3,1},{4,6},{5,7},{6,4},{7,5},{8,10},{9,11},{10,... | collective-permute-start | bytes 61448 | tf_op jit(solution)/shard_map/ppermute | solution.py:321
  22.6 2.3 %collective-permute-start.7 = (f32[40,128]{1,0:T(8,128)S(1)}, f32[40,128]{1,0:T(8,128)S(1)}, u32[]{:S(2)}, u32[]{:S(2)}) collective-permute-start(f32[40,128]{1,0:T(8,128)S(1)} %grams.1.refs_3_), channel_id=1, source_target_pairs={{0,1},{1,0},{2,3},{3,2},{4,5},{5,4},{6,7},{7,6},{8,9},{9,8},{10,11... | collective-permute-start | bytes 61448 | tf_op jit(solution)/shard_map/ppermute | solution.py:321

commit v25 on v23

--- a/solution.py
+++ b/solution.py
@@ -10,7 +10,7 @@
 damping = 0.5
 VMEM_LIMIT = 32 * 1024 * 1024
 SMALL = 4
-SOURCES = {1: (), 2: ((1, 0),), 4: ((2, 0, 3, 1), (1, 3, 0, 2), (3, 2, 1, 0))}
+SOURCES = {1: (), 2: ((1, 0),), 4: ((1, 0, 3, 2), (3, 2, 0, 1), (2, 3, 1, 0))}
 
 
 def token_weights(seq_ids, counts, first):

time: 26.1 us -> 27.7 us (1.061)
  waiting for transfers between devices: 8.54 us -> 11.3 us
  starting transfers between devices: 12.3 us -> 11.1 us
    ppermute x3, waiting for transfers between devices: 3.55 us -> 5.57 us  [from_all(): return [lax.ppermute(value, axis, swap) for swap in swaps] + [value]]
    ppermute x3, starting transfers between devices: 6.94 us -> 5.82 us  [from_all(): return [lax.ppermute(value, axis, swap) for swap in swaps] + [value]]
    ppermute x5, waiting for transfers between devices: 4.99 us -> 5.73 us  [from_partner(): return lax.ppermute(value, axis, [(i, i ^ m) for i in range(size)])]
where the time goes in v25:
time: 27.7 us; the launch traced here: 27.6 us
  waiting for transfers between devices  11.3 us (41%)
  starting transfers between devices  11.1 us (40%)
  Pallas kernels  4.88 us (18%)
    ppermute x3, starting transfers between devices, from_all(): return [lax.ppermute(value, axis, swap) for swap in swaps] + [value]  5.82 us
    ppermute x5, waiting for transfers between devices, from_partner(): return lax.ppermute(value, axis, [(i, i ^ m) for i in range(size)])  5.73 us
    ppermute x3, waiting for transfers between devices, from_all(): return [lax.ppermute(value, axis, swap) for swap in swaps] + [value]  5.57 us
    ppermute x5, starting transfers between devices, from_partner(): return lax.ppermute(value, axis, [(i, i ^ m) for i in range(size)])  5.32 us
    pallas_call x1, Pallas kernels, project(): pl.pallas_call(functools.partial(project_kernel, own), out_shape=[jax.Sha...  2.19 us
    pallas_call x1, Pallas kernels, solve(): pl.pallas_call(functools.partial(solve_kernel, seqs), out_shape=jax.Shape...  1.82 us
  transfers between devices with their start and end apart: 8, of which 6 were waited for; matrix products, arithmetic and copies ran while one was open for 1% of the time, Pallas kernels for 1%

profile of v25, /device:TPU:0, one launch (start us, length us, event | category | flops | bytes accessed | tf_op | source)
XLA Modules:
  0.0 27.6 jit_solution(2332477572414304747)
XLA Ops:
  0.0 2.2 %project.1 = (f32[96,256]{1,0:T(8,128)S(1)}, f32[96,256]{1,0:T(8,128)S(1)}) custom-call(s32[1]{0:T(128)} %bitcast.1.rank_ref, bf16[2752,256]{1,0:T(8,128)(2,1)} %bitcast.5, bf16[256,1024]{1,0:T(8,128)(2,1)} %g_hbm.1, bf16[64,2752]{1,0:T(8,128)(2,1)} %bitcast.6, bf16[64,1024]{1,0:T(8,128)(2,1)} %bitcast.7), custom_call_target="tpu_custom_call" | custom-call | tf_op jit(solution)/shard_map/project/pallas_call | solution.py:109
  2.2 0.5 %collective-permute-start = (f32[96,256]{1,0:T(8,128)S(1)}, f32[96,256]{1,0:T(8,128)S(1)}, u32[]{:S(2)}, u32[]{:S(2)}) collective-permute-start(f32[96,256]{1,0:T(8,128)S(1)} %get-tuple-element.10), channel_id=1, source_target_pairs={{0,1},{1,0},{2,3},{3,2},{4,5},{5,4},{6,7},{7,6},{8,9},{9,8},{10,11... | collective-permute-start | bytes 294920 | tf_op jit(solution)/shard_map/ppermute | solution.py:319
  2.7 0.0 copy-done.2
  2.8 0.1 convert_reduce_fusion
  2.9 0.8 %collective-permute-done.came_ref = f32[96,256]{1,0:T(8,128)S(1)} collective-permute-done((f32[96,256]{1,0:T(8,128)S(1)}, f32[96,256]{1,0:T(8,128)S(1)}, u32[]{:S(2)}, u32[]{:S(2)}) %collective-permute-start) | collective-permute-done | bytes 98336 | tf_op jit(solution)/shard_map/ppermute | solution.py:319
  3.7 2.9 %collective-permute-start.1 = (f32[64,256]{1,0:T(8,128)S(1)}, f32[64,256]{1,0:T(8,128)S(1)}, u32[]{:S(2)}, u32[]{:S(2)}) collective-permute-start(f32[64,256]{1,0:T(8,128)S(1)} %get-tuple-element.12), channel_id=1, source_target_pairs={{0,2},{1,3},{2,0},{3,1},{4,6},{5,7},{6,4},{7,5},{8,10},{9,11},{10,... | collective-permute-start | bytes 196616 | tf_op jit(solution)/shard_map/ppermute | solution.py:319
  6.6 0.1 fusion.1.weights_ref
  6.7 0.2 pick.1.asked_ref
  6.8 2.2 %collective-permute-done.1.came_ref = f32[64,256]{1,0:T(8,128)S(1)} collective-permute-done((f32[64,256]{1,0:T(8,128)S(1)}, f32[64,256]{1,0:T(8,128)S(1)}, u32[]{:S(2)}, u32[]{:S(2)}) %collective-permute-start.1) | collective-permute-done | bytes 65568 | tf_op jit(solution)/shard_map/ppermute | solution.py:319
  9.0 0.4 %gradients.1.refs_3_ = f32[160,128]{1,0:T(8,128)S(1)} custom-call(f32[16,256]{1,0:T(8,128)S(1)} %fusion.1.weights_ref, f32[64,256]{1,0:T(8,128)S(1)} %get-tuple-element.11.kept_ref, f32[64,256]{1,0:T(8,128)S(1)} %collective-permute-done.1.came_ref, f32[32,128]{1,0:T(8,128)S(1)} %pick.1.asked_ref), custom_call_target="tpu_custom_call" | custom-call | tf_op jit(solution)/shard_map/gradients/pallas_call | solution.py:223
  9.4 2.0 %collective-permute-start.2 = (f32[160,128]{1,0:T(8,128)S(1)}, f32[160,128]{1,0:T(8,128)S(1)}, u32[]{:S(2)}, u32[]{:S(2)}) collective-permute-start(f32[160,128]{1,0:T(8,128)S(1)} %gradients.1.refs_3_), channel_id=1, source_target_pairs={{4,0},{0,4},{12,8},{8,12},{5,1},{1,5},{13,9},{9,13},{6,2},{2,6},{1... | collective-permute-start | bytes 245768 | tf_op jit(solution)/shard_map/ppermute | solution.py:328
  11.4 2.6 %collective-permute-start.3 = (f32[160,128]{1,0:T(8,128)S(1)}, f32[160,128]{1,0:T(8,128)S(1)}, u32[]{:S(2)}, u32[]{:S(2)}) collective-permute-start(f32[160,128]{1,0:T(8,128)S(1)} %gradients.1.refs_3_), channel_id=1, source_target_pairs={{12,0},{8,4},{0,8},{4,12},{13,1},{9,5},{1,9},{5,13},{14,2},{10,6},... | collective-permute-start | bytes 245768 | tf_op jit(solution)/shard_map/ppermute | solution.py:328
  14.0 1.2 %collective-permute-start.4 = (f32[160,128]{1,0:T(8,128)S(1)}, f32[160,128]{1,0:T(8,128)S(1)}, u32[]{:S(2)}, u32[]{:S(2)}) collective-permute-start(f32[160,128]{1,0:T(8,128)S(1)} %gradients.1.refs_3_), channel_id=1, source_target_pairs={{8,0},{12,4},{4,8},{0,12},{9,1},{13,5},{5,9},{1,13},{10,2},{14,6},... | collective-permute-start | bytes 245768 | tf_op jit(solution)/shard_map/ppermute | solution.py:328
  15.2 0.0 collective-permute-done.2.refs_0_
  15.2 2.8 %collective-permute-done.3.refs_1_ = f32[160,128]{1,0:T(8,128)S(1)} collective-permute-done((f32[160,128]{1,0:T(8,128)S(1)}, f32[160,128]{1,0:T(8,128)S(1)}, u32[]{:S(2)}, u32[]{:S(2)}) %collective-permute-start.3) | collective-permute-done | bytes 81952 | tf_op jit(solution)/shard_map/ppermute | solution.py:328
  18.0 2.7 %collective-permute-done.4.refs_2_ = f32[160,128]{1,0:T(8,128)S(1)} collective-permute-done((f32[160,128]{1,0:T(8,128)S(1)}, f32[160,128]{1,0:T(8,128)S(1)}, u32[]{:S(2)}, u32[]{:S(2)}) %collective-permute-start.4) | collective-permute-done | bytes 81952 | tf_op jit(solution)/shard_map/ppermute | solution.py:328
  20.8 0.3 %grams.1.refs_3_ = f32[40,128]{1,0:T(8,128)S(1)} custom-call(s32[1]{0:T(128)} %bitcast.me_ref, f32[160,128]{1,0:T(8,128)S(1)} %collective-permute-done.2.refs_0_, f32[160,128]{1,0:T(8,128)S(1)} %collective-permute-done.3.refs_1_, f32[160,128]{1,0:T(8,128)S(1)} %collective-permute-done.4.refs_2_, f32[160,128]{1,0:T(8,128)S(1)} %gradients.1.refs_3_), custom_call_target="tpu_custom_call" | custom-call | tf_op jit(solution)/shard_map/grams/pallas_call | solution.py:258
  21.1 0.6 %collective-permute-start.5 = (f32[40,128]{1,0:T(8,128)S(1)}, f32[40,128]{1,0:T(8,128)S(1)}, u32[]{:S(2)}, u32[]{:S(2)}) collective-permute-start(f32[40,128]{1,0:T(8,128)S(1)} %grams.1.refs_3_), channel_id=1, source_target_pairs={{0,3},{1,2},{2,1},{3,0},{4,7},{5,6},{6,5},{7,4},{8,11},{9,10},{10,... | collective-permute-start | bytes 61448 | tf_op jit(solution)/shard_map/ppermute | solution.py:319
  21.8 0.9 %collective-permute-start.6 = (f32[40,128]{1,0:T(8,128)S(1)}, f32[40,128]{1,0:T(8,128)S(1)}, u32[]{:S(2)}, u32[]{:S(2)}) collective-permute-start(f32[40,128]{1,0:T(8,128)S(1)} %grams.1.refs_3_), channel_id=1, source_target_pairs={{0,2},{1,3},{2,0},{3,1},{4,6},{5,7},{6,4},{7,5},{8,10},{9,11},{10,... | collective-permute-start | bytes 61448 | tf_op jit(solution)/shard_map/ppermute | solution.py:319
  22.7 0.3 %collective-permute-start.7 = (f32[40,128]{1,0:T(8,128)S(1)}, f32[40,128]{1,0:T(8,128)S(1)}, u32[]{:S(2)}, u32[]{:S(2)}) collective-permute-start(f32[40,128]{1,0:T(8,128)S(1)} %grams.1.refs_3_), channel_id=1, source_target_pairs={{0,1},{1,0},{2,3},{3,2},{4,5},{5,4},{6,7},{7,6},{8,9},{9,8},{10,11... | collective-permute-start | bytes 61448 | tf_op jit(solution)/shard_map/ppermute | solution.py:319
  23.0 1.5 %collective-permute-done.5.refs_0_ = f32[40,128]{1,0:T(8,128)S(1)} collective-permute-done((f32[40,128]{1,0:T(8,128)S(1)}, f32[40,128]{1,0:T(8,128)S(1)}, u32[]{:S(2)}, u32[]{:S(2)}) %collective-permute-start.5) | collective-permute-done | bytes 20512 | tf_op jit(solution)/shard_map/ppermute | solution.py:319
  24.5 1.2 %collective-permute-done.6.refs_1_ = f32[40,128]{1,0:T(8,128)S(1)} collective-permute-done((f32[40,128]{1,0:T(8,128)S(1)}, f32[40,128]{1,0:T(8,128)S(1)}, u32[]{:S(2)}, u32[]{:S(2)}) %collective-permute-start.6) | collective-permute-done | bytes 20512 | tf_op jit(solution)/shard_map/ppermute | solution.py:319
  25.8 0.0 collective-permute-done.7.refs_2_
  25.8 1.8 %solve.1 = f32[16,16]{1,0:T(8,128)} custom-call(f32[40,128]{1,0:T(8,128)S(1)} %collective-permute-done.5.refs_0_, f32[40,128]{1,0:T(8,128)S(1)} %collective-permute-done.6.refs_1_, f32[40,128]{1,0:T(8,128)S(1)} %collective-permute-done.7.refs_2_, f32[40,128]{1,0:T(8,128)S(1)} %grams.1.refs_3_), custom_call_target="tpu_custom_call" | custom-call | tf_op jit(solution)/shard_map/solve/pallas_call | solution.py:310
  (8 shorter events, 0.0 us)
Async XLA Ops:
  0.0 2.7 %copy-start.2 = (s32[16]{0:T(128)S(1)}, s32[16]{0:T(128)}, u32[]{:S(2)}) copy-start(s32[16]{0:T(128)} %param.12) | copy-start | bytes 196
  0.0 2.8 %copy-start.1 = (s32[256]{0:T(256)S(1)}, s32[256]{0:T(256)}, u32[]{:S(2)}) copy-start(s32[256]{0:T(256)} %param.11) | copy-start | bytes 3076
  0.0 6.7 %copy-start = (f32[4,4096]{1,0:T(4,128)S(1)}, f32[4,4096]{1,0:T(4,128)}, u32[]{:S(2)}) copy-start(f32[4,4096]{1,0:T(4,128)} %queries_ref.1) | copy-start | bytes 196612
  2.2 1.5 %collective-permute-start = (f32[96,256]{1,0:T(8,128)S(1)}, f32[96,256]{1,0:T(8,128)S(1)}, u32[]{:S(2)}, u32[]{:S(2)}) collective-permute-start(f32[96,256]{1,0:T(8,128)S(1)} %get-tuple-element.10), channel_id=1, source_target_pairs={{0,1},{1,0},{2,3},{3,2},{4,5},{5,4},{6,7},{7,6},{8,9},{9,8},{10,11... | collective-permute-start | bytes 294920 | tf_op jit(solution)/shard_map/ppermute | solution.py:319
  3.7 5.3 %collective-permute-start.1 = (f32[64,256]{1,0:T(8,128)S(1)}, f32[64,256]{1,0:T(8,128)S(1)}, u32[]{:S(2)}, u32[]{:S(2)}) collective-permute-start(f32[64,256]{1,0:T(8,128)S(1)} %get-tuple-element.12), channel_id=1, source_target_pairs={{0,2},{1,3},{2,0},{3,1},{4,6},{5,7},{6,4},{7,5},{8,10},{9,11},{10,... | collective-permute-start | bytes 196616 | tf_op jit(solution)/shard_map/ppermute | solution.py:319
  9.4 5.8 %collective-permute-start.2 = (f32[160,128]{1,0:T(8,128)S(1)}, f32[160,128]{1,0:T(8,128)S(1)}, u32[]{:S(2)}, u32[]{:S(2)}) collective-permute-start(f32[160,128]{1,0:T(8,128)S(1)} %gradients.1.refs_3_), channel_id=1, source_target_pairs={{4,0},{0,4},{12,8},{8,12},{5,1},{1,5},{13,9},{9,13},{6,2},{2,6},{1... | collective-permute-start | bytes 245768 | tf_op jit(solution)/shard_map/ppermute | solution.py:328
  11.4 6.7 %collective-permute-start.3 = (f32[160,128]{1,0:T(8,128)S(1)}, f32[160,128]{1,0:T(8,128)S(1)}, u32[]{:S(2)}, u32[]{:S(2)}) collective-permute-start(f32[160,128]{1,0:T(8,128)S(1)} %gradients.1.refs_3_), channel_id=1, source_target_pairs={{12,0},{8,4},{0,8},{4,12},{13,1},{9,5},{1,9},{5,13},{14,2},{10,6},... | collective-permute-start | bytes 245768 | tf_op jit(solution)/shard_map/ppermute | solution.py:328
  14.0 6.8 %collective-permute-start.4 = (f32[160,128]{1,0:T(8,128)S(1)}, f32[160,128]{1,0:T(8,128)S(1)}, u32[]{:S(2)}, u32[]{:S(2)}) collective-permute-start(f32[160,128]{1,0:T(8,128)S(1)} %gradients.1.refs_3_), channel_id=1, source_target_pairs={{8,0},{12,4},{4,8},{0,12},{9,1},{13,5},{5,9},{1,13},{10,2},{14,6},... | collective-permute-start | bytes 245768 | tf_op jit(solution)/shard_map/ppermute | solution.py:328
  21.1 3.4 %collective-permute-start.5 = (f32[40,128]{1,0:T(8,128)S(1)}, f32[40,128]{1,0:T(8,128)S(1)}, u32[]{:S(2)}, u32[]{:S(2)}) collective-permute-start(f32[40,128]{1,0:T(8,128)S(1)} %grams.1.refs_3_), channel_id=1, source_target_pairs={{0,3},{1,2},{2,1},{3,0},{4,7},{5,6},{6,5},{7,4},{8,11},{9,10},{10,... | collective-permute-start | bytes 61448 | tf_op jit(solution)/shard_map/ppermute | solution.py:319
  21.8 4.0 %collective-permute-start.6 = (f32[40,128]{1,0:T(8,128)S(1)}, f32[40,128]{1,0:T(8,128)S(1)}, u32[]{:S(2)}, u32[]{:S(2)}) collective-permute-start(f32[40,128]{1,0:T(8,128)S(1)} %grams.1.refs_3_), channel_id=1, source_target_pairs={{0,2},{1,3},{2,0},{3,1},{4,6},{5,7},{6,4},{7,5},{8,10},{9,11},{10,... | collective-permute-start | bytes 61448 | tf_op jit(solution)/shard_map/ppermute | solution.py:319
  22.7 3.0 %collective-permute-start.7 = (f32[40,128]{1,0:T(8,128)S(1)}, f32[40,128]{1,0:T(8,128)S(1)}, u32[]{:S(2)}, u32[]{:S(2)}) collective-permute-start(f32[40,128]{1,0:T(8,128)S(1)} %grams.1.refs_3_), channel_id=1, source_target_pairs={{0,1},{1,0},{2,3},{3,2},{4,5},{5,4},{6,7},{7,6},{8,9},{9,8},{10,11... | collective-permute-start | bytes 61448 | tf_op jit(solution)/shard_map/ppermute | solution.py:319

commit v26 on v14

--- a/solution.py
+++ b/solution.py
@@ -228,7 +228,11 @@
 
 
 def grams_kernel(steps, seqs, me_ref, *refs):
-    blocks, out_ref = refs[-2::-1], refs[-1]
+    own_ref, others, out_ref = refs[-2], refs[:-2], refs[-1]
+    odd = me_ref[1] == 1
+    blocks = [own_ref[...]] + [
+        jnp.where(odd, lower[...], upper[...]) for lower, upper in zip(others, others[::-1])
+    ]
     count = steps * seqs
     asked = (blocks[0].shape[0] - count) // steps
     given = [block[count:, :] for block in blocks]
@@ -322,9 +326,17 @@
     return [from_partner(value, axis, size, m) for m in reversed(range(1, size))] + [value]
 
 
-def from_all(value, axis, size):
-    shifts = [[(i, (i + s) % size) for i in range(size)] for s in range(1, size)]
-    return [lax.ppermute(value, axis, shift) for shift in shifts] + [value]
+def from_all(value, sizes):
+    parts, blocks = sizes
+    came = []
+    for s in range(1, blocks):
+        pairs = []
+        for i in range(blocks):
+            for r in range(parts):
+                to = (i + (s if r % 2 == 0 else blocks - s)) % blocks
+                pairs.append((i * parts + r, to * parts + r))
+        came.append(lax.ppermute(value, ("dp", "tensor"), pairs))
+    return came + [value]
 
 
 def finish_long(message, steps, first, seq_dev):
@@ -371,7 +383,7 @@
     steps = own * own // message.shape[1]
     if blocks > SMALL:
         return finish_long(message, steps, first, seq_dev)
-    partial = grams(place.reshape(1), from_all(message, "dp", blocks), steps, seq_dev)
+    partial = grams(jnp.stack([place, me % 2]), from_all(message, sizes), steps, seq_dev)
     partial = from_partners(partial, "tensor", parts)
     return solve(partial, blocks * seq_dev, blocks * queries.shape[0], seq_dev)
 

time: 25.3 us -> 27.5 us (1.087)
  waiting for transfers between devices: 8.79 us -> 10.3 us
  Pallas kernels: 4.88 us -> 5.42 us
    ppermute x5, waiting for transfers between devices: 4.99 us -> 5.81 us  [from_partner(): return lax.ppermute(value, axis, [(i, i ^ m) for i in range(size)])]
    ppermute x3, waiting for transfers between devices: 3.8 us -> 4.51 us  [from_all(): came.append(lax.ppermute(value, ('dp', 'tensor'), pairs))]
    pallas_call x1, Pallas kernels: 0.34 us -> 0.88 us  [grams(): pl.pallas_call(functools.partial(grams_kernel, steps, seqs), out_shape=ja...]
where the time goes in v26:
time: 27.5 us; the launch traced here: 27.3 us
  starting transfers between devices  11.2 us (41%)
  waiting for transfers between devices  10.3 us (37%)
  Pallas kernels  5.42 us (20%)
    ppermute x3, starting transfers between devices, from_all(): came.append(lax.ppermute(value, ('dp', 'tensor'), pairs))  5.93 us
    ppermute x5, waiting for transfers between devices, from_partner(): return lax.ppermute(value, axis, [(i, i ^ m) for i in range(size)])  5.81 us
    ppermute x5, starting transfers between devices, from_partner(): return lax.ppermute(value, axis, [(i, i ^ m) for i in range(size)])  5.32 us
    ppermute x3, waiting for transfers between devices, from_all(): came.append(lax.ppermute(value, ('dp', 'tensor'), pairs))  4.51 us
    pallas_call x1, Pallas kernels, project(): pl.pallas_call(functools.partial(project_kernel, own), out_shape=[jax.Sha...  2.19 us
    pallas_call x1, Pallas kernels, solve(): pl.pallas_call(functools.partial(solve_kernel, seqs), out_shape=jax.Shape...  1.82 us
    pallas_call x1, Pallas kernels, grams(): pl.pallas_call(functools.partial(grams_kernel, steps, seqs), out_shape=ja...  0.88 us
  transfers between devices with their start and end apart: 8, of which 7 were waited for; matrix products, arithmetic and copies ran while one was open for 1% of the time, Pallas kernels for 1%

profile of v26, /device:TPU:0, one launch (start us, length us, event | category | flops | bytes accessed | tf_op | source)
XLA Modules:
  0.0 27.3 jit_solution(12252915876165158971)
XLA Ops:
  0.0 2.2 %project.1 = (f32[96,256]{1,0:T(8,128)S(1)}, f32[96,256]{1,0:T(8,128)S(1)}) custom-call(s32[1]{0:T(128)} %bitcast.2.rank_ref, bf16[2752,256]{1,0:T(8,128)(2,1)} %bitcast.6, bf16[256,1024]{1,0:T(8,128)(2,1)} %g_hbm.1, bf16[64,2752]{1,0:T(8,128)(2,1)} %bitcast.7, bf16[64,1024]{1,0:T(8,128)(2,1)} %bitcast.8), custom_call_target="tpu_custom_call" | custom-call | tf_op jit(solution)/shard_map/project/pallas_call | solution.py:108
  2.2 0.5 %collective-permute-start = (f32[96,256]{1,0:T(8,128)S(1)}, f32[96,256]{1,0:T(8,128)S(1)}, u32[]{:S(2)}, u32[]{:S(2)}) collective-permute-start(f32[96,256]{1,0:T(8,128)S(1)} %get-tuple-element.10), channel_id=1, source_target_pairs={{0,1},{1,0},{2,3},{3,2},{4,5},{5,4},{6,7},{7,6},{8,9},{9,8},{10,11... | collective-permute-start | bytes 294920 | tf_op jit(solution)/shard_map/ppermute | solution.py:322
  2.8 0.1 convert_reduce_fusion
  2.9 0.8 %collective-permute-done.came_ref = f32[96,256]{1,0:T(8,128)S(1)} collective-permute-done((f32[96,256]{1,0:T(8,128)S(1)}, f32[96,256]{1,0:T(8,128)S(1)}, u32[]{:S(2)}, u32[]{:S(2)}) %collective-permute-start) | collective-permute-done | bytes 98336 | tf_op jit(solution)/shard_map/ppermute | solution.py:322
  3.7 2.9 %collective-permute-start.1 = (f32[64,256]{1,0:T(8,128)S(1)}, f32[64,256]{1,0:T(8,128)S(1)}, u32[]{:S(2)}, u32[]{:S(2)}) collective-permute-start(f32[64,256]{1,0:T(8,128)S(1)} %get-tuple-element.12), channel_id=1, source_target_pairs={{0,2},{1,3},{2,0},{3,1},{4,6},{5,7},{6,4},{7,5},{8,10},{9,11},{10,... | collective-permute-start | bytes 196616 | tf_op jit(solution)/shard_map/ppermute | solution.py:322
  6.6 0.1 fusion.1.weights_ref
  6.7 0.2 pick.1.asked_ref
  6.9 2.2 %collective-permute-done.1.came_ref = f32[64,256]{1,0:T(8,128)S(1)} collective-permute-done((f32[64,256]{1,0:T(8,128)S(1)}, f32[64,256]{1,0:T(8,128)S(1)}, u32[]{:S(2)}, u32[]{:S(2)}) %collective-permute-start.1) | collective-permute-done | bytes 65568 | tf_op jit(solution)/shard_map/ppermute | solution.py:322
  9.0 0.4 %gradients.1.refs_3_ = f32[160,128]{1,0:T(8,128)S(1)} custom-call(f32[16,256]{1,0:T(8,128)S(1)} %fusion.1.weights_ref, f32[64,256]{1,0:T(8,128)S(1)} %get-tuple-element.11.kept_ref, f32[64,256]{1,0:T(8,128)S(1)} %collective-permute-done.1.came_ref, f32[32,128]{1,0:T(8,128)S(1)} %pick.1.asked_ref), custom_call_target="tpu_custom_call" | custom-call | tf_op jit(solution)/shard_map/gradients/pallas_call | solution.py:222
  9.4 2.0 %collective-permute-start.2 = (f32[160,128]{1,0:T(8,128)S(1)}, f32[160,128]{1,0:T(8,128)S(1)}, u32[]{:S(2)}, u32[]{:S(2)}) collective-permute-start(f32[160,128]{1,0:T(8,128)S(1)} %gradients.1.refs_3_), channel_id=1, source_target_pairs={{0,4},{1,13},{2,6},{3,15},{4,8},{5,1},{6,10},{7,3},{8,12},{9,5},{1... | collective-permute-start | bytes 245768 | tf_op jit(solution)/shard_map/ppermute | solution.py:338
  11.4 2.6 %collective-permute-start.3 = (f32[160,128]{1,0:T(8,128)S(1)}, f32[160,128]{1,0:T(8,128)S(1)}, u32[]{:S(2)}, u32[]{:S(2)}) collective-permute-start(f32[160,128]{1,0:T(8,128)S(1)} %gradients.1.refs_3_), channel_id=1, source_target_pairs={{0,8},{1,9},{2,10},{3,11},{4,12},{5,13},{6,14},{7,15},{8,0},{9,1},... | collective-permute-start | bytes 245768 | tf_op jit(solution)/shard_map/ppermute | solution.py:338
  14.0 1.3 %collective-permute-start.4 = (f32[160,128]{1,0:T(8,128)S(1)}, f32[160,128]{1,0:T(8,128)S(1)}, u32[]{:S(2)}, u32[]{:S(2)}) collective-permute-start(f32[160,128]{1,0:T(8,128)S(1)} %gradients.1.refs_3_), channel_id=1, source_target_pairs={{0,12},{1,5},{2,14},{3,7},{4,0},{5,9},{6,2},{7,11},{8,4},{9,13},{1... | collective-permute-start | bytes 245768 | tf_op jit(solution)/shard_map/ppermute | solution.py:338
  15.3 0.1 pad_add_fusion.me_ref
  15.4 0.7 %collective-permute-done.2.refs_0_ = f32[160,128]{1,0:T(8,128)S(1)} collective-permute-done((f32[160,128]{1,0:T(8,128)S(1)}, f32[160,128]{1,0:T(8,128)S(1)}, u32[]{:S(2)}, u32[]{:S(2)}) %collective-permute-start.2) | collective-permute-done | bytes 81952 | tf_op jit(solution)/shard_map/ppermute | solution.py:338
  16.1 3.6 %collective-permute-done.3.refs_1_ = f32[160,128]{1,0:T(8,128)S(1)} collective-permute-done((f32[160,128]{1,0:T(8,128)S(1)}, f32[160,128]{1,0:T(8,128)S(1)}, u32[]{:S(2)}, u32[]{:S(2)}) %collective-permute-start.3) | collective-permute-done | bytes 81952 | tf_op jit(solution)/shard_map/ppermute | solution.py:338
  19.7 0.2 collective-permute-done.4.refs_2_
  19.9 0.9 %grams.1.refs_3_ = f32[40,128]{1,0:T(8,128)S(1)} custom-call(s32[2]{0:T(128)S(1)} %pad_add_fusion.me_ref, f32[160,128]{1,0:T(8,128)S(1)} %collective-permute-done.2.refs_0_, f32[160,128]{1,0:T(8,128)S(1)} %collective-permute-done.3.refs_1_, f32[160,128]{1,0:T(8,128)S(1)} %collective-permute-done.4.refs_2_, f32[160,128]{1,0:T(8,128)S(1)} %gradients.1.refs_3_), custom_call_target="tpu_custom_call" | custom-call | tf_op jit(solution)/shard_map/grams/pallas_call | solution.py:261
  20.8 0.9 %collective-permute-start.5 = (f32[40,128]{1,0:T(8,128)S(1)}, f32[40,128]{1,0:T(8,128)S(1)}, u32[]{:S(2)}, u32[]{:S(2)}) collective-permute-start(f32[40,128]{1,0:T(8,128)S(1)} %grams.1.refs_3_), channel_id=1, source_target_pairs={{0,3},{1,2},{2,1},{3,0},{4,7},{5,6},{6,5},{7,4},{8,11},{9,10},{10,... | collective-permute-start | bytes 61448 | tf_op jit(solution)/shard_map/ppermute | solution.py:322
  21.7 0.7 %collective-permute-start.6 = (f32[40,128]{1,0:T(8,128)S(1)}, f32[40,128]{1,0:T(8,128)S(1)}, u32[]{:S(2)}, u32[]{:S(2)}) collective-permute-start(f32[40,128]{1,0:T(8,128)S(1)} %grams.1.refs_3_), channel_id=1, source_target_pairs={{0,2},{1,3},{2,0},{3,1},{4,6},{5,7},{6,4},{7,5},{8,10},{9,11},{10,... | collective-permute-start | bytes 61448 | tf_op jit(solution)/shard_map/ppermute | solution.py:322
  22.4 0.3 %collective-permute-start.7 = (f32[40,128]{1,0:T(8,128)S(1)}, f32[40,128]{1,0:T(8,128)S(1)}, u32[]{:S(2)}, u32[]{:S(2)}) collective-permute-start(f32[40,128]{1,0:T(8,128)S(1)} %grams.1.refs_3_), channel_id=1, source_target_pairs={{0,1},{1,0},{2,3},{3,2},{4,5},{5,4},{6,7},{7,6},{8,9},{9,8},{10,11... | collective-permute-start | bytes 61448 | tf_op jit(solution)/shard_map/ppermute | solution.py:322
  22.7 1.5 %collective-permute-done.5.refs_0_ = f32[40,128]{1,0:T(8,128)S(1)} collective-permute-done((f32[40,128]{1,0:T(8,128)S(1)}, f32[40,128]{1,0:T(8,128)S(1)}, u32[]{:S(2)}, u32[]{:S(2)}) %collective-permute-start.5) | collective-permute-done | bytes 20512 | tf_op jit(solution)/shard_map/ppermute | solution.py:322
  24.2 1.3 %collective-permute-done.6.refs_1_ = f32[40,128]{1,0:T(8,128)S(1)} collective-permute-done((f32[40,128]{1,0:T(8,128)S(1)}, f32[40,128]{1,0:T(8,128)S(1)}, u32[]{:S(2)}, u32[]{:S(2)}) %collective-permute-start.6) | collective-permute-done | bytes 20512 | tf_op jit(solution)/shard_map/ppermute | solution.py:322
  25.5 0.0 collective-permute-done.7.refs_2_
  25.5 1.8 %solve.1 = f32[16,16]{1,0:T(8,128)} custom-call(f32[40,128]{1,0:T(8,128)S(1)} %collective-permute-done.5.refs_0_, f32[40,128]{1,0:T(8,128)S(1)} %collective-permute-done.6.refs_1_, f32[40,128]{1,0:T(8,128)S(1)} %collective-permute-done.7.refs_2_, f32[40,128]{1,0:T(8,128)S(1)} %grams.1.refs_3_), custom_call_target="tpu_custom_call" | custom-call | tf_op jit(solution)/shard_map/solve/pallas_call | solution.py:313
  (9 shorter events, 0.0 us)
Async XLA Ops:
  0.0 2.7 %copy-start.2 = (s32[16]{0:T(128)S(1)}, s32[16]{0:T(128)}, u32[]{:S(2)}) copy-start(s32[16]{0:T(128)} %param.12) | copy-start | bytes 196
  0.0 2.8 %copy-start.1 = (s32[256]{0:T(256)S(1)}, s32[256]{0:T(256)}, u32[]{:S(2)}) copy-start(s32[256]{0:T(256)} %param.11) | copy-start | bytes 3076
  0.0 6.7 %copy-start = (f32[4,4096]{1,0:T(4,128)S(1)}, f32[4,4096]{1,0:T(4,128)}, u32[]{:S(2)}) copy-start(f32[4,4096]{1,0:T(4,128)} %queries_ref.1) | copy-start | bytes 196612
  2.2 1.5 %collective-permute-start = (f32[96,256]{1,0:T(8,128)S(1)}, f32[96,256]{1,0:T(8,128)S(1)}, u32[]{:S(2)}, u32[]{:S(2)}) collective-permute-start(f32[96,256]{1,0:T(8,128)S(1)} %get-tuple-element.10), channel_id=1, source_target_pairs={{0,1},{1,0},{2,3},{3,2},{4,5},{5,4},{6,7},{7,6},{8,9},{9,8},{10,11... | collective-permute-start | bytes 294920 | tf_op jit(solution)/shard_map/ppermute | solution.py:322
  3.7 5.3 %collective-permute-start.1 = (f32[64,256]{1,0:T(8,128)S(1)}, f32[64,256]{1,0:T(8,128)S(1)}, u32[]{:S(2)}, u32[]{:S(2)}) collective-permute-start(f32[64,256]{1,0:T(8,128)S(1)} %get-tuple-element.12), channel_id=1, source_target_pairs={{0,2},{1,3},{2,0},{3,1},{4,6},{5,7},{6,4},{7,5},{8,10},{9,11},{10,... | collective-permute-start | bytes 196616 | tf_op jit(solution)/shard_map/ppermute | solution.py:322
  9.4 6.7 %collective-permute-start.2 = (f32[160,128]{1,0:T(8,128)S(1)}, f32[160,128]{1,0:T(8,128)S(1)}, u32[]{:S(2)}, u32[]{:S(2)}) collective-permute-start(f32[160,128]{1,0:T(8,128)S(1)} %gradients.1.refs_3_), channel_id=1, source_target_pairs={{0,4},{1,13},{2,6},{3,15},{4,8},{5,1},{6,10},{7,3},{8,12},{9,5},{1... | collective-permute-start | bytes 245768 | tf_op jit(solution)/shard_map/ppermute | solution.py:338
  11.4 8.3 %collective-permute-start.3 = (f32[160,128]{1,0:T(8,128)S(1)}, f32[160,128]{1,0:T(8,128)S(1)}, u32[]{:S(2)}, u32[]{:S(2)}) collective-permute-start(f32[160,128]{1,0:T(8,128)S(1)} %gradients.1.refs_3_), channel_id=1, source_target_pairs={{0,8},{1,9},{2,10},{3,11},{4,12},{5,13},{6,14},{7,15},{8,0},{9,1},... | collective-permute-start | bytes 245768 | tf_op jit(solution)/shard_map/ppermute | solution.py:338
  14.0 5.9 %collective-permute-start.4 = (f32[160,128]{1,0:T(8,128)S(1)}, f32[160,128]{1,0:T(8,128)S(1)}, u32[]{:S(2)}, u32[]{:S(2)}) collective-permute-start(f32[160,128]{1,0:T(8,128)S(1)} %gradients.1.refs_3_), channel_id=1, source_target_pairs={{0,12},{1,5},{2,14},{3,7},{4,0},{5,9},{6,2},{7,11},{8,4},{9,13},{1... | collective-permute-start | bytes 245768 | tf_op jit(solution)/shard_map/ppermute | solution.py:338
  20.8 3.4 %collective-permute-start.5 = (f32[40,128]{1,0:T(8,128)S(1)}, f32[40,128]{1,0:T(8,128)S(1)}, u32[]{:S(2)}, u32[]{:S(2)}) collective-permute-start(f32[40,128]{1,0:T(8,128)S(1)} %grams.1.refs_3_), channel_id=1, source_target_pairs={{0,3},{1,2},{2,1},{3,0},{4,7},{5,6},{6,5},{7,4},{8,11},{9,10},{10,... | collective-permute-start | bytes 61448 | tf_op jit(solution)/shard_map/ppermute | solution.py:322
  21.7 3.8 %collective-permute-start.6 = (f32[40,128]{1,0:T(8,128)S(1)}, f32[40,128]{1,0:T(8,128)S(1)}, u32[]{:S(2)}, u32[]{:S(2)}) collective-permute-start(f32[40,128]{1,0:T(8,128)S(1)} %grams.1.refs_3_), channel_id=1, source_target_pairs={{0,2},{1,3},{2,0},{3,1},{4,6},{5,7},{6,4},{7,5},{8,10},{9,11},{10,... | collective-permute-start | bytes 61448 | tf_op jit(solution)/shard_map/ppermute | solution.py:322
  22.4 3.1 %collective-permute-start.7 = (f32[40,128]{1,0:T(8,128)S(1)}, f32[40,128]{1,0:T(8,128)S(1)}, u32[]{:S(2)}, u32[]{:S(2)}) collective-permute-start(f32[40,128]{1,0:T(8,128)S(1)} %grams.1.refs_3_), channel_id=1, source_target_pairs={{0,1},{1,0},{2,3},{3,2},{4,5},{5,4},{6,7},{7,6},{8,9},{9,8},{10,11... | collective-permute-start | bytes 61448 | tf_op jit(solution)/shard_map/ppermute | solution.py:322

commit v27 on v26

--- a/solution.py
+++ b/solution.py
@@ -10,6 +10,7 @@
 damping = 0.5
 VMEM_LIMIT = 32 * 1024 * 1024
 SMALL = 4
+SHIFTS = {1: ((), ()), 2: ((1,), (1,)), 4: ((1, 2, 3), (2, 1, 3))}
 
 
 def token_weights(seq_ids, counts, first):
@@ -230,8 +231,10 @@
 def grams_kernel(steps, seqs, me_ref, *refs):
     own_ref, others, out_ref = refs[-2], refs[:-2], refs[-1]
     odd = me_ref[1] == 1
+    even, uneven = SHIFTS[len(others) + 1]
     blocks = [own_ref[...]] + [
-        jnp.where(odd, lower[...], upper[...]) for lower, upper in zip(others, others[::-1])
+        jnp.where(odd, others[uneven.index(s)][...], others[even.index(s)][...])
+        for s in range(len(others), 0, -1)
     ]
     count = steps * seqs
     asked = (blocks[0].shape[0] - count) // steps
@@ -329,12 +332,11 @@
 def from_all(value, sizes):
     parts, blocks = sizes
     came = []
-    for s in range(1, blocks):
+    for shifts in zip(*SHIFTS[blocks]):
         pairs = []
         for i in range(blocks):
             for r in range(parts):
-                to = (i + (s if r % 2 == 0 else blocks - s)) % blocks
-                pairs.append((i * parts + r, to * parts + r))
+                pairs.append((i * parts + r, (i + shifts[r % 2]) % blocks * parts + r))
         came.append(lax.ppermute(value, ("dp", "tensor"), pairs))
     return came + [value]
 

time: 27.5 us -> 26.1 us (0.949)
  waiting for transfers between devices: 10.3 us -> 8.97 us
    ppermute x5, waiting for transfers between devices: 5.81 us -> 4.98 us  [from_partner(): return lax.ppermute(value, axis, [(i, i ^ m) for i in range(size)])]
    ppermute x3, waiting for transfers between devices: 4.51 us -> 3.99 us  [from_all(): came.append(lax.ppermute(value, ('dp', 'tensor'), pairs))]
where the time goes in v27:
time: 26.1 us; the launch traced here: 26 us
  starting transfers between devices  11.2 us (43%)
  waiting for transfers between devices  8.97 us (34%)
  Pallas kernels  5.42 us (21%)
  other arithmetic  0.27 us (1%)
    ppermute x3, starting transfers between devices, from_all(): came.append(lax.ppermute(value, ('dp', 'tensor'), pairs))  5.93 us
    ppermute x5, starting transfers between devices, from_partner(): return lax.ppermute(value, axis, [(i, i ^ m) for i in range(size)])  5.31 us
    ppermute x5, waiting for transfers between devices, from_partner(): return lax.ppermute(value, axis, [(i, i ^ m) for i in range(size)])  4.98 us
    ppermute x3, waiting for transfers between devices, from_all(): came.append(lax.ppermute(value, ('dp', 'tensor'), pairs))  3.99 us
    pallas_call x1, Pallas kernels, project(): pl.pallas_call(functools.partial(project_kernel, own), out_shape=[jax.Sha...  2.19 us
    pallas_call x1, Pallas kernels, solve(): pl.pallas_call(functools.partial(solve_kernel, seqs), out_shape=jax.Shape...  1.82 us
    pallas_call x1, Pallas kernels, grams(): pl.pallas_call(functools.partial(grams_kernel, steps, seqs), out_shape=ja...  0.89 us
  transfers between devices with their start and end apart: 8, of which 7 were waited for; matrix products, arithmetic and copies ran while one was open for 1% of the time, Pallas kernels for 1%

profile of v27, /device:TPU:0, one launch (start us, length us, event | category | flops | bytes accessed | tf_op | source)
XLA Modules:
  0.0 26.0 jit_solution(3869064849431231329)
XLA Ops:
  0.0 2.2 %project.1 = (f32[96,256]{1,0:T(8,128)S(1)}, f32[96,256]{1,0:T(8,128)S(1)}) custom-call(s32[1]{0:T(128)} %bitcast.2.rank_ref, bf16[2752,256]{1,0:T(8,128)(2,1)} %bitcast.6, bf16[256,1024]{1,0:T(8,128)(2,1)} %g_hbm.1, bf16[64,2752]{1,0:T(8,128)(2,1)} %bitcast.7, bf16[64,1024]{1,0:T(8,128)(2,1)} %bitcast.8), custom_call_target="tpu_custom_call" | custom-call | tf_op jit(solution)/shard_map/project/pallas_call | solution.py:109
  2.2 0.5 %collective-permute-start = (f32[96,256]{1,0:T(8,128)S(1)}, f32[96,256]{1,0:T(8,128)S(1)}, u32[]{:S(2)}, u32[]{:S(2)}) collective-permute-start(f32[96,256]{1,0:T(8,128)S(1)} %get-tuple-element.10), channel_id=1, source_target_pairs={{0,1},{1,0},{2,3},{3,2},{4,5},{5,4},{6,7},{7,6},{8,9},{9,8},{10,11... | collective-permute-start | bytes 294920 | tf_op jit(solution)/shard_map/ppermute | solution.py:325
  2.8 0.1 convert_reduce_fusion
  2.9 0.8 %collective-permute-done.came_ref = f32[96,256]{1,0:T(8,128)S(1)} collective-permute-done((f32[96,256]{1,0:T(8,128)S(1)}, f32[96,256]{1,0:T(8,128)S(1)}, u32[]{:S(2)}, u32[]{:S(2)}) %collective-permute-start) | collective-permute-done | bytes 98336 | tf_op jit(solution)/shard_map/ppermute | solution.py:325
  3.7 2.9 %collective-permute-start.1 = (f32[64,256]{1,0:T(8,128)S(1)}, f32[64,256]{1,0:T(8,128)S(1)}, u32[]{:S(2)}, u32[]{:S(2)}) collective-permute-start(f32[64,256]{1,0:T(8,128)S(1)} %get-tuple-element.12), channel_id=1, source_target_pairs={{0,2},{1,3},{2,0},{3,1},{4,6},{5,7},{6,4},{7,5},{8,10},{9,11},{10,... | collective-permute-start | bytes 196616 | tf_op jit(solution)/shard_map/ppermute | solution.py:325
  6.6 0.1 fusion.1.weights_ref
  6.7 0.2 pick.1.asked_ref
  6.9 2.2 %collective-permute-done.1.came_ref = f32[64,256]{1,0:T(8,128)S(1)} collective-permute-done((f32[64,256]{1,0:T(8,128)S(1)}, f32[64,256]{1,0:T(8,128)S(1)}, u32[]{:S(2)}, u32[]{:S(2)}) %collective-permute-start.1) | collective-permute-done | bytes 65568 | tf_op jit(solution)/shard_map/ppermute | solution.py:325
  9.0 0.4 %gradients.1.refs_3_ = f32[160,128]{1,0:T(8,128)S(1)} custom-call(f32[16,256]{1,0:T(8,128)S(1)} %fusion.1.weights_ref, f32[64,256]{1,0:T(8,128)S(1)} %get-tuple-element.11.kept_ref, f32[64,256]{1,0:T(8,128)S(1)} %collective-permute-done.1.came_ref, f32[32,128]{1,0:T(8,128)S(1)} %pick.1.asked_ref), custom_call_target="tpu_custom_call" | custom-call | tf_op jit(solution)/shard_map/gradients/pallas_call | solution.py:223
  9.4 2.0 %collective-permute-start.2 = (f32[160,128]{1,0:T(8,128)S(1)}, f32[160,128]{1,0:T(8,128)S(1)}, u32[]{:S(2)}, u32[]{:S(2)}) collective-permute-start(f32[160,128]{1,0:T(8,128)S(1)} %gradients.1.refs_3_), channel_id=1, source_target_pairs={{0,4},{1,9},{2,6},{3,11},{4,8},{5,13},{6,10},{7,15},{8,12},{9,1},{... | collective-permute-start | bytes 245768 | tf_op jit(solution)/shard_map/ppermute | solution.py:340
  11.4 2.6 %collective-permute-start.3 = (f32[160,128]{1,0:T(8,128)S(1)}, f32[160,128]{1,0:T(8,128)S(1)}, u32[]{:S(2)}, u32[]{:S(2)}) collective-permute-start(f32[160,128]{1,0:T(8,128)S(1)} %gradients.1.refs_3_), channel_id=1, source_target_pairs={{0,8},{1,5},{2,10},{3,7},{4,12},{5,9},{6,14},{7,11},{8,0},{9,13},{... | collective-permute-start | bytes 245768 | tf_op jit(solution)/shard_map/ppermute | solution.py:340
  14.0 1.3 %collective-permute-start.4 = (f32[160,128]{1,0:T(8,128)S(1)}, f32[160,128]{1,0:T(8,128)S(1)}, u32[]{:S(2)}, u32[]{:S(2)}) collective-permute-start(f32[160,128]{1,0:T(8,128)S(1)} %gradients.1.refs_3_), channel_id=1, source_target_pairs={{0,12},{1,13},{2,14},{3,15},{4,0},{5,1},{6,2},{7,3},{8,4},{9,5},{1... | collective-permute-start | bytes 245768 | tf_op jit(solution)/shard_map/ppermute | solution.py:340
  15.3 0.1 pad_add_fusion.me_ref
  15.4 1.0 %collective-permute-done.2.refs_0_ = f32[160,128]{1,0:T(8,128)S(1)} collective-permute-done((f32[160,128]{1,0:T(8,128)S(1)}, f32[160,128]{1,0:T(8,128)S(1)}, u32[]{:S(2)}, u32[]{:S(2)}) %collective-permute-start.2) | collective-permute-done | bytes 81952 | tf_op jit(solution)/shard_map/ppermute | solution.py:340
  16.4 2.8 %collective-permute-done.3.refs_1_ = f32[160,128]{1,0:T(8,128)S(1)} collective-permute-done((f32[160,128]{1,0:T(8,128)S(1)}, f32[160,128]{1,0:T(8,128)S(1)}, u32[]{:S(2)}, u32[]{:S(2)}) %collective-permute-start.3) | collective-permute-done | bytes 81952 | tf_op jit(solution)/shard_map/ppermute | solution.py:340
  19.2 0.2 collective-permute-done.4.refs_2_
  19.4 0.9 %grams.1.refs_3_ = f32[40,128]{1,0:T(8,128)S(1)} custom-call(s32[2]{0:T(128)S(1)} %pad_add_fusion.me_ref, f32[160,128]{1,0:T(8,128)S(1)} %collective-permute-done.2.refs_0_, f32[160,128]{1,0:T(8,128)S(1)} %collective-permute-done.3.refs_1_, f32[160,128]{1,0:T(8,128)S(1)} %collective-permute-done.4.refs_2_, f32[160,128]{1,0:T(8,128)S(1)} %gradients.1.refs_3_), custom_call_target="tpu_custom_call" | custom-call | tf_op jit(solution)/shard_map/grams/pallas_call | solution.py:264
  20.3 0.0 collective-permute-start.5
  20.3 1.6 %collective-permute-start.6 = (f32[40,128]{1,0:T(8,128)S(1)}, f32[40,128]{1,0:T(8,128)S(1)}, u32[]{:S(2)}, u32[]{:S(2)}) collective-permute-start(f32[40,128]{1,0:T(8,128)S(1)} %grams.1.refs_3_), channel_id=1, source_target_pairs={{0,2},{1,3},{2,0},{3,1},{4,6},{5,7},{6,4},{7,5},{8,10},{9,11},{10,... | collective-permute-start | bytes 61448 | tf_op jit(solution)/shard_map/ppermute | solution.py:325
  21.9 0.3 %collective-permute-start.7 = (f32[40,128]{1,0:T(8,128)S(1)}, f32[40,128]{1,0:T(8,128)S(1)}, u32[]{:S(2)}, u32[]{:S(2)}) collective-permute-start(f32[40,128]{1,0:T(8,128)S(1)} %grams.1.refs_3_), channel_id=1, source_target_pairs={{0,1},{1,0},{2,3},{3,2},{4,5},{5,4},{6,7},{7,6},{8,9},{9,8},{10,11... | collective-permute-start | bytes 61448 | tf_op jit(solution)/shard_map/ppermute | solution.py:325
  22.2 1.5 %collective-permute-done.5.refs_0_ = f32[40,128]{1,0:T(8,128)S(1)} collective-permute-done((f32[40,128]{1,0:T(8,128)S(1)}, f32[40,128]{1,0:T(8,128)S(1)}, u32[]{:S(2)}, u32[]{:S(2)}) %collective-permute-start.5) | collective-permute-done | bytes 20512 | tf_op jit(solution)/shard_map/ppermute | solution.py:325
  23.7 0.5 %collective-permute-done.6.refs_1_ = f32[40,128]{1,0:T(8,128)S(1)} collective-permute-done((f32[40,128]{1,0:T(8,128)S(1)}, f32[40,128]{1,0:T(8,128)S(1)}, u32[]{:S(2)}, u32[]{:S(2)}) %collective-permute-start.6) | collective-permute-done | bytes 20512 | tf_op jit(solution)/shard_map/ppermute | solution.py:325
  24.2 0.0 collective-permute-done.7.refs_2_
  24.2 1.8 %solve.1 = f32[16,16]{1,0:T(8,128)} custom-call(f32[40,128]{1,0:T(8,128)S(1)} %collective-permute-done.5.refs_0_, f32[40,128]{1,0:T(8,128)S(1)} %collective-permute-done.6.refs_1_, f32[40,128]{1,0:T(8,128)S(1)} %collective-permute-done.7.refs_2_, f32[40,128]{1,0:T(8,128)S(1)} %grams.1.refs_3_), custom_call_target="tpu_custom_call" | custom-call | tf_op jit(solution)/shard_map/solve/pallas_call | solution.py:316
  (9 shorter events, 0.0 us)
Async XLA Ops:
  0.0 2.7 %copy-start.2 = (s32[16]{0:T(128)S(1)}, s32[16]{0:T(128)}, u32[]{:S(2)}) copy-start(s32[16]{0:T(128)} %param.12) | copy-start | bytes 196
  0.0 2.8 %copy-start.1 = (s32[256]{0:T(256)S(1)}, s32[256]{0:T(256)}, u32[]{:S(2)}) copy-start(s32[256]{0:T(256)} %param.11) | copy-start | bytes 3076
  0.0 6.7 %copy-start = (f32[4,4096]{1,0:T(4,128)S(1)}, f32[4,4096]{1,0:T(4,128)}, u32[]{:S(2)}) copy-start(f32[4,4096]{1,0:T(4,128)} %queries_ref.1) | copy-start | bytes 196612
  2.2 1.5 %collective-permute-start = (f32[96,256]{1,0:T(8,128)S(1)}, f32[96,256]{1,0:T(8,128)S(1)}, u32[]{:S(2)}, u32[]{:S(2)}) collective-permute-start(f32[96,256]{1,0:T(8,128)S(1)} %get-tuple-element.10), channel_id=1, source_target_pairs={{0,1},{1,0},{2,3},{3,2},{4,5},{5,4},{6,7},{7,6},{8,9},{9,8},{10,11... | collective-permute-start | bytes 294920 | tf_op jit(solution)/shard_map/ppermute | solution.py:325
  3.7 5.3 %collective-permute-start.1 = (f32[64,256]{1,0:T(8,128)S(1)}, f32[64,256]{1,0:T(8,128)S(1)}, u32[]{:S(2)}, u32[]{:S(2)}) collective-permute-start(f32[64,256]{1,0:T(8,128)S(1)} %get-tuple-element.12), channel_id=1, source_target_pairs={{0,2},{1,3},{2,0},{3,1},{4,6},{5,7},{6,4},{7,5},{8,10},{9,11},{10,... | collective-permute-start | bytes 196616 | tf_op jit(solution)/shard_map/ppermute | solution.py:325
  9.4 7.0 %collective-permute-start.2 = (f32[160,128]{1,0:T(8,128)S(1)}, f32[160,128]{1,0:T(8,128)S(1)}, u32[]{:S(2)}, u32[]{:S(2)}) collective-permute-start(f32[160,128]{1,0:T(8,128)S(1)} %gradients.1.refs_3_), channel_id=1, source_target_pairs={{0,4},{1,9},{2,6},{3,11},{4,8},{5,13},{6,10},{7,15},{8,12},{9,1},{... | collective-permute-start | bytes 245768 | tf_op jit(solution)/shard_map/ppermute | solution.py:340
  11.4 7.8 %collective-permute-start.3 = (f32[160,128]{1,0:T(8,128)S(1)}, f32[160,128]{1,0:T(8,128)S(1)}, u32[]{:S(2)}, u32[]{:S(2)}) collective-permute-start(f32[160,128]{1,0:T(8,128)S(1)} %gradients.1.refs_3_), channel_id=1, source_target_pairs={{0,8},{1,5},{2,10},{3,7},{4,12},{5,9},{6,14},{7,11},{8,0},{9,13},{... | collective-permute-start | bytes 245768 | tf_op jit(solution)/shard_map/ppermute | solution.py:340
  14.0 5.4 %collective-permute-start.4 = (f32[160,128]{1,0:T(8,128)S(1)}, f32[160,128]{1,0:T(8,128)S(1)}, u32[]{:S(2)}, u32[]{:S(2)}) collective-permute-start(f32[160,128]{1,0:T(8,128)S(1)} %gradients.1.refs_3_), channel_id=1, source_target_pairs={{0,12},{1,13},{2,14},{3,15},{4,0},{5,1},{6,2},{7,3},{8,4},{9,5},{1... | collective-permute-start | bytes 245768 | tf_op jit(solution)/shard_map/ppermute | solution.py:340
  20.3 3.4 %collective-permute-start.5 = (f32[40,128]{1,0:T(8,128)S(1)}, f32[40,128]{1,0:T(8,128)S(1)}, u32[]{:S(2)}, u32[]{:S(2)}) collective-permute-start(f32[40,128]{1,0:T(8,128)S(1)} %grams.1.refs_3_), channel_id=1, source_target_pairs={{0,3},{1,2},{2,1},{3,0},{4,7},{5,6},{6,5},{7,4},{8,11},{9,10},{10,... | collective-permute-start | bytes 61448 | tf_op jit(solution)/shard_map/ppermute | solution.py:325
  20.3 3.8 %collective-permute-start.6 = (f32[40,128]{1,0:T(8,128)S(1)}, f32[40,128]{1,0:T(8,128)S(1)}, u32[]{:S(2)}, u32[]{:S(2)}) collective-permute-start(f32[40,128]{1,0:T(8,128)S(1)} %grams.1.refs_3_), channel_id=1, source_target_pairs={{0,2},{1,3},{2,0},{3,1},{4,6},{5,7},{6,4},{7,5},{8,10},{9,11},{10,... | collective-permute-start | bytes 61448 | tf_op jit(solution)/shard_map/ppermute | solution.py:325
  21.9 2.3 %collective-permute-start.7 = (f32[40,128]{1,0:T(8,128)S(1)}, f32[40,128]{1,0:T(8,128)S(1)}, u32[]{:S(2)}, u32[]{:S(2)}) collective-permute-start(f32[40,128]{1,0:T(8,128)S(1)} %grams.1.refs_3_), channel_id=1, source_target_pairs={{0,1},{1,0},{2,3},{3,2},{4,5},{5,4},{6,7},{7,6},{8,9},{9,8},{10,11... | collective-permute-start | bytes 61448 | tf_op jit(solution)/shard_map/ppermute | solution.py:325

commit v28 on v14

--- a/solution.py
+++ b/solution.py
@@ -194,24 +194,26 @@
     group = out_ref.shape[1] // own
     inputs_t = summed[own:, :]
     zero = jnp.zeros_like(inputs_t)
+    half = group // 2
     right = jnp.concatenate(
         [
-            jnp.concatenate([inputs_t if j == k else zero for k in range(group)], axis=1)
-            for j in range(group)
+            jnp.concatenate([inputs_t if j == k else zero for k in range(half)], axis=1)
+            for j in range(half)
         ],
         axis=0,
     )
-    rows = []
-    for i in range(own // group):
-        rows.append(
-            jnp.concatenate(
-                [weights * summed[group * i + j : group * i + j + 1, :] for j in range(group)],
-                axis=1,
+    made = []
+    for first in (0, half):
+        rows = []
+        for i in range(first, own, group):
+            rows.append(
+                jnp.concatenate(
+                    [weights * summed[i + j : i + j + 1, :] for j in range(half)], axis=1
+                )
             )
-        )
-    left = jnp.concatenate(rows, axis=0)
-    count = left.shape[0]
-    out_ref[:count, :] = dot_nt(left, right)
+        made.append(dot_nt(jnp.concatenate(rows, axis=0), right))
+    count = made[0].shape[0]
+    out_ref[:count, :] = jnp.concatenate(made, axis=1)
     out_ref[count:, :] = asked_ref[...]
 
 

time: 25.3 us -> 25.4 us (level)
  no operation moved by 1% of the time
where the time goes in v28:
time: 25.4 us; the launch traced here: 25.2 us
  starting transfers between devices  11.2 us (44%)
  waiting for transfers between devices  8.77 us (35%)
  Pallas kernels  4.93 us (19%)
    ppermute x3, starting transfers between devices, from_all(): return [lax.ppermute(value, axis, shift) for shift in shifts] + [value]  5.94 us
    ppermute x5, starting transfers between devices, from_partner(): return lax.ppermute(value, axis, [(i, i ^ m) for i in range(size)])  5.31 us
    ppermute x5, waiting for transfers between devices, from_partner(): return lax.ppermute(value, axis, [(i, i ^ m) for i in range(size)])  4.99 us
    ppermute x3, waiting for transfers between devices, from_all(): return [lax.ppermute(value, axis, shift) for shift in shifts] + [value]  3.78 us
    pallas_call x1, Pallas kernels, project(): pl.pallas_call(functools.partial(project_kernel, own), out_shape=[jax.Sha...  2.19 us
    pallas_call x1, Pallas kernels, solve(): pl.pallas_call(functools.partial(solve_kernel, seqs), out_shape=jax.Shape...  1.82 us
  transfers between devices with their start and end apart: 8, of which 7 were waited for; matrix products, arithmetic and copies ran while one was open for 1% of the time, Pallas kernels for 1%

profile of v28, /device:TPU:0, one launch (start us, length us, event | category | flops | bytes accessed | tf_op | source)
XLA Modules:
  0.0 25.2 jit_solution(13759247565483320629)
XLA Ops:
  0.0 2.2 %project.1 = (f32[96,256]{1,0:T(8,128)S(1)}, f32[96,256]{1,0:T(8,128)S(1)}) custom-call(s32[1]{0:T(128)} %bitcast.1.rank_ref, bf16[2752,256]{1,0:T(8,128)(2,1)} %bitcast.5, bf16[256,1024]{1,0:T(8,128)(2,1)} %g_hbm.1, bf16[64,2752]{1,0:T(8,128)(2,1)} %bitcast.6, bf16[64,1024]{1,0:T(8,128)(2,1)} %bitcast.7), custom_call_target="tpu_custom_call" | custom-call | tf_op jit(solution)/shard_map/project/pallas_call | solution.py:108
  2.2 0.5 %collective-permute-start = (f32[96,256]{1,0:T(8,128)S(1)}, f32[96,256]{1,0:T(8,128)S(1)}, u32[]{:S(2)}, u32[]{:S(2)}) collective-permute-start(f32[96,256]{1,0:T(8,128)S(1)} %get-tuple-element.10), channel_id=1, source_target_pairs={{0,1},{1,0},{2,3},{3,2},{4,5},{5,4},{6,7},{7,6},{8,9},{9,8},{10,11... | collective-permute-start | bytes 294920 | tf_op jit(solution)/shard_map/ppermute | solution.py:320
  2.8 0.0 copy-done.1
  2.8 0.1 convert_reduce_fusion
  2.9 0.8 %collective-permute-done.came_ref = f32[96,256]{1,0:T(8,128)S(1)} collective-permute-done((f32[96,256]{1,0:T(8,128)S(1)}, f32[96,256]{1,0:T(8,128)S(1)}, u32[]{:S(2)}, u32[]{:S(2)}) %collective-permute-start) | collective-permute-done | bytes 98336 | tf_op jit(solution)/shard_map/ppermute | solution.py:320
  3.7 2.9 %collective-permute-start.1 = (f32[64,256]{1,0:T(8,128)S(1)}, f32[64,256]{1,0:T(8,128)S(1)}, u32[]{:S(2)}, u32[]{:S(2)}) collective-permute-start(f32[64,256]{1,0:T(8,128)S(1)} %get-tuple-element.12), channel_id=1, source_target_pairs={{0,2},{1,3},{2,0},{3,1},{4,6},{5,7},{6,4},{7,5},{8,10},{9,11},{10,... | collective-permute-start | bytes 196616 | tf_op jit(solution)/shard_map/ppermute | solution.py:320
  6.6 0.1 fusion.1.weights_ref
  6.7 0.2 pick.1.asked_ref
  6.8 2.2 %collective-permute-done.1.came_ref = f32[64,256]{1,0:T(8,128)S(1)} collective-permute-done((f32[64,256]{1,0:T(8,128)S(1)}, f32[64,256]{1,0:T(8,128)S(1)}, u32[]{:S(2)}, u32[]{:S(2)}) %collective-permute-start.1) | collective-permute-done | bytes 65568 | tf_op jit(solution)/shard_map/ppermute | solution.py:320
  9.0 0.4 %gradients.1.refs_3_ = f32[160,128]{1,0:T(8,128)S(1)} custom-call(f32[16,256]{1,0:T(8,128)S(1)} %fusion.1.weights_ref, f32[64,256]{1,0:T(8,128)S(1)} %get-tuple-element.11.kept_ref, f32[64,256]{1,0:T(8,128)S(1)} %collective-permute-done.1.came_ref, f32[32,128]{1,0:T(8,128)S(1)} %pick.1.asked_ref), custom_call_target="tpu_custom_call" | custom-call | tf_op jit(solution)/shard_map/gradients/pallas_call | solution.py:224
  9.4 2.0 %collective-permute-start.2 = (f32[160,128]{1,0:T(8,128)S(1)}, f32[160,128]{1,0:T(8,128)S(1)}, u32[]{:S(2)}, u32[]{:S(2)}) collective-permute-start(f32[160,128]{1,0:T(8,128)S(1)} %gradients.1.refs_3_), channel_id=1, source_target_pairs={{0,4},{4,8},{8,12},{12,0},{1,5},{5,9},{9,13},{13,1},{2,6},{6,10},{... | collective-permute-start | bytes 245768 | tf_op jit(solution)/shard_map/ppermute | solution.py:329
  11.4 2.6 %collective-permute-start.3 = (f32[160,128]{1,0:T(8,128)S(1)}, f32[160,128]{1,0:T(8,128)S(1)}, u32[]{:S(2)}, u32[]{:S(2)}) collective-permute-start(f32[160,128]{1,0:T(8,128)S(1)} %gradients.1.refs_3_), channel_id=1, source_target_pairs={{0,8},{4,12},{8,0},{12,4},{1,9},{5,13},{9,1},{13,5},{2,10},{6,14},... | collective-permute-start | bytes 245768 | tf_op jit(solution)/shard_map/ppermute | solution.py:329
  14.0 1.4 %collective-permute-start.4 = (f32[160,128]{1,0:T(8,128)S(1)}, f32[160,128]{1,0:T(8,128)S(1)}, u32[]{:S(2)}, u32[]{:S(2)}) collective-permute-start(f32[160,128]{1,0:T(8,128)S(1)} %gradients.1.refs_3_), channel_id=1, source_target_pairs={{0,12},{4,0},{8,4},{12,8},{1,13},{5,1},{9,5},{13,9},{2,14},{6,2},{... | collective-permute-start | bytes 245768 | tf_op jit(solution)/shard_map/ppermute | solution.py:329
  15.4 1.5 %collective-permute-done.2.refs_0_ = f32[160,128]{1,0:T(8,128)S(1)} collective-permute-done((f32[160,128]{1,0:T(8,128)S(1)}, f32[160,128]{1,0:T(8,128)S(1)}, u32[]{:S(2)}, u32[]{:S(2)}) %collective-permute-start.2) | collective-permute-done | bytes 81952 | tf_op jit(solution)/shard_map/ppermute | solution.py:329
  16.9 2.2 %collective-permute-done.3.refs_1_ = f32[160,128]{1,0:T(8,128)S(1)} collective-permute-done((f32[160,128]{1,0:T(8,128)S(1)}, f32[160,128]{1,0:T(8,128)S(1)}, u32[]{:S(2)}, u32[]{:S(2)}) %collective-permute-start.3) | collective-permute-done | bytes 81952 | tf_op jit(solution)/shard_map/ppermute | solution.py:329
  19.1 0.1 collective-permute-done.4.refs_2_
  19.2 0.3 %grams.1.refs_3_ = f32[40,128]{1,0:T(8,128)S(1)} custom-call(s32[1]{0:T(128)} %bitcast.me_ref, f32[160,128]{1,0:T(8,128)S(1)} %collective-permute-done.2.refs_0_, f32[160,128]{1,0:T(8,128)S(1)} %collective-permute-done.3.refs_1_, f32[160,128]{1,0:T(8,128)S(1)} %collective-permute-done.4.refs_2_, f32[160,128]{1,0:T(8,128)S(1)} %gradients.1.refs_3_), custom_call_target="tpu_custom_call" | custom-call | tf_op jit(solution)/shard_map/grams/pallas_call | solution.py:259
  19.5 0.0 collective-permute-start.5
  19.5 1.5 %collective-permute-start.6 = (f32[40,128]{1,0:T(8,128)S(1)}, f32[40,128]{1,0:T(8,128)S(1)}, u32[]{:S(2)}, u32[]{:S(2)}) collective-permute-start(f32[40,128]{1,0:T(8,128)S(1)} %grams.1.refs_3_), channel_id=1, source_target_pairs={{0,2},{1,3},{2,0},{3,1},{4,6},{5,7},{6,4},{7,5},{8,10},{9,11},{10,... | collective-permute-start | bytes 61448 | tf_op jit(solution)/shard_map/ppermute | solution.py:320
  21.1 0.3 %collective-permute-start.7 = (f32[40,128]{1,0:T(8,128)S(1)}, f32[40,128]{1,0:T(8,128)S(1)}, u32[]{:S(2)}, u32[]{:S(2)}) collective-permute-start(f32[40,128]{1,0:T(8,128)S(1)} %grams.1.refs_3_), channel_id=1, source_target_pairs={{0,1},{1,0},{2,3},{3,2},{4,5},{5,4},{6,7},{7,6},{8,9},{9,8},{10,11... | collective-permute-start | bytes 61448 | tf_op jit(solution)/shard_map/ppermute | solution.py:320
  21.4 1.6 %collective-permute-done.5.refs_0_ = f32[40,128]{1,0:T(8,128)S(1)} collective-permute-done((f32[40,128]{1,0:T(8,128)S(1)}, f32[40,128]{1,0:T(8,128)S(1)}, u32[]{:S(2)}, u32[]{:S(2)}) %collective-permute-start.5) | collective-permute-done | bytes 20512 | tf_op jit(solution)/shard_map/ppermute | solution.py:320
  22.9 0.4 %collective-permute-done.6.refs_1_ = f32[40,128]{1,0:T(8,128)S(1)} collective-permute-done((f32[40,128]{1,0:T(8,128)S(1)}, f32[40,128]{1,0:T(8,128)S(1)}, u32[]{:S(2)}, u32[]{:S(2)}) %collective-permute-start.6) | collective-permute-done | bytes 20512 | tf_op jit(solution)/shard_map/ppermute | solution.py:320
  23.4 0.0 collective-permute-done.7.refs_2_
  23.4 1.8 %solve.1 = f32[16,16]{1,0:T(8,128)} custom-call(f32[40,128]{1,0:T(8,128)S(1)} %collective-permute-done.5.refs_0_, f32[40,128]{1,0:T(8,128)S(1)} %collective-permute-done.6.refs_1_, f32[40,128]{1,0:T(8,128)S(1)} %collective-permute-done.7.refs_2_, f32[40,128]{1,0:T(8,128)S(1)} %grams.1.refs_3_), custom_call_target="tpu_custom_call" | custom-call | tf_op jit(solution)/shard_map/solve/pallas_call | solution.py:311
  (8 shorter events, 0.0 us)
Async XLA Ops:
  0.0 2.7 %copy-start.2 = (s32[16]{0:T(128)S(1)}, s32[16]{0:T(128)}, u32[]{:S(2)}) copy-start(s32[16]{0:T(128)} %param.12) | copy-start | bytes 196
  0.0 2.8 %copy-start.1 = (s32[256]{0:T(256)S(1)}, s32[256]{0:T(256)}, u32[]{:S(2)}) copy-start(s32[256]{0:T(256)} %param.11) | copy-start | bytes 3076
  0.0 6.7 %copy-start = (f32[4,4096]{1,0:T(4,128)S(1)}, f32[4,4096]{1,0:T(4,128)}, u32[]{:S(2)}) copy-start(f32[4,4096]{1,0:T(4,128)} %queries_ref.1) | copy-start | bytes 196612
  2.2 1.5 %collective-permute-start = (f32[96,256]{1,0:T(8,128)S(1)}, f32[96,256]{1,0:T(8,128)S(1)}, u32[]{:S(2)}, u32[]{:S(2)}) collective-permute-start(f32[96,256]{1,0:T(8,128)S(1)} %get-tuple-element.10), channel_id=1, source_target_pairs={{0,1},{1,0},{2,3},{3,2},{4,5},{5,4},{6,7},{7,6},{8,9},{9,8},{10,11... | collective-permute-start | bytes 294920 | tf_op jit(solution)/shard_map/ppermute | solution.py:320
  3.7 5.3 %collective-permute-start.1 = (f32[64,256]{1,0:T(8,128)S(1)}, f32[64,256]{1,0:T(8,128)S(1)}, u32[]{:S(2)}, u32[]{:S(2)}) collective-permute-start(f32[64,256]{1,0:T(8,128)S(1)} %get-tuple-element.12), channel_id=1, source_target_pairs={{0,2},{1,3},{2,0},{3,1},{4,6},{5,7},{6,4},{7,5},{8,10},{9,11},{10,... | collective-permute-start | bytes 196616 | tf_op jit(solution)/shard_map/ppermute | solution.py:320
  9.4 7.4 %collective-permute-start.2 = (f32[160,128]{1,0:T(8,128)S(1)}, f32[160,128]{1,0:T(8,128)S(1)}, u32[]{:S(2)}, u32[]{:S(2)}) collective-permute-start(f32[160,128]{1,0:T(8,128)S(1)} %gradients.1.refs_3_), channel_id=1, source_target_pairs={{0,4},{4,8},{8,12},{12,0},{1,5},{5,9},{9,13},{13,1},{2,6},{6,10},{... | collective-permute-start | bytes 245768 | tf_op jit(solution)/shard_map/ppermute | solution.py:329
  11.4 7.6 %collective-permute-start.3 = (f32[160,128]{1,0:T(8,128)S(1)}, f32[160,128]{1,0:T(8,128)S(1)}, u32[]{:S(2)}, u32[]{:S(2)}) collective-permute-start(f32[160,128]{1,0:T(8,128)S(1)} %gradients.1.refs_3_), channel_id=1, source_target_pairs={{0,8},{4,12},{8,0},{12,4},{1,9},{5,13},{9,1},{13,5},{2,10},{6,14},... | collective-permute-start | bytes 245768 | tf_op jit(solution)/shard_map/ppermute | solution.py:329
  14.0 5.1 %collective-permute-start.4 = (f32[160,128]{1,0:T(8,128)S(1)}, f32[160,128]{1,0:T(8,128)S(1)}, u32[]{:S(2)}, u32[]{:S(2)}) collective-permute-start(f32[160,128]{1,0:T(8,128)S(1)} %gradients.1.refs_3_), channel_id=1, source_target_pairs={{0,12},{4,0},{8,4},{12,8},{1,13},{5,1},{9,5},{13,9},{2,14},{6,2},{... | collective-permute-start | bytes 245768 | tf_op jit(solution)/shard_map/ppermute | solution.py:329
  19.5 3.4 %collective-permute-start.5 = (f32[40,128]{1,0:T(8,128)S(1)}, f32[40,128]{1,0:T(8,128)S(1)}, u32[]{:S(2)}, u32[]{:S(2)}) collective-permute-start(f32[40,128]{1,0:T(8,128)S(1)} %grams.1.refs_3_), channel_id=1, source_target_pairs={{0,3},{1,2},{2,1},{3,0},{4,7},{5,6},{6,5},{7,4},{8,11},{9,10},{10,... | collective-permute-start | bytes 61448 | tf_op jit(solution)/shard_map/ppermute | solution.py:320
  19.5 3.8 %collective-permute-start.6 = (f32[40,128]{1,0:T(8,128)S(1)}, f32[40,128]{1,0:T(8,128)S(1)}, u32[]{:S(2)}, u32[]{:S(2)}) collective-permute-start(f32[40,128]{1,0:T(8,128)S(1)} %grams.1.refs_3_), channel_id=1, source_target_pairs={{0,2},{1,3},{2,0},{3,1},{4,6},{5,7},{6,4},{7,5},{8,10},{9,11},{10,... | collective-permute-start | bytes 61448 | tf_op jit(solution)/shard_map/ppermute | solution.py:320
  21.1 2.3 %collective-permute-start.7 = (f32[40,128]{1,0:T(8,128)S(1)}, f32[40,128]{1,0:T(8,128)S(1)}, u32[]{:S(2)}, u32[]{:S(2)}) collective-permute-start(f32[40,128]{1,0:T(8,128)S(1)} %grams.1.refs_3_), channel_id=1, source_target_pairs={{0,1},{1,0},{2,3},{3,2},{4,5},{5,4},{6,7},{7,6},{8,9},{9,8},{10,11... | collective-permute-start | bytes 61448 | tf_op jit(solution)/shard_map/ppermute | solution.py:320
